TPU v7x, 32 devices: a whole 2x2x4 slice. The times are simulated.
32 devices in a mesh: grid: 8 (over z, y), tile: 4 (over x, core).
Axes of the slice: x: 2, y: 2, z: 4, core: 2. Of those that a mesh axis runs over, the one named last changes fastest.
Arguments:
- basis_values: bfloat16 [768, 256, 128], P(('grid', 'tile')), may hold values from -6 to 6
- blocks: int32 [768, 2], P(('grid', 'tile')), may hold values from 0 to 47, as said below
- counts: int32 [768], P(('grid', 'tile')), may hold values from 1 to 256, as said below
- weighted_potential: float32 [768, 256], P(('grid', 'tile')), may hold values from -0.12 to 0.12
- xc_kernel: float32 [768, 256], P(('grid', 'tile')), may hold values from -0.002 to -0.0002
- occ_coef: bfloat16 [8192, 512], P('grid'), may hold values from -0.5 to 0.5
- virt_coef: bfloat16 [8192, 7680], P('grid', 'tile'), may hold values from -0.0625 to 0.0625
- occ_energy: float32 [512], replicated, may hold values from -2 to -0.5
- virt_energy: float32 [7680], P('tile'), may hold values from 0.3 to 8
Outputs:
- response_coef: bfloat16 [8192, 512], P('grid')
- response_potential: float32 [768, 256], P(('grid', 'tile'))
Inputs may be any that keep to these rules, and one draw needn't show every extreme that they name: Each row names 2 different blocks of the window of 48 blocks around the batch's region. The live points of batch b are its first counts[b] slots; every device holds at least one full batch.
All inputs are finite; a program needn't handle non-finite values.
Results may differ from a plain program's by a relative error of at most 0.0061.
Values may be sent and summed in bfloat16 or wider, within the bound.
No kernel may reach another device: no remote copies, remote signals or barrier semaphores. Data moves between devices by JAX's collectives and lax.ppermute only.
A program may use at most 128 MiB of HBM per device.

v0:
```python
import jax
import jax.numpy as jnp
from jax import lax
from jax.sharding import PartitionSpec as P


def with_halo(array, sides, width):
    for axis, dim in sides:
        size, length = (lax.axis_size(axis), array.shape[dim])
        up = [(i, (i + 1) % size) for i in range(size)]
        down = [(j, i) for i, j in up]
        last = lax.slice_in_dim(array, length - width, length, axis=dim)
        initial = lax.slice_in_dim(array, 0, width, axis=dim)
        before = lax.ppermute(last, axis, up)
        after = lax.ppermute(initial, axis, down)
        array = jnp.concatenate([before, array, after], axis=dim)
    return array


def window_rows(window, blocks, block_rows):
    stacked = window.reshape(-1, block_rows, window.shape[1])
    picked = jnp.take(stacked, blocks, axis=0)
    return picked.reshape(blocks.shape[0], -1, window.shape[1])


def per_device(
    basis_values,
    blocks,
    counts,
    weighted_potential,
    xc_kernel,
    occ_coef,
    virt_coef,
    occ_energy,
    virt_energy,
):
    nbatch, points, columns = basis_values.shape
    per_batch = blocks.shape[1]
    block_rows = columns // per_batch
    region_rows = occ_coef.shape[0]
    occ_count = occ_coef.shape[1]
    win_blocks = 3 * region_rows // block_rows
    live_mask = lax.broadcasted_iota(jnp.int32, (nbatch, points), 1) < counts[:, None]
    occ_window = with_halo(occ_coef, (("grid", 0),), region_rows)
    occ_rows = window_rows(occ_window, blocks, block_rows)
    occ_values = jnp.einsum(
        "bpk,bko->bpo", basis_values, occ_rows, preferred_element_type=jnp.float32
    )
    weights = jnp.where(live_mask, weighted_potential, 0.0)
    scaled = (weights[:, :, None] * occ_values).astype(jnp.bfloat16)
    contrib = jnp.einsum("bpk,bpo->bko", basis_values, scaled, preferred_element_type=jnp.float32)
    contrib = contrib.reshape(nbatch * per_batch, block_rows * occ_count)
    selector = (
        blocks.reshape(1, -1) == lax.broadcasted_iota(jnp.int32, (win_blocks, 1), 0)
    ).astype(jnp.float32)
    window_sums = jnp.dot(
        selector, contrib, precision=lax.Precision.HIGHEST, preferred_element_type=jnp.float32
    )
    window_sums = window_sums.reshape(3 * region_rows, occ_count)
    padded = with_halo(window_sums, (("grid", 0),), region_rows)
    own_part = (
        padded[:region_rows] + padded[2 * region_rows : 3 * region_rows] + padded[4 * region_rows :]
    )
    ham_occ = lax.psum(own_part, "tile").astype(jnp.bfloat16)
    tile_virt = virt_coef.shape[1]
    contract_rows = (((0,), (0,)), ((), ()))
    share_rows = tile_virt // lax.axis_size("grid")
    columns_slice = virt_coef
    virt_share = lax.psum_scatter(
        lax.dot_general(columns_slice, ham_occ, contract_rows, preferred_element_type=jnp.float32),
        "grid",
        scatter_dimension=0,
        tiled=True,
    )
    energy_share = lax.dynamic_slice_in_dim(
        virt_energy, lax.axis_index("grid") * share_rows, share_rows, 0
    )
    rotation_share = (virt_share / (occ_energy[None, :] - energy_share[:, None])).astype(
        jnp.bfloat16
    )
    columns_slice = virt_coef
    coef_part = jnp.dot(
        columns_slice,
        lax.all_gather(rotation_share, "grid", axis=0, tiled=True),
        preferred_element_type=jnp.float32,
    )
    response_coef = lax.psum(coef_part, "tile").astype(jnp.bfloat16)
    coef_window = with_halo(response_coef, (("grid", 0),), region_rows)
    coef_rows = window_rows(coef_window, blocks, block_rows)
    resp_values = jnp.einsum(
        "bpk,bko->bpo", basis_values, coef_rows, preferred_element_type=jnp.float32
    )
    density = 4.0 * jnp.sum(occ_values * resp_values, axis=2)
    response_potential = jnp.where(live_mask, xc_kernel * density, 0.0)
    return (response_coef, response_potential)


def solution(mesh):
    in_specs = (
        P(("grid", "tile"), None, None),
        P(("grid", "tile"), None),
        P(("grid", "tile")),
        P(("grid", "tile"), None),
        P(("grid", "tile"), None),
        P("grid", None),
        P("grid", "tile"),
        P(),
        P("tile"),
    )
    out_specs = (P("grid", None), P(("grid", "tile"), None))
    return jax.shard_map(
        per_device, mesh=mesh, in_specs=in_specs, out_specs=out_specs, check_vma=False
    )
```

profile of v0, /device:TPU:0, one launch (start us, length us, event | category | flops | bytes accessed | tf_op | source)
XLA Modules:
  0.0 514.3 jit_solution(7330100477666764973)
XLA Ops:
  7.2 3.0 collective-permute-start
  10.2 3.1 collective-permute-start.1
  13.3 0.8 copy.40
  14.1 0.7 compare_select_fusion
  14.9 0.1 reshape.59
  15.0 0.7 compare_and_fusion
  15.7 0.1 copy.41
  15.9 0.8 fusion.4
  16.7 38.8 %collective-permute-done = bf16[1024,512]{1,0:T(8,128)(2,1)S(1)} collective-permute-done((bf16[1024,512]{1,0:T(8,128)(2,1)}, bf16[1024,512]{1,0:T(8,128)(2,1)S(1)}, u32[]{:S(2)}, u32[]{:S(2)}) %collective-permute-start) | collective-permute-done | bytes 1048608 | tf_op jit(solution)/shard_map/ppermute | solution.py:14
  55.4 2.2 collective-permute-done.1
  57.6 3.0 pad_maximum_fusion
  60.6 4.4 gather_fusion
  65.0 2.2 broadcast_select_fusion.1
  67.3 1.8 fusion.8
  69.1 4.5 copy-done.1
  73.7 4.4 fusion.2
  78.1 6.6 %copy.44 = f32[24,128,512]{2,1,0:T(8,128)} copy(f32[24,128,512]{1,2,0:T(8,128)} %fusion.2) | data formatting | bytes 12582912 | tf_op jit(solution)/shard_map/bpk,bpo->bko/dot_general | solution.py:51
  84.7 7.2 %reshape.36 = f32[48,32768]{1,0:T(8,128)} reshape(f32[24,128,512]{2,1,0:T(8,128)} %copy.44) | data formatting | bytes 12582912 | tf_op jit(solution)/shard_map/reshape | solution.py:52
  91.8 5.3 %fusion.5 = f32[48,32768]{1,0:T(8,128)S(1)} fusion(f32[48,32768]{1,0:T(8,128)} %reshape.36, s32[48]{0:T(128)S(1)} %eq.15), kind=kOutput, calls=%fused_computation.20 | convolution fusion | flops 905971968 | bytes 12583104 | tf_op jit(solution)/shard_map/dot_general | solution.py:56
  97.1 2.8 fusion.7
  99.9 2.7 slice.19
  102.6 0.2 collective-permute-start.2
  102.8 2.7 slice.23
  105.5 4.5 collective-permute-start.3
  110.1 2.8 slice.21
  112.8 79.2 %collective-permute-done.2 = f32[1024,512]{1,0:T(8,128)} collective-permute-done((f32[1024,512]{1,0:T(8,128)}, f32[1024,512]{1,0:T(8,128)}, u32[]{:S(2)}, u32[]{:S(2)}) %collective-permute-start.2) | collective-permute-done | bytes 2097184 | tf_op jit(solution)/shard_map/ppermute | solution.py:14
  192.1 4.7 collective-permute-done.3
  196.7 5.0 add_add_fusion
  201.7 42.3 %all-reduce.2 = bf16[1024,512]{1,0:T(8,128)(2,1)S(1)} all-reduce(f32[1024,512]{1,0:T(8,128)} %add_add_fusion), channel_id=1, replica_groups=mesh['grid'=8,'tile'=4] {'tile'}, use_global_device_ids=true, to_apply=%region_0.0 | all-reduce | flops 524288 | bytes 3145728 | tf_op jit(solution)/shard_map/psum | solution.py:64
  244.0 6.4 %convolution_bitcast_fusion = f32[1920,512]{0,1:T(8,128)} fusion(bf16[1024,1920]{1,0:T(8,128)(2,1)} %param.17, bf16[1024,512]{1,0:T(8,128)(2,1)S(1)} %all-reduce.2), kind=kOutput, calls=%fused_computation.6 | convolution fusion | flops 2013265920 | bytes 8912896 | tf_op jit(solution)/shard_map/dot_general | solution.py:70
  250.3 5.5 %copy.53 = f32[1920,512]{1,0:T(8,128)} copy(f32[1920,512]{0,1:T(8,128)} %convolution_bitcast_fusion) | data formatting | bytes 7864320
  255.9 0.8 dynamic_slice.3
  256.6 82.3 %reduce-scatter.4.cloned.1.call-done = f32[240,512]{1,0:T(8,128)} async-done(((f32[1920,512]{1,0:T(8,128)}), f32[240,512]{1,0:T(8,128)}) %reduce-scatter.4.cloned.1.call-update) | async-done | bytes 491536 | tf_op jit(solution)/shard_map/reduce_scatter | solution.py:69
  338.9 1.9 divide_convert_fusion
  340.8 48.3 %all-gather.2.cloned.1.call-done = bf16[1920,512]{1,0:T(8,128)(2,1)} async-done(((bf16[240,512]{1,0:T(8,128)(2,1)}), bf16[1920,512]{1,0:T(8,128)(2,1)}) %all-gather.2.cloned.1.call-update) | async-done | bytes 1966096 | tf_op jit(solution)/shard_map/all_gather | solution.py:84
  389.2 6.4 %convolution_bitcast_fusion.1 = f32[1024,512]{0,1:T(8,128)} fusion(bf16[1920,512]{1,0:T(8,128)(2,1)} %all-gather.2.cloned.1.call-done, bf16[1024,1920]{1,0:T(8,128)(2,1)} %param.17), kind=kOutput, calls=%fused_computation.13 | convolution fusion | flops 2013265920 | bytes 7995392 | tf_op jit(solution)/shard_map/dot_general | solution.py:82
  395.6 41.0 %all-reduce.3 = bf16[1024,512]{0,1:T(8,128)(2,1)S(1)} all-reduce(f32[1024,512]{0,1:T(8,128)} %convolution_bitcast_fusion.1), channel_id=1, replica_groups=mesh['grid'=8,'tile'=4] {'tile'}, use_global_device_ids=true, to_apply=%region_2.4 | all-reduce | flops 524288 | bytes 3145728 | tf_op jit(solution)/shard_map/psum | solution.py:87
  436.6 0.6 collective-permute-start.4
  437.2 4.2 collective-permute-start.5
  441.4 1.3 copy.50
  442.7 40.3 %collective-permute-done.4 = bf16[1024,512]{0,1:T(8,128)(2,1)} collective-permute-done((bf16[1024,512]{0,1:T(8,128)(2,1)S(1)}, bf16[1024,512]{0,1:T(8,128)(2,1)}, u32[]{:S(2)}, u32[]{:S(2)}) %collective-permute-start.4) | collective-permute-done | bytes 1048608 | tf_op jit(solution)/shard_map/ppermute | solution.py:14
  483.0 3.0 collective-permute-done.5
  486.0 3.0 pad_maximum_fusion.1
  488.9 4.7 copy.47
  493.6 4.4 gather_fusion.1
  498.0 2.2 broadcast_select_fusion
  500.3 6.5 %multiply_reduce_fusion = f32[24,256]{1,0:T(8,128)S(1)} fusion(f32[24,512,256]{2,1,0:T(8,128)} %copy-done.1, bf16[24,128,512]{2,1,0:T(8,128)(2,1)S(1)} %bitcast.23, bf16[24,256,128]{2,1,0:T(8,128)(2,1)S(1)} %copy-done), kind=kOutput, calls=%fused_computation.2 | convolution fusion | flops 811591680 | bytes 17326080 | tf_op jit(solution)/shard_map/bpk,bko->bpo/dot_general | solution.py:90
  506.8 0.7 multiply_select_fusion
  (16 shorter events, 0.3 us)
Async XLA Ops:
  7.2 60.1 %copy-start = (bf16[24,256,128]{2,1,0:T(8,128)(2,1)S(1)}, bf16[24,256,128]{2,1,0:T(8,128)(2,1)}, u32[]{:S(2)}) copy-start(bf16[24,256,128]{2,1,0:T(8,128)(2,1)} %param.11) | copy-start | bytes 4718596
  7.2 331.8 %reduce-scatter.4.cloned.1.call-start = ((), (), s32[]{:S(2)}) async-start(), calls=%async_computation.2 | async-start | bytes 4423680 | tf_op jit(solution)/shard_map/reduce_scatter | solution.py:69
  7.2 48.2 %collective-permute-start = (bf16[1024,512]{1,0:T(8,128)(2,1)}, bf16[1024,512]{1,0:T(8,128)(2,1)S(1)}, u32[]{:S(2)}, u32[]{:S(2)}) collective-permute-start(bf16[1024,512]{1,0:T(8,128)(2,1)} %param.16), channel_id=1, source_target_pairs={{0,4},{4,8},{8,12},{12,16},{16,20},{20,24},{24,28},{28,0},{1,5},{5... | collective-permute-start | bytes 3145736 | tf_op jit(solution)/shard_map/ppermute | solution.py:14
  10.2 47.4 %collective-permute-start.1 = (bf16[1024,512]{1,0:T(8,128)(2,1)}, bf16[1024,512]{1,0:T(8,128)(2,1)}, u32[]{:S(2)}, u32[]{:S(2)}) collective-permute-start(bf16[1024,512]{1,0:T(8,128)(2,1)} %param.16), channel_id=1, source_target_pairs={{4,0},{8,4},{12,8},{16,12},{20,16},{24,20},{28,24},{0,28},{5,1},{9... | collective-permute-start | bytes 3145736 | tf_op jit(solution)/shard_map/ppermute | solution.py:15
  69.1 4.5 copy-start.1
  102.6 89.5 %collective-permute-start.2 = (f32[1024,512]{1,0:T(8,128)}, f32[1024,512]{1,0:T(8,128)}, u32[]{:S(2)}, u32[]{:S(2)}) collective-permute-start(f32[1024,512]{1,0:T(8,128)} %slice.19), channel_id=1, source_target_pairs={{0,4},{4,8},{8,12},{12,16},{16,20},{20,24},{24,28},{28,0},{1,5},{5... | collective-permute-start | bytes 6291464 | tf_op jit(solution)/shard_map/ppermute | solution.py:14
  105.5 91.2 %collective-permute-start.3 = (f32[1024,512]{1,0:T(8,128)}, f32[1024,512]{1,0:T(8,128)}, u32[]{:S(2)}, u32[]{:S(2)}) collective-permute-start(f32[1024,512]{1,0:T(8,128)} %slice.23), channel_id=1, source_target_pairs={{4,0},{8,4},{12,8},{16,12},{20,16},{24,20},{28,24},{0,28},{5,1},{9... | collective-permute-start | bytes 6291464 | tf_op jit(solution)/shard_map/ppermute | solution.py:15
  255.8 83.2 %copy-start.3 = (f32[512]{0:T(512)S(1)}, f32[512]{0:T(512)}, u32[]{:S(2)}) copy-start(f32[512]{0:T(512)} %param.18) | copy-start | bytes 6148
  255.8 133.4 %all-gather.2.cloned.1.call-start = ((), (), s32[]{:S(2)}) async-start(), calls=%async_computation.1 | async-start | bytes 2211840 | tf_op jit(solution)/shard_map/all_gather | solution.py:84
  436.6 46.4 %collective-permute-start.4 = (bf16[1024,512]{0,1:T(8,128)(2,1)S(1)}, bf16[1024,512]{0,1:T(8,128)(2,1)}, u32[]{:S(2)}, u32[]{:S(2)}) collective-permute-start(bf16[1024,512]{0,1:T(8,128)(2,1)S(1)} %all-reduce.3), channel_id=1, source_target_pairs={{0,4},{4,8},{8,12},{12,16},{16,20},{20,24},{24,28},{28,0},{1,5},{5... | collective-permute-start | bytes 3145736 | tf_op jit(solution)/shard_map/ppermute | solution.py:14
  437.2 48.8 %collective-permute-start.5 = (bf16[1024,512]{0,1:T(8,128)(2,1)S(1)}, bf16[1024,512]{0,1:T(8,128)(2,1)}, u32[]{:S(2)}, u32[]{:S(2)}) collective-permute-start(bf16[1024,512]{0,1:T(8,128)(2,1)S(1)} %all-reduce.3), channel_id=1, source_target_pairs={{4,0},{8,4},{12,8},{16,12},{20,16},{24,20},{28,24},{0,28},{5,1},{9... | collective-permute-start | bytes 3145736 | tf_op jit(solution)/shard_map/ppermute | solution.py:15
  500.3 6.5 %copy-start.2 = (f32[24,256]{1,0:T(8,128)S(1)}, f32[24,256]{1,0:T(8,128)}, u32[]{:S(2)}) copy-start(f32[24,256]{1,0:T(8,128)} %param.15) | copy-start | bytes 73732
  500.3 6.5 %copy-start.4 = (s32[24]{0:T(128)S(1)}, s32[24]{0:T(128)}, u32[]{:S(2)}) copy-start(s32[24]{0:T(128)} %param.13) | copy-start | bytes 292
Sparse Core Ops, SparseCore 0:
  255.9 82.9 reduce-scatter.3
  341.9 47.1 all-gather.1
where the time goes:
time: 515 us; the launch traced here: 514 us
  waiting for transfers between devices  299 us (58%)
  blocking collectives  83.3 us (16%)
  local copies, waits for them, and re-layouts  51.5 us (10%)
  matrix products  30.8 us (6%)
  other arithmetic  20.1 us (4%)
  starting transfers between devices  15.7 us (3%)
  between operations  14.2 us (3%)
    ppermute x3, waiting for transfers between devices, with_halo(): before = lax.ppermute(last, axis, up)  158 us
    reduce_scatter x1, waiting for transfers between devices, per_device(): lax.psum_scatter(lax.dot_general(columns_slice, ham_occ, contract_rows, p...  82.3 us
    all_gather x1, waiting for transfers between devices, per_device(): lax.all_gather(rotation_share, 'grid', axis=0, tiled=True)  48.3 us
    psum x1, blocking collectives, per_device(): ham_occ = lax.psum(own_part, 'tile').astype(jnp.bfloat16)  42.3 us
    psum x1, blocking collectives, per_device(): response_coef = lax.psum(coef_part, 'tile').astype(jnp.bfloat16)  41 us
    unnamed x13, local copies, waits for them, and re-layouts  12.1 us
    ppermute x3, starting transfers between devices, with_halo(): after = lax.ppermute(initial, axis, down)  11.8 us
  transfers between devices with their start and end apart: 8, of which 8 were waited for; matrix products, arithmetic and copies ran while one was open for 2% of the time, Pallas kernels for 0%

commit v1 on v0

v1 whole, which is shorter than its diff:
```python
import functools

import jax
import jax.numpy as jnp
from jax import lax
from jax.experimental import pallas as pl
from jax.experimental.pallas import tpu as pltpu
from jax.sharding import PartitionSpec as P

VMEM = pl.BlockSpec(memory_space=pltpu.VMEM)
SMEM = pl.BlockSpec(memory_space=pltpu.SMEM)
LIMIT = 40 * 1024 * 1024
LANES = 128
F32 = jnp.float32
BF16 = jnp.bfloat16
NT = (((1,), (1,)), ((), ()))


def params():
    return pltpu.CompilerParams(vmem_limit_bytes=LIMIT)


def split_dot(full, other, dims):
    high = full.astype(BF16)
    low = (full - high.astype(F32)).astype(BF16)
    return lax.dot_general(high, other, dims, preferred_element_type=F32) + lax.dot_general(
        low, other, dims, preferred_element_type=F32
    )


def integrate_kernel(basis_ref, weights_ref, out_ref):
    def step(b, carry):
        values = basis_ref[b]
        weighted = values.astype(F32).T * weights_ref[b]
        out_ref[b] = split_dot(weighted, values, (((1,), (0,)), ((), ()))).astype(BF16)
        return carry

    lax.fori_loop(0, basis_ref.shape[0], step, 0, unroll=4)


def integrate(basis_values, weights):
    nbatch, points, columns = basis_values.shape
    return pl.pallas_call(
        integrate_kernel,
        out_shape=jax.ShapeDtypeStruct((nbatch, columns, columns), BF16),
        in_specs=[VMEM, VMEM],
        out_specs=VMEM,
        compiler_params=params(),
        cost_estimate=pl.CostEstimate(
            flops=4 * nbatch * points * columns * columns,
            bytes_accessed=basis_values.size * 2 + nbatch * columns * columns * 2,
            transcendentals=0,
        ),
    )(basis_values, weights.reshape(nbatch, 1, points))


def apply_kernel(pieces, per_batch, rows, *refs):
    block_refs, ham_refs = refs[:pieces], refs[pieces : 2 * pieces]
    before_ref, own_ref, after_ref = refs[2 * pieces : 2 * pieces + 3]
    out_before, out_own, out_after = refs[2 * pieces + 3 : 2 * pieces + 6]
    window, total = refs[2 * pieces + 6 :]
    region = own_ref.shape[0]
    window[:region] = before_ref[...]
    window[region : 2 * region] = own_ref[...]
    window[2 * region :] = after_ref[...]
    total[...] = jnp.zeros_like(total)
    nbatch = ham_refs[0].shape[0]

    def step(b, carry):
        places, products = [], []
        for p in range(pieces):
            place = [
                pl.ds(pl.multiple_of(block_refs[p][b, j] * rows, rows), rows)
                for j in range(per_batch)
            ]
            picked = jnp.concatenate([window[at, :] for at in place], axis=0)
            products.append(jnp.dot(ham_refs[p][b], picked, preferred_element_type=F32))
            places.append(place)
        for place, product in zip(places, products):
            for j, at in enumerate(place):
                total[at, :] += product[j * rows : (j + 1) * rows]
        return carry

    lax.fori_loop(0, nbatch, step, 0, unroll=2)
    out_before[...] = total[:region].astype(BF16)
    out_own[...] = total[region : 2 * region]
    out_after[...] = total[2 * region :].astype(BF16)


def apply_window(blocks, hams, before, own, after):
    pieces, per_batch = len(hams), blocks[0].shape[1]
    nbatch, columns = hams[0].shape[:2]
    region, width = own.shape
    return pl.pallas_call(
        functools.partial(apply_kernel, pieces, per_batch, columns // per_batch),
        out_shape=[
            jax.ShapeDtypeStruct((region, width), BF16),
            jax.ShapeDtypeStruct((region, width), F32),
            jax.ShapeDtypeStruct((region, width), BF16),
        ],
        in_specs=[SMEM] * pieces + [VMEM] * (pieces + 3),
        out_specs=[VMEM] * 3,
        scratch_shapes=[
            pltpu.VMEM((3 * region, width), BF16),
            pltpu.VMEM((3 * region, width), F32),
        ],
        compiler_params=params(),
        cost_estimate=pl.CostEstimate(
            flops=2 * pieces * nbatch * columns * columns * width,
            bytes_accessed=pieces * nbatch * columns * columns * 2 + 14 * region * width,
            transcendentals=0,
        ),
    )(*blocks, *hams, before, own, after)


def overlap_kernel(pieces, per_batch, rows, *refs):
    block_refs = refs[:pieces]
    occ_refs = refs[pieces : pieces + 6]
    resp_refs = refs[pieces + 6 : pieces + 12]
    out_refs = refs[pieces + 12 : 2 * pieces + 12]
    occ, resp = refs[2 * pieces + 12 :]
    region, width = occ_refs[0].shape
    for target, sources in ((occ, occ_refs), (resp, resp_refs)):
        for i, source in enumerate(sources):
            side, part = i // 2, i % 2
            target[side * region : (side + 1) * region, part * width : (part + 1) * width] = (
                source[...]
            )
    nbatch = out_refs[0].shape[0]

    def step(b, carry):
        for p in range(pieces):
            place = [
                pl.ds(pl.multiple_of(block_refs[p][b, j] * rows, rows), rows)
                for j in range(per_batch)
            ]
            left = jnp.concatenate([resp[at, :] for at in place], axis=0)
            right = jnp.concatenate([occ[at, :] for at in place], axis=0)
            product = lax.dot_general(left, right, NT, preferred_element_type=F32)
            out_refs[p][b] = product.astype(out_refs[p].dtype)
        return carry

    lax.fori_loop(0, nbatch, step, 0, unroll=2)


def overlaps(blocks, columns, occ_parts, resp_parts, types):
    pieces = len(blocks)
    nbatch, per_batch = blocks[0].shape
    region, width = occ_parts[0].shape
    return pl.pallas_call(
        functools.partial(overlap_kernel, pieces, per_batch, columns // per_batch),
        out_shape=[jax.ShapeDtypeStruct((nbatch, columns, columns), kind) for kind in types],
        in_specs=[SMEM] * pieces + [VMEM] * 12,
        out_specs=[VMEM] * pieces,
        scratch_shapes=[pltpu.VMEM((3 * region, 2 * width), BF16)] * 2,
        compiler_params=params(),
        cost_estimate=pl.CostEstimate(
            flops=4 * pieces * nbatch * columns * columns * width,
            bytes_accessed=24 * region * width + pieces * nbatch * columns * columns * 3,
            transcendentals=0,
        ),
    )(*blocks, *occ_parts, *resp_parts)


def density_kernel(basis_ref, first_ref, second_ref, scale_ref, out_ref):
    def step(b, carry):
        values = basis_ref[b]
        overlap = first_ref[b] + second_ref[b].astype(F32)
        product = split_dot(overlap, values, NT)
        density = jnp.sum(product * values.astype(F32).T, axis=0, keepdims=True)
        out_ref[b] = scale_ref[b] * density
        return carry

    lax.fori_loop(0, basis_ref.shape[0], step, 0, unroll=4)


def density(basis_values, first, second, scale):
    nbatch, points, columns = basis_values.shape
    out = pl.pallas_call(
        density_kernel,
        out_shape=jax.ShapeDtypeStruct((nbatch, 1, points), F32),
        in_specs=[VMEM] * 4,
        out_specs=VMEM,
        compiler_params=params(),
        cost_estimate=pl.CostEstimate(
            flops=4 * nbatch * points * columns * columns,
            bytes_accessed=basis_values.size * 2 + nbatch * columns * columns * 6,
            transcendentals=0,
        ),
    )(basis_values, first, second, scale.reshape(nbatch, 1, points))
    return out.reshape(nbatch, points)


def flip(array, axis, mask):
    return lax.ppermute(array, axis, [(i, i ^ mask) for i in range(lax.axis_size(axis))])


def neighbours(array):
    size = lax.axis_size("grid")
    before = lax.ppermute(array, "grid", [(i, (i + 1) % size) for i in range(size)])
    after = lax.ppermute(array, "grid", [((i + 1) % size, i) for i in range(size)])
    return before, after


def column_part(array, index, width):
    return lax.dynamic_slice_in_dim(array, index * width, width, 1)


def rotate(part, occ_energy, virt_energy):
    size = lax.axis_size("grid")
    if size != 8:
        total = lax.psum(part, "grid")
        return (total / (occ_energy[:, None] - virt_energy[None, :])).astype(BF16)
    index = lax.axis_index("grid")
    half = part.shape[0] // 2
    side, place = index % 2, index // 2
    keep = lax.dynamic_slice_in_dim(part, side * half, half, 0)
    send = lax.dynamic_slice_in_dim(part, (1 - side) * half, half, 0).astype(BF16)
    total = keep + flip(send, "grid", 1).astype(F32)
    inward = [(0, 2), (1, 3), (6, 4), (7, 5)]
    across = [(2, 4), (3, 5), (4, 2), (5, 3)]
    outward = [(j, i) for i, j in inward]
    total = total + lax.ppermute(total.astype(BF16), "grid", inward).astype(F32)
    total = total + lax.ppermute(total.astype(BF16), "grid", across).astype(F32)
    energy = lax.dynamic_slice_in_dim(occ_energy, side * half, half, 0)
    own = (total / (energy[:, None] - virt_energy[None, :])).astype(BF16)
    outer = (place == 0) | (place == 3)
    own = jnp.where(outer, lax.ppermute(own, "grid", outward), own)
    other = flip(own, "grid", 1)
    low, high = jnp.where(side == 0, own, other), jnp.where(side == 0, other, own)
    return jnp.concatenate([low, high], axis=0)


def per_device(
    basis_values,
    blocks,
    counts,
    weighted_potential,
    xc_kernel,
    occ_coef,
    virt_coef,
    occ_energy,
    virt_energy,
):
    nbatch, points, columns = basis_values.shape
    region, occ_count = occ_coef.shape
    width = occ_count // lax.axis_size("tile")
    tile = lax.axis_index("tile")
    chip, core = tile // 2, tile % 2
    quarter = 2 * core + chip
    live_mask = lax.broadcasted_iota(jnp.int32, (nbatch, points), 1) < counts[:, None]

    occ_own = column_part(occ_coef, quarter, width)
    occ_before, occ_after = neighbours(occ_own)

    blocks_near = flip(blocks, "tile", 1)
    blocks_far = flip(blocks, "tile", 2)
    blocks_last = flip(blocks_far, "tile", 1)
    ham = integrate(basis_values, jnp.where(live_mask, weighted_potential, 0.0))
    ham_far = flip(ham, "tile", 2)
    ham_near = flip(ham, "tile", 1)
    ham_last = flip(ham_far, "tile", 1)
    virt_near = flip(virt_coef, "tile", 1)
    energy_near = flip(virt_energy, "tile", 1)

    to_before, own_sum, to_after = apply_window(
        [blocks, blocks_near, blocks_far, blocks_last],
        [ham, ham_near, ham_far, ham_last],
        occ_before,
        occ_own,
        occ_after,
    )
    size = lax.axis_size("grid")
    from_before = lax.ppermute(to_after, "grid", [(i, (i + 1) % size) for i in range(size)])
    from_after = lax.ppermute(to_before, "grid", [((i + 1) % size, i) for i in range(size)])
    ham_own = (own_sum + from_before.astype(F32) + from_after.astype(F32)).astype(BF16)
    ham_half = jnp.concatenate([ham_own, flip(ham_own, "tile", 2)], axis=1)

    occ_far = column_part(occ_coef, quarter ^ 1, width)
    late_before, late_after, _ = lax.optimization_barrier((occ_before, occ_after, ham_half))
    before_far, after_far = flip(late_before, "tile", 2), flip(late_after, "tile", 2)

    energy_half = jnp.concatenate(
        [
            lax.dynamic_slice_in_dim(occ_energy, quarter * width, width, 0),
            lax.dynamic_slice_in_dim(occ_energy, (quarter ^ 1) * width, width, 0),
        ]
    )
    tile_virt = virt_coef.shape[1]
    cut = -(-tile_virt // (2 * LANES)) * LANES
    coef_part = None
    for virt, energy in ((virt_coef, virt_energy), (virt_near, energy_near)):
        for start, stop in ((0, cut), (cut, tile_virt)):
            columns_slice = virt[:, start:stop]
            part = lax.dot_general(
                ham_half, columns_slice, (((0,), (0,)), ((), ())), preferred_element_type=F32
            )
            rotation = rotate(part, energy_half, energy[start:stop])
            term = lax.dot_general(columns_slice, rotation, NT, preferred_element_type=F32)
            coef_part = term if coef_part is None else coef_part + term
    coef_far = flip(coef_part[:, width:].astype(BF16), "tile", 2)
    resp_own = (coef_part[:, :width] + coef_far.astype(F32)).astype(BF16)

    resp_before, resp_after = neighbours(resp_own)
    resp_far = flip(resp_own, "tile", 2)
    resp_before_far, resp_after_far = flip(resp_before, "tile", 2), flip(resp_after, "tile", 2)
    first = chip == 0
    half = jnp.concatenate(
        [jnp.where(first, resp_own, resp_far), jnp.where(first, resp_far, resp_own)], axis=1
    )
    half_near = flip(half, "tile", 1)
    first = core == 0
    response_coef = jnp.concatenate(
        [jnp.where(first, half, half_near), jnp.where(first, half_near, half)], axis=1
    )

    overlap_own, overlap_near = overlaps(
        [blocks, blocks_near],
        columns,
        [occ_before, before_far, occ_own, occ_far, occ_after, after_far],
        [resp_before, resp_before_far, resp_own, resp_far, resp_after, resp_after_far],
        [F32, BF16],
    )
    scale = jnp.where(live_mask, 4.0 * xc_kernel, 0.0)
    response_potential = density(basis_values, overlap_own, flip(overlap_near, "tile", 1), scale)
    return (response_coef, response_potential)


def solution(mesh):
    in_specs = (
        P(("grid", "tile"), None, None),
        P(("grid", "tile"), None),
        P(("grid", "tile")),
        P(("grid", "tile"), None),
        P(("grid", "tile"), None),
        P("grid", None),
        P("grid", "tile"),
        P(),
        P("tile"),
    )
    out_specs = (P("grid", None), P(("grid", "tile"), None))
    return jax.shard_map(
        per_device, mesh=mesh, in_specs=in_specs, out_specs=out_specs, check_vma=False
    )
```

time: 515 us -> 205 us (0.40)
  waiting for transfers between devices: 299 us -> 97.1 us
  blocking collectives: 83.3 us -> 0 us
  local copies, waits for them, and re-layouts: 51.5 us -> 11 us
  starting transfers between devices: 15.7 us -> 56.2 us
  matrix products: 30.8 us -> 15.5 us
  Pallas kernels: 0 us -> 13.7 us
  between operations: 14.2 us -> 1.17 us
  other arithmetic: 20.1 us -> 9.75 us
    psum x2 -> x0, blocking collectives: 83.3 us -> none  [the longest x1 42.3 us: per_device(): ham_occ = lax.psum(own_part, 'tile').astype(jnp.bfloat16)]
    reduce_scatter x1 -> x0, waiting for transfers between devices: 82.3 us -> none  [per_device(): lax.psum_scatter(lax.dot_general(columns_slice, ham_occ, contract_rows, p...]
    ppermute x6 -> x43, waiting for transfers between devices: 168 us -> 97.1 us  [the longest x25 54.1 us: flip(): lax.ppermute(array, axis, [(i, i ^ mask) for i in range(lax.axis_size(axi...]
    all_gather x1 -> x0, waiting for transfers between devices: 48.3 us -> none  [per_device(): lax.all_gather(rotation_share, 'grid', axis=0, tiled=True)]
    ppermute x6 -> x43, starting transfers between devices: 15.6 us -> 56.2 us  [the longest x25 24 us: flip(): lax.ppermute(array, axis, [(i, i ^ mask) for i in range(lax.axis_size(axi...]
    dot_general x6 -> x8, matrix products: 30.8 us -> 15.5 us  [the longest x4 9.41 us: per_device(): lax.dot_general(ham_half, columns_slice, (((0,), (0,)), ((), ())), prefer...]
    pallas_call x0 -> x4, Pallas kernels: none -> 13.7 us  [the longest x1 5.12 us: overlaps(): pl.pallas_call(functools.partial(overlap_kernel, pieces, per_batch, colum...]
    unnamed x13 -> x30, local copies, waits for them, and re-layouts: 12.1 us -> 3.1 us
  transfers between devices with their start and end apart: 8 -> 43, of which waited for: 8 -> 24; matrix products, arithmetic and copies ran while one was open for 2% -> 15% of each run, Pallas kernels for 0% -> 6%
where the time goes in v1:
time: 205 us; the launch traced here: 204 us
  waiting for transfers between devices  97.1 us (47%)
  starting transfers between devices  56.2 us (27%)
  matrix products  15.5 us (8%)
  Pallas kernels  13.7 us (7%)
  local copies, waits for them, and re-layouts  11 us (5%)
  other arithmetic  9.75 us (5%)
    ppermute x25, waiting for transfers between devices, flip(): lax.ppermute(array, axis, [(i, i ^ mask) for i in range(lax.axis_size(axi...  54.1 us
    ppermute x25, starting transfers between devices, flip(): lax.ppermute(array, axis, [(i, i ^ mask) for i in range(lax.axis_size(axi...  24 us
    ppermute x4, waiting for transfers between devices, rotate(): own = jnp.where(outer, lax.ppermute(own, 'grid', outward), own)  17.2 us
    dot_general x4, matrix products, per_device(): lax.dot_general(ham_half, columns_slice, (((0,), (0,)), ((), ())), prefer...  9.41 us
    ppermute x4, starting transfers between devices, rotate(): total = total + lax.ppermute(total.astype(BF16), 'grid', inward).astype(F32)  8.82 us
    ppermute x2, waiting for transfers between devices, neighbours(): lax.ppermute(array, 'grid', [(i, (i + 1) % size) for i in range(size)])  8.61 us
    ppermute x1, waiting for transfers between devices, per_device(): lax.ppermute(to_after, 'grid', [(i, (i + 1) % size) for i in range(size)])  6.58 us
    ppermute x2, starting transfers between devices, neighbours(): lax.ppermute(array, 'grid', [((i + 1) % size, i) for i in range(size)])  6.48 us
  transfers between devices with their start and end apart: 43, of which 24 were waited for; matrix products, arithmetic and copies ran while one was open for 15% of the time, Pallas kernels for 6%

profile of v1, /device:TPU:0, one launch (start us, length us, event | category | flops | bytes accessed | tf_op | source)
XLA Modules:
  0.0 204.5 jit_solution(16469602169940751550)
XLA Ops:
  3.4 2.1 %shard_map.104.refs_4_ = bf16[24,128,128]{2,1,0:T(8,128)(2,1)S(1)} custom-call(bf16[24,256,128]{2,1,0:T(8,128)(2,1)S(1)} %copy-done, f32[24,1,256]{2,1,0:T(1,128)S(1)} %copy.13.weights_ref), custom_call_target="tpu_custom_call" | custom-call | flops 402653184 | bytes 2359296 | tf_op jit(solution)/shard_map/pallas_call | solution.py:43
  5.6 2.6 %collective-permute-start.4 = (bf16[24,128,128]{2,1,0:T(8,128)(2,1)S(1)}, bf16[24,128,128]{2,1,0:T(8,128)(2,1)S(1)}, u32[]{:S(2)}, u32[]{:S(2)}) collective-permute-start(bf16[24,128,128]{2,1,0:T(8,128)(2,1)S(1)} %shard_map.104.refs_4_), channel_id=1, source_target_pairs={{0,2},{1,3},{2,0},{3,1},{4,6},{5,7},{6,4},{7,5},{8,10},{9,11},{10,... | collective-permute-start | bytes 2359304 | tf_op jit(solution)/shard_map/ppermute | solution.py:195
  8.4 18.0 %collective-permute-done.4.refs_6_ = bf16[24,128,128]{2,1,0:T(8,128)(2,1)S(1)} collective-permute-done((bf16[24,128,128]{2,1,0:T(8,128)(2,1)S(1)}, bf16[24,128,128]{2,1,0:T(8,128)(2,1)S(1)}, u32[]{:S(2)}, u32[]{:S(2)}) %collective-permute-start.4) | collective-permute-done | bytes 786464 | tf_op jit(solution)/shard_map/ppermute | solution.py:195
  26.4 1.7 collective-permute-start.1
  30.1 1.8 collective-permute-start.6
  32.0 4.2 %collective-permute-start.7 = (bf16[1024,128]{1,0:T(8,128)(2,1)S(1)}, bf16[1024,128]{1,0:T(8,128)(2,1)S(1)}, u32[]{:S(2)}, u32[]{:S(2)}) collective-permute-start(bf16[1024,128]{1,0:T(8,128)(2,1)S(1)} %get-tuple-element.17.refs_9_.refs_4_), channel_id=1, source_target_pairs={{4,0},{8,4},{12,8},{16,12},{20,16},{24,20},{28,24},{0,28},{5,1},{9... | collective-permute-start | bytes 786440 | tf_op jit(solution)/shard_map/ppermute | solution.py:201
  36.1 7.6 %collective-permute-done.6.refs_8_.refs_2_ = bf16[1024,128]{1,0:T(8,128)(2,1)S(1)} collective-permute-done((bf16[1024,128]{1,0:T(8,128)(2,1)S(1)}, bf16[1024,128]{1,0:T(8,128)(2,1)S(1)}, u32[]{:S(2)}, u32[]{:S(2)}) %collective-permute-start.6) | collective-permute-done | bytes 262176 | tf_op jit(solution)/shard_map/ppermute | solution.py:200
  43.8 2.2 %collective-permute-done.7.refs_10_.refs_6_ = bf16[1024,128]{1,0:T(8,128)(2,1)S(1)} collective-permute-done((bf16[1024,128]{1,0:T(8,128)(2,1)S(1)}, bf16[1024,128]{1,0:T(8,128)(2,1)S(1)}, u32[]{:S(2)}, u32[]{:S(2)}) %collective-permute-start.7) | collective-permute-done | bytes 262176 | tf_op jit(solution)/shard_map/ppermute | solution.py:201
  46.0 4.6 %shard_map.105 = (bf16[1024,128]{1,0:T(8,128)(2,1)S(1)}, f32[1024,128]{1,0:T(8,128)S(1)}, bf16[1024,128]{1,0:T(8,128)(2,1)S(1)}) custom-call(s32[24,2]{1,0:T(8,128)S(1)} %copy.14.refs_0_, s32[24,2]{1,0:T(8,128)S(1)} %collective-permute-done.refs_1_, s32[24,2]{1,0:T(8,128)S(1)} %collective-permute-done.1.refs_2_, s32[24,2]{1,0:T(8,128)S(1)} %collective-permute-done.2.refs_3_, ...), custom_call_target="tpu_custom_call" | custom-call | flops 402653184 | bytes 4980736 | tf_op jit(solution)/shard_map/pallas_call | solution.py:94
  50.9 4.4 %collective-permute-start.9 = (bf16[1024,128]{1,0:T(8,128)(2,1)S(1)}, bf16[1024,128]{1,0:T(8,128)(2,1)S(1)}, u32[]{:S(2)}, u32[]{:S(2)}) collective-permute-start(bf16[1024,128]{1,0:T(8,128)(2,1)S(1)} %get-tuple-element.11), channel_id=1, source_target_pairs={{4,0},{8,4},{12,8},{16,12},{20,16},{24,20},{28,24},{0,28},{5,1},{9... | collective-permute-start | bytes 786440 | tf_op jit(solution)/shard_map/ppermute | solution.py:275
  55.3 6.6 %collective-permute-done.8 = bf16[1024,128]{1,0:T(8,128)(2,1)S(1)} collective-permute-done((bf16[1024,128]{1,0:T(8,128)(2,1)S(1)}, bf16[1024,128]{1,0:T(8,128)(2,1)S(1)}, u32[]{:S(2)}, u32[]{:S(2)}) %collective-permute-start.8) | collective-permute-done | bytes 262176 | tf_op jit(solution)/shard_map/ppermute | solution.py:274
  61.9 3.2 %collective-permute-done.9 = bf16[1024,128]{1,0:T(8,128)(2,1)S(1)} collective-permute-done((bf16[1024,128]{1,0:T(8,128)(2,1)S(1)}, bf16[1024,128]{1,0:T(8,128)(2,1)S(1)}, u32[]{:S(2)}, u32[]{:S(2)}) %collective-permute-start.9) | collective-permute-done | bytes 262176 | tf_op jit(solution)/shard_map/ppermute | solution.py:275
  65.3 1.6 collective-permute-start.10
  66.9 5.8 %collective-permute-done.10 = bf16[1024,128]{1,0:T(8,128)(2,1)S(1)} collective-permute-done((bf16[1024,128]{1,0:T(8,128)(2,1)S(1)}, bf16[1024,128]{1,0:T(8,128)(2,1)S(1)}, u32[]{:S(2)}, u32[]{:S(2)}) %collective-permute-start.10) | collective-permute-done | bytes 262176 | tf_op jit(solution)/shard_map/ppermute | solution.py:195
  72.7 2.3 %fusion.14 = f32[256,896]{1,0:T(8,128)S(1)} fusion(bf16[1024,1920]{1,0:T(8,128)(2,1)} %param.15, bf16[1024,128]{1,0:T(8,128)(2,1)S(1)} %collective-permute-done.10, bf16[1024,128]{1,0:T(8,128)(2,1)S(1)} %add_convert_fusion), kind=kOutput, calls=%fused_computation.14 | convolution fusion | flops 470810624 | bytes 3276800 | tf_op jit(solution)/shard_map/dot_general | solution.py:295
  75.8 2.4 %fusion.6 = f32[256,1024]{1,0:T(8,128)S(1)} fusion(bf16[1024,1920]{1,0:T(8,128)(2,1)} %param.15, bf16[1024,128]{1,0:T(8,128)(2,1)} %copy-done.5, bf16[1024,128]{1,0:T(8,128)(2,1)S(1)} %add_convert_fusion), kind=kOutput, calls=%fused_computation.6 | convolution fusion | flops 537919488 | bytes 3670016 | tf_op jit(solution)/shard_map/dot_general | solution.py:295
  79.0 2.0 collective-permute-start.11
  86.8 4.2 %collective-permute-start.17 = (bf16[128,896]{1,0:T(8,128)(2,1)S(1)}, bf16[128,896]{1,0:T(8,128)(2,1)S(1)}, u32[]{:S(2)}, u32[]{:S(2)}) collective-permute-start(bf16[128,896]{1,0:T(8,128)(2,1)S(1)} %fusion.47), channel_id=1, source_target_pairs={{0,8},{4,12},{24,16},{28,20},{1,9},{5,13},{25,17},{29,21},{2,10},{... | collective-permute-start | bytes 688136 | tf_op jit(solution)/shard_map/ppermute | solution.py:223
  92.1 1.7 collective-permute-start.12
  93.8 2.4 %fusion.2 = f32[256,1024]{1,0:T(8,128)S(1)} fusion(bf16[1024,1920]{1,0:T(8,128)(2,1)} %collective-permute-done.21, bf16[1024,128]{1,0:T(8,128)(2,1)} %copy-done.5, bf16[1024,128]{1,0:T(8,128)(2,1)S(1)} %add_convert_fusion), kind=kOutput, calls=%fused_computation.2 | convolution fusion | flops 537919488 | bytes 3670016 | tf_op jit(solution)/shard_map/dot_general | solution.py:295
  96.6 2.2 %fusion.10 = f32[256,896]{1,0:T(8,128)S(1)} fusion(bf16[1024,1920]{1,0:T(8,128)(2,1)} %collective-permute-done.21, bf16[1024,128]{1,0:T(8,128)(2,1)S(1)} %copy-done.6, bf16[1024,128]{1,0:T(8,128)(2,1)S(1)} %add_convert_fusion), kind=kOutput, calls=%fused_computation.10 | convolution fusion | flops 470810624 | bytes 3276800 | tf_op jit(solution)/shard_map/dot_general | solution.py:295
  98.9 1.8 collective-permute-start.28
  101.5 6.1 %collective-permute-done.28 = bf16[128,896]{1,0:T(8,128)(2,1)S(1)} collective-permute-done((bf16[128,896]{1,0:T(8,128)(2,1)S(1)}, bf16[128,896]{1,0:T(8,128)(2,1)S(1)}, u32[]{:S(2)}, u32[]{:S(2)}) %collective-permute-start.28) | collective-permute-done | bytes 229408 | tf_op jit(solution)/shard_map/ppermute | solution.py:195
  107.7 1.6 collective-permute-start.29
  112.4 2.1 %collective-permute-done.29 = bf16[128,896]{1,0:T(8,128)(2,1)S(1)} collective-permute-done((bf16[128,896]{1,0:T(8,128)(2,1)S(1)}, bf16[128,896]{1,0:T(8,128)(2,1)S(1)}, u32[]{:S(2)}, u32[]{:S(2)}) %collective-permute-start.29) | collective-permute-done | bytes 229408 | tf_op jit(solution)/shard_map/ppermute | solution.py:223
  115.3 2.0 collective-permute-done.23
  121.2 1.5 divide_convert_fusion.1
  125.3 9.7 %collective-permute-done.19 = bf16[128,896]{1,0:T(8,128)(2,1)S(1)} collective-permute-done((bf16[128,896]{1,0:T(8,128)(2,1)S(1)}, bf16[128,896]{1,0:T(8,128)(2,1)S(1)}, u32[]{:S(2)}, u32[]{:S(2)}) %collective-permute-start.19) | collective-permute-done | bytes 229408 | tf_op jit(solution)/shard_map/ppermute | solution.py:228
  136.1 3.8 %collective-permute-done.31 = bf16[128,896]{1,0:T(8,128)(2,1)S(1)} collective-permute-done((bf16[128,896]{1,0:T(8,128)(2,1)S(1)}, bf16[128,896]{1,0:T(8,128)(2,1)S(1)}, u32[]{:S(2)}, u32[]{:S(2)}) %collective-permute-start.31) | collective-permute-done | bytes 229408 | tf_op jit(solution)/shard_map/ppermute | solution.py:228
  141.0 2.4 %collective-permute-done.14 = bf16[128,1024]{1,0:T(8,128)(2,1)S(1)} collective-permute-done((bf16[128,1024]{1,0:T(8,128)(2,1)S(1)}, bf16[128,1024]{1,0:T(8,128)(2,1)S(1)}, u32[]{:S(2)}, u32[]{:S(2)}) %collective-permute-start.14) | collective-permute-done | bytes 262176 | tf_op jit(solution)/shard_map/ppermute | solution.py:228
  148.5 2.2 %fusion.8 = f32[256,1024]{0,1:T(8,128)S(1)} fusion(bf16[1024,1920]{1,0:T(8,128)(2,1)} %collective-permute-done.21, bf16[128,896]{1,0:T(8,128)(2,1)S(1)} %get-tuple-element.29, bf16[128,896]{1,0:T(8,128)(2,1)S(1)} %get-tuple-element.28), kind=kOutput, calls=%fused_computation.8 | convolution fusion | flops 470679552 | bytes 3342336 | tf_op jit(solution)/shard_map/dot_general | solution.py:299
  151.8 2.8 %collective-permute-done.27 = bf16[128,1024]{1,0:T(8,128)(2,1)S(1)} collective-permute-done((bf16[128,1024]{1,0:T(8,128)(2,1)S(1)}, bf16[128,1024]{1,0:T(8,128)(2,1)S(1)}, u32[]{:S(2)}, u32[]{:S(2)}) %collective-permute-start.27) | collective-permute-done | bytes 262176 | tf_op jit(solution)/shard_map/ppermute | solution.py:195
  154.7 2.3 %fusion = f32[256,1024]{0,1:T(8,128)S(1)} fusion(bf16[1024,1920]{1,0:T(8,128)(2,1)} %collective-permute-done.21, bf16[128,1024]{1,0:T(8,128)(2,1)S(1)} %get-tuple-element.25, bf16[128,1024]{1,0:T(8,128)(2,1)S(1)} %get-tuple-element.24), kind=kOutput, calls=%fused_computation | convolution fusion | flops 537919488 | bytes 3670016 | tf_op jit(solution)/shard_map/dot_general | solution.py:299
  157.8 1.5 collective-permute-start.33
  159.3 4.9 %collective-permute-done.33 = bf16[1024,128]{1,0:T(8,128)(2,1)S(1)} collective-permute-done((bf16[1024,128]{1,0:T(8,128)(2,1)S(1)}, bf16[1024,128]{1,0:T(8,128)(2,1)S(1)}, u32[]{:S(2)}, u32[]{:S(2)}) %collective-permute-start.33) | collective-permute-done | bytes 262176 | tf_op jit(solution)/shard_map/ppermute | solution.py:195
  164.3 2.5 %collective-permute-start.38 = (bf16[1024,128]{1,0:T(8,128)(2,1)S(1)}, bf16[1024,128]{1,0:T(8,128)(2,1)S(1)}, u32[]{:S(2)}, u32[]{:S(2)}) collective-permute-start(bf16[1024,128]{1,0:T(8,128)(2,1)S(1)} %fusion.28.refs_10_), channel_id=1, source_target_pairs={{0,4},{4,8},{8,12},{12,16},{16,20},{20,24},{24,28},{28,0},{1,5},{5... | collective-permute-start | bytes 786440 | tf_op jit(solution)/shard_map/ppermute | solution.py:200
  166.8 2.3 %collective-permute-start.40 = (bf16[1024,128]{1,0:T(8,128)(2,1)S(1)}, bf16[1024,128]{1,0:T(8,128)(2,1)S(1)}, u32[]{:S(2)}, u32[]{:S(2)}) collective-permute-start(bf16[1024,128]{1,0:T(8,128)(2,1)S(1)} %fusion.28.refs_10_), channel_id=1, source_target_pairs={{4,0},{8,4},{12,8},{16,12},{20,16},{24,20},{28,24},{0,28},{5,1},{9... | collective-permute-start | bytes 786440 | tf_op jit(solution)/shard_map/ppermute | solution.py:201
  169.1 1.5 collective-permute-start.34
  171.1 1.5 collective-permute-start.37
  173.5 1.5 collective-permute-start.39
  175.9 1.5 collective-permute-start.41
  179.3 4.6 %collective-permute-done.36.refs_3_ = bf16[1024,128]{1,0:T(8,128)(2,1)S(1)} collective-permute-done((bf16[1024,128]{1,0:T(8,128)(2,1)S(1)}, bf16[1024,128]{1,0:T(8,128)(2,1)S(1)}, u32[]{:S(2)}, u32[]{:S(2)}) %collective-permute-start.36) | collective-permute-done | bytes 262176 | tf_op jit(solution)/shard_map/ppermute | solution.py:195
  183.9 3.7 %collective-permute-done.37.refs_7_ = bf16[1024,128]{1,0:T(8,128)(2,1)S(1)} collective-permute-done((bf16[1024,128]{1,0:T(8,128)(2,1)S(1)}, bf16[1024,128]{1,0:T(8,128)(2,1)S(1)}, u32[]{:S(2)}, u32[]{:S(2)}) %collective-permute-start.37) | collective-permute-done | bytes 262176 | tf_op jit(solution)/shard_map/ppermute | solution.py:195
  187.6 2.8 %collective-permute-done.39.refs_9_ = bf16[1024,128]{1,0:T(8,128)(2,1)S(1)} collective-permute-done((bf16[1024,128]{1,0:T(8,128)(2,1)S(1)}, bf16[1024,128]{1,0:T(8,128)(2,1)S(1)}, u32[]{:S(2)}, u32[]{:S(2)}) %collective-permute-start.39) | collective-permute-done | bytes 262176 | tf_op jit(solution)/shard_map/ppermute | solution.py:195
  190.4 2.8 %collective-permute-done.41.refs_13_ = bf16[1024,128]{1,0:T(8,128)(2,1)S(1)} collective-permute-done((bf16[1024,128]{1,0:T(8,128)(2,1)S(1)}, bf16[1024,128]{1,0:T(8,128)(2,1)S(1)}, u32[]{:S(2)}, u32[]{:S(2)}) %collective-permute-start.41) | collective-permute-done | bytes 262176 | tf_op jit(solution)/shard_map/ppermute | solution.py:195
  194.2 5.1 %shard_map.106 = (f32[24,128,128]{2,1,0:T(8,128)S(1)}, bf16[24,128,128]{2,1,0:T(8,128)(2,1)}) custom-call(s32[24,2]{1,0:T(8,128)S(1)} %copy.14.refs_0_, s32[24,2]{1,0:T(8,128)S(1)} %collective-permute-done.refs_1_, bf16[1024,128]{1,0:T(8,128)(2,1)S(1)} %collective-permute-done.6.refs_8_.refs_2_, bf16[1024,128]{1,0:T(8,128)(2,1)S(1)} %collective-permute-done.36.refs_3_, ...), custom_call_target="tpu_custom_call" | custom-call | flops 402653184 | bytes 5505024 | tf_op jit(solution)/shard_map/pallas_call | solution.py:150
  199.4 1.5 broadcast_select_fusion.1
  201.9 1.9 shard_map.107
  (120 shorter events, 41.6 us)
Async XLA Ops:
  0.6 25.7 %copy-start.12 = (s32[24,2]{0,1:T(2,128)S(1)}, s32[24,2]{0,1:T(2,128)}, u32[]{:S(2)}) copy-start(s32[24,2]{0,1:T(2,128)} %param.10) | copy-start | bytes 580
  0.6 93.2 %collective-permute-start.21 = (bf16[1024,1920]{1,0:T(8,128)(2,1)}, bf16[1024,1920]{1,0:T(8,128)(2,1)}, u32[]{:S(2)}, u32[]{:S(2)}) collective-permute-start(bf16[1024,1920]{1,0:T(8,128)(2,1)} %param.15), channel_id=1, source_target_pairs={{0,1},{1,0},{2,3},{3,2},{4,5},{5,4},{6,7},{7,6},{8,9},{9,8},{10,11... | collective-permute-start | bytes 11796488 | tf_op jit(solution)/shard_map/ppermute | solution.py:195
  5.6 20.8 %collective-permute-start.4 = (bf16[24,128,128]{2,1,0:T(8,128)(2,1)S(1)}, bf16[24,128,128]{2,1,0:T(8,128)(2,1)S(1)}, u32[]{:S(2)}, u32[]{:S(2)}) collective-permute-start(bf16[24,128,128]{2,1,0:T(8,128)(2,1)S(1)} %shard_map.104.refs_4_), channel_id=1, source_target_pairs={{0,2},{1,3},{2,0},{3,1},{4,6},{5,7},{6,4},{7,5},{8,10},{9,11},{10,... | collective-permute-start | bytes 2359304 | tf_op jit(solution)/shard_map/ppermute | solution.py:195
  8.1 37.8 %collective-permute-start.3 = (bf16[24,128,128]{2,1,0:T(8,128)(2,1)S(1)}, bf16[24,128,128]{2,1,0:T(8,128)(2,1)S(1)}, u32[]{:S(2)}, u32[]{:S(2)}) collective-permute-start(bf16[24,128,128]{2,1,0:T(8,128)(2,1)S(1)} %shard_map.104.refs_4_), channel_id=1, source_target_pairs={{0,1},{1,0},{2,3},{3,2},{4,5},{5,4},{6,7},{7,6},{8,9},{9,8},{10,11... | collective-permute-start | bytes 2359304 | tf_op jit(solution)/shard_map/ppermute | solution.py:195
  26.3 19.6 %collective-permute-start.5 = (bf16[24,128,128]{2,1,0:T(8,128)(2,1)S(1)}, bf16[24,128,128]{2,1,0:T(8,128)(2,1)}, u32[]{:S(2)}, u32[]{:S(2)}) collective-permute-start(bf16[24,128,128]{2,1,0:T(8,128)(2,1)S(1)} %collective-permute-done.4.refs_6_), channel_id=1, source_target_pairs={{0,1},{1,0},{2,3},{3,2},{4,5},{5,4},{6,7},{7,6},{8,9},{9,8},{10,11... | collective-permute-start | bytes 2359304 | tf_op jit(solution)/shard_map/ppermute | solution.py:195
  26.4 3.7 %collective-permute-start.1 = (s32[24,2]{1,0:T(8,128)S(1)}, s32[24,2]{1,0:T(8,128)S(1)}, u32[]{:S(2)}, u32[]{:S(2)}) collective-permute-start(s32[24,2]{1,0:T(8,128)S(1)} %copy.14.refs_0_), channel_id=1, source_target_pairs={{0,2},{1,3},{2,0},{3,1},{4,6},{5,7},{6,4},{7,5},{8,10},{9,11},{10,... | collective-permute-start | bytes 584 | tf_op jit(solution)/shard_map/ppermute | solution.py:195
  28.2 2.0 collective-permute-start
  30.1 1.8 collective-permute-start.2
  30.1 36.7 %copy-start.13 = (f32[512]{0:T(512)S(1)}, f32[512]{0:T(512)}, u32[]{:S(2)}) copy-start(f32[512]{0:T(512)} %param.16) | copy-start | bytes 6148
  30.1 13.6 %collective-permute-start.6 = (bf16[1024,128]{1,0:T(8,128)(2,1)S(1)}, bf16[1024,128]{1,0:T(8,128)(2,1)S(1)}, u32[]{:S(2)}, u32[]{:S(2)}) collective-permute-start(bf16[1024,128]{1,0:T(8,128)(2,1)S(1)} %get-tuple-element.17.refs_9_.refs_4_), channel_id=1, source_target_pairs={{0,4},{4,8},{8,12},{12,16},{16,20},{20,24},{24,28},{28,0},{1,5},{5... | collective-permute-start | bytes 786440 | tf_op jit(solution)/shard_map/ppermute | solution.py:200
  32.0 14.0 %collective-permute-start.7 = (bf16[1024,128]{1,0:T(8,128)(2,1)S(1)}, bf16[1024,128]{1,0:T(8,128)(2,1)S(1)}, u32[]{:S(2)}, u32[]{:S(2)}) collective-permute-start(bf16[1024,128]{1,0:T(8,128)(2,1)S(1)} %get-tuple-element.17.refs_9_.refs_4_), channel_id=1, source_target_pairs={{4,0},{8,4},{12,8},{16,12},{20,16},{24,20},{28,24},{0,28},{5,1},{9... | collective-permute-start | bytes 786440 | tf_op jit(solution)/shard_map/ppermute | solution.py:201
  50.6 11.4 %collective-permute-start.8 = (bf16[1024,128]{1,0:T(8,128)(2,1)S(1)}, bf16[1024,128]{1,0:T(8,128)(2,1)S(1)}, u32[]{:S(2)}, u32[]{:S(2)}) collective-permute-start(bf16[1024,128]{1,0:T(8,128)(2,1)S(1)} %get-tuple-element.10), channel_id=1, source_target_pairs={{0,4},{4,8},{8,12},{12,16},{16,20},{20,24},{24,28},{28,0},{1,5},{5... | collective-permute-start | bytes 786440 | tf_op jit(solution)/shard_map/ppermute | solution.py:274
  50.9 14.3 %collective-permute-start.9 = (bf16[1024,128]{1,0:T(8,128)(2,1)S(1)}, bf16[1024,128]{1,0:T(8,128)(2,1)S(1)}, u32[]{:S(2)}, u32[]{:S(2)}) collective-permute-start(bf16[1024,128]{1,0:T(8,128)(2,1)S(1)} %get-tuple-element.11), channel_id=1, source_target_pairs={{4,0},{8,4},{12,8},{16,12},{20,16},{24,20},{28,24},{0,28},{5,1},{9... | collective-permute-start | bytes 786440 | tf_op jit(solution)/shard_map/ppermute | solution.py:275
  65.3 7.5 %collective-permute-start.10 = (bf16[1024,128]{1,0:T(8,128)(2,1)S(1)}, bf16[1024,128]{1,0:T(8,128)(2,1)S(1)}, u32[]{:S(2)}, u32[]{:S(2)}) collective-permute-start(bf16[1024,128]{1,0:T(8,128)(2,1)S(1)} %add_convert_fusion), channel_id=1, source_target_pairs={{0,2},{1,3},{2,0},{3,1},{4,6},{5,7},{6,4},{7,5},{8,10},{9,11},{10,... | collective-permute-start | bytes 786440 | tf_op jit(solution)/shard_map/ppermute | solution.py:195
  66.8 18.6 %collective-permute-start.25 = (f32[1920]{0:T(1024)}, f32[1920]{0:T(1024)}, u32[]{:S(2)}, u32[]{:S(2)}) collective-permute-start(f32[1920]{0:T(1024)} %param.17), channel_id=1, source_target_pairs={{0,1},{1,0},{2,3},{3,2},{4,5},{5,4},{6,7},{7,6},{8,9},{9,8},{10,11... | collective-permute-start | bytes 23048 | tf_op jit(solution)/shard_map/ppermute | solution.py:195
  75.8 10.9 %collective-permute-start.16 = (bf16[128,896]{1,0:T(8,128)(2,1)}, bf16[128,896]{1,0:T(8,128)(2,1)S(1)}, u32[]{:S(2)}, u32[]{:S(2)}) collective-permute-start(bf16[128,896]{1,0:T(8,128)(2,1)} %dynamic-slice_convert_fusion.3), channel_id=1, source_target_pairs={{0,4},{4,0},{8,12},{12,8},{16,20},{20,16},{24,28},{28,24},{1,5},{5... | collective-permute-start | bytes 688136 | tf_op jit(solution)/shard_map/ppermute | solution.py:195
  79.0 12.1 %collective-permute-start.11 = (bf16[128,1024]{1,0:T(8,128)(2,1)}, bf16[128,1024]{1,0:T(8,128)(2,1)}, u32[]{:S(2)}, u32[]{:S(2)}) collective-permute-start(bf16[128,1024]{1,0:T(8,128)(2,1)} %dynamic-slice_convert_fusion.1), channel_id=1, source_target_pairs={{0,4},{4,0},{8,12},{12,8},{16,20},{20,16},{24,28},{28,24},{1,5},{5... | collective-permute-start | bytes 786440 | tf_op jit(solution)/shard_map/ppermute | solution.py:195
  86.8 13.9 %collective-permute-start.17 = (bf16[128,896]{1,0:T(8,128)(2,1)S(1)}, bf16[128,896]{1,0:T(8,128)(2,1)S(1)}, u32[]{:S(2)}, u32[]{:S(2)}) collective-permute-start(bf16[128,896]{1,0:T(8,128)(2,1)S(1)} %fusion.47), channel_id=1, source_target_pairs={{0,8},{4,12},{24,16},{28,20},{1,9},{5,13},{25,17},{29,21},{2,10},{... | collective-permute-start | bytes 688136 | tf_op jit(solution)/shard_map/ppermute | solution.py:223
  92.1 18.6 %collective-permute-start.12 = (bf16[128,1024]{1,0:T(8,128)(2,1)S(1)}, bf16[128,1024]{1,0:T(8,128)(2,1)S(1)}, u32[]{:S(2)}, u32[]{:S(2)}) collective-permute-start(bf16[128,1024]{1,0:T(8,128)(2,1)S(1)} %fusion.45), channel_id=1, source_target_pairs={{0,8},{4,12},{24,16},{28,20},{1,9},{5,13},{25,17},{29,21},{2,10},{... | collective-permute-start | bytes 786440 | tf_op jit(solution)/shard_map/ppermute | solution.py:223
  96.3 12.9 %collective-permute-start.22 = (bf16[128,1024]{1,0:T(8,128)(2,1)S(1)}, bf16[128,1024]{1,0:T(8,128)(2,1)S(1)}, u32[]{:S(2)}, u32[]{:S(2)}) collective-permute-start(bf16[128,1024]{1,0:T(8,128)(2,1)S(1)} %dynamic-slice_convert_fusion), channel_id=1, source_target_pairs={{0,4},{4,0},{8,12},{12,8},{16,20},{20,16},{24,28},{28,24},{1,5},{5... | collective-permute-start | bytes 786440 | tf_op jit(solution)/shard_map/ppermute | solution.py:195
  98.9 8.7 %collective-permute-start.28 = (bf16[128,896]{1,0:T(8,128)(2,1)S(1)}, bf16[128,896]{1,0:T(8,128)(2,1)S(1)}, u32[]{:S(2)}, u32[]{:S(2)}) collective-permute-start(bf16[128,896]{1,0:T(8,128)(2,1)S(1)} %dynamic-slice_convert_fusion.2), channel_id=1, source_target_pairs={{0,4},{4,0},{8,12},{12,8},{16,20},{20,16},{24,28},{28,24},{1,5},{5... | collective-permute-start | bytes 688136 | tf_op jit(solution)/shard_map/ppermute | solution.py:195
  100.8 17.3 %collective-permute-start.18 = (bf16[128,896]{1,0:T(8,128)(2,1)S(1)}, bf16[128,896]{1,0:T(8,128)(2,1)S(1)}, u32[]{:S(2)}, u32[]{:S(2)}) collective-permute-start(bf16[128,896]{1,0:T(8,128)(2,1)S(1)} %fusion.43), channel_id=1, source_target_pairs={{8,16},{12,20},{16,8},{20,12},{9,17},{13,21},{17,9},{21,13},{10,18... | collective-permute-start | bytes 688136 | tf_op jit(solution)/shard_map/ppermute | solution.py:224
  107.7 6.9 %collective-permute-start.29 = (bf16[128,896]{1,0:T(8,128)(2,1)S(1)}, bf16[128,896]{1,0:T(8,128)(2,1)S(1)}, u32[]{:S(2)}, u32[]{:S(2)}) collective-permute-start(bf16[128,896]{1,0:T(8,128)(2,1)S(1)} %fusion.48), channel_id=1, source_target_pairs={{0,8},{4,12},{24,16},{28,20},{1,9},{5,13},{25,17},{29,21},{2,10},{... | collective-permute-start | bytes 688136 | tf_op jit(solution)/shard_map/ppermute | solution.py:223
  109.3 8.0 %collective-permute-start.23 = (bf16[128,1024]{1,0:T(8,128)(2,1)S(1)}, bf16[128,1024]{1,0:T(8,128)(2,1)S(1)}, u32[]{:S(2)}, u32[]{:S(2)}) collective-permute-start(bf16[128,1024]{1,0:T(8,128)(2,1)S(1)} %fusion.46), channel_id=1, source_target_pairs={{0,8},{4,12},{24,16},{28,20},{1,9},{5,13},{25,17},{29,21},{2,10},{... | collective-permute-start | bytes 786440 | tf_op jit(solution)/shard_map/ppermute | solution.py:223
  111.7 9.4 %collective-permute-start.13 = (bf16[128,1024]{1,0:T(8,128)(2,1)S(1)}, bf16[128,1024]{1,0:T(8,128)(2,1)S(1)}, u32[]{:S(2)}, u32[]{:S(2)}) collective-permute-start(bf16[128,1024]{1,0:T(8,128)(2,1)S(1)} %fusion.41), channel_id=1, source_target_pairs={{8,16},{12,20},{16,8},{20,12},{9,17},{13,21},{17,9},{21,13},{10,18... | collective-permute-start | bytes 786440 | tf_op jit(solution)/shard_map/ppermute | solution.py:224
  114.6 3.5 %collective-permute-start.30 = (bf16[128,896]{1,0:T(8,128)(2,1)S(1)}, bf16[128,896]{1,0:T(8,128)(2,1)S(1)}, u32[]{:S(2)}, u32[]{:S(2)}) collective-permute-start(bf16[128,896]{1,0:T(8,128)(2,1)S(1)} %fusion.44), channel_id=1, source_target_pairs={{8,16},{12,20},{16,8},{20,12},{9,17},{13,21},{17,9},{21,13},{10,18... | collective-permute-start | bytes 688136 | tf_op jit(solution)/shard_map/ppermute | solution.py:224
  117.4 3.7 %collective-permute-start.24 = (bf16[128,1024]{1,0:T(8,128)(2,1)S(1)}, bf16[128,1024]{1,0:T(8,128)(2,1)S(1)}, u32[]{:S(2)}, u32[]{:S(2)}) collective-permute-start(bf16[128,1024]{1,0:T(8,128)(2,1)S(1)} %fusion.42), channel_id=1, source_target_pairs={{8,16},{12,20},{16,8},{20,12},{9,17},{13,21},{17,9},{21,13},{10,18... | collective-permute-start | bytes 786440 | tf_op jit(solution)/shard_map/ppermute | solution.py:224
  118.5 16.5 %collective-permute-start.19 = (bf16[128,896]{1,0:T(8,128)(2,1)S(1)}, bf16[128,896]{1,0:T(8,128)(2,1)S(1)}, u32[]{:S(2)}, u32[]{:S(2)}) collective-permute-start(bf16[128,896]{1,0:T(8,128)(2,1)S(1)} %get-tuple-element.36), channel_id=1, source_target_pairs={{8,0},{12,4},{16,24},{20,28},{9,1},{13,5},{17,25},{21,29},{10,2},{... | collective-permute-start | bytes 688136 | tf_op jit(solution)/shard_map/ppermute | solution.py:228
  119.8 20.1 %collective-permute-start.31 = (bf16[128,896]{1,0:T(8,128)(2,1)S(1)}, bf16[128,896]{1,0:T(8,128)(2,1)S(1)}, u32[]{:S(2)}, u32[]{:S(2)}) collective-permute-start(bf16[128,896]{1,0:T(8,128)(2,1)S(1)} %get-tuple-element.37), channel_id=1, source_target_pairs={{8,0},{12,4},{16,24},{20,28},{9,1},{13,5},{17,25},{21,29},{10,2},{... | collective-permute-start | bytes 688136 | tf_op jit(solution)/shard_map/ppermute | solution.py:228
  121.1 26.6 %copy-start.4 = (bf16[1024,1920]{1,0:T(8,128)(2,1)S(1)}, bf16[1024,1920]{1,0:T(8,128)(2,1)}, u32[]{:S(2)}) copy-start(bf16[1024,1920]{1,0:T(8,128)(2,1)} %param.15) | copy-start | bytes 11796484
  122.7 20.7 %collective-permute-start.14 = (bf16[128,1024]{1,0:T(8,128)(2,1)S(1)}, bf16[128,1024]{1,0:T(8,128)(2,1)S(1)}, u32[]{:S(2)}, u32[]{:S(2)}) collective-permute-start(bf16[128,1024]{1,0:T(8,128)(2,1)S(1)} %get-tuple-element.34), channel_id=1, source_target_pairs={{8,0},{12,4},{16,24},{20,28},{9,1},{13,5},{17,25},{21,29},{10,2},{... | collective-permute-start | bytes 786440 | tf_op jit(solution)/shard_map/ppermute | solution.py:228
  124.0 22.2 %collective-permute-start.26 = (bf16[128,1024]{1,0:T(8,128)(2,1)S(1)}, bf16[128,1024]{1,0:T(8,128)(2,1)S(1)}, u32[]{:S(2)}, u32[]{:S(2)}) collective-permute-start(bf16[128,1024]{1,0:T(8,128)(2,1)S(1)} %get-tuple-element.35), channel_id=1, source_target_pairs={{8,0},{12,4},{16,24},{20,28},{9,1},{13,5},{17,25},{21,29},{10,2},{... | collective-permute-start | bytes 786440 | tf_op jit(solution)/shard_map/ppermute | solution.py:228
  135.0 12.6 %collective-permute-start.20 = (bf16[128,896]{1,0:T(8,128)(2,1)S(1)}, bf16[128,896]{1,0:T(8,128)(2,1)S(1)}, u32[]{:S(2)}, u32[]{:S(2)}) collective-permute-start(bf16[128,896]{1,0:T(8,128)(2,1)S(1)} %broadcast_select_fusion.11), channel_id=1, source_target_pairs={{0,4},{4,0},{8,12},{12,8},{16,20},{20,16},{24,28},{28,24},{1,5},{5... | collective-permute-start | bytes 688136 | tf_op jit(solution)/shard_map/ppermute | solution.py:195
  139.9 8.5 %collective-permute-start.32 = (bf16[128,896]{1,0:T(8,128)(2,1)S(1)}, bf16[128,896]{1,0:T(8,128)(2,1)S(1)}, u32[]{:S(2)}, u32[]{:S(2)}) collective-permute-start(bf16[128,896]{1,0:T(8,128)(2,1)S(1)} %broadcast_select_fusion.10), channel_id=1, source_target_pairs={{0,4},{4,0},{8,12},{12,8},{16,20},{20,16},{24,28},{28,24},{1,5},{5... | collective-permute-start | bytes 688136 | tf_op jit(solution)/shard_map/ppermute | solution.py:195
  143.4 8.4 %collective-permute-start.15 = (bf16[128,1024]{1,0:T(8,128)(2,1)S(1)}, bf16[128,1024]{1,0:T(8,128)(2,1)S(1)}, u32[]{:S(2)}, u32[]{:S(2)}) collective-permute-start(bf16[128,1024]{1,0:T(8,128)(2,1)S(1)} %broadcast_select_fusion.3), channel_id=1, source_target_pairs={{0,4},{4,0},{8,12},{12,8},{16,20},{20,16},{24,28},{28,24},{1,5},{5... | collective-permute-start | bytes 786440 | tf_op jit(solution)/shard_map/ppermute | solution.py:195
  146.2 8.4 %collective-permute-start.27 = (bf16[128,1024]{1,0:T(8,128)(2,1)S(1)}, bf16[128,1024]{1,0:T(8,128)(2,1)S(1)}, u32[]{:S(2)}, u32[]{:S(2)}) collective-permute-start(bf16[128,1024]{1,0:T(8,128)(2,1)S(1)} %broadcast_select_fusion.2), channel_id=1, source_target_pairs={{0,4},{4,0},{8,12},{12,8},{16,20},{20,16},{24,28},{28,24},{1,5},{5... | collective-permute-start | bytes 786440 | tf_op jit(solution)/shard_map/ppermute | solution.py:195
  157.8 6.4 %collective-permute-start.33 = (bf16[1024,128]{1,0:T(8,128)(2,1)S(1)}, bf16[1024,128]{1,0:T(8,128)(2,1)S(1)}, u32[]{:S(2)}, u32[]{:S(2)}) collective-permute-start(bf16[1024,128]{1,0:T(8,128)(2,1)S(1)} %slice.75), channel_id=1, source_target_pairs={{0,2},{1,3},{2,0},{3,1},{4,6},{5,7},{6,4},{7,5},{8,10},{9,11},{10,... | collective-permute-start | bytes 786440 | tf_op jit(solution)/shard_map/ppermute | solution.py:195
  164.3 9.2 %collective-permute-start.38 = (bf16[1024,128]{1,0:T(8,128)(2,1)S(1)}, bf16[1024,128]{1,0:T(8,128)(2,1)S(1)}, u32[]{:S(2)}, u32[]{:S(2)}) collective-permute-start(bf16[1024,128]{1,0:T(8,128)(2,1)S(1)} %fusion.28.refs_10_), channel_id=1, source_target_pairs={{0,4},{4,8},{8,12},{12,16},{16,20},{20,24},{24,28},{28,0},{1,5},{5... | collective-permute-start | bytes 786440 | tf_op jit(solution)/shard_map/ppermute | solution.py:200
  166.8 9.2 %collective-permute-start.40 = (bf16[1024,128]{1,0:T(8,128)(2,1)S(1)}, bf16[1024,128]{1,0:T(8,128)(2,1)S(1)}, u32[]{:S(2)}, u32[]{:S(2)}) collective-permute-start(bf16[1024,128]{1,0:T(8,128)(2,1)S(1)} %fusion.28.refs_10_), channel_id=1, source_target_pairs={{4,0},{8,4},{12,8},{16,12},{20,16},{24,20},{28,24},{0,28},{5,1},{9... | collective-permute-start | bytes 786440 | tf_op jit(solution)/shard_map/ppermute | solution.py:201
  169.1 9.2 %collective-permute-start.34 = (bf16[1024,128]{1,0:T(8,128)(2,1)S(1)}, bf16[1024,128]{1,0:T(8,128)(2,1)S(1)}, u32[]{:S(2)}, u32[]{:S(2)}) collective-permute-start(bf16[1024,128]{1,0:T(8,128)(2,1)S(1)} %fusion.28.refs_10_), channel_id=1, source_target_pairs={{0,2},{1,3},{2,0},{3,1},{4,6},{5,7},{6,4},{7,5},{8,10},{9,11},{10,... | collective-permute-start | bytes 786440 | tf_op jit(solution)/shard_map/ppermute | solution.py:195
  170.5 13.4 %collective-permute-start.36 = (bf16[1024,128]{1,0:T(8,128)(2,1)S(1)}, bf16[1024,128]{1,0:T(8,128)(2,1)S(1)}, u32[]{:S(2)}, u32[]{:S(2)}) collective-permute-start(bf16[1024,128]{1,0:T(8,128)(2,1)S(1)} %collective-permute-done.6.refs_8_.refs_2_), channel_id=1, source_target_pairs={{0,2},{1,3},{2,0},{3,1},{4,6},{5,7},{6,4},{7,5},{8,10},{9,11},{10,... | collective-permute-start | bytes 786440 | tf_op jit(solution)/shard_map/ppermute | solution.py:195
  171.1 16.5 %collective-permute-start.37 = (bf16[1024,128]{1,0:T(8,128)(2,1)S(1)}, bf16[1024,128]{1,0:T(8,128)(2,1)S(1)}, u32[]{:S(2)}, u32[]{:S(2)}) collective-permute-start(bf16[1024,128]{1,0:T(8,128)(2,1)S(1)} %collective-permute-done.7.refs_10_.refs_6_), channel_id=1, source_target_pairs={{0,2},{1,3},{2,0},{3,1},{4,6},{5,7},{6,4},{7,5},{8,10},{9,11},{10,... | collective-permute-start | bytes 786440 | tf_op jit(solution)/shard_map/ppermute | solution.py:195
  173.5 16.9 %collective-permute-start.39 = (bf16[1024,128]{1,0:T(8,128)(2,1)S(1)}, bf16[1024,128]{1,0:T(8,128)(2,1)S(1)}, u32[]{:S(2)}, u32[]{:S(2)}) collective-permute-start(bf16[1024,128]{1,0:T(8,128)(2,1)S(1)} %collective-permute-done.38.refs_8_), channel_id=1, source_target_pairs={{0,2},{1,3},{2,0},{3,1},{4,6},{5,7},{6,4},{7,5},{8,10},{9,11},{10,... | collective-permute-start | bytes 786440 | tf_op jit(solution)/shard_map/ppermute | solution.py:195
  175.9 17.3 %copy-start.2 = (bf16[1024,128]{1,0:T(8,128)(2,1)}, bf16[1024,128]{1,0:T(8,128)(2,1)S(1)}, u32[]{:S(2)}) copy-start(bf16[1024,128]{1,0:T(8,128)(2,1)S(1)} %collective-permute-done.40.refs_12_) | copy-start | bytes 786436
  175.9 17.3 %collective-permute-start.41 = (bf16[1024,128]{1,0:T(8,128)(2,1)S(1)}, bf16[1024,128]{1,0:T(8,128)(2,1)S(1)}, u32[]{:S(2)}, u32[]{:S(2)}) collective-permute-start(bf16[1024,128]{1,0:T(8,128)(2,1)S(1)} %collective-permute-done.40.refs_12_), channel_id=1, source_target_pairs={{0,2},{1,3},{2,0},{3,1},{4,6},{5,7},{6,4},{7,5},{8,10},{9,11},{10,... | collective-permute-start | bytes 786440 | tf_op jit(solution)/shard_map/ppermute | solution.py:195
  178.4 14.9 %copy-start.7 = (bf16[1024,128]{1,0:T(8,128)(2,1)}, bf16[1024,128]{1,0:T(8,128)(2,1)S(1)}, u32[]{:S(2)}) copy-start(bf16[1024,128]{1,0:T(8,128)(2,1)S(1)} %get-tuple-element.20) | copy-start | bytes 786436
  179.3 20.1 %collective-permute-start.35 = (bf16[1024,256]{1,0:T(8,128)(2,1)}, bf16[1024,256]{1,0:T(8,128)(2,1)}, u32[]{:S(2)}, u32[]{:S(2)}) collective-permute-start(bf16[1024,256]{1,0:T(8,128)(2,1)} %pad_maximum_fusion.2), channel_id=1, source_target_pairs={{0,1},{1,0},{2,3},{3,2},{4,5},{5,4},{6,7},{7,6},{8,9},{9,8},{10,11... | collective-permute-start | bytes 1572872 | tf_op jit(solution)/shard_map/ppermute | solution.py:195
  199.3 2.6 %collective-permute-start.42 = (bf16[24,128,128]{2,1,0:T(8,128)(2,1)}, bf16[24,128,128]{2,1,0:T(8,128)(2,1)S(1)}, u32[]{:S(2)}, u32[]{:S(2)}) collective-permute-start(bf16[24,128,128]{2,1,0:T(8,128)(2,1)} %get-tuple-element.15), channel_id=1, source_target_pairs={{0,1},{1,0},{2,3},{3,2},{4,5},{5,4},{6,7},{7,6},{8,9},{9,8},{10,11... | collective-permute-start | bytes 2359304 | tf_op jit(solution)/shard_map/ppermute | solution.py:195
  (9 other events, 51.7 us)

commit v2 on v1

--- a/solution.py
+++ b/solution.py
@@ -10,7 +10,6 @@
 VMEM = pl.BlockSpec(memory_space=pltpu.VMEM)
 SMEM = pl.BlockSpec(memory_space=pltpu.SMEM)
 LIMIT = 40 * 1024 * 1024
-LANES = 128
 F32 = jnp.float32
 BF16 = jnp.bfloat16
 NT = (((1,), (1,)), ((), ()))
@@ -28,30 +27,94 @@
     )
 
 
-def integrate_kernel(basis_ref, weights_ref, out_ref):
+def triangle(size):
+    rows = lax.broadcasted_iota(jnp.int32, (size, size), 0)
+    return rows, lax.broadcasted_iota(jnp.int32, (size, size), 1)
+
+
+def integrate_kernel(basis_ref, weights_ref, full_ref, packed_ref, diagonal):
+    nbatch = basis_ref.shape[0]
+    half = basis_ref.shape[2] // 2
+    row, column = triangle(half)
+    diagonal[...] = jnp.zeros_like(diagonal)
+
     def step(b, carry):
         values = basis_ref[b]
         weighted = values.astype(F32).T * weights_ref[b]
-        out_ref[b] = split_dot(weighted, values, (((1,), (0,)), ((), ()))).astype(BF16)
+        ham = split_dot(weighted, values, (((1,), (0,)), ((), ())))
+        full_ref[b] = ham.astype(BF16)
+        last = ham[half:, half:]
+        mixed = jnp.where(row >= column, ham[:half, :half], last)
+        packed = jnp.concatenate([ham[:half, half:], mixed], axis=1)
+        packed_ref[pl.ds(pl.multiple_of(b * half, half), half), :] = packed.astype(BF16)
+        line = jnp.sum(jnp.where(row == column, last, 0.0), axis=0, keepdims=True)
+        diagonal[pl.ds(b, 1), :] = jnp.concatenate([line, jnp.zeros_like(line)], axis=1)
         return carry
 
-    lax.fori_loop(0, basis_ref.shape[0], step, 0, unroll=4)
+    lax.fori_loop(0, nbatch, step, 0, unroll=4)
+    packed_ref[nbatch * half :, :] = diagonal[...].astype(BF16)
+
+
+def padded_rows(nbatch):
+    return -(-nbatch // 32) * 32
 
 
 def integrate(basis_values, weights):
     nbatch, points, columns = basis_values.shape
+    extra = padded_rows(nbatch)
     return pl.pallas_call(
         integrate_kernel,
-        out_shape=jax.ShapeDtypeStruct((nbatch, columns, columns), BF16),
+        out_shape=[
+            jax.ShapeDtypeStruct((nbatch, columns, columns), BF16),
+            jax.ShapeDtypeStruct((nbatch * columns // 2 + extra, columns), BF16),
+        ],
         in_specs=[VMEM, VMEM],
-        out_specs=VMEM,
+        out_specs=[VMEM, VMEM],
+        scratch_shapes=[pltpu.VMEM((extra, columns), F32)],
         compiler_params=params(),
         cost_estimate=pl.CostEstimate(
             flops=4 * nbatch * points * columns * columns,
-            bytes_accessed=basis_values.size * 2 + nbatch * columns * columns * 2,
+            bytes_accessed=basis_values.size * 2 + nbatch * columns * columns * 3,
             transcendentals=0,
         ),
     )(basis_values, weights.reshape(nbatch, 1, points))
+
+
+def unpack_kernel(packed_ref, full_ref, diagonal):
+    nbatch = full_ref.shape[0]
+    half = full_ref.shape[1] // 2
+    row, column = triangle(half)
+    diagonal[...] = packed_ref[nbatch * half :, :].astype(F32)
+
+    def step(b, carry):
+        packed = packed_ref[pl.ds(pl.multiple_of(b * half, half), half), :].astype(F32)
+        turned = packed.T
+        mixed, mixed_turned = packed[:, half:], turned[half:]
+        first = jnp.where(row >= column, mixed, mixed_turned)
+        last = jnp.where(row < column, mixed, mixed_turned)
+        last = jnp.where(row == column, diagonal[pl.ds(b, 1), :][:, :half], last)
+        upper = jnp.concatenate([first, packed[:, :half]], axis=1)
+        lower = jnp.concatenate([turned[:half], last], axis=1)
+        full_ref[b] = jnp.concatenate([upper, lower], axis=0).astype(BF16)
+        return carry
+
+    lax.fori_loop(0, nbatch, step, 0, unroll=4)
+
+
+def unpack(packed, nbatch, columns):
+    return pl.pallas_call(
+        unpack_kernel,
+        out_shape=jax.ShapeDtypeStruct((nbatch, columns, columns), BF16),
+        in_specs=[VMEM],
+        out_specs=VMEM,
+        scratch_shapes=[pltpu.VMEM((padded_rows(nbatch), columns), F32)],
+        compiler_params=params(),
+        cost_estimate=pl.CostEstimate(
+            flops=nbatch * columns * columns * 4,
+            bytes_accessed=nbatch * columns * columns * 3,
+            transcendentals=0,
+        ),
+    )(packed)
 
 
 def apply_kernel(pieces, per_batch, rows, *refs):
@@ -256,9 +319,11 @@
     blocks_near = flip(blocks, "tile", 1)
     blocks_far = flip(blocks, "tile", 2)
     blocks_last = flip(blocks_far, "tile", 1)
-    ham = integrate(basis_values, jnp.where(live_mask, weighted_potential, 0.0))
-    ham_far = flip(ham, "tile", 2)
+    weights = jnp.where(live_mask, weighted_potential, 0.0)
+    ham, ham_packed = integrate(basis_values, weights)
     ham_near = flip(ham, "tile", 1)
+    ham_far = unpack(flip(ham_packed, "tile", 2), nbatch, columns)
+    ham_far, occ_before, occ_after = lax.optimization_barrier((ham_far, occ_before, occ_after))
     ham_last = flip(ham_far, "tile", 1)
     virt_near = flip(virt_coef, "tile", 1)
     energy_near = flip(virt_energy, "tile", 1)
@@ -274,32 +339,28 @@
     from_before = lax.ppermute(to_after, "grid", [(i, (i + 1) % size) for i in range(size)])
     from_after = lax.ppermute(to_before, "grid", [((i + 1) % size, i) for i in range(size)])
     ham_own = (own_sum + from_before.astype(F32) + from_after.astype(F32)).astype(BF16)
-    ham_half = jnp.concatenate([ham_own, flip(ham_own, "tile", 2)], axis=1)
+    ham_sums = [ham_own, flip(ham_own, "tile", 2)]
 
     occ_far = column_part(occ_coef, quarter ^ 1, width)
-    late_before, late_after, _ = lax.optimization_barrier((occ_before, occ_after, ham_half))
+    late_before, late_after, _ = lax.optimization_barrier((occ_before, occ_after, ham_sums[1]))
     before_far, after_far = flip(late_before, "tile", 2), flip(late_after, "tile", 2)
 
-    energy_half = jnp.concatenate(
-        [
-            lax.dynamic_slice_in_dim(occ_energy, quarter * width, width, 0),
-            lax.dynamic_slice_in_dim(occ_energy, (quarter ^ 1) * width, width, 0),
-        ]
-    )
-    tile_virt = virt_coef.shape[1]
-    cut = -(-tile_virt // (2 * LANES)) * LANES
-    coef_part = None
-    for virt, energy in ((virt_coef, virt_energy), (virt_near, energy_near)):
-        for start, stop in ((0, cut), (cut, tile_virt)):
-            columns_slice = virt[:, start:stop]
-            part = lax.dot_general(
-                ham_half, columns_slice, (((0,), (0,)), ((), ())), preferred_element_type=F32
-            )
-            rotation = rotate(part, energy_half, energy[start:stop])
-            term = lax.dot_general(columns_slice, rotation, NT, preferred_element_type=F32)
-            coef_part = term if coef_part is None else coef_part + term
-    coef_far = flip(coef_part[:, width:].astype(BF16), "tile", 2)
-    resp_own = (coef_part[:, :width] + coef_far.astype(F32)).astype(BF16)
+    levels = [
+        lax.dynamic_slice_in_dim(occ_energy, place * width, width, 0)
+        for place in (quarter, quarter ^ 1)
+    ]
+    virtuals = [(virt_coef, virt_energy), (virt_near, energy_near)]
+    coefs = [None, None]
+    for part, share in ((0, 0), (1, 0), (1, 1), (0, 1)):
+        virt, energy = virtuals[share]
+        virt_ham = lax.dot_general(
+            ham_sums[part], virt, (((0,), (0,)), ((), ())), preferred_element_type=F32
+        )
+        rotation = rotate(virt_ham, levels[part], energy)
+        term = lax.dot_general(virt, rotation, NT, preferred_element_type=F32)
+        coefs[part] = term if coefs[part] is None else coefs[part] + term
+    coef_far = flip(coefs[1].astype(BF16), "tile", 2)
+    resp_own = (coefs[0] + coef_far.astype(F32)).astype(BF16)
 
     resp_before, resp_after = neighbours(resp_own)
     resp_far = flip(resp_own, "tile", 2)

time: 205 us -> 212 us (1.034)
  matrix products: 15.5 us -> 24.6 us
  local copies, waits for them, and re-layouts: 11 us -> 5.46 us
  Pallas kernels: 13.7 us -> 17.6 us
  starting transfers between devices: 56.2 us -> 52.4 us
    ppermute x4, waiting for transfers between devices: 17.2 us -> 34.2 us  [rotate(): own = jnp.where(outer, lax.ppermute(own, 'grid', outward), own)]
    ppermute x25, waiting for transfers between devices: 54.1 us -> 39.6 us  [flip(): lax.ppermute(array, axis, [(i, i ^ mask) for i in range(lax.axis_size(axi...]
    dot_general x8, matrix products: 15.5 us -> 24.6 us  [the longest x4 13.2 us: per_device(): term = lax.dot_general(virt, rotation, NT, preferred_element_type=F32)]
    ppermute x25, starting transfers between devices: 24 us -> 18.2 us  [flip(): lax.ppermute(array, axis, [(i, i ^ mask) for i in range(lax.axis_size(axi...]
    ppermute x2, waiting for transfers between devices: 8.61 us -> 4.34 us  [neighbours(): lax.ppermute(array, 'grid', [(i, (i + 1) % size) for i in range(size)])]
    slice x5 -> x0, local copies, waits for them, and re-layouts: 3.95 us -> none  [the longest x4 3.91 us: per_device(): rotation = rotate(part, energy_half, energy[start:stop])]
    ppermute x4, starting transfers between devices: 8.82 us -> 12 us  [rotate(): total = total + lax.ppermute(total.astype(BF16), 'grid', inward).astype(F32)]
    pallas_call x1 -> x2, Pallas kernels: 2.13 us -> 4.78 us  [the longest x1 2.97 us: integrate(): pl.pallas_call(integrate_kernel, out_shape=[jax.ShapeDtypeStruct((nbatch,...]
  transfers between devices with their start and end apart: 43 -> 43, of which waited for: 24 -> 27; matrix products, arithmetic and copies ran while one was open for 15% -> 15% of each run, Pallas kernels for 6% -> 3%
where the time goes in v2:
time: 212 us; the launch traced here: 211 us
  waiting for transfers between devices  98.6 us (47%)
  starting transfers between devices  52.4 us (25%)
  matrix products  24.6 us (12%)
  Pallas kernels  17.6 us (8%)
  other arithmetic  11.3 us (5%)
  local copies, waits for them, and re-layouts  5.46 us (3%)
    ppermute x25, waiting for transfers between devices, flip(): lax.ppermute(array, axis, [(i, i ^ mask) for i in range(lax.axis_size(axi...  39.6 us
    ppermute x4, waiting for transfers between devices, rotate(): own = jnp.where(outer, lax.ppermute(own, 'grid', outward), own)  34.2 us
    ppermute x25, starting transfers between devices, flip(): lax.ppermute(array, axis, [(i, i ^ mask) for i in range(lax.axis_size(axi...  18.2 us
    dot_general x4, matrix products, per_device(): term = lax.dot_general(virt, rotation, NT, preferred_element_type=F32)  13.2 us
    ppermute x4, starting transfers between devices, rotate(): total = total + lax.ppermute(total.astype(BF16), 'grid', inward).astype(F32)  12 us
    dot_general x4, matrix products, per_device(): lax.dot_general(ham_sums[part], virt, (((0,), (0,)), ((), ())), preferred...  11.4 us
    ppermute x2, starting transfers between devices, neighbours(): lax.ppermute(array, 'grid', [((i + 1) % size, i) for i in range(size)])  6.24 us
    ppermute x4, waiting for transfers between devices, rotate(): total = total + lax.ppermute(total.astype(BF16), 'grid', inward).astype(F32)  6.23 us
  transfers between devices with their start and end apart: 43, of which 27 were waited for; matrix products, arithmetic and copies ran while one was open for 15% of the time, Pallas kernels for 3%

profile of v2, /device:TPU:0, one launch (start us, length us, event | category | flops | bytes accessed | tf_op | source)
XLA Modules:
  0.0 211.1 jit_solution(7080310220518004203)
XLA Ops:
  3.5 3.0 %shard_map.104 = (bf16[24,128,128]{2,1,0:T(8,128)(2,1)S(1)}, bf16[1568,128]{1,0:T(8,128)(2,1)S(1)}) custom-call(bf16[24,256,128]{2,1,0:T(8,128)(2,1)S(1)} %copy-done, f32[24,1,256]{2,1,0:T(1,128)S(1)} %copy.13.weights_ref), custom_call_target="tpu_custom_call" | custom-call | flops 402653184 | bytes 2752512 | tf_op jit(solution)/shard_map/pallas_call | solution.py:65
  6.5 3.0 %collective-permute-start.4 = (bf16[1568,128]{1,0:T(8,128)(2,1)S(1)}, bf16[1568,128]{1,0:T(8,128)(2,1)S(1)}, u32[]{:S(2)}, u32[]{:S(2)}) collective-permute-start(bf16[1568,128]{1,0:T(8,128)(2,1)S(1)} %get-tuple-element.15), channel_id=1, source_target_pairs={{0,2},{1,3},{2,0},{3,1},{4,6},{5,7},{6,4},{7,5},{8,10},{9,11},{10,... | collective-permute-start | bytes 1204232 | tf_op jit(solution)/shard_map/ppermute | solution.py:258
  10.6 1.6 collective-permute-start.5
  12.2 3.2 %collective-permute-start.6 = (bf16[1024,128]{1,0:T(8,128)(2,1)S(1)}, bf16[1024,128]{1,0:T(8,128)(2,1)S(1)}, u32[]{:S(2)}, u32[]{:S(2)}) collective-permute-start(bf16[1024,128]{1,0:T(8,128)(2,1)S(1)} %get-tuple-element.27.refs_9_.refs_4_), channel_id=1, source_target_pairs={{4,0},{8,4},{12,8},{16,12},{20,16},{24,20},{28,24},{0,28},{5,1},{9... | collective-permute-start | bytes 786440 | tf_op jit(solution)/shard_map/ppermute | solution.py:264
  15.4 3.4 %collective-permute-done.4.packed_ref = bf16[1568,128]{1,0:T(8,128)(2,1)S(1)} collective-permute-done((bf16[1568,128]{1,0:T(8,128)(2,1)S(1)}, bf16[1568,128]{1,0:T(8,128)(2,1)S(1)}, u32[]{:S(2)}, u32[]{:S(2)}) %collective-permute-start.4) | collective-permute-done | bytes 401440 | tf_op jit(solution)/shard_map/ppermute | solution.py:258
  18.8 1.8 shard_map.105.refs_6_
  20.6 2.5 %collective-permute-done.5.refs_8_.refs_2_ = bf16[1024,128]{1,0:T(8,128)(2,1)S(1)} collective-permute-done((bf16[1024,128]{1,0:T(8,128)(2,1)S(1)}, bf16[1024,128]{1,0:T(8,128)(2,1)S(1)}, u32[]{:S(2)}, u32[]{:S(2)}) %collective-permute-start.5) | collective-permute-done | bytes 262176 | tf_op jit(solution)/shard_map/ppermute | solution.py:263
  23.1 2.2 %collective-permute-done.6.refs_10_.refs_6_ = bf16[1024,128]{1,0:T(8,128)(2,1)S(1)} collective-permute-done((bf16[1024,128]{1,0:T(8,128)(2,1)S(1)}, bf16[1024,128]{1,0:T(8,128)(2,1)S(1)}, u32[]{:S(2)}, u32[]{:S(2)}) %collective-permute-start.6) | collective-permute-done | bytes 262176 | tf_op jit(solution)/shard_map/ppermute | solution.py:264
  26.1 2.9 %collective-permute-done.1.refs_2_ = s32[24,2]{1,0:T(8,128)S(1)} collective-permute-done((s32[24,2]{1,0:T(8,128)S(1)}, s32[24,2]{1,0:T(8,128)S(1)}, u32[]{:S(2)}, u32[]{:S(2)}) %collective-permute-start.1) | collective-permute-done | bytes 224 | tf_op jit(solution)/shard_map/ppermute | solution.py:258
  30.2 4.6 %shard_map.106 = (bf16[1024,128]{1,0:T(8,128)(2,1)S(1)}, f32[1024,128]{1,0:T(8,128)S(1)}, bf16[1024,128]{1,0:T(8,128)(2,1)S(1)}) custom-call(s32[24,2]{1,0:T(8,128)S(1)} %copy.14.refs_0_, s32[24,2]{1,0:T(8,128)S(1)} %collective-permute-done.refs_1_, s32[24,2]{1,0:T(8,128)S(1)} %collective-permute-done.1.refs_2_, s32[24,2]{1,0:T(8,128)S(1)} %collective-permute-done.2.refs_3_, ...), custom_call_target="tpu_custom_call" | custom-call | flops 402653184 | bytes 4980736 | tf_op jit(solution)/shard_map/pallas_call | solution.py:157
  35.7 3.3 %collective-permute-start.9 = (bf16[1024,128]{1,0:T(8,128)(2,1)S(1)}, bf16[1024,128]{1,0:T(8,128)(2,1)S(1)}, u32[]{:S(2)}, u32[]{:S(2)}) collective-permute-start(bf16[1024,128]{1,0:T(8,128)(2,1)S(1)} %get-tuple-element.21), channel_id=1, source_target_pairs={{4,0},{8,4},{12,8},{16,12},{20,16},{24,20},{28,24},{0,28},{5,1},{9... | collective-permute-start | bytes 786440 | tf_op jit(solution)/shard_map/ppermute | solution.py:340
  39.0 5.9 %collective-permute-done.9 = bf16[1024,128]{1,0:T(8,128)(2,1)S(1)} collective-permute-done((bf16[1024,128]{1,0:T(8,128)(2,1)S(1)}, bf16[1024,128]{1,0:T(8,128)(2,1)S(1)}, u32[]{:S(2)}, u32[]{:S(2)}) %collective-permute-start.9) | collective-permute-done | bytes 262176 | tf_op jit(solution)/shard_map/ppermute | solution.py:340
  44.9 4.9 %collective-permute-done.8 = bf16[1024,128]{1,0:T(8,128)(2,1)S(1)} collective-permute-done((bf16[1024,128]{1,0:T(8,128)(2,1)S(1)}, bf16[1024,128]{1,0:T(8,128)(2,1)S(1)}, u32[]{:S(2)}, u32[]{:S(2)}) %collective-permute-start.8) | collective-permute-done | bytes 262176 | tf_op jit(solution)/shard_map/ppermute | solution.py:339
  51.5 2.9 %fusion.32 = f32[128,1920]{1,0:T(8,128)S(1)} fusion(bf16[1024,128]{1,0:T(8,128)(2,1)S(1)} %add_convert_fusion, bf16[1024,1920]{1,0:T(8,128)(2,1)} %param.15), kind=kOutput, calls=%fused_computation.75 | convolution fusion | flops 503316480 | bytes 5177344 | tf_op jit(solution)/shard_map/dot_general | solution.py:356
  55.6 2.6 %collective-permute-done.22 = bf16[1024,128]{1,0:T(8,128)(2,1)S(1)} collective-permute-done((bf16[1024,128]{1,0:T(8,128)(2,1)S(1)}, bf16[1024,128]{1,0:T(8,128)(2,1)S(1)}, u32[]{:S(2)}, u32[]{:S(2)}) %collective-permute-start.22) | collective-permute-done | bytes 262176 | tf_op jit(solution)/shard_map/ppermute | solution.py:258
  58.2 2.9 %fusion.34 = f32[128,1920]{1,0:T(8,128)S(1)} fusion(bf16[1024,128]{1,0:T(8,128)(2,1)S(1)} %collective-permute-done.22, bf16[1024,1920]{1,0:T(8,128)(2,1)} %param.15), kind=kOutput, calls=%fused_computation.77 | convolution fusion | flops 503316480 | bytes 5177344 | tf_op jit(solution)/shard_map/dot_general | solution.py:356
  61.1 2.1 %collective-permute-start.23 = (bf16[64,1920]{1,0:T(8,128)(2,1)S(1)}, bf16[64,1920]{1,0:T(8,128)(2,1)S(1)}, u32[]{:S(2)}, u32[]{:S(2)}) collective-permute-start(bf16[64,1920]{1,0:T(8,128)(2,1)S(1)} %dynamic-slice_convert_fusion.1), channel_id=1, source_target_pairs={{0,4},{4,0},{8,12},{12,8},{16,20},{20,16},{24,28},{28,24},{1,5},{5... | collective-permute-start | bytes 737288 | tf_op jit(solution)/shard_map/ppermute | solution.py:258
  63.3 3.5 %collective-permute-start.11 = (bf16[64,1920]{1,0:T(8,128)(2,1)S(1)}, bf16[64,1920]{1,0:T(8,128)(2,1)S(1)}, u32[]{:S(2)}, u32[]{:S(2)}) collective-permute-start(bf16[64,1920]{1,0:T(8,128)(2,1)S(1)} %fusion.23), channel_id=1, source_target_pairs={{0,8},{4,12},{24,16},{28,20},{1,9},{5,13},{25,17},{29,21},{2,10},{... | collective-permute-start | bytes 737288 | tf_op jit(solution)/shard_map/ppermute | solution.py:286
  66.8 1.8 collective-permute-done.23
  68.7 3.5 %collective-permute-start.24 = (bf16[64,1920]{1,0:T(8,128)(2,1)S(1)}, bf16[64,1920]{1,0:T(8,128)(2,1)S(1)}, u32[]{:S(2)}, u32[]{:S(2)}) collective-permute-start(bf16[64,1920]{1,0:T(8,128)(2,1)S(1)} %fusion.25), channel_id=1, source_target_pairs={{0,8},{4,12},{24,16},{28,20},{1,9},{5,13},{25,17},{29,21},{2,10},{... | collective-permute-start | bytes 737288 | tf_op jit(solution)/shard_map/ppermute | solution.py:286
  74.3 2.0 collective-permute-done.24
  78.6 2.5 %divide_convert_fusion.3 = (bf16[64,1920]{1,0:T(8,128)(2,1)}, bf16[64,1920]{1,0:T(8,128)(2,1)}) fusion(bf16[64,1920]{1,0:T(8,128)(2,1)} %collective-permute-done.12, bf16[64,1920]{1,0:T(8,128)(2,1)S(1)} %collective-permute-done.11, f32[1920]{0:T(1024)S(1)} %copy-done.10, f32[64]{0:T(128)S(1)} %get-tuple-element.45, ...), kind=kLoop, calls=%fused_computation.38 | loop fusion | flops 2211840 | bytes 2957316 | tf_op jit(solution)/shard_map/convert_element_type | solution.py:289
  83.9 14.0 %collective-permute-done.26 = bf16[64,1920]{1,0:T(8,128)(2,1)S(1)} collective-permute-done((bf16[64,1920]{1,0:T(8,128)(2,1)}, bf16[64,1920]{1,0:T(8,128)(2,1)S(1)}, u32[]{:S(2)}, u32[]{:S(2)}) %collective-permute-start.26) | collective-permute-done | bytes 245792 | tf_op jit(solution)/shard_map/ppermute | solution.py:291
  98.9 2.8 %collective-permute-done.13 = bf16[64,1920]{1,0:T(8,128)(2,1)S(1)} collective-permute-done((bf16[64,1920]{1,0:T(8,128)(2,1)}, bf16[64,1920]{1,0:T(8,128)(2,1)S(1)}, u32[]{:S(2)}, u32[]{:S(2)}) %collective-permute-start.13) | collective-permute-done | bytes 245792 | tf_op jit(solution)/shard_map/ppermute | solution.py:291
  102.8 2.9 %fusion.35 = f32[128,1920]{1,0:T(8,128)S(1)} fusion(bf16[1024,128]{1,0:T(8,128)(2,1)S(1)} %collective-permute-done.22, bf16[1024,1920]{1,0:T(8,128)(2,1)} %collective-permute-done.15), kind=kOutput, calls=%fused_computation.78 | convolution fusion | flops 503316480 | bytes 5177344 | tf_op jit(solution)/shard_map/dot_general | solution.py:356
  106.8 2.9 %fusion.33 = f32[128,1920]{1,0:T(8,128)S(1)} fusion(bf16[1024,128]{1,0:T(8,128)(2,1)S(1)} %add_convert_fusion, bf16[1024,1920]{1,0:T(8,128)(2,1)} %collective-permute-done.15), kind=kOutput, calls=%fused_computation.76 | convolution fusion | flops 503316480 | bytes 5177344 | tf_op jit(solution)/shard_map/dot_general | solution.py:356
  110.8 5.2 %collective-permute-done.28 = bf16[64,1920]{1,0:T(8,128)(2,1)S(1)} collective-permute-done((bf16[64,1920]{1,0:T(8,128)(2,1)S(1)}, bf16[64,1920]{1,0:T(8,128)(2,1)S(1)}, u32[]{:S(2)}, u32[]{:S(2)}) %collective-permute-start.28) | collective-permute-done | bytes 245792 | tf_op jit(solution)/shard_map/ppermute | solution.py:258
  116.0 2.5 %collective-permute-start.29 = (bf16[64,1920]{1,0:T(8,128)(2,1)S(1)}, bf16[64,1920]{1,0:T(8,128)(2,1)S(1)}, u32[]{:S(2)}, u32[]{:S(2)}) collective-permute-start(bf16[64,1920]{1,0:T(8,128)(2,1)S(1)} %fusion.26), channel_id=1, source_target_pairs={{0,8},{4,12},{24,16},{28,20},{1,9},{5,13},{25,17},{29,21},{2,10},{... | collective-permute-start | bytes 737288 | tf_op jit(solution)/shard_map/ppermute | solution.py:286
  120.0 2.5 %collective-permute-start.17 = (bf16[64,1920]{1,0:T(8,128)(2,1)S(1)}, bf16[64,1920]{1,0:T(8,128)(2,1)S(1)}, u32[]{:S(2)}, u32[]{:S(2)}) collective-permute-start(bf16[64,1920]{1,0:T(8,128)(2,1)S(1)} %fusion.24), channel_id=1, source_target_pairs={{0,8},{4,12},{24,16},{28,20},{1,9},{5,13},{25,17},{29,21},{2,10},{... | collective-permute-start | bytes 737288 | tf_op jit(solution)/shard_map/ppermute | solution.py:286
  123.7 3.8 %collective-permute-done.17 = bf16[64,1920]{1,0:T(8,128)(2,1)S(1)} collective-permute-done((bf16[64,1920]{1,0:T(8,128)(2,1)S(1)}, bf16[64,1920]{1,0:T(8,128)(2,1)S(1)}, u32[]{:S(2)}, u32[]{:S(2)}) %collective-permute-start.17) | collective-permute-done | bytes 245792 | tf_op jit(solution)/shard_map/ppermute | solution.py:286
  131.6 15.8 %collective-permute-done.31 = bf16[64,1920]{1,0:T(8,128)(2,1)S(1)} collective-permute-done((bf16[64,1920]{1,0:T(8,128)(2,1)S(1)}, bf16[64,1920]{1,0:T(8,128)(2,1)S(1)}, u32[]{:S(2)}, u32[]{:S(2)}) %collective-permute-start.31) | collective-permute-done | bytes 245792 | tf_op jit(solution)/shard_map/ppermute | solution.py:291
  148.5 1.6 collective-permute-done.20
  151.1 4.4 %collective-permute-done.32 = bf16[64,1920]{1,0:T(8,128)(2,1)S(1)} collective-permute-done((bf16[64,1920]{1,0:T(8,128)(2,1)S(1)}, bf16[64,1920]{1,0:T(8,128)(2,1)S(1)}, u32[]{:S(2)}, u32[]{:S(2)}) %collective-permute-start.32) | collective-permute-done | bytes 245792 | tf_op jit(solution)/shard_map/ppermute | solution.py:258
  155.5 3.3 %fusion.15 = f32[128,1024]{0,1:T(8,128)S(1)} fusion(bf16[1024,1920]{1,0:T(8,128)(2,1)} %collective-permute-done.15, bf16[64,1920]{1,0:T(8,128)(2,1)S(1)} %get-tuple-element.37, bf16[64,1920]{1,0:T(8,128)(2,1)S(1)} %get-tuple-element.36), kind=kOutput, calls=%fused_computation.22 | convolution fusion | flops 504299520 | bytes 4947968 | tf_op jit(solution)/shard_map/dot_general | solution.py:360
  158.8 3.3 %fusion.4 = bf16[1024,128]{1,0:T(8,128)(2,1)S(1)} fusion(f32[128,1024]{0,1:T(8,128)S(1)} %fusion.15, bf16[1024,1920]{1,0:T(8,128)(2,1)} %param.15, bf16[64,1920]{1,0:T(8,128)(2,1)S(1)} %get-tuple-element.35, bf16[64,1920]{1,0:T(8,128)(2,1)S(1)} %get-tuple-element.34), kind=kOutput, calls=%fused_computation.6 | convolution fusion | flops 504561664 | bytes 5210112 | tf_op jit(solution)/shard_map/dot_general | solution.py:360
  162.8 3.3 %fusion.8 = f32[128,1024]{0,1:T(8,128)S(1)} fusion(bf16[1024,1920]{1,0:T(8,128)(2,1)} %collective-permute-done.15, bf16[64,1920]{1,0:T(8,128)(2,1)S(1)} %get-tuple-element.39, bf16[64,1920]{1,0:T(8,128)(2,1)S(1)} %get-tuple-element.38), kind=kOutput, calls=%fused_computation.15 | convolution fusion | flops 504299520 | bytes 4947968 | tf_op jit(solution)/shard_map/dot_general | solution.py:360
  166.1 2.5 %collective-permute-done.33 = bf16[1024,128]{1,0:T(8,128)(2,1)S(1)} collective-permute-done((bf16[1024,128]{1,0:T(8,128)(2,1)S(1)}, bf16[1024,128]{1,0:T(8,128)(2,1)S(1)}, u32[]{:S(2)}, u32[]{:S(2)}) %collective-permute-start.33) | collective-permute-done | bytes 262176 | tf_op jit(solution)/shard_map/ppermute | solution.py:258
  168.6 3.3 %fusion.2.refs_10_ = bf16[1024,128]{1,0:T(8,128)(2,1)S(1)} fusion(f32[128,1024]{0,1:T(8,128)S(1)} %fusion.8, bf16[1024,1920]{1,0:T(8,128)(2,1)} %param.15, bf16[1024,128]{1,0:T(8,128)(2,1)S(1)} %collective-permute-done.33, bf16[64,1920]{1,0:T(8,128)(2,1)S(1)} %get-tuple-element.33, bf16[64,1920]{1,0:T(8,128)(2,1)S(1)} %get-tuple-element.32), kind=kOutput, calls=%fused_computation.4 | convolution fusion | flops 504823808 | bytes 5472256 | tf_op jit(solution)/shard_map/dot_general | solution.py:360
  171.9 1.7 collective-permute-start.38
  173.6 3.1 %collective-permute-start.40 = (bf16[1024,128]{1,0:T(8,128)(2,1)S(1)}, bf16[1024,128]{1,0:T(8,128)(2,1)}, u32[]{:S(2)}, u32[]{:S(2)}) collective-permute-start(bf16[1024,128]{1,0:T(8,128)(2,1)S(1)} %fusion.2.refs_10_), channel_id=1, source_target_pairs={{4,0},{8,4},{12,8},{16,12},{20,16},{24,20},{28,24},{0,28},{5,1},{9... | collective-permute-start | bytes 786440 | tf_op jit(solution)/shard_map/ppermute | solution.py:264
  179.2 1.9 collective-permute-done.38.refs_8_
  183.4 2.5 %collective-permute-done.34.refs_11_ = bf16[1024,128]{1,0:T(8,128)(2,1)S(1)} collective-permute-done((bf16[1024,128]{1,0:T(8,128)(2,1)S(1)}, bf16[1024,128]{1,0:T(8,128)(2,1)S(1)}, u32[]{:S(2)}, u32[]{:S(2)}) %collective-permute-start.34) | collective-permute-done | bytes 262176 | tf_op jit(solution)/shard_map/ppermute | solution.py:258
  186.9 3.1 %collective-permute-done.36.refs_3_ = bf16[1024,128]{1,0:T(8,128)(2,1)S(1)} collective-permute-done((bf16[1024,128]{1,0:T(8,128)(2,1)S(1)}, bf16[1024,128]{1,0:T(8,128)(2,1)S(1)}, u32[]{:S(2)}, u32[]{:S(2)}) %collective-permute-start.36) | collective-permute-done | bytes 262176 | tf_op jit(solution)/shard_map/ppermute | solution.py:258
  190.1 2.8 %collective-permute-done.37.refs_7_ = bf16[1024,128]{1,0:T(8,128)(2,1)S(1)} collective-permute-done((bf16[1024,128]{1,0:T(8,128)(2,1)S(1)}, bf16[1024,128]{1,0:T(8,128)(2,1)S(1)}, u32[]{:S(2)}, u32[]{:S(2)}) %collective-permute-start.37) | collective-permute-done | bytes 262176 | tf_op jit(solution)/shard_map/ppermute | solution.py:258
  192.9 2.8 %collective-permute-done.39.refs_9_ = bf16[1024,128]{1,0:T(8,128)(2,1)S(1)} collective-permute-done((bf16[1024,128]{1,0:T(8,128)(2,1)S(1)}, bf16[1024,128]{1,0:T(8,128)(2,1)S(1)}, u32[]{:S(2)}, u32[]{:S(2)}) %collective-permute-start.39) | collective-permute-done | bytes 262176 | tf_op jit(solution)/shard_map/ppermute | solution.py:258
  195.7 2.8 %collective-permute-done.41.refs_13_ = bf16[1024,128]{1,0:T(8,128)(2,1)S(1)} collective-permute-done((bf16[1024,128]{1,0:T(8,128)(2,1)}, bf16[1024,128]{1,0:T(8,128)(2,1)S(1)}, u32[]{:S(2)}, u32[]{:S(2)}) %collective-permute-start.41) | collective-permute-done | bytes 262176 | tf_op jit(solution)/shard_map/ppermute | solution.py:258
  198.5 5.1 %shard_map.107 = (f32[24,128,128]{2,1,0:T(8,128)S(1)}, bf16[24,128,128]{2,1,0:T(8,128)(2,1)}) custom-call(s32[24,2]{1,0:T(8,128)S(1)} %copy.14.refs_0_, s32[24,2]{1,0:T(8,128)S(1)} %collective-permute-done.refs_1_, bf16[1024,128]{1,0:T(8,128)(2,1)S(1)} %collective-permute-done.5.refs_8_.refs_2_, bf16[1024,128]{1,0:T(8,128)(2,1)S(1)} %collective-permute-done.36.refs_3_, ...), custom_call_target="tpu_custom_call" | custom-call | flops 402653184 | bytes 5505024 | tf_op jit(solution)/shard_map/pallas_call | solution.py:213
  207.4 3.0 %shard_map.108 = f32[24,1,256]{2,1,0:T(1,128)S(1)} custom-call(bf16[24,256,128]{2,1,0:T(8,128)(2,1)S(1)} %copy-done.1, f32[24,128,128]{2,1,0:T(8,128)S(1)} %copy-done.3, bf16[24,128,128]{2,1,0:T(8,128)(2,1)} %collective-permute-done.42.second_ref, f32[24,1,256]{2,1,0:T(1,128)S(1)} %reshape.19.scale_ref), custom_call_target="tpu_custom_call" | custom-call | flops 402653184 | bytes 3932160 | tf_op jit(solution)/shard_map/pallas_call | solution.py:242
  (111 shorter events, 41.0 us)
Async XLA Ops:
  0.6 24.6 %copy-start.11 = (s32[24,2]{0,1:T(2,128)S(1)}, s32[24,2]{0,1:T(2,128)}, u32[]{:S(2)}) copy-start(s32[24,2]{0,1:T(2,128)} %param.10) | copy-start | bytes 580
  6.5 12.3 %collective-permute-start.4 = (bf16[1568,128]{1,0:T(8,128)(2,1)S(1)}, bf16[1568,128]{1,0:T(8,128)(2,1)S(1)}, u32[]{:S(2)}, u32[]{:S(2)}) collective-permute-start(bf16[1568,128]{1,0:T(8,128)(2,1)S(1)} %get-tuple-element.15), channel_id=1, source_target_pairs={{0,2},{1,3},{2,0},{3,1},{4,6},{5,7},{6,4},{7,5},{8,10},{9,11},{10,... | collective-permute-start | bytes 1204232 | tf_op jit(solution)/shard_map/ppermute | solution.py:258
  10.6 12.5 %collective-permute-start.5 = (bf16[1024,128]{1,0:T(8,128)(2,1)S(1)}, bf16[1024,128]{1,0:T(8,128)(2,1)S(1)}, u32[]{:S(2)}, u32[]{:S(2)}) collective-permute-start(bf16[1024,128]{1,0:T(8,128)(2,1)S(1)} %get-tuple-element.27.refs_9_.refs_4_), channel_id=1, source_target_pairs={{0,4},{4,8},{8,12},{12,16},{16,20},{20,24},{24,28},{28,0},{1,5},{5... | collective-permute-start | bytes 786440 | tf_op jit(solution)/shard_map/ppermute | solution.py:263
  12.2 13.1 %collective-permute-start.6 = (bf16[1024,128]{1,0:T(8,128)(2,1)S(1)}, bf16[1024,128]{1,0:T(8,128)(2,1)S(1)}, u32[]{:S(2)}, u32[]{:S(2)}) collective-permute-start(bf16[1024,128]{1,0:T(8,128)(2,1)S(1)} %get-tuple-element.27.refs_9_.refs_4_), channel_id=1, source_target_pairs={{4,0},{8,4},{12,8},{16,12},{20,16},{24,20},{28,24},{0,28},{5,1},{9... | collective-permute-start | bytes 786440 | tf_op jit(solution)/shard_map/ppermute | solution.py:264
  15.4 14.9 %collective-permute-start.3 = (bf16[24,128,128]{2,1,0:T(8,128)(2,1)S(1)}, bf16[24,128,128]{2,1,0:T(8,128)(2,1)}, u32[]{:S(2)}, u32[]{:S(2)}) collective-permute-start(bf16[24,128,128]{2,1,0:T(8,128)(2,1)S(1)} %get-tuple-element.14.refs_4_), channel_id=1, source_target_pairs={{0,1},{1,0},{2,3},{3,2},{4,5},{5,4},{6,7},{7,6},{8,9},{9,8},{10,11... | collective-permute-start | bytes 2359304 | tf_op jit(solution)/shard_map/ppermute | solution.py:258
  25.3 5.0 %collective-permute-start.7 = (bf16[24,128,128]{2,1,0:T(8,128)(2,1)S(1)}, bf16[24,128,128]{2,1,0:T(8,128)(2,1)}, u32[]{:S(2)}, u32[]{:S(2)}) collective-permute-start(bf16[24,128,128]{2,1,0:T(8,128)(2,1)S(1)} %shard_map.105.refs_6_), channel_id=1, source_target_pairs={{0,1},{1,0},{2,3},{3,2},{4,5},{5,4},{6,7},{7,6},{8,9},{9,8},{10,11... | collective-permute-start | bytes 2359304 | tf_op jit(solution)/shard_map/ppermute | solution.py:258
  25.4 3.7 %collective-permute-start.1 = (s32[24,2]{1,0:T(8,128)S(1)}, s32[24,2]{1,0:T(8,128)S(1)}, u32[]{:S(2)}, u32[]{:S(2)}) collective-permute-start(s32[24,2]{1,0:T(8,128)S(1)} %copy.14.refs_0_), channel_id=1, source_target_pairs={{0,2},{1,3},{2,0},{3,1},{4,6},{5,7},{6,4},{7,5},{8,10},{9,11},{10,... | collective-permute-start | bytes 584 | tf_op jit(solution)/shard_map/ppermute | solution.py:258
  25.9 3.2 %collective-permute-start = (s32[24,2]{1,0:T(8,128)S(1)}, s32[24,2]{1,0:T(8,128)S(1)}, u32[]{:S(2)}, u32[]{:S(2)}) collective-permute-start(s32[24,2]{1,0:T(8,128)S(1)} %copy.14.refs_0_), channel_id=1, source_target_pairs={{0,1},{1,0},{2,3},{3,2},{4,5},{5,4},{6,7},{7,6},{8,9},{9,8},{10,11... | collective-permute-start | bytes 584 | tf_op jit(solution)/shard_map/ppermute | solution.py:258
  29.1 1.2 collective-permute-start.2
  35.7 9.2 %collective-permute-start.9 = (bf16[1024,128]{1,0:T(8,128)(2,1)S(1)}, bf16[1024,128]{1,0:T(8,128)(2,1)S(1)}, u32[]{:S(2)}, u32[]{:S(2)}) collective-permute-start(bf16[1024,128]{1,0:T(8,128)(2,1)S(1)} %get-tuple-element.21), channel_id=1, source_target_pairs={{4,0},{8,4},{12,8},{16,12},{20,16},{24,20},{28,24},{0,28},{5,1},{9... | collective-permute-start | bytes 786440 | tf_op jit(solution)/shard_map/ppermute | solution.py:340
  39.0 10.8 %collective-permute-start.8 = (bf16[1024,128]{1,0:T(8,128)(2,1)S(1)}, bf16[1024,128]{1,0:T(8,128)(2,1)S(1)}, u32[]{:S(2)}, u32[]{:S(2)}) collective-permute-start(bf16[1024,128]{1,0:T(8,128)(2,1)S(1)} %get-tuple-element.20), channel_id=1, source_target_pairs={{0,4},{4,8},{8,12},{12,16},{16,20},{20,24},{24,28},{28,0},{1,5},{5... | collective-permute-start | bytes 786440 | tf_op jit(solution)/shard_map/ppermute | solution.py:339
  39.0 63.8 %collective-permute-start.15 = (bf16[1024,1920]{1,0:T(8,128)(2,1)}, bf16[1024,1920]{1,0:T(8,128)(2,1)}, u32[]{:S(2)}, u32[]{:S(2)}) collective-permute-start(bf16[1024,1920]{1,0:T(8,128)(2,1)} %param.15), channel_id=1, source_target_pairs={{0,1},{1,0},{2,3},{3,2},{4,5},{5,4},{6,7},{7,6},{8,9},{9,8},{10,11... | collective-permute-start | bytes 11796488 | tf_op jit(solution)/shard_map/ppermute | solution.py:258
  50.9 7.3 %collective-permute-start.22 = (bf16[1024,128]{1,0:T(8,128)(2,1)S(1)}, bf16[1024,128]{1,0:T(8,128)(2,1)S(1)}, u32[]{:S(2)}, u32[]{:S(2)}) collective-permute-start(bf16[1024,128]{1,0:T(8,128)(2,1)S(1)} %add_convert_fusion), channel_id=1, source_target_pairs={{0,2},{1,3},{2,0},{3,1},{4,6},{5,7},{6,4},{7,5},{8,10},{9,11},{10,... | collective-permute-start | bytes 786440 | tf_op jit(solution)/shard_map/ppermute | solution.py:258
  54.4 24.1 %copy-start.12 = (f32[512]{0:T(512)S(1)}, f32[512]{0:T(512)}, u32[]{:S(2)}) copy-start(f32[512]{0:T(512)} %param.16) | copy-start | bytes 6148
  54.5 24.2 %copy-start.10 = (f32[1920]{0:T(1024)S(1)}, f32[1920]{0:T(1024)}, u32[]{:S(2)}) copy-start(f32[1920]{0:T(1024)} %param.17) | copy-start | bytes 23044
  54.5 8.8 %collective-permute-start.10 = (bf16[64,1920]{1,0:T(8,128)(2,1)S(1)}, bf16[64,1920]{1,0:T(8,128)(2,1)S(1)}, u32[]{:S(2)}, u32[]{:S(2)}) collective-permute-start(bf16[64,1920]{1,0:T(8,128)(2,1)S(1)} %dynamic-slice_convert_fusion.3), channel_id=1, source_target_pairs={{0,4},{4,0},{8,12},{12,8},{16,20},{20,16},{24,28},{28,24},{1,5},{5... | collective-permute-start | bytes 737288 | tf_op jit(solution)/shard_map/ppermute | solution.py:258
  61.1 7.5 %collective-permute-start.23 = (bf16[64,1920]{1,0:T(8,128)(2,1)S(1)}, bf16[64,1920]{1,0:T(8,128)(2,1)S(1)}, u32[]{:S(2)}, u32[]{:S(2)}) collective-permute-start(bf16[64,1920]{1,0:T(8,128)(2,1)S(1)} %dynamic-slice_convert_fusion.1), channel_id=1, source_target_pairs={{0,4},{4,0},{8,12},{12,8},{16,20},{20,16},{24,28},{28,24},{1,5},{5... | collective-permute-start | bytes 737288 | tf_op jit(solution)/shard_map/ppermute | solution.py:258
  63.3 8.8 %collective-permute-start.11 = (bf16[64,1920]{1,0:T(8,128)(2,1)S(1)}, bf16[64,1920]{1,0:T(8,128)(2,1)S(1)}, u32[]{:S(2)}, u32[]{:S(2)}) collective-permute-start(bf16[64,1920]{1,0:T(8,128)(2,1)S(1)} %fusion.23), channel_id=1, source_target_pairs={{0,8},{4,12},{24,16},{28,20},{1,9},{5,13},{25,17},{29,21},{2,10},{... | collective-permute-start | bytes 737288 | tf_op jit(solution)/shard_map/ppermute | solution.py:286
  68.7 7.7 %collective-permute-start.24 = (bf16[64,1920]{1,0:T(8,128)(2,1)S(1)}, bf16[64,1920]{1,0:T(8,128)(2,1)S(1)}, u32[]{:S(2)}, u32[]{:S(2)}) collective-permute-start(bf16[64,1920]{1,0:T(8,128)(2,1)S(1)} %fusion.25), channel_id=1, source_target_pairs={{0,8},{4,12},{24,16},{28,20},{1,9},{5,13},{25,17},{29,21},{2,10},{... | collective-permute-start | bytes 737288 | tf_op jit(solution)/shard_map/ppermute | solution.py:286
  72.9 5.7 %collective-permute-start.12 = (bf16[64,1920]{1,0:T(8,128)(2,1)}, bf16[64,1920]{1,0:T(8,128)(2,1)}, u32[]{:S(2)}, u32[]{:S(2)}) collective-permute-start(bf16[64,1920]{1,0:T(8,128)(2,1)} %fusion.19), channel_id=1, source_target_pairs={{8,16},{12,20},{16,8},{20,12},{9,17},{13,21},{17,9},{21,13},{10,18... | collective-permute-start | bytes 737288 | tf_op jit(solution)/shard_map/ppermute | solution.py:287
  77.2 1.5 collective-permute-start.25
  81.2 16.7 %collective-permute-start.26 = (bf16[64,1920]{1,0:T(8,128)(2,1)}, bf16[64,1920]{1,0:T(8,128)(2,1)S(1)}, u32[]{:S(2)}, u32[]{:S(2)}) collective-permute-start(bf16[64,1920]{1,0:T(8,128)(2,1)} %get-tuple-element.41), channel_id=1, source_target_pairs={{8,0},{12,4},{16,24},{20,28},{9,1},{13,5},{17,25},{21,29},{10,2},{... | collective-permute-start | bytes 737288 | tf_op jit(solution)/shard_map/ppermute | solution.py:291
  82.4 45.9 %collective-permute-start.19 = (f32[1920]{0:T(1024)S(1)}, f32[1920]{0:T(1024)S(1)}, u32[]{:S(2)}, u32[]{:S(2)}) collective-permute-start(f32[1920]{0:T(1024)S(1)} %copy-done.10), channel_id=1, source_target_pairs={{0,1},{1,0},{2,3},{3,2},{4,5},{5,4},{6,7},{7,6},{8,9},{9,8},{10,11... | collective-permute-start | bytes 23048 | tf_op jit(solution)/shard_map/ppermute | solution.py:258
  82.6 19.2 %collective-permute-start.13 = (bf16[64,1920]{1,0:T(8,128)(2,1)}, bf16[64,1920]{1,0:T(8,128)(2,1)S(1)}, u32[]{:S(2)}, u32[]{:S(2)}) collective-permute-start(bf16[64,1920]{1,0:T(8,128)(2,1)} %get-tuple-element.40), channel_id=1, source_target_pairs={{8,0},{12,4},{16,24},{20,28},{9,1},{13,5},{17,25},{21,29},{10,2},{... | collective-permute-start | bytes 737288 | tf_op jit(solution)/shard_map/ppermute | solution.py:291
  97.9 30.4 %collective-permute-start.27 = (bf16[64,1920]{1,0:T(8,128)(2,1)S(1)}, bf16[64,1920]{1,0:T(8,128)(2,1)S(1)}, u32[]{:S(2)}, u32[]{:S(2)}) collective-permute-start(bf16[64,1920]{1,0:T(8,128)(2,1)S(1)} %broadcast_select_fusion.5), channel_id=1, source_target_pairs={{0,4},{4,0},{8,12},{12,8},{16,20},{20,16},{24,28},{28,24},{1,5},{5... | collective-permute-start | bytes 737288 | tf_op jit(solution)/shard_map/ppermute | solution.py:258
  101.8 28.3 %collective-permute-start.14 = (bf16[64,1920]{1,0:T(8,128)(2,1)S(1)}, bf16[64,1920]{1,0:T(8,128)(2,1)S(1)}, u32[]{:S(2)}, u32[]{:S(2)}) collective-permute-start(bf16[64,1920]{1,0:T(8,128)(2,1)S(1)} %broadcast_select_fusion.7), channel_id=1, source_target_pairs={{0,4},{4,0},{8,12},{12,8},{16,20},{20,16},{24,28},{28,24},{1,5},{5... | collective-permute-start | bytes 737288 | tf_op jit(solution)/shard_map/ppermute | solution.py:258
  105.7 10.3 %collective-permute-start.28 = (bf16[64,1920]{1,0:T(8,128)(2,1)S(1)}, bf16[64,1920]{1,0:T(8,128)(2,1)S(1)}, u32[]{:S(2)}, u32[]{:S(2)}) collective-permute-start(bf16[64,1920]{1,0:T(8,128)(2,1)S(1)} %dynamic-slice_convert_fusion), channel_id=1, source_target_pairs={{0,4},{4,0},{8,12},{12,8},{16,20},{20,16},{24,28},{28,24},{1,5},{5... | collective-permute-start | bytes 737288 | tf_op jit(solution)/shard_map/ppermute | solution.py:258
  109.7 10.2 %collective-permute-start.16 = (bf16[64,1920]{1,0:T(8,128)(2,1)S(1)}, bf16[64,1920]{1,0:T(8,128)(2,1)S(1)}, u32[]{:S(2)}, u32[]{:S(2)}) collective-permute-start(bf16[64,1920]{1,0:T(8,128)(2,1)S(1)} %dynamic-slice_convert_fusion.2), channel_id=1, source_target_pairs={{0,4},{4,0},{8,12},{12,8},{16,20},{20,16},{24,28},{28,24},{1,5},{5... | collective-permute-start | bytes 737288 | tf_op jit(solution)/shard_map/ppermute | solution.py:258
  116.0 6.9 %collective-permute-start.29 = (bf16[64,1920]{1,0:T(8,128)(2,1)S(1)}, bf16[64,1920]{1,0:T(8,128)(2,1)S(1)}, u32[]{:S(2)}, u32[]{:S(2)}) collective-permute-start(bf16[64,1920]{1,0:T(8,128)(2,1)S(1)} %fusion.26), channel_id=1, source_target_pairs={{0,8},{4,12},{24,16},{28,20},{1,9},{5,13},{25,17},{29,21},{2,10},{... | collective-permute-start | bytes 737288 | tf_op jit(solution)/shard_map/ppermute | solution.py:286
  120.0 7.5 %collective-permute-start.17 = (bf16[64,1920]{1,0:T(8,128)(2,1)S(1)}, bf16[64,1920]{1,0:T(8,128)(2,1)S(1)}, u32[]{:S(2)}, u32[]{:S(2)}) collective-permute-start(bf16[64,1920]{1,0:T(8,128)(2,1)S(1)} %fusion.24), channel_id=1, source_target_pairs={{0,8},{4,12},{24,16},{28,20},{1,9},{5,13},{25,17},{29,21},{2,10},{... | collective-permute-start | bytes 737288 | tf_op jit(solution)/shard_map/ppermute | solution.py:286
  123.0 5.3 %collective-permute-start.30 = (bf16[64,1920]{1,0:T(8,128)(2,1)S(1)}, bf16[64,1920]{1,0:T(8,128)(2,1)S(1)}, u32[]{:S(2)}, u32[]{:S(2)}) collective-permute-start(bf16[64,1920]{1,0:T(8,128)(2,1)S(1)} %fusion.22), channel_id=1, source_target_pairs={{8,16},{12,20},{16,8},{20,12},{9,17},{13,21},{17,9},{21,13},{10,18... | collective-permute-start | bytes 737288 | tf_op jit(solution)/shard_map/ppermute | solution.py:287
  127.6 0.8 collective-permute-start.18
  128.8 18.6 %collective-permute-start.31 = (bf16[64,1920]{1,0:T(8,128)(2,1)S(1)}, bf16[64,1920]{1,0:T(8,128)(2,1)S(1)}, u32[]{:S(2)}, u32[]{:S(2)}) collective-permute-start(bf16[64,1920]{1,0:T(8,128)(2,1)S(1)} %get-tuple-element.42), channel_id=1, source_target_pairs={{8,0},{12,4},{16,24},{20,28},{9,1},{13,5},{17,25},{21,29},{10,2},{... | collective-permute-start | bytes 737288 | tf_op jit(solution)/shard_map/ppermute | solution.py:291
  130.1 19.9 %collective-permute-start.20 = (bf16[64,1920]{1,0:T(8,128)(2,1)S(1)}, bf16[64,1920]{1,0:T(8,128)(2,1)S(1)}, u32[]{:S(2)}, u32[]{:S(2)}) collective-permute-start(bf16[64,1920]{1,0:T(8,128)(2,1)S(1)} %get-tuple-element.43), channel_id=1, source_target_pairs={{8,0},{12,4},{16,24},{20,28},{9,1},{13,5},{17,25},{21,29},{10,2},{... | collective-permute-start | bytes 737288 | tf_op jit(solution)/shard_map/ppermute | solution.py:291
  147.4 8.1 %collective-permute-start.32 = (bf16[64,1920]{1,0:T(8,128)(2,1)S(1)}, bf16[64,1920]{1,0:T(8,128)(2,1)S(1)}, u32[]{:S(2)}, u32[]{:S(2)}) collective-permute-start(bf16[64,1920]{1,0:T(8,128)(2,1)S(1)} %broadcast_select_fusion.4), channel_id=1, source_target_pairs={{0,4},{4,0},{8,12},{12,8},{16,20},{20,16},{24,28},{28,24},{1,5},{5... | collective-permute-start | bytes 737288 | tf_op jit(solution)/shard_map/ppermute | solution.py:258
  150.1 12.7 %collective-permute-start.21 = (bf16[64,1920]{1,0:T(8,128)(2,1)S(1)}, bf16[64,1920]{1,0:T(8,128)(2,1)S(1)}, u32[]{:S(2)}, u32[]{:S(2)}) collective-permute-start(bf16[64,1920]{1,0:T(8,128)(2,1)S(1)} %broadcast_select_fusion.6), channel_id=1, source_target_pairs={{0,4},{4,0},{8,12},{12,8},{16,20},{20,16},{24,28},{28,24},{1,5},{5... | collective-permute-start | bytes 737288 | tf_op jit(solution)/shard_map/ppermute | solution.py:258
  162.2 6.4 %collective-permute-start.33 = (bf16[1024,128]{1,0:T(8,128)(2,1)S(1)}, bf16[1024,128]{1,0:T(8,128)(2,1)S(1)}, u32[]{:S(2)}, u32[]{:S(2)}) collective-permute-start(bf16[1024,128]{1,0:T(8,128)(2,1)S(1)} %fusion.4), channel_id=1, source_target_pairs={{0,2},{1,3},{2,0},{3,1},{4,6},{5,7},{6,4},{7,5},{8,10},{9,11},{10,... | collective-permute-start | bytes 786440 | tf_op jit(solution)/shard_map/ppermute | solution.py:258
  171.9 32.9 %copy-start.9 = (f32[24,256]{1,0:T(8,128)S(1)}, f32[24,256]{1,0:T(8,128)}, u32[]{:S(2)}) copy-start(f32[24,256]{1,0:T(8,128)} %get-tuple-element.46) | copy-start | bytes 73732
  171.9 9.2 %collective-permute-start.38 = (bf16[1024,128]{1,0:T(8,128)(2,1)S(1)}, bf16[1024,128]{1,0:T(8,128)(2,1)S(1)}, u32[]{:S(2)}, u32[]{:S(2)}) collective-permute-start(bf16[1024,128]{1,0:T(8,128)(2,1)S(1)} %fusion.2.refs_10_), channel_id=1, source_target_pairs={{0,4},{4,8},{8,12},{12,16},{16,20},{20,24},{24,28},{28,0},{1,5},{5... | collective-permute-start | bytes 786440 | tf_op jit(solution)/shard_map/ppermute | solution.py:263
  173.6 9.3 %collective-permute-start.40 = (bf16[1024,128]{1,0:T(8,128)(2,1)S(1)}, bf16[1024,128]{1,0:T(8,128)(2,1)}, u32[]{:S(2)}, u32[]{:S(2)}) collective-permute-start(bf16[1024,128]{1,0:T(8,128)(2,1)S(1)} %fusion.2.refs_10_), channel_id=1, source_target_pairs={{4,0},{8,4},{12,8},{16,12},{20,16},{24,20},{28,24},{0,28},{5,1},{9... | collective-permute-start | bytes 786440 | tf_op jit(solution)/shard_map/ppermute | solution.py:264
  176.7 9.2 %collective-permute-start.34 = (bf16[1024,128]{1,0:T(8,128)(2,1)S(1)}, bf16[1024,128]{1,0:T(8,128)(2,1)S(1)}, u32[]{:S(2)}, u32[]{:S(2)}) collective-permute-start(bf16[1024,128]{1,0:T(8,128)(2,1)S(1)} %fusion.2.refs_10_), channel_id=1, source_target_pairs={{0,2},{1,3},{2,0},{3,1},{4,6},{5,7},{6,4},{7,5},{8,10},{9,11},{10,... | collective-permute-start | bytes 786440 | tf_op jit(solution)/shard_map/ppermute | solution.py:258
  177.2 12.8 %collective-permute-start.36 = (bf16[1024,128]{1,0:T(8,128)(2,1)S(1)}, bf16[1024,128]{1,0:T(8,128)(2,1)S(1)}, u32[]{:S(2)}, u32[]{:S(2)}) collective-permute-start(bf16[1024,128]{1,0:T(8,128)(2,1)S(1)} %collective-permute-done.5.refs_8_.refs_2_), channel_id=1, source_target_pairs={{0,2},{1,3},{2,0},{3,1},{4,6},{5,7},{6,4},{7,5},{8,10},{9,11},{10,... | collective-permute-start | bytes 786440 | tf_op jit(solution)/shard_map/ppermute | solution.py:258
  178.7 14.2 %collective-permute-start.37 = (bf16[1024,128]{1,0:T(8,128)(2,1)S(1)}, bf16[1024,128]{1,0:T(8,128)(2,1)S(1)}, u32[]{:S(2)}, u32[]{:S(2)}) collective-permute-start(bf16[1024,128]{1,0:T(8,128)(2,1)S(1)} %collective-permute-done.6.refs_10_.refs_6_), channel_id=1, source_target_pairs={{0,2},{1,3},{2,0},{3,1},{4,6},{5,7},{6,4},{7,5},{8,10},{9,11},{10,... | collective-permute-start | bytes 786440 | tf_op jit(solution)/shard_map/ppermute | solution.py:258
  181.1 14.5 %collective-permute-start.39 = (bf16[1024,128]{1,0:T(8,128)(2,1)S(1)}, bf16[1024,128]{1,0:T(8,128)(2,1)S(1)}, u32[]{:S(2)}, u32[]{:S(2)}) collective-permute-start(bf16[1024,128]{1,0:T(8,128)(2,1)S(1)} %collective-permute-done.38.refs_8_), channel_id=1, source_target_pairs={{0,2},{1,3},{2,0},{3,1},{4,6},{5,7},{6,4},{7,5},{8,10},{9,11},{10,... | collective-permute-start | bytes 786440 | tf_op jit(solution)/shard_map/ppermute | solution.py:258
  182.9 15.6 %collective-permute-start.41 = (bf16[1024,128]{1,0:T(8,128)(2,1)}, bf16[1024,128]{1,0:T(8,128)(2,1)S(1)}, u32[]{:S(2)}, u32[]{:S(2)}) collective-permute-start(bf16[1024,128]{1,0:T(8,128)(2,1)} %collective-permute-done.40.refs_12_), channel_id=1, source_target_pairs={{0,2},{1,3},{2,0},{3,1},{4,6},{5,7},{6,4},{7,5},{8,10},{9,11},{10,... | collective-permute-start | bytes 786440 | tf_op jit(solution)/shard_map/ppermute | solution.py:258
  186.9 20.5 %copy-start.1 = (bf16[24,256,128]{2,1,0:T(8,128)(2,1)S(1)}, bf16[24,256,128]{2,1,0:T(8,128)(2,1)}, u32[]{:S(2)}) copy-start(bf16[24,256,128]{2,1,0:T(8,128)(2,1)} %basis_ref.3) | copy-start | bytes 4718596
  186.9 17.9 %collective-permute-start.35 = (bf16[1024,256]{1,0:T(8,128)(2,1)}, bf16[1024,256]{1,0:T(8,128)(2,1)}, u32[]{:S(2)}, u32[]{:S(2)}) collective-permute-start(bf16[1024,256]{1,0:T(8,128)(2,1)} %pad_maximum_fusion.1), channel_id=1, source_target_pairs={{0,1},{1,0},{2,3},{3,2},{4,5},{5,4},{6,7},{7,6},{8,9},{9,8},{10,11... | collective-permute-start | bytes 1572872 | tf_op jit(solution)/shard_map/ppermute | solution.py:258
  204.8 2.6 %collective-permute-start.42 = (bf16[24,128,128]{2,1,0:T(8,128)(2,1)}, bf16[24,128,128]{2,1,0:T(8,128)(2,1)}, u32[]{:S(2)}, u32[]{:S(2)}) collective-permute-start(bf16[24,128,128]{2,1,0:T(8,128)(2,1)} %get-tuple-element.25), channel_id=1, source_target_pairs={{0,1},{1,0},{2,3},{3,2},{4,5},{5,4},{6,7},{7,6},{8,9},{9,8},{10,11... | collective-permute-start | bytes 2359304 | tf_op jit(solution)/shard_map/ppermute | solution.py:258
  (8 other events, 58.5 us)

commit v3 on v2

--- a/solution.py
+++ b/solution.py
@@ -32,15 +32,15 @@
     return rows, lax.broadcasted_iota(jnp.int32, (size, size), 1)
 
 
-def integrate_kernel(basis_ref, weights_ref, full_ref, packed_ref, diagonal):
-    nbatch = basis_ref.shape[0]
-    half = basis_ref.shape[2] // 2
+def integrate_kernel(start, basis_ref, weights_ref, full_ref, packed_ref, diagonal):
+    nbatch = full_ref.shape[0]
+    half = full_ref.shape[2] // 2
     row, column = triangle(half)
     diagonal[...] = jnp.zeros_like(diagonal)
 
     def step(b, carry):
-        values = basis_ref[b]
-        weighted = values.astype(F32).T * weights_ref[b]
+        values = basis_ref[start + b]
+        weighted = values.astype(F32).T * weights_ref[start + b]
         ham = split_dot(weighted, values, (((1,), (0,)), ((), ())))
         full_ref[b] = ham.astype(BF16)
         last = ham[half:, half:]
@@ -59,11 +59,12 @@
     return -(-nbatch // 32) * 32
 
 
-def integrate(basis_values, weights):
-    nbatch, points, columns = basis_values.shape
+def integrate(basis_values, weights, start, stop):
+    _, points, columns = basis_values.shape
+    nbatch = stop - start
     extra = padded_rows(nbatch)
     return pl.pallas_call(
-        integrate_kernel,
+        functools.partial(integrate_kernel, start),
         out_shape=[
             jax.ShapeDtypeStruct((nbatch, columns, columns), BF16),
             jax.ShapeDtypeStruct((nbatch * columns // 2 + extra, columns), BF16),
@@ -74,10 +75,10 @@
         compiler_params=params(),
         cost_estimate=pl.CostEstimate(
             flops=4 * nbatch * points * columns * columns,
-            bytes_accessed=basis_values.size * 2 + nbatch * columns * columns * 3,
+            bytes_accessed=nbatch * columns * (points * 2 + columns * 3),
             transcendentals=0,
         ),
-    )(basis_values, weights.reshape(nbatch, 1, points))
+    )(basis_values, weights.reshape(-1, 1, points))
 
 
 def unpack_kernel(packed_ref, full_ref, diagonal):
@@ -269,29 +270,57 @@
     return lax.dynamic_slice_in_dim(array, index * width, width, 1)
 
 
-def rotate(part, occ_energy, virt_energy):
-    size = lax.axis_size("grid")
+def rotations(parts, levels, energies, ties, finish):
+    count, size = len(parts), lax.axis_size("grid")
     if size != 8:
-        total = lax.psum(part, "grid")
-        return (total / (occ_energy[:, None] - virt_energy[None, :])).astype(BF16)
+        for k, part in enumerate(parts):
+            total = lax.psum(part, "grid")
+            finish(k, (total / (levels[k][:, None] - energies[k][None, :])).astype(BF16))
+        return
     index = lax.axis_index("grid")
-    half = part.shape[0] // 2
+    half = parts[0].shape[0] // 2
     side, place = index % 2, index // 2
-    keep = lax.dynamic_slice_in_dim(part, side * half, half, 0)
-    send = lax.dynamic_slice_in_dim(part, (1 - side) * half, half, 0).astype(BF16)
-    total = keep + flip(send, "grid", 1).astype(F32)
+    outer = (place == 0) | (place == 3)
     inward = [(0, 2), (1, 3), (6, 4), (7, 5)]
+    outward = [(j, i) for i, j in inward]
     across = [(2, 4), (3, 5), (4, 2), (5, 3)]
-    outward = [(j, i) for i, j in inward]
-    total = total + lax.ppermute(total.astype(BF16), "grid", inward).astype(F32)
-    total = total + lax.ppermute(total.astype(BF16), "grid", across).astype(F32)
-    energy = lax.dynamic_slice_in_dim(occ_energy, side * half, half, 0)
-    own = (total / (energy[:, None] - virt_energy[None, :])).astype(BF16)
-    outer = (place == 0) | (place == 3)
-    own = jnp.where(outer, lax.ppermute(own, "grid", outward), own)
-    other = flip(own, "grid", 1)
-    low, high = jnp.where(side == 0, own, other), jnp.where(side == 0, other, own)
-    return jnp.concatenate([low, high], axis=0)
+    sums, turned, done = {}, {}, {}
+    for slot in range(count + 4):
+        moved = {}
+        if slot < count:
+            send = lax.dynamic_slice_in_dim(parts[slot], (1 - side) * half, half, 0)
+            moved["first"] = flip(send.astype(BF16), "grid", 1)
+        if 0 <= slot - 4:
+            moved["last"] = flip(turned[slot - 4], "grid", 1)
+        coming, going = slot - 1, slot - 3
+        if 0 <= coming < count and 0 <= going < count:
+            payload = jnp.where(outer, sums[coming].astype(BF16), turned[going])
+            moved["ends"] = lax.ppermute(payload, "grid", inward + outward)
+        elif 0 <= coming < count:
+            moved["ends"] = lax.ppermute(sums[coming].astype(BF16), "grid", inward)
+        elif 0 <= going < count:
+            moved["ends"] = lax.ppermute(turned[going], "grid", outward)
+        if 0 <= slot - 2 < count:
+            moved["middle"] = lax.ppermute(sums[slot - 2].astype(BF16), "grid", across)
+        moved, _ = lax.optimization_barrier((moved, ties.pop(slot, ())))
+        if "first" in moved:
+            keep = lax.dynamic_slice_in_dim(parts[slot], side * half, half, 0)
+            sums[slot] = keep + moved["first"].astype(F32)
+        if 0 <= going < count:
+            turned[going] = jnp.where(outer, moved["ends"], turned[going])
+        if 0 <= coming < count:
+            sums[coming] = sums[coming] + moved["ends"].astype(F32)
+        if "middle" in moved:
+            k = slot - 2
+            level = lax.dynamic_slice_in_dim(levels[k], side * half, half, 0)
+            total = sums[k] + moved["middle"].astype(F32)
+            turned[k] = (total / (level[:, None] - energies[k][None, :])).astype(BF16)
+        if "last" in moved:
+            own, other = turned[slot - 4], moved["last"]
+            low, high = jnp.where(side == 0, own, other), jnp.where(side == 0, other, own)
+            tie = finish(slot - 4, jnp.concatenate([low, high], axis=0))
+            if slot + 2 < count + 4:
+                ties.setdefault(slot + 1, []).append(tie)
 
 
 def per_device(
@@ -316,21 +345,31 @@
     occ_own = column_part(occ_coef, quarter, width)
     occ_before, occ_after = neighbours(occ_own)
 
-    blocks_near = flip(blocks, "tile", 1)
-    blocks_far = flip(blocks, "tile", 2)
-    blocks_last = flip(blocks_far, "tile", 1)
     weights = jnp.where(live_mask, weighted_potential, 0.0)
-    ham, ham_packed = integrate(basis_values, weights)
-    ham_near = flip(ham, "tile", 1)
-    ham_far = unpack(flip(ham_packed, "tile", 2), nbatch, columns)
-    ham_far, occ_before, occ_after = lax.optimization_barrier((ham_far, occ_before, occ_after))
-    ham_last = flip(ham_far, "tile", 1)
+    weights, occ_own = lax.optimization_barrier((weights, occ_own))
+    middle = -(-nbatch // 2)
+    lists = [blocks, flip(blocks, "tile", 1), flip(blocks, "tile", 2)]
+    lists.append(flip(lists[2], "tile", 1))
+    fulls, arrived = [], []
+    for start, stop in ((0, middle), (middle, nbatch)):
+        full, packed = integrate(basis_values, weights, start, stop)
+        fulls.append(full)
+        arrived.append(flip(packed, "tile", 2))
+    lists, arrived[1], occ_before, occ_after = lax.optimization_barrier(
+        (lists, arrived[1], occ_before, occ_after)
+    )
+    hams, places = [], []
+    for i, (start, stop) in enumerate(((0, middle), (middle, nbatch))):
+        far = unpack(arrived[i], stop - start, columns)
+        hams += [fulls[i], flip(fulls[i], "tile", 1), far, flip(far, "tile", 1)]
+        places += [array[start:stop] for array in lists]
+    blocks_near = lists[1]
     virt_near = flip(virt_coef, "tile", 1)
     energy_near = flip(virt_energy, "tile", 1)
 
     to_before, own_sum, to_after = apply_window(
-        [blocks, blocks_near, blocks_far, blocks_last],
-        [ham, ham_near, ham_far, ham_last],
+        places,
+        hams,
         occ_before,
         occ_own,
         occ_after,
@@ -351,19 +390,36 @@
     ]
     virtuals = [(virt_coef, virt_energy), (virt_near, energy_near)]
     coefs = [None, None]
-    for part, share in ((0, 0), (1, 0), (1, 1), (0, 1)):
-        virt, energy = virtuals[share]
-        virt_ham = lax.dot_general(
-            ham_sums[part], virt, (((0,), (0,)), ((), ())), preferred_element_type=F32
-        )
-        rotation = rotate(virt_ham, levels[part], energy)
-        term = lax.dot_general(virt, rotation, NT, preferred_element_type=F32)
+    order = ((0, 0), (1, 0), (1, 1), (0, 1))
+
+    def finish(k, rotation):
+        part, share = order[k]
+        term = lax.dot_general(virtuals[share][0], rotation, NT, preferred_element_type=F32)
         coefs[part] = term if coefs[part] is None else coefs[part] + term
+        return term
+
+    rotations(
+        [
+            lax.dot_general(
+                ham_sums[part],
+                virtuals[share][0],
+                (((0,), (0,)), ((), ())),
+                preferred_element_type=F32,
+            )
+            for part, share in order
+        ],
+        [levels[part] for part, share in order],
+        [virtuals[share][1] for part, share in order],
+        {3: [before_far, after_far]},
+        finish,
+    )
     coef_far = flip(coefs[1].astype(BF16), "tile", 2)
     resp_own = (coefs[0] + coef_far.astype(F32)).astype(BF16)
 
     resp_before, resp_after = neighbours(resp_own)
-    resp_far = flip(resp_own, "tile", 2)
+    resp_far, resp_before, resp_after = lax.optimization_barrier(
+        (flip(resp_own, "tile", 2), resp_before, resp_after)
+    )
     resp_before_far, resp_after_far = flip(resp_before, "tile", 2), flip(resp_after, "tile", 2)
     first = chip == 0
     half = jnp.concatenate(
@@ -375,8 +431,9 @@
         [jnp.where(first, half, half_near), jnp.where(first, half_near, half)], axis=1
     )
 
+    lists, response_coef = lax.optimization_barrier(([blocks, blocks_near], response_coef))
     overlap_own, overlap_near = overlaps(
-        [blocks, blocks_near],
+        lists,
         columns,
         [occ_before, before_far, occ_own, occ_far, occ_after, after_far],
         [resp_before, resp_before_far, resp_own, resp_far, resp_after, resp_after_far],

time: 212 us -> 195 us (0.920)
  waiting for transfers between devices: 98.6 us -> 73.1 us
  other arithmetic: 11.3 us -> 18.7 us
  local copies, waits for them, and re-layouts: 5.46 us -> 9.64 us
  matrix products: 24.6 us -> 20.7 us
  Pallas kernels: 17.6 us -> 14.9 us
  starting transfers between devices: 52.4 us -> 54.7 us
    ppermute x12 -> x10, waiting for transfers between devices: 40.4 us -> 14.4 us  [the longest x2 10.6 us: rotations(): moved['ends'] = lax.ppermute(turned[going], 'grid', outward)]
    ppermute x25 -> x28, starting transfers between devices: 18.2 us -> 25.4 us  [flip(): lax.ppermute(array, axis, [(i, i ^ mask) for i in range(lax.axis_size(axi...]
    ppermute x1, waiting for transfers between devices: 5.89 us -> 11.9 us  [per_device(): lax.ppermute(to_before, 'grid', [((i + 1) % size, i) for i in range(size)])]
    select_n x8 -> x10, other arithmetic: 0.34 us -> 5.48 us  [the longest x2 3.33 us: rotations(): payload = jnp.where(outer, sums[coming].astype(BF16), turned[going])]
    ppermute x12 -> x10, starting transfers between devices: 21.4 us -> 16.4 us  [the longest x2 6.81 us: rotations(): moved['ends'] = lax.ppermute(payload, 'grid', inward + outward)]
    ppermute x1, waiting for transfers between devices: 4.9 us -> 0.01 us  [per_device(): lax.ppermute(to_after, 'grid', [(i, (i + 1) % size) for i in range(size)])]
    dot_general x8, matrix products: 24.6 us -> 20.7 us  [the longest x4 11.7 us: per_device(): lax.dot_general(ham_sums[part], virtuals[share][0], (((0,), (0,)), ((), (...]
    convert_element_type x10 -> x8, other arithmetic: 4.87 us -> 8.31 us  [the longest x4 4.12 us: rotations(): moved['middle'] = lax.ppermute(sums[slot - 2].astype(BF16), 'grid', across)]
  transfers between devices with their start and end apart: 43 -> 44, of which waited for: 27 -> 21; matrix products, arithmetic and copies ran while one was open for 15% -> 16% of each run, Pallas kernels for 3% -> 5%
where the time goes in v3:
time: 195 us; the launch traced here: 193 us
  waiting for transfers between devices  73.1 us (37%)
  starting transfers between devices  54.7 us (28%)
  matrix products  20.7 us (11%)
  other arithmetic  18.7 us (10%)
  Pallas kernels  14.9 us (8%)
  local copies, waits for them, and re-layouts  9.64 us (5%)
    ppermute x28, waiting for transfers between devices, flip(): lax.ppermute(array, axis, [(i, i ^ mask) for i in range(lax.axis_size(axi...  39.7 us
    ppermute x28, starting transfers between devices, flip(): lax.ppermute(array, axis, [(i, i ^ mask) for i in range(lax.axis_size(axi...  25.4 us
    ppermute x1, waiting for transfers between devices, per_device(): lax.ppermute(to_before, 'grid', [((i + 1) % size, i) for i in range(size)])  11.9 us
    dot_general x4, matrix products, per_device(): lax.dot_general(ham_sums[part], virtuals[share][0], (((0,), (0,)), ((), (...  11.7 us
    ppermute x2, waiting for transfers between devices, rotations(): moved['ends'] = lax.ppermute(turned[going], 'grid', outward)  10.6 us
    dot_general x4, matrix products, finish(): lax.dot_general(virtuals[share][0], rotation, NT, preferred_element_type=...  8.96 us
    ppermute x2, starting transfers between devices, neighbours(): lax.ppermute(array, 'grid', [((i + 1) % size, i) for i in range(size)])  7.76 us
    unnamed x66, local copies, waits for them, and re-layouts  7.43 us
  transfers between devices with their start and end apart: 44, of which 21 were waited for; matrix products, arithmetic and copies ran while one was open for 16% of the time, Pallas kernels for 5%

profile of v3, /device:TPU:0, one launch (start us, length us, event | category | flops | bytes accessed | tf_op | source)
XLA Modules:
  0.0 193.0 jit_solution(15864986607063072435)
XLA Ops:
  1.8 3.0 %collective-permute-start.4 = (bf16[1024,128]{1,0:T(8,128)(2,1)S(1)}, bf16[1024,128]{1,0:T(8,128)(2,1)S(1)}, u32[]{:S(2)}, u32[]{:S(2)}) collective-permute-start(bf16[1024,128]{1,0:T(8,128)(2,1)S(1)} %get-tuple-element.55.refs_17_.refs_4_), channel_id=1, source_target_pairs={{0,4},{4,8},{8,12},{12,16},{16,20},{20,24},{24,28},{28,0},{1,5},{5... | collective-permute-start | bytes 786440 | tf_op jit(solution)/shard_map/ppermute | solution.py:264
  4.8 3.1 %collective-permute-start.5 = (bf16[1024,128]{1,0:T(8,128)(2,1)S(1)}, bf16[1024,128]{1,0:T(8,128)(2,1)S(1)}, u32[]{:S(2)}, u32[]{:S(2)}) collective-permute-start(bf16[1024,128]{1,0:T(8,128)(2,1)S(1)} %get-tuple-element.55.refs_17_.refs_4_), channel_id=1, source_target_pairs={{4,0},{8,4},{12,8},{16,12},{20,16},{24,20},{28,24},{0,28},{5,1},{9... | collective-permute-start | bytes 786440 | tf_op jit(solution)/shard_map/ppermute | solution.py:265
  10.8 1.5 shard_map.105
  12.3 1.7 collective-permute-start.7
  13.9 1.5 shard_map.104
  16.0 1.6 collective-permute-start.1
  17.6 5.9 %collective-permute-done.1 = s32[24,2]{1,0:T(8,128)S(1)} collective-permute-done((s32[24,2]{1,0:T(8,128)S(1)}, s32[24,2]{1,0:T(8,128)S(1)}, u32[]{:S(2)}, u32[]{:S(2)}) %collective-permute-start.1) | collective-permute-done | bytes 224 | tf_op jit(solution)/shard_map/ppermute | solution.py:259
  31.0 3.9 %shard_map.108 = (bf16[1024,128]{1,0:T(8,128)(2,1)S(1)}, f32[1024,128]{1,0:T(8,128)S(1)}, bf16[1024,128]{1,0:T(8,128)(2,1)S(1)}) custom-call(s32[12,2]{1,0:T(8,128)S(1)} %get-tuple-element.118.refs_0_, s32[12,2]{1,0:T(8,128)S(1)} %get-tuple-element.109.refs_1_, s32[12,2]{1,0:T(8,128)S(1)} %get-tuple-element.116.refs_2_, ...), custom_call_target="tpu_custom_call" | custom-call | flops 402653184 | bytes 4980736 | tf_op jit(solution)/shard_map/pallas_call | solution.py:158
  35.0 1.7 collective-permute-start.12
  37.1 11.9 %collective-permute-done.12 = bf16[1024,128]{1,0:T(8,128)(2,1)S(1)} collective-permute-done((bf16[1024,128]{1,0:T(8,128)(2,1)S(1)}, bf16[1024,128]{1,0:T(8,128)(2,1)S(1)}, u32[]{:S(2)}, u32[]{:S(2)}) %collective-permute-start.12) | collective-permute-done | bytes 262176 | tf_op jit(solution)/shard_map/ppermute | solution.py:379
  49.1 3.0 %fusion.35 = f32[128,1920]{1,0:T(8,128)S(1)} fusion(bf16[1024,128]{1,0:T(8,128)(2,1)S(1)} %add_convert_fusion, bf16[1024,1920]{1,0:T(8,128)(2,1)} %param.15), kind=kOutput, calls=%fused_computation.81 | convolution fusion | flops 503316480 | bytes 5177344 | tf_op jit(solution)/shard_map/dot_general | solution.py:403
  52.2 1.6 collective-permute-start.13
  53.8 5.6 %collective-permute-done.15 = bf16[64,1920]{1,0:T(8,128)(2,1)S(1)} collective-permute-done((bf16[64,1920]{1,0:T(8,128)(2,1)S(1)}, bf16[64,1920]{1,0:T(8,128)(2,1)S(1)}, u32[]{:S(2)}, u32[]{:S(2)}) %collective-permute-start.15) | collective-permute-done | bytes 245792 | tf_op jit(solution)/shard_map/ppermute | solution.py:259
  60.2 2.7 %collective-permute-start.16 = (bf16[64,1920]{1,0:T(8,128)(2,1)}, bf16[64,1920]{1,0:T(8,128)(2,1)}, u32[]{:S(2)}, u32[]{:S(2)}) collective-permute-start(bf16[64,1920]{1,0:T(8,128)(2,1)} %fusion.21), channel_id=1, source_target_pairs={{0,8},{4,12},{24,16},{28,20},{1,9},{5,13},{25,17},{29,21},{2,10},{... | collective-permute-start | bytes 737288 | tf_op jit(solution)/shard_map/ppermute | solution.py:300
  62.9 3.0 %fusion.34 = f32[128,1920]{1,0:T(8,128)S(1)} fusion(bf16[1024,128]{1,0:T(8,128)(2,1)S(1)} %collective-permute-done.13, bf16[1024,1920]{1,0:T(8,128)(2,1)} %param.15), kind=kOutput, calls=%fused_computation.80 | convolution fusion | flops 503316480 | bytes 5177344 | tf_op jit(solution)/shard_map/dot_general | solution.py:403
  66.6 1.7 collective-permute-start.17
  68.4 1.5 collective-permute-start.24
  70.5 3.2 %collective-permute-done.17 = bf16[64,1920]{1,0:T(8,128)(2,1)} collective-permute-done((bf16[64,1920]{1,0:T(8,128)(2,1)}, bf16[64,1920]{1,0:T(8,128)(2,1)}, u32[]{:S(2)}, u32[]{:S(2)}) %collective-permute-start.17) | collective-permute-done | bytes 245792 | tf_op jit(solution)/shard_map/ppermute | solution.py:259
  77.8 3.0 %fusion.33 = f32[128,1920]{1,0:T(8,128)S(1)} fusion(bf16[1024,128]{1,0:T(8,128)(2,1)} %copy-done.24, bf16[1024,1920]{1,0:T(8,128)(2,1)} %collective-permute-done.14), kind=kOutput, calls=%fused_computation.79 | convolution fusion | flops 503316480 | bytes 5177344 | tf_op jit(solution)/shard_map/dot_general | solution.py:403
  80.8 1.8 collective-permute-start.19
  82.7 2.9 %fusion.36 = f32[128,1920]{1,0:T(8,128)S(1)} fusion(bf16[1024,128]{1,0:T(8,128)(2,1)S(1)} %copy-done.15, bf16[1024,1920]{1,0:T(8,128)(2,1)} %collective-permute-done.14), kind=kOutput, calls=%fused_computation.82 | convolution fusion | flops 503316480 | bytes 5177344 | tf_op jit(solution)/shard_map/dot_general | solution.py:403
  86.2 2.4 %collective-permute-done.19 = bf16[64,1920]{1,0:T(8,128)(2,1)S(1)} collective-permute-done((bf16[64,1920]{1,0:T(8,128)(2,1)S(1)}, bf16[64,1920]{1,0:T(8,128)(2,1)S(1)}, u32[]{:S(2)}, u32[]{:S(2)}) %collective-permute-start.19) | collective-permute-done | bytes 245792 | tf_op jit(solution)/shard_map/ppermute | solution.py:259
  90.0 1.8 collective-permute-start.21
  93.6 2.6 %collective-permute-done.21 = bf16[64,1920]{1,0:T(8,128)(2,1)S(1)} collective-permute-done((bf16[64,1920]{1,0:T(8,128)(2,1)S(1)}, bf16[64,1920]{1,0:T(8,128)(2,1)S(1)}, u32[]{:S(2)}, u32[]{:S(2)}) %collective-permute-start.21) | collective-permute-done | bytes 245792 | tf_op jit(solution)/shard_map/ppermute | solution.py:298
  97.8 2.0 %convert_select_fusion = (bf16[64,1920]{1,0:T(8,128)(2,1)}, bf16[64,1920]{1,0:T(8,128)(2,1)}) fusion(pred[]{:T(512)S(6)} %or.3, bf16[64,1920]{1,0:T(8,128)(2,1)S(1)} %collective-permute-done.22, f32[128,1920]{1,0:T(8,128)S(1)} %fusion.36, s32[]{:T(128)S(6)} %select_n.151, f32[1920]{0:T(1024)} %param.17, f32[64]{0:T(128)S(1)} %get-tuple-element.112, ...), kind=kLoop, calls=%fused_computation.48 | loop fusion | flops 1597440 | bytes 2465541 | tf_op jit(solution)/shard_map/jit(_where)/select_n | solution.py:297
  99.8 5.0 %collective-permute-start.26 = (bf16[64,1920]{1,0:T(8,128)(2,1)}, bf16[64,1920]{1,0:T(8,128)(2,1)S(1)}, u32[]{:S(2)}, u32[]{:S(2)}) collective-permute-start(bf16[64,1920]{1,0:T(8,128)(2,1)} %get-tuple-element.86), channel_id=1, source_target_pairs={{0,8},{4,12},{24,16},{28,20},{8,0},{12,4},{16,24},{20,28},{1,9},{5... | collective-permute-start | bytes 737288 | tf_op jit(solution)/shard_map/ppermute | solution.py:298
  104.8 2.5 %collective-permute-start.27 = (bf16[64,1920]{1,0:T(8,128)(2,1)}, bf16[64,1920]{1,0:T(8,128)(2,1)S(1)}, u32[]{:S(2)}, u32[]{:S(2)}) collective-permute-start(bf16[64,1920]{1,0:T(8,128)(2,1)} %broadcast_select_fusion.7), channel_id=1, source_target_pairs={{0,4},{4,0},{8,12},{12,8},{16,20},{20,16},{24,28},{28,24},{1,5},{5... | collective-permute-start | bytes 737288 | tf_op jit(solution)/shard_map/ppermute | solution.py:259
  109.1 2.5 %collective-permute-done.27 = bf16[64,1920]{1,0:T(8,128)(2,1)S(1)} collective-permute-done((bf16[64,1920]{1,0:T(8,128)(2,1)}, bf16[64,1920]{1,0:T(8,128)(2,1)S(1)}, u32[]{:S(2)}, u32[]{:S(2)}) %collective-permute-start.27) | collective-permute-done | bytes 245792 | tf_op jit(solution)/shard_map/ppermute | solution.py:259
  112.8 1.5 divide_convert_fusion.1
  115.8 2.1 %collective-permute-start.31 = (bf16[64,1920]{1,0:T(8,128)(2,1)S(1)}, bf16[64,1920]{1,0:T(8,128)(2,1)S(1)}, u32[]{:S(2)}, u32[]{:S(2)}) collective-permute-start(bf16[64,1920]{1,0:T(8,128)(2,1)S(1)} %broadcast_select_fusion.6), channel_id=1, source_target_pairs={{0,4},{4,0},{8,12},{12,8},{16,20},{20,16},{24,28},{28,24},{1,5},{5... | collective-permute-start | bytes 737288 | tf_op jit(solution)/shard_map/ppermute | solution.py:259
  120.9 3.9 %collective-permute-done.30 = bf16[64,1920]{1,0:T(8,128)(2,1)S(1)} collective-permute-done((bf16[64,1920]{1,0:T(8,128)(2,1)S(1)}, bf16[64,1920]{1,0:T(8,128)(2,1)S(1)}, u32[]{:S(2)}, u32[]{:S(2)}) %collective-permute-start.30) | collective-permute-done | bytes 245792 | tf_op jit(solution)/shard_map/ppermute | solution.py:302
  125.8 1.5 collective-permute-start.33
  128.6 6.7 %collective-permute-done.33 = bf16[64,1920]{1,0:T(8,128)(2,1)S(1)} collective-permute-done((bf16[64,1920]{1,0:T(8,128)(2,1)S(1)}, bf16[64,1920]{1,0:T(8,128)(2,1)S(1)}, u32[]{:S(2)}, u32[]{:S(2)}) %collective-permute-start.33) | collective-permute-done | bytes 245792 | tf_op jit(solution)/shard_map/ppermute | solution.py:302
  135.4 2.1 %collective-permute-start.35 = (bf16[64,1920]{1,0:T(8,128)(2,1)S(1)}, bf16[64,1920]{1,0:T(8,128)(2,1)S(1)}, u32[]{:S(2)}, u32[]{:S(2)}) collective-permute-start(bf16[64,1920]{1,0:T(8,128)(2,1)S(1)} %broadcast_select_fusion.4), channel_id=1, source_target_pairs={{0,4},{4,0},{8,12},{12,8},{16,20},{20,16},{24,28},{28,24},{1,5},{5... | collective-permute-start | bytes 737288 | tf_op jit(solution)/shard_map/ppermute | solution.py:259
  137.4 3.3 %fusion.4 = bf16[1024,128]{1,0:T(8,128)(2,1)S(1)} fusion(f32[1024,128]{1,0:T(8,128)S(1)} %convolution_bitcast_fusion.2, bf16[1024,1920]{1,0:T(8,128)(2,1)} %collective-permute-done.14, bf16[64,1920]{1,0:T(8,128)(2,1)S(1)} %get-tuple-element.99, bf16[64,1920]{1,0:T(8,128)(2,1)S(1)} %get-tuple-element.98), kind=kOutput, calls=%fused_computation.8 | convolution fusion | flops 504561664 | bytes 5210112 | tf_op jit(solution)/shard_map/dot_general | solution.py:397
  140.8 1.6 collective-permute-start.36
  142.4 5.5 %collective-permute-done.36 = bf16[1024,128]{1,0:T(8,128)(2,1)S(1)} collective-permute-done((bf16[1024,128]{1,0:T(8,128)(2,1)S(1)}, bf16[1024,128]{1,0:T(8,128)(2,1)S(1)}, u32[]{:S(2)}, u32[]{:S(2)}) %collective-permute-start.36) | collective-permute-done | bytes 262176 | tf_op jit(solution)/shard_map/ppermute | solution.py:259
  147.9 3.3 %fusion.3.refs_10_ = bf16[1024,128]{1,0:T(8,128)(2,1)S(1)} fusion(f32[1024,128]{1,0:T(8,128)S(1)} %convolution_bitcast_fusion.3, bf16[1024,1920]{1,0:T(8,128)(2,1)} %collective-permute-done.14, bf16[1024,128]{1,0:T(8,128)(2,1)S(1)} %collective-permute-done.36, bf16[64,1920]{1,0:T(8,128)(2,1)S(1)} %get-tuple-element.97, ...), kind=kOutput, calls=%fused_computation.7 | convolution fusion | flops 504823808 | bytes 5472256 | tf_op jit(solution)/shard_map/dot_general | solution.py:397
  151.2 1.6 collective-permute-start.37
  152.8 4.7 %collective-permute-start.39 = (bf16[1024,128]{1,0:T(8,128)(2,1)S(1)}, bf16[1024,128]{1,0:T(8,128)(2,1)S(1)}, u32[]{:S(2)}, u32[]{:S(2)}) collective-permute-start(bf16[1024,128]{1,0:T(8,128)(2,1)S(1)} %fusion.3.refs_10_), channel_id=1, source_target_pairs={{4,0},{8,4},{12,8},{16,12},{20,16},{24,20},{28,24},{0,28},{5,1},{9... | collective-permute-start | bytes 786440 | tf_op jit(solution)/shard_map/ppermute | solution.py:265
  157.7 4.2 %collective-permute-done.38.refs_8_ = bf16[1024,128]{1,0:T(8,128)(2,1)S(1)} collective-permute-done((bf16[1024,128]{1,0:T(8,128)(2,1)S(1)}, bf16[1024,128]{1,0:T(8,128)(2,1)S(1)}, u32[]{:S(2)}, u32[]{:S(2)}) %collective-permute-start.38) | collective-permute-done | bytes 262176 | tf_op jit(solution)/shard_map/ppermute | solution.py:264
  161.9 2.8 %collective-permute-done.39.refs_12_ = bf16[1024,128]{1,0:T(8,128)(2,1)S(1)} collective-permute-done((bf16[1024,128]{1,0:T(8,128)(2,1)S(1)}, bf16[1024,128]{1,0:T(8,128)(2,1)S(1)}, u32[]{:S(2)}, u32[]{:S(2)}) %collective-permute-start.39) | collective-permute-done | bytes 262176 | tf_op jit(solution)/shard_map/ppermute | solution.py:265
  166.9 1.5 collective-permute-start.42
  171.1 4.7 %collective-permute-done.41.refs_9_ = bf16[1024,128]{1,0:T(8,128)(2,1)} collective-permute-done((bf16[1024,128]{1,0:T(8,128)(2,1)}, bf16[1024,128]{1,0:T(8,128)(2,1)}, u32[]{:S(2)}, u32[]{:S(2)}) %collective-permute-start.41) | collective-permute-done | bytes 262176 | tf_op jit(solution)/shard_map/ppermute | solution.py:259
  175.8 5.2 %collective-permute-done.42.refs_13_ = bf16[1024,128]{1,0:T(8,128)(2,1)} collective-permute-done((bf16[1024,128]{1,0:T(8,128)(2,1)}, bf16[1024,128]{1,0:T(8,128)(2,1)}, u32[]{:S(2)}, u32[]{:S(2)}) %collective-permute-start.42) | collective-permute-done | bytes 262176 | tf_op jit(solution)/shard_map/ppermute | solution.py:259
  183.8 4.3 %shard_map.109 = (f32[24,128,128]{2,1,0:T(8,128)S(1)}, bf16[24,128,128]{2,1,0:T(8,128)(2,1)S(1)}) custom-call(s32[24,2]{1,0:T(8,128)S(1)} %copy.21.refs_0_, s32[24,2]{1,0:T(8,128)S(1)} %collective-permute-done.refs_1_, bf16[1024,128]{1,0:T(8,128)(2,1)S(1)} %collective-permute-done.4.refs_16_.refs_2_, bf16[1024,128]{1,0:T(8,128)(2,1)S(1)} %collective-permute-done.24.refs_3_, ...), custom_call_target="tpu_custom_call" | custom-call | flops 402653184 | bytes 5505024 | tf_op jit(solution)/shard_map/pallas_call | solution.py:214
  188.3 2.2 %collective-permute-done.43.second_ref = bf16[24,128,128]{2,1,0:T(8,128)(2,1)S(1)} collective-permute-done((bf16[24,128,128]{2,1,0:T(8,128)(2,1)S(1)}, bf16[24,128,128]{2,1,0:T(8,128)(2,1)S(1)}, u32[]{:S(2)}, u32[]{:S(2)}) %collective-permute-start.43) | collective-permute-done | bytes 786464 | tf_op jit(solution)/shard_map/ppermute | solution.py:259
  190.5 1.9 shard_map.110
  (157 shorter events, 42.7 us)
Async XLA Ops:
  1.8 23.8 %collective-permute-start.4 = (bf16[1024,128]{1,0:T(8,128)(2,1)S(1)}, bf16[1024,128]{1,0:T(8,128)(2,1)S(1)}, u32[]{:S(2)}, u32[]{:S(2)}) collective-permute-start(bf16[1024,128]{1,0:T(8,128)(2,1)S(1)} %get-tuple-element.55.refs_17_.refs_4_), channel_id=1, source_target_pairs={{0,4},{4,8},{8,12},{12,16},{16,20},{20,24},{24,28},{28,0},{1,5},{5... | collective-permute-start | bytes 786440 | tf_op jit(solution)/shard_map/ppermute | solution.py:264
  4.8 21.2 %collective-permute-start.5 = (bf16[1024,128]{1,0:T(8,128)(2,1)S(1)}, bf16[1024,128]{1,0:T(8,128)(2,1)S(1)}, u32[]{:S(2)}, u32[]{:S(2)}) collective-permute-start(bf16[1024,128]{1,0:T(8,128)(2,1)S(1)} %get-tuple-element.55.refs_17_.refs_4_), channel_id=1, source_target_pairs={{4,0},{8,4},{12,8},{16,12},{20,16},{24,20},{28,24},{0,28},{5,1},{9... | collective-permute-start | bytes 786440 | tf_op jit(solution)/shard_map/ppermute | solution.py:265
  12.3 11.3 %collective-permute-start.7 = (bf16[800,128]{1,0:T(8,128)(2,1)S(1)}, bf16[800,128]{1,0:T(8,128)(2,1)S(1)}, u32[]{:S(2)}, u32[]{:S(2)}) collective-permute-start(bf16[800,128]{1,0:T(8,128)(2,1)S(1)} %get-tuple-element.51), channel_id=1, source_target_pairs={{0,2},{1,3},{2,0},{3,1},{4,6},{5,7},{6,4},{7,5},{8,10},{9,11},{10,... | collective-permute-start | bytes 614408 | tf_op jit(solution)/shard_map/ppermute | solution.py:259
  15.4 10.1 %collective-permute-start.3 = (bf16[800,128]{1,0:T(8,128)(2,1)S(1)}, bf16[800,128]{1,0:T(8,128)(2,1)S(1)}, u32[]{:S(2)}, u32[]{:S(2)}) collective-permute-start(bf16[800,128]{1,0:T(8,128)(2,1)S(1)} %get-tuple-element.45), channel_id=1, source_target_pairs={{0,2},{1,3},{2,0},{3,1},{4,6},{5,7},{6,4},{7,5},{8,10},{9,11},{10,... | collective-permute-start | bytes 614408 | tf_op jit(solution)/shard_map/ppermute | solution.py:259
  16.0 7.5 %collective-permute-start.1 = (s32[24,2]{1,0:T(8,128)S(1)}, s32[24,2]{1,0:T(8,128)S(1)}, u32[]{:S(2)}, u32[]{:S(2)}) collective-permute-start(s32[24,2]{1,0:T(8,128)S(1)} %copy.11), channel_id=1, source_target_pairs={{0,2},{1,3},{2,0},{3,1},{4,6},{5,7},{6,4},{7,5},{8,10},{9,11},{10,... | collective-permute-start | bytes 584 | tf_op jit(solution)/shard_map/ppermute | solution.py:259
  23.5 1.4 collective-permute-start
  23.5 1.4 collective-permute-start.2
  24.9 2.1 %collective-permute-start.6 = (bf16[12,128,128]{2,1,0:T(8,128)(2,1)S(1)}, bf16[12,128,128]{2,1,0:T(8,128)(2,1)S(1)}, u32[]{:S(2)}, u32[]{:S(2)}) collective-permute-start(bf16[12,128,128]{2,1,0:T(8,128)(2,1)S(1)} %get-tuple-element.50.refs_8_), channel_id=1, source_target_pairs={{0,1},{1,0},{2,3},{3,2},{4,5},{5,4},{6,7},{7,6},{8,9},{9,8},{10,11... | collective-permute-start | bytes 1179656 | tf_op jit(solution)/shard_map/ppermute | solution.py:259
  25.0 3.0 %collective-permute-start.9 = (bf16[12,128,128]{2,1,0:T(8,128)(2,1)S(1)}, bf16[12,128,128]{2,1,0:T(8,128)(2,1)}, u32[]{:S(2)}, u32[]{:S(2)}) collective-permute-start(bf16[12,128,128]{2,1,0:T(8,128)(2,1)S(1)} %get-tuple-element.52.refs_12_), channel_id=1, source_target_pairs={{0,1},{1,0},{2,3},{3,2},{4,5},{5,4},{6,7},{7,6},{8,9},{9,8},{10,11... | collective-permute-start | bytes 1179656 | tf_op jit(solution)/shard_map/ppermute | solution.py:259
  25.5 52.3 %collective-permute-start.14 = (bf16[1024,1920]{1,0:T(8,128)(2,1)}, bf16[1024,1920]{1,0:T(8,128)(2,1)}, u32[]{:S(2)}, u32[]{:S(2)}) collective-permute-start(bf16[1024,1920]{1,0:T(8,128)(2,1)} %param.15), channel_id=1, source_target_pairs={{0,1},{1,0},{2,3},{3,2},{4,5},{5,4},{6,7},{7,6},{8,9},{9,8},{10,11... | collective-permute-start | bytes 11796488 | tf_op jit(solution)/shard_map/ppermute | solution.py:259
  25.6 3.5 %collective-permute-start.8 = (bf16[12,128,128]{2,1,0:T(8,128)(2,1)S(1)}, bf16[12,128,128]{2,1,0:T(8,128)(2,1)}, u32[]{:S(2)}, u32[]{:S(2)}) collective-permute-start(bf16[12,128,128]{2,1,0:T(8,128)(2,1)S(1)} %shard_map.106.refs_10_), channel_id=1, source_target_pairs={{0,1},{1,0},{2,3},{3,2},{4,5},{5,4},{6,7},{7,6},{8,9},{9,8},{10,11... | collective-permute-start | bytes 1179656 | tf_op jit(solution)/shard_map/ppermute | solution.py:259
  27.0 3.1 %collective-permute-start.10 = (bf16[12,128,128]{2,1,0:T(8,128)(2,1)S(1)}, bf16[12,128,128]{2,1,0:T(8,128)(2,1)S(1)}, u32[]{:S(2)}, u32[]{:S(2)}) collective-permute-start(bf16[12,128,128]{2,1,0:T(8,128)(2,1)S(1)} %shard_map.107.refs_14_), channel_id=1, source_target_pairs={{0,1},{1,0},{2,3},{3,2},{4,5},{5,4},{6,7},{7,6},{8,9},{9,8},{10,11... | collective-permute-start | bytes 1179656 | tf_op jit(solution)/shard_map/ppermute | solution.py:259
  35.0 14.0 %collective-permute-start.12 = (bf16[1024,128]{1,0:T(8,128)(2,1)S(1)}, bf16[1024,128]{1,0:T(8,128)(2,1)S(1)}, u32[]{:S(2)}, u32[]{:S(2)}) collective-permute-start(bf16[1024,128]{1,0:T(8,128)(2,1)S(1)} %get-tuple-element.59), channel_id=1, source_target_pairs={{4,0},{8,4},{12,8},{16,12},{20,16},{24,20},{28,24},{0,28},{5,1},{9... | collective-permute-start | bytes 786440 | tf_op jit(solution)/shard_map/ppermute | solution.py:379
  36.7 12.3 %collective-permute-start.11 = (bf16[1024,128]{1,0:T(8,128)(2,1)S(1)}, bf16[1024,128]{1,0:T(8,128)(2,1)S(1)}, u32[]{:S(2)}, u32[]{:S(2)}) collective-permute-start(bf16[1024,128]{1,0:T(8,128)(2,1)S(1)} %get-tuple-element.58), channel_id=1, source_target_pairs={{0,4},{4,8},{8,12},{12,16},{16,20},{20,24},{24,28},{28,0},{1,5},{5... | collective-permute-start | bytes 786440 | tf_op jit(solution)/shard_map/ppermute | solution.py:378
  52.1 23.9 %copy-start.11 = (f32[128,1920]{1,0:T(8,128)}, f32[128,1920]{1,0:T(8,128)S(1)}, u32[]{:S(2)}) copy-start(f32[128,1920]{1,0:T(8,128)S(1)} %fusion.35) | copy-start | bytes 2949124
  52.1 7.2 %collective-permute-start.15 = (bf16[64,1920]{1,0:T(8,128)(2,1)S(1)}, bf16[64,1920]{1,0:T(8,128)(2,1)S(1)}, u32[]{:S(2)}, u32[]{:S(2)}) collective-permute-start(bf16[64,1920]{1,0:T(8,128)(2,1)S(1)} %dynamic-slice_convert_fusion.3), channel_id=1, source_target_pairs={{0,4},{4,0},{8,12},{12,8},{16,20},{20,16},{24,28},{28,24},{1,5},{5... | collective-permute-start | bytes 737288 | tf_op jit(solution)/shard_map/ppermute | solution.py:259
  52.2 10.7 %collective-permute-start.13 = (bf16[1024,128]{1,0:T(8,128)(2,1)S(1)}, bf16[1024,128]{1,0:T(8,128)(2,1)S(1)}, u32[]{:S(2)}, u32[]{:S(2)}) collective-permute-start(bf16[1024,128]{1,0:T(8,128)(2,1)S(1)} %add_convert_fusion), channel_id=1, source_target_pairs={{0,2},{1,3},{2,0},{3,1},{4,6},{5,7},{6,4},{7,5},{8,10},{9,11},{10,... | collective-permute-start | bytes 786440 | tf_op jit(solution)/shard_map/ppermute | solution.py:259
  60.2 10.3 %collective-permute-start.16 = (bf16[64,1920]{1,0:T(8,128)(2,1)}, bf16[64,1920]{1,0:T(8,128)(2,1)}, u32[]{:S(2)}, u32[]{:S(2)}) collective-permute-start(bf16[64,1920]{1,0:T(8,128)(2,1)} %fusion.21), channel_id=1, source_target_pairs={{0,8},{4,12},{24,16},{28,20},{1,9},{5,13},{25,17},{29,21},{2,10},{... | collective-permute-start | bytes 737288 | tf_op jit(solution)/shard_map/ppermute | solution.py:300
  66.6 7.1 %collective-permute-start.17 = (bf16[64,1920]{1,0:T(8,128)(2,1)}, bf16[64,1920]{1,0:T(8,128)(2,1)}, u32[]{:S(2)}, u32[]{:S(2)}) collective-permute-start(bf16[64,1920]{1,0:T(8,128)(2,1)} %dynamic-slice_convert_fusion.2), channel_id=1, source_target_pairs={{0,4},{4,0},{8,12},{12,8},{16,20},{20,16},{24,28},{28,24},{1,5},{5... | collective-permute-start | bytes 737288 | tf_op jit(solution)/shard_map/ppermute | solution.py:259
  68.4 29.4 %copy-start.30 = (f32[64]{0:T(128)}, f32[64]{0:T(128)S(1)}, u32[]{:S(2)}) copy-start(f32[64]{0:T(128)S(1)} %get-tuple-element.112) | copy-start | bytes 772
  68.4 25.1 %collective-permute-start.24 = (bf16[1024,128]{1,0:T(8,128)(2,1)S(1)}, bf16[1024,128]{1,0:T(8,128)(2,1)S(1)}, u32[]{:S(2)}, u32[]{:S(2)}) collective-permute-start(bf16[1024,128]{1,0:T(8,128)(2,1)S(1)} %collective-permute-done.4.refs_16_.refs_2_), channel_id=1, source_target_pairs={{0,2},{1,3},{2,0},{3,1},{4,6},{5,7},{6,4},{7,5},{8,10},{9,11},{10,... | collective-permute-start | bytes 786440 | tf_op jit(solution)/shard_map/ppermute | solution.py:259
  69.9 23.6 %collective-permute-start.25 = (bf16[1024,128]{1,0:T(8,128)(2,1)S(1)}, bf16[1024,128]{1,0:T(8,128)(2,1)S(1)}, u32[]{:S(2)}, u32[]{:S(2)}) collective-permute-start(bf16[1024,128]{1,0:T(8,128)(2,1)S(1)} %collective-permute-done.5.refs_18_.refs_6_), channel_id=1, source_target_pairs={{0,2},{1,3},{2,0},{3,1},{4,6},{5,7},{6,4},{7,5},{8,10},{9,11},{10,... | collective-permute-start | bytes 786440 | tf_op jit(solution)/shard_map/ppermute | solution.py:259
  74.6 10.9 %collective-permute-start.18 = (bf16[64,1920]{1,0:T(8,128)(2,1)S(1)}, bf16[64,1920]{1,0:T(8,128)(2,1)S(1)}, u32[]{:S(2)}, u32[]{:S(2)}) collective-permute-start(bf16[64,1920]{1,0:T(8,128)(2,1)S(1)} %fusion.22), channel_id=1, source_target_pairs={{0,8},{4,12},{24,16},{28,20},{1,9},{5,13},{25,17},{29,21},{2,10},{... | collective-permute-start | bytes 737288 | tf_op jit(solution)/shard_map/ppermute | solution.py:300
  77.1 9.1 %collective-permute-start.20 = (bf16[64,1920]{1,0:T(8,128)(2,1)S(1)}, bf16[64,1920]{1,0:T(8,128)(2,1)S(1)}, u32[]{:S(2)}, u32[]{:S(2)}) collective-permute-start(bf16[64,1920]{1,0:T(8,128)(2,1)S(1)} %fusion.17), channel_id=1, source_target_pairs={{8,16},{12,20},{16,8},{20,12},{9,17},{13,21},{17,9},{21,13},{10,18... | collective-permute-start | bytes 737288 | tf_op jit(solution)/shard_map/ppermute | solution.py:304
  80.8 7.8 %collective-permute-start.19 = (bf16[64,1920]{1,0:T(8,128)(2,1)S(1)}, bf16[64,1920]{1,0:T(8,128)(2,1)S(1)}, u32[]{:S(2)}, u32[]{:S(2)}) collective-permute-start(bf16[64,1920]{1,0:T(8,128)(2,1)S(1)} %dynamic-slice_convert_fusion.1), channel_id=1, source_target_pairs={{0,4},{4,0},{8,12},{12,8},{16,20},{20,16},{24,28},{28,24},{1,5},{5... | collective-permute-start | bytes 737288 | tf_op jit(solution)/shard_map/ppermute | solution.py:259
  85.6 8.0 %collective-permute-start.22 = (bf16[64,1920]{1,0:T(8,128)(2,1)S(1)}, bf16[64,1920]{1,0:T(8,128)(2,1)S(1)}, u32[]{:S(2)}, u32[]{:S(2)}) collective-permute-start(bf16[64,1920]{1,0:T(8,128)(2,1)S(1)} %dynamic-slice_convert_fusion), channel_id=1, source_target_pairs={{0,4},{4,0},{8,12},{12,8},{16,20},{20,16},{24,28},{28,24},{1,5},{5... | collective-permute-start | bytes 737288 | tf_op jit(solution)/shard_map/ppermute | solution.py:259
  90.0 6.3 %collective-permute-start.21 = (bf16[64,1920]{1,0:T(8,128)(2,1)S(1)}, bf16[64,1920]{1,0:T(8,128)(2,1)S(1)}, u32[]{:S(2)}, u32[]{:S(2)}) collective-permute-start(bf16[64,1920]{1,0:T(8,128)(2,1)S(1)} %get-tuple-element.88), channel_id=1, source_target_pairs={{0,8},{4,12},{24,16},{28,20},{8,0},{12,4},{16,24},{20,28},{1,9},{5... | collective-permute-start | bytes 737288 | tf_op jit(solution)/shard_map/ppermute | solution.py:298
  92.8 3.4 %collective-permute-start.23 = (bf16[64,1920]{1,0:T(8,128)(2,1)S(1)}, bf16[64,1920]{1,0:T(8,128)(2,1)S(1)}, u32[]{:S(2)}, u32[]{:S(2)}) collective-permute-start(bf16[64,1920]{1,0:T(8,128)(2,1)S(1)} %fusion.18), channel_id=1, source_target_pairs={{8,16},{12,20},{16,8},{20,12},{9,17},{13,21},{17,9},{21,13},{10,18... | collective-permute-start | bytes 737288 | tf_op jit(solution)/shard_map/ppermute | solution.py:304
  99.8 9.3 %collective-permute-start.26 = (bf16[64,1920]{1,0:T(8,128)(2,1)}, bf16[64,1920]{1,0:T(8,128)(2,1)S(1)}, u32[]{:S(2)}, u32[]{:S(2)}) collective-permute-start(bf16[64,1920]{1,0:T(8,128)(2,1)} %get-tuple-element.86), channel_id=1, source_target_pairs={{0,8},{4,12},{24,16},{28,20},{8,0},{12,4},{16,24},{20,28},{1,9},{5... | collective-permute-start | bytes 737288 | tf_op jit(solution)/shard_map/ppermute | solution.py:298
  104.8 6.9 %collective-permute-start.27 = (bf16[64,1920]{1,0:T(8,128)(2,1)}, bf16[64,1920]{1,0:T(8,128)(2,1)S(1)}, u32[]{:S(2)}, u32[]{:S(2)}) collective-permute-start(bf16[64,1920]{1,0:T(8,128)(2,1)} %broadcast_select_fusion.7), channel_id=1, source_target_pairs={{0,4},{4,0},{8,12},{12,8},{16,20},{20,16},{24,28},{28,24},{1,5},{5... | collective-permute-start | bytes 737288 | tf_op jit(solution)/shard_map/ppermute | solution.py:259
  107.2 4.4 %collective-permute-start.28 = (bf16[64,1920]{1,0:T(8,128)(2,1)}, bf16[64,1920]{1,0:T(8,128)(2,1)S(1)}, u32[]{:S(2)}, u32[]{:S(2)}) collective-permute-start(bf16[64,1920]{1,0:T(8,128)(2,1)} %fusion.19), channel_id=1, source_target_pairs={{8,16},{12,20},{16,8},{20,12},{9,17},{13,21},{17,9},{21,13},{10,18... | collective-permute-start | bytes 737288 | tf_op jit(solution)/shard_map/ppermute | solution.py:304
  107.9 4.9 %collective-permute-start.29 = (f32[1920]{0:T(1024)}, f32[1920]{0:T(1024)}, u32[]{:S(2)}, u32[]{:S(2)}) collective-permute-start(f32[1920]{0:T(1024)} %param.17), channel_id=1, source_target_pairs={{0,1},{1,0},{2,3},{3,2},{4,5},{5,4},{6,7},{7,6},{8,9},{9,8},{10,11... | collective-permute-start | bytes 23048 | tf_op jit(solution)/shard_map/ppermute | solution.py:259
  114.4 10.4 %collective-permute-start.30 = (bf16[64,1920]{1,0:T(8,128)(2,1)S(1)}, bf16[64,1920]{1,0:T(8,128)(2,1)S(1)}, u32[]{:S(2)}, u32[]{:S(2)}) collective-permute-start(bf16[64,1920]{1,0:T(8,128)(2,1)S(1)} %divide_convert_fusion.1), channel_id=1, source_target_pairs={{8,0},{12,4},{16,24},{20,28},{9,1},{13,5},{17,25},{21,29},{10,2},{... | collective-permute-start | bytes 737288 | tf_op jit(solution)/shard_map/ppermute | solution.py:302
  115.8 9.0 %collective-permute-start.31 = (bf16[64,1920]{1,0:T(8,128)(2,1)S(1)}, bf16[64,1920]{1,0:T(8,128)(2,1)S(1)}, u32[]{:S(2)}, u32[]{:S(2)}) collective-permute-start(bf16[64,1920]{1,0:T(8,128)(2,1)S(1)} %broadcast_select_fusion.6), channel_id=1, source_target_pairs={{0,4},{4,0},{8,12},{12,8},{16,20},{20,16},{24,28},{28,24},{1,5},{5... | collective-permute-start | bytes 737288 | tf_op jit(solution)/shard_map/ppermute | solution.py:259
  117.9 6.9 %collective-permute-start.32 = (bf16[64,1920]{1,0:T(8,128)(2,1)S(1)}, bf16[64,1920]{1,0:T(8,128)(2,1)S(1)}, u32[]{:S(2)}, u32[]{:S(2)}) collective-permute-start(bf16[64,1920]{1,0:T(8,128)(2,1)S(1)} %fusion.20), channel_id=1, source_target_pairs={{8,16},{12,20},{16,8},{20,12},{9,17},{13,21},{17,9},{21,13},{10,18... | collective-permute-start | bytes 737288 | tf_op jit(solution)/shard_map/ppermute | solution.py:304
  125.8 9.5 %collective-permute-start.33 = (bf16[64,1920]{1,0:T(8,128)(2,1)S(1)}, bf16[64,1920]{1,0:T(8,128)(2,1)S(1)}, u32[]{:S(2)}, u32[]{:S(2)}) collective-permute-start(bf16[64,1920]{1,0:T(8,128)(2,1)S(1)} %divide_convert_fusion), channel_id=1, source_target_pairs={{8,0},{12,4},{16,24},{20,28},{9,1},{13,5},{17,25},{21,29},{10,2},{... | collective-permute-start | bytes 737288 | tf_op jit(solution)/shard_map/ppermute | solution.py:302
  127.3 8.0 %collective-permute-start.34 = (bf16[64,1920]{1,0:T(8,128)(2,1)S(1)}, bf16[64,1920]{1,0:T(8,128)(2,1)S(1)}, u32[]{:S(2)}, u32[]{:S(2)}) collective-permute-start(bf16[64,1920]{1,0:T(8,128)(2,1)S(1)} %broadcast_select_fusion.5), channel_id=1, source_target_pairs={{0,4},{4,0},{8,12},{12,8},{16,20},{20,16},{24,28},{28,24},{1,5},{5... | collective-permute-start | bytes 737288 | tf_op jit(solution)/shard_map/ppermute | solution.py:259
  135.4 6.9 %collective-permute-start.35 = (bf16[64,1920]{1,0:T(8,128)(2,1)S(1)}, bf16[64,1920]{1,0:T(8,128)(2,1)S(1)}, u32[]{:S(2)}, u32[]{:S(2)}) collective-permute-start(bf16[64,1920]{1,0:T(8,128)(2,1)S(1)} %broadcast_select_fusion.4), channel_id=1, source_target_pairs={{0,4},{4,0},{8,12},{12,8},{16,20},{20,16},{24,28},{28,24},{1,5},{5... | collective-permute-start | bytes 737288 | tf_op jit(solution)/shard_map/ppermute | solution.py:259
  140.8 7.1 %collective-permute-start.36 = (bf16[1024,128]{1,0:T(8,128)(2,1)S(1)}, bf16[1024,128]{1,0:T(8,128)(2,1)S(1)}, u32[]{:S(2)}, u32[]{:S(2)}) collective-permute-start(bf16[1024,128]{1,0:T(8,128)(2,1)S(1)} %fusion.4), channel_id=1, source_target_pairs={{0,2},{1,3},{2,0},{3,1},{4,6},{5,7},{6,4},{7,5},{8,10},{9,11},{10,... | collective-permute-start | bytes 786440 | tf_op jit(solution)/shard_map/ppermute | solution.py:259
  151.2 6.4 %collective-permute-start.37 = (bf16[1024,128]{1,0:T(8,128)(2,1)S(1)}, bf16[1024,128]{1,0:T(8,128)(2,1)S(1)}, u32[]{:S(2)}, u32[]{:S(2)}) collective-permute-start(bf16[1024,128]{1,0:T(8,128)(2,1)S(1)} %fusion.3.refs_10_), channel_id=1, source_target_pairs={{0,2},{1,3},{2,0},{3,1},{4,6},{5,7},{6,4},{7,5},{8,10},{9,11},{10,... | collective-permute-start | bytes 786440 | tf_op jit(solution)/shard_map/ppermute | solution.py:259
  152.8 9.1 %collective-permute-start.38 = (bf16[1024,128]{1,0:T(8,128)(2,1)S(1)}, bf16[1024,128]{1,0:T(8,128)(2,1)S(1)}, u32[]{:S(2)}, u32[]{:S(2)}) collective-permute-start(bf16[1024,128]{1,0:T(8,128)(2,1)S(1)} %fusion.3.refs_10_), channel_id=1, source_target_pairs={{0,4},{4,8},{8,12},{12,16},{16,20},{20,24},{24,28},{28,0},{1,5},{5... | collective-permute-start | bytes 786440 | tf_op jit(solution)/shard_map/ppermute | solution.py:264
  152.8 11.8 %collective-permute-start.39 = (bf16[1024,128]{1,0:T(8,128)(2,1)S(1)}, bf16[1024,128]{1,0:T(8,128)(2,1)S(1)}, u32[]{:S(2)}, u32[]{:S(2)}) collective-permute-start(bf16[1024,128]{1,0:T(8,128)(2,1)S(1)} %fusion.3.refs_10_), channel_id=1, source_target_pairs={{4,0},{8,4},{12,8},{16,12},{20,16},{24,20},{28,24},{0,28},{5,1},{9... | collective-permute-start | bytes 786440 | tf_op jit(solution)/shard_map/ppermute | solution.py:265
  166.2 22.0 %copy-start.26 = (f32[24,256]{1,0:T(8,128)S(1)}, f32[24,256]{1,0:T(8,128)}, u32[]{:S(2)}) copy-start(f32[24,256]{1,0:T(8,128)} %get-tuple-element.114) | copy-start | bytes 73732
  166.2 24.3 %copy-start.1 = (bf16[24,256,128]{2,1,0:T(8,128)(2,1)S(1)}, bf16[24,256,128]{2,1,0:T(8,128)(2,1)}, u32[]{:S(2)}) copy-start(bf16[24,256,128]{2,1,0:T(8,128)(2,1)} %basis_ref.5) | copy-start | bytes 4718596
  166.2 2.3 %collective-permute-start.40 = (bf16[1024,256]{1,0:T(8,128)(2,1)}, bf16[1024,256]{1,0:T(8,128)(2,1)}, u32[]{:S(2)}, u32[]{:S(2)}) collective-permute-start(bf16[1024,256]{1,0:T(8,128)(2,1)} %pad_maximum_fusion.1), channel_id=1, source_target_pairs={{0,1},{1,0},{2,3},{3,2},{4,5},{5,4},{6,7},{7,6},{8,9},{9,8},{10,11... | collective-permute-start | bytes 1572872 | tf_op jit(solution)/shard_map/ppermute | solution.py:259
  166.3 9.5 %collective-permute-start.41 = (bf16[1024,128]{1,0:T(8,128)(2,1)}, bf16[1024,128]{1,0:T(8,128)(2,1)}, u32[]{:S(2)}, u32[]{:S(2)}) collective-permute-start(bf16[1024,128]{1,0:T(8,128)(2,1)} %copy-done.6), channel_id=1, source_target_pairs={{0,2},{1,3},{2,0},{3,1},{4,6},{5,7},{6,4},{7,5},{8,10},{9,11},{10,... | collective-permute-start | bytes 786440 | tf_op jit(solution)/shard_map/ppermute | solution.py:259
  166.9 14.1 %collective-permute-start.42 = (bf16[1024,128]{1,0:T(8,128)(2,1)}, bf16[1024,128]{1,0:T(8,128)(2,1)}, u32[]{:S(2)}, u32[]{:S(2)}) collective-permute-start(bf16[1024,128]{1,0:T(8,128)(2,1)} %copy-done.8), channel_id=1, source_target_pairs={{0,2},{1,3},{2,0},{3,1},{4,6},{5,7},{6,4},{7,5},{8,10},{9,11},{10,... | collective-permute-start | bytes 786440 | tf_op jit(solution)/shard_map/ppermute | solution.py:259
  188.1 2.4 %collective-permute-start.43 = (bf16[24,128,128]{2,1,0:T(8,128)(2,1)S(1)}, bf16[24,128,128]{2,1,0:T(8,128)(2,1)S(1)}, u32[]{:S(2)}, u32[]{:S(2)}) collective-permute-start(bf16[24,128,128]{2,1,0:T(8,128)(2,1)S(1)} %get-tuple-element.85), channel_id=1, source_target_pairs={{0,1},{1,0},{2,3},{3,2},{4,5},{5,4},{6,7},{7,6},{8,9},{9,8},{10,11... | collective-permute-start | bytes 2359304 | tf_op jit(solution)/shard_map/ppermute | solution.py:259
  (28 other events, 206.7 us)

commit v4 on v3

v4 whole, which is shorter than its diff:
```python
import functools

import jax
import jax.numpy as jnp
from jax import lax
from jax.experimental import pallas as pl
from jax.experimental.pallas import tpu as pltpu
from jax.sharding import PartitionSpec as P

VMEM = pl.BlockSpec(memory_space=pltpu.VMEM)
SMEM = pl.BlockSpec(memory_space=pltpu.SMEM)
HBM = pl.BlockSpec(memory_space=pl.ANY)
MIB = 1024 * 1024
F32 = jnp.float32
BF16 = jnp.bfloat16
NT = (((1,), (1,)), ((), ()))


def params(mib=20):
    return pltpu.CompilerParams(vmem_limit_bytes=mib * MIB)


def split_dot(full, other, dims):
    high = full.astype(BF16)
    low = (full - high.astype(F32)).astype(BF16)
    return lax.dot_general(high, other, dims, preferred_element_type=F32) + lax.dot_general(
        low, other, dims, preferred_element_type=F32
    )


def triangle(size):
    rows = lax.broadcasted_iota(jnp.int32, (size, size), 0)
    return rows, lax.broadcasted_iota(jnp.int32, (size, size), 1)


def live_row(values_ref, counts_ref, b):
    row = values_ref[pl.ds(b, 1), :]
    points = lax.broadcasted_iota(jnp.int32, row.shape, 1)
    return jnp.where(points < counts_ref[b], row, 0.0)


def integrate_kernel(start, counts_ref, basis_ref, weights_ref, full_ref, packed_ref, diagonal):
    steps, here = pl.num_programs(0), basis_ref.shape[0]
    half = full_ref.shape[2] // 2
    row, column = triangle(half)
    now = pl.program_id(0)

    @pl.when(now == 0)
    def _():
        diagonal[...] = jnp.zeros_like(diagonal)

    for b in range(here):
        place = now * here + b
        values = basis_ref[b]
        weighted = values.astype(F32).T * live_row(weights_ref, counts_ref, start + place)
        ham = split_dot(weighted, values, (((1,), (0,)), ((), ())))
        full_ref[b] = ham.astype(BF16)
        last = ham[half:, half:]
        mixed = jnp.where(row >= column, ham[:half, :half], last)
        packed = jnp.concatenate([ham[:half, half:], mixed], axis=1)
        packed_ref[pl.ds(pl.multiple_of(place * half, half), half), :] = packed.astype(BF16)
        line = jnp.sum(jnp.where(row == column, last, 0.0), axis=0, keepdims=True)
        diagonal[pl.ds(place, 1), :] = jnp.concatenate([line, jnp.zeros_like(line)], axis=1)

    @pl.when(now == steps - 1)
    def _():
        packed_ref[steps * here * half :, :] = diagonal[...].astype(BF16)


def padded_rows(nbatch):
    return -(-nbatch // 32) * 32


def step_size(nbatch, most):
    return max(k for k in range(1, most + 1) if nbatch % k == 0)


def integrate(basis_values, counts, weights, start, stop):
    _, points, columns = basis_values.shape
    nbatch = stop - start
    here = step_size(nbatch, 4)
    rows = nbatch * columns // 2 + padded_rows(nbatch)
    first = start // here
    return pl.pallas_call(
        functools.partial(integrate_kernel, start),
        grid=(nbatch // here,),
        out_shape=[
            jax.ShapeDtypeStruct((nbatch, columns, columns), BF16),
            jax.ShapeDtypeStruct((rows, columns), BF16),
        ],
        in_specs=[
            SMEM,
            pl.BlockSpec((here, points, columns), lambda i: (first + i, 0, 0)),
            pl.BlockSpec(weights.shape, lambda i: (0, 0)),
        ],
        out_specs=[
            pl.BlockSpec((here, columns, columns), lambda i: (i, 0, 0)),
            pl.BlockSpec((rows, columns), lambda i: (0, 0)),
        ],
        scratch_shapes=[pltpu.VMEM((padded_rows(nbatch), columns), F32)],
        compiler_params=params(60),
        cost_estimate=pl.CostEstimate(
            flops=4 * nbatch * points * columns * columns,
            bytes_accessed=nbatch * columns * (points * 2 + columns * 3),
            transcendentals=0,
        ),
    )(counts, basis_values, weights)


def unpack_kernel(packed_ref, full_ref, diagonal):
    nbatch = full_ref.shape[0]
    half = full_ref.shape[1] // 2
    row, column = triangle(half)
    diagonal[...] = packed_ref[nbatch * half :, :].astype(F32)

    def step(b, carry):
        packed = packed_ref[pl.ds(pl.multiple_of(b * half, half), half), :].astype(F32)
        turned = packed.T
        mixed, mixed_turned = packed[:, half:], turned[half:]
        first = jnp.where(row >= column, mixed, mixed_turned)
        last = jnp.where(row < column, mixed, mixed_turned)
        last = jnp.where(row == column, diagonal[pl.ds(b, 1), :][:, :half], last)
        upper = jnp.concatenate([first, packed[:, :half]], axis=1)
        lower = jnp.concatenate([turned[:half], last], axis=1)
        full_ref[b] = jnp.concatenate([upper, lower], axis=0).astype(BF16)
        return carry

    lax.fori_loop(0, nbatch, step, 0, unroll=4)


def unpack(packed, nbatch, columns):
    return pl.pallas_call(
        unpack_kernel,
        out_shape=jax.ShapeDtypeStruct((nbatch, columns, columns), BF16),
        in_specs=[VMEM],
        out_specs=VMEM,
        scratch_shapes=[pltpu.VMEM((padded_rows(nbatch), columns), F32)],
        compiler_params=params(),
        cost_estimate=pl.CostEstimate(
            flops=nbatch * columns * columns * 4,
            bytes_accessed=nbatch * columns * columns * 3,
            transcendentals=0,
        ),
    )(packed)


def fetch(copies, semaphores):
    started = [
        pltpu.make_async_copy(source, target, semaphores.at[i])
        for i, (source, target) in enumerate(copies)
    ]
    for copy in started:
        copy.start()
    for copy in started:
        copy.wait()


def row_places(block_ref, b, rows):
    return [
        pl.ds(pl.multiple_of(block_ref[b, j] * rows, rows), rows) for j in range(block_ref.shape[1])
    ]


def apply_kernel(pieces, rows, *refs):
    block_refs, ham_refs = refs[:pieces], refs[pieces : 2 * pieces]
    window_refs = refs[2 * pieces : 2 * pieces + 3]
    out_before, out_own, out_after = refs[2 * pieces + 3 : 2 * pieces + 6]
    hams, window, total, semaphores = refs[2 * pieces + 6 :]
    region = window_refs[0].shape[0]
    copies = [(ref, hams.at[p]) for p, ref in enumerate(ham_refs)]
    for side, ref in enumerate(window_refs):
        copies.append((ref, window.at[pl.ds(side * region, region), :]))
    fetch(copies, semaphores)
    total[...] = jnp.zeros_like(total)

    def step(b, carry):
        places, products = [], []
        for p in range(pieces):
            place = row_places(block_refs[p], b, rows)
            picked = jnp.concatenate([window[at, :] for at in place], axis=0)
            products.append(jnp.dot(hams[p, b], picked, preferred_element_type=F32))
            places.append(place)
        for place, product in zip(places, products):
            for j, at in enumerate(place):
                total[at, :] += product[j * rows : (j + 1) * rows]
        return carry

    lax.fori_loop(0, hams.shape[1], step, 0)
    out_before[...] = total[:region].astype(BF16)
    out_own[...] = total[region : 2 * region]
    out_after[...] = total[2 * region :].astype(BF16)


def apply_window(blocks, hams, before, own, after):
    pieces, per_batch = len(hams), blocks[0].shape[1]
    nbatch, columns = hams[0].shape[:2]
    region, width = own.shape
    return pl.pallas_call(
        functools.partial(apply_kernel, pieces, columns // per_batch),
        out_shape=[
            jax.ShapeDtypeStruct((region, width), BF16),
            jax.ShapeDtypeStruct((region, width), F32),
            jax.ShapeDtypeStruct((region, width), BF16),
        ],
        in_specs=[SMEM] * pieces + [HBM] * (pieces + 3),
        out_specs=[VMEM] * 3,
        scratch_shapes=[
            pltpu.VMEM((pieces, nbatch, columns, columns), BF16),
            pltpu.VMEM((3 * region, width), BF16),
            pltpu.VMEM((3 * region, width), F32),
            pltpu.SemaphoreType.DMA((pieces + 3,)),
        ],
        compiler_params=params(),
        cost_estimate=pl.CostEstimate(
            flops=2 * pieces * nbatch * columns * columns * width,
            bytes_accessed=pieces * nbatch * columns * columns * 2 + 14 * region * width,
            transcendentals=0,
        ),
    )(*blocks, *hams, before, own, after)


def overlap_kernel(pieces, rows, *refs):
    block_refs = refs[:pieces]
    sources = refs[pieces : pieces + 12]
    out_refs = refs[pieces + 12 : 2 * pieces + 12]
    occ, resp, semaphores = refs[2 * pieces + 12 :]
    region, width = sources[0].shape
    copies = []
    for i, source in enumerate(sources):
        target, side, part = (occ, resp)[i // 6], i % 6 // 2, i % 2
        place = (pl.ds(side * region, region), pl.ds(part * width, width))
        copies.append((source, target.at[place]))
    fetch(copies, semaphores)

    def step(b, carry):
        for p in range(pieces):
            place = row_places(block_refs[p], b, rows)
            left = jnp.concatenate([resp[at, :] for at in place], axis=0)
            right = jnp.concatenate([occ[at, :] for at in place], axis=0)
            product = lax.dot_general(left, right, NT, preferred_element_type=F32)
            out_refs[p][b] = product.astype(out_refs[p].dtype)
        return carry

    lax.fori_loop(0, out_refs[0].shape[0], step, 0, unroll=4)


def overlaps(blocks, columns, occ_parts, resp_parts, types):
    pieces = len(blocks)
    nbatch, per_batch = blocks[0].shape
    region, width = occ_parts[0].shape
    return pl.pallas_call(
        functools.partial(overlap_kernel, pieces, columns // per_batch),
        out_shape=[jax.ShapeDtypeStruct((nbatch, columns, columns), kind) for kind in types],
        in_specs=[SMEM] * pieces + [HBM] * 12,
        out_specs=[VMEM] * pieces,
        scratch_shapes=[
            pltpu.VMEM((3 * region, 2 * width), BF16),
            pltpu.VMEM((3 * region, 2 * width), BF16),
            pltpu.SemaphoreType.DMA((12,)),
        ],
        compiler_params=params(),
        cost_estimate=pl.CostEstimate(
            flops=4 * pieces * nbatch * columns * columns * width,
            bytes_accessed=24 * region * width + pieces * nbatch * columns * columns * 3,
            transcendentals=0,
        ),
    )(*blocks, *occ_parts, *resp_parts)


def density_kernel(counts_ref, basis_ref, first_ref, second_ref, scale_ref, out_ref):
    def step(b, carry):
        values = basis_ref[b]
        overlap = first_ref[b] + second_ref[b].astype(F32)
        product = split_dot(overlap, values, NT)
        density = 4.0 * jnp.sum(product * values.astype(F32).T, axis=0, keepdims=True)
        out_ref[pl.ds(b, 1), :] = live_row(scale_ref, counts_ref, b) * density
        return carry

    lax.fori_loop(0, basis_ref.shape[0], step, 0, unroll=4)


def density(basis_values, counts, first, second, scale):
    nbatch, points, columns = basis_values.shape
    return pl.pallas_call(
        density_kernel,
        out_shape=jax.ShapeDtypeStruct((nbatch, points), F32),
        in_specs=[SMEM] + [VMEM] * 4,
        out_specs=VMEM,
        compiler_params=params(),
        cost_estimate=pl.CostEstimate(
            flops=4 * nbatch * points * columns * columns,
            bytes_accessed=basis_values.size * 2 + nbatch * columns * columns * 6,
            transcendentals=0,
        ),
    )(counts, basis_values, first, second, scale)


def flip(array, axis, mask):
    return lax.ppermute(array, axis, [(i, i ^ mask) for i in range(lax.axis_size(axis))])


def neighbours(array):
    size = lax.axis_size("grid")
    before = lax.ppermute(array, "grid", [(i, (i + 1) % size) for i in range(size)])
    after = lax.ppermute(array, "grid", [((i + 1) % size, i) for i in range(size)])
    return before, after


def column_part(array, index, width):
    return lax.dynamic_slice_in_dim(array, index * width, width, 1)


def trade(array, rows, choice):
    keep = lax.dynamic_slice_in_dim(array, choice * rows, rows, 1)
    return keep, lax.dynamic_slice_in_dim(array, (1 - choice) * rows, rows, 1).astype(BF16)


def join(own, other, choice):
    low, high = jnp.where(choice == 0, own, other), jnp.where(choice == 0, other, own)
    return jnp.concatenate([low, high], axis=1)


def partners(masks):
    size, tiles = lax.axis_size("grid"), lax.axis_size("tile")
    return [
        (g * tiles + t, (g ^ masks[t % 2]) * tiles + t) for g in range(size) for t in range(tiles)
    ]


def swap(array, masks):
    return lax.ppermute(array, ("grid", "tile"), partners(masks))


def rotate(parts, levels, energies):
    if lax.axis_size("grid") != 8:
        total = lax.psum(parts, "grid")
        return (total / (levels[None, :, None] - energies[:, None, :])).astype(BF16)
    grid, core = lax.axis_index("grid"), lax.axis_index("tile") % 2
    first, second = (grid >> core) & 1, (grid >> (1 - core)) & 1
    half = parts.shape[1] // 2
    quarter = half // 2
    keep, send = trade(parts, half, first)
    total = keep + swap(send, (1, 2)).astype(F32)
    keep, send = trade(total, quarter, second)
    total = keep + swap(send, (2, 1)).astype(F32)
    total = total + swap(total.astype(BF16), (4, 4)).astype(F32)
    level = lax.dynamic_slice_in_dim(levels, first * half + second * quarter, quarter, 0)
    own = (total / (level[None, :, None] - energies[:, None, :])).astype(BF16)
    own = join(own, swap(own, (2, 1)), second)
    return join(own, swap(own, (1, 2)), first)


def per_device(
    basis_values,
    blocks,
    counts,
    weighted_potential,
    xc_kernel,
    occ_coef,
    virt_coef,
    occ_energy,
    virt_energy,
):
    nbatch, _, columns = basis_values.shape
    region, occ_count = occ_coef.shape
    width = occ_count // lax.axis_size("tile")
    tile = lax.axis_index("tile")
    chip, core = tile // 2, tile % 2
    quarter = 2 * core + chip

    occ_own = column_part(occ_coef, quarter, width)
    occ_before, occ_after = neighbours(occ_own)

    potential, occ_own = lax.optimization_barrier((weighted_potential, occ_own))
    middle = -(-nbatch // 2)
    lists = [blocks, flip(blocks, "tile", 1), flip(blocks, "tile", 2)]
    lists.append(flip(lists[2], "tile", 1))
    fulls, arrived = [], []
    for start, stop in ((0, middle), (middle, nbatch)):
        full, packed = integrate(basis_values, counts, potential, start, stop)
        fulls.append(full)
        arrived.append(flip(packed, "tile", 2))
        potential, lists = lax.optimization_barrier((potential, lists))
    lists, arrived[1], occ_before, occ_after = lax.optimization_barrier(
        (lists, arrived[1], occ_before, occ_after)
    )
    hams, places = [], []
    for i, (start, stop) in enumerate(((0, middle), (middle, nbatch))):
        far = unpack(arrived[i], stop - start, columns)
        hams += [fulls[i], flip(fulls[i], "tile", 1), far, flip(far, "tile", 1)]
        places += [array[start:stop] for array in lists]
    blocks_near = lists[1]
    virt_near = flip(virt_coef, "tile", 1)
    energies = jnp.stack([virt_energy, flip(virt_energy, "tile", 1)])

    to_before, own_sum, to_after = apply_window(
        places,
        hams,
        occ_before,
        occ_own,
        occ_after,
    )
    levels = [
        lax.dynamic_slice_in_dim(occ_energy, place * width, width, 0)
        for place in (quarter, quarter ^ 1)
    ]
    own_sum, energies, levels = lax.optimization_barrier((own_sum, energies, levels))
    size = lax.axis_size("grid")
    from_before = lax.ppermute(to_after, "grid", [(i, (i + 1) % size) for i in range(size)])
    from_after = lax.ppermute(to_before, "grid", [((i + 1) % size, i) for i in range(size)])
    ham_own = (own_sum + from_before.astype(F32) + from_after.astype(F32)).astype(BF16)
    ham_sums = [ham_own, flip(ham_own, "tile", 2)]

    occ_far = column_part(occ_coef, quarter ^ 1, width)
    late_before, late_after, _ = lax.optimization_barrier((occ_before, occ_after, ham_sums[1]))
    before_far, after_far = flip(late_before, "tile", 2), flip(late_after, "tile", 2)

    virtuals = [virt_coef, virt_near]
    parts = []
    for ham_sum in ham_sums:
        ham_sum, parts = lax.optimization_barrier((ham_sum, parts))
        products = [
            lax.dot_general(ham_sum, virt, (((0,), (0,)), ((), ())), preferred_element_type=F32)
            for virt in virtuals
        ]
        parts.append(jnp.stack(products))
    rotated = [rotate(part, level, energies) for part, level in zip(parts, levels)]
    rotated[0], before_far, after_far = lax.optimization_barrier(
        (rotated[0], before_far, after_far)
    )
    coefs = []
    for rotation in rotated:
        terms = [
            lax.dot_general(virt, rotation[i], NT, preferred_element_type=F32)
            for i, virt in enumerate(virtuals)
        ]
        coefs.append(terms[0] + terms[1])
    coef_far = flip(coefs[1].astype(BF16), "tile", 2)
    resp_own = (coefs[0] + coef_far.astype(F32)).astype(BF16)

    resp_before, resp_after = neighbours(resp_own)
    resp_far, resp_before, resp_after = lax.optimization_barrier(
        (flip(resp_own, "tile", 2), resp_before, resp_after)
    )
    resp_before_far, resp_after_far = flip(resp_before, "tile", 2), flip(resp_after, "tile", 2)
    first = chip == 0
    half = jnp.concatenate(
        [jnp.where(first, resp_own, resp_far), jnp.where(first, resp_far, resp_own)], axis=1
    )
    half_near = flip(half, "tile", 1)
    first = core == 0
    response_coef = jnp.concatenate(
        [jnp.where(first, half, half_near), jnp.where(first, half_near, half)], axis=1
    )

    lists, response_coef = lax.optimization_barrier(([blocks, blocks_near], response_coef))
    overlap_own, overlap_near = overlaps(
        lists,
        columns,
        [occ_before, before_far, occ_own, occ_far, occ_after, after_far],
        [resp_before, resp_before_far, resp_own, resp_far, resp_after, resp_after_far],
        [F32, BF16],
    )
    response_potential = density(
        basis_values, counts, overlap_own, flip(overlap_near, "tile", 1), xc_kernel
    )
    return (response_coef, response_potential)


def solution(mesh):
    in_specs = (
        P(("grid", "tile"), None, None),
        P(("grid", "tile"), None),
        P(("grid", "tile")),
        P(("grid", "tile"), None),
        P(("grid", "tile"), None),
        P("grid", None),
        P("grid", "tile"),
        P(),
        P("tile"),
    )
    out_specs = (P("grid", None), P(("grid", "tile"), None))
    return jax.shard_map(
        per_device, mesh=mesh, in_specs=in_specs, out_specs=out_specs, check_vma=False
    )
```

time: 195 us -> 180 us (0.923)
  starting transfers between devices: 54.7 us -> 37.5 us
  other arithmetic: 18.7 us -> 8.35 us
  Pallas kernels: 14.9 us -> 24.5 us
  waiting for transfers between devices: 73.1 us -> 77.5 us
  local copies, waits for them, and re-layouts: 9.64 us -> 12.1 us
  matrix products: 20.7 us -> 18.4 us
    ppermute x10, waiting for transfers between devices: 14.4 us -> 37.4 us  [swap(): return lax.ppermute(array, ('grid', 'tile'), partners(masks))]
    ppermute x28 -> x20, waiting for transfers between devices: 39.7 us -> 24.4 us  [flip(): lax.ppermute(array, axis, [(i, i ^ mask) for i in range(lax.axis_size(axi...]
    ppermute x28 -> x20, starting transfers between devices: 25.4 us -> 11.9 us  [flip(): lax.ppermute(array, axis, [(i, i ^ mask) for i in range(lax.axis_size(axi...]
    ppermute x1, waiting for transfers between devices: 11.9 us -> 2.13 us  [per_device(): lax.ppermute(to_before, 'grid', [((i + 1) % size, i) for i in range(size)])]
    pallas_call x5, Pallas kernels: 13.1 us -> 22.7 us  [the longest x1 7.87 us: apply_window(): pl.pallas_call(functools.partial(apply_kernel, pieces, columns // per_bat...]
    ppermute x1, waiting for transfers between devices: 0.01 us -> 7.22 us  [per_device(): lax.ppermute(to_after, 'grid', [(i, (i + 1) % size) for i in range(size)])]
    ppermute x10, starting transfers between devices: 16.4 us -> 10.4 us  [swap(): return lax.ppermute(array, ('grid', 'tile'), partners(masks))]
    select_n x11 -> x4, other arithmetic: 6.93 us -> 1.39 us  [the longest x3 1.22 us: join(): jnp.where(choice == 0, own, other)]
  transfers between devices with their start and end apart: 44 -> 36, of which waited for: 21 -> 23; matrix products, arithmetic and copies ran while one was open for 16% -> 13% of each run, Pallas kernels for 5% -> 10%
where the time goes in v4:
time: 180 us; the launch traced here: 179 us
  waiting for transfers between devices  77.5 us (43%)
  starting transfers between devices  37.5 us (21%)
  Pallas kernels  24.5 us (14%)
  matrix products  18.4 us (10%)
  local copies, waits for them, and re-layouts  12.1 us (7%)
  other arithmetic  8.35 us (5%)
    ppermute x10, waiting for transfers between devices, swap(): return lax.ppermute(array, ('grid', 'tile'), partners(masks))  37.4 us
    ppermute x20, waiting for transfers between devices, flip(): lax.ppermute(array, axis, [(i, i ^ mask) for i in range(lax.axis_size(axi...  24.4 us
    ppermute x20, starting transfers between devices, flip(): lax.ppermute(array, axis, [(i, i ^ mask) for i in range(lax.axis_size(axi...  11.9 us
    unnamed x47, local copies, waits for them, and re-layouts  10.5 us
    ppermute x10, starting transfers between devices, swap(): return lax.ppermute(array, ('grid', 'tile'), partners(masks))  10.4 us
    dot_general x4, matrix products, per_device(): lax.dot_general(ham_sum, virt, (((0,), (0,)), ((), ())), preferred_elemen...  9.47 us
    dot_general x4, matrix products, per_device(): lax.dot_general(virt, rotation[i], NT, preferred_element_type=F32)  8.95 us
    pallas_call x1, Pallas kernels, apply_window(): pl.pallas_call(functools.partial(apply_kernel, pieces, columns // per_bat...  7.87 us
  transfers between devices with their start and end apart: 36, of which 23 were waited for; matrix products, arithmetic and copies ran while one was open for 13% of the time, Pallas kernels for 10%

profile of v4, /device:TPU:0, one launch (start us, length us, event | category | flops | bytes accessed | tf_op | source)
XLA Modules:
  0.0 179.4 jit_solution(7550792722598520237)
XLA Ops:
  1.2 1.1 constant_dynamic-slice_fusion
  2.2 2.6 %collective-permute-start.4 = (bf16[1024,128]{1,0:T(8,128)(2,1)S(1)}, bf16[1024,128]{1,0:T(8,128)(2,1)S(1)}, u32[]{:S(2)}, u32[]{:S(2)}) collective-permute-start(bf16[1024,128]{1,0:T(8,128)(2,1)S(1)} %get-tuple-element.70.refs_17_.refs_4_), channel_id=1, source_target_pairs={{0,4},{4,8},{8,12},{12,16},{16,20},{20,24},{24,28},{28,0},{1,5},{5... | collective-permute-start | bytes 786440 | tf_op jit(solution)/shard_map/ppermute | solution.py:304
  4.9 3.1 %collective-permute-start.5 = (bf16[1024,128]{1,0:T(8,128)(2,1)S(1)}, bf16[1024,128]{1,0:T(8,128)(2,1)S(1)}, u32[]{:S(2)}, u32[]{:S(2)}) collective-permute-start(bf16[1024,128]{1,0:T(8,128)(2,1)S(1)} %get-tuple-element.70.refs_17_.refs_4_), channel_id=1, source_target_pairs={{4,0},{8,4},{12,8},{16,12},{20,16},{24,20},{28,24},{0,28},{5,1},{9... | collective-permute-start | bytes 786440 | tf_op jit(solution)/shard_map/ppermute | solution.py:305
  8.7 1.6 collective-permute-start.1
  10.3 3.7 %shard_map.105 = (bf16[12,128,128]{2,1,0:T(8,128)(2,1)}, bf16[800,128]{1,0:T(8,128)(2,1)}) custom-call(s32[24]{0:T(128)} %counts_ref.5, bf16[24,256,128]{2,1,0:T(8,128)(2,1)} %basis_ref.5, f32[24,256]{1,0:T(8,128)} %weights_ref.1), custom_call_target="tpu_custom_call" | custom-call | flops 201326592 | bytes 1376256 | tf_op jit(solution)/shard_map/pallas_call | solution.py:84
  15.5 3.7 %shard_map.104 = (bf16[12,128,128]{2,1,0:T(8,128)(2,1)}, bf16[800,128]{1,0:T(8,128)(2,1)}) custom-call(s32[24]{0:T(128)} %counts_ref.5, bf16[24,256,128]{2,1,0:T(8,128)(2,1)} %basis_ref.5, f32[24,256]{1,0:T(8,128)} %weights_ref.1), custom_call_target="tpu_custom_call" | custom-call | flops 201326592 | bytes 1376256 | tf_op jit(solution)/shard_map/pallas_call | solution.py:84
  19.2 1.2 collective-permute-start.3
  20.4 1.5 collective-permute-done.7.packed_ref
  22.8 3.9 %collective-permute-done.3.packed_ref = bf16[800,128]{1,0:T(8,128)(2,1)S(1)} collective-permute-done((bf16[800,128]{1,0:T(8,128)(2,1)}, bf16[800,128]{1,0:T(8,128)(2,1)S(1)}, u32[]{:S(2)}, u32[]{:S(2)}) %collective-permute-start.3) | collective-permute-done | bytes 204832 | tf_op jit(solution)/shard_map/ppermute | solution.py:299
  30.6 1.0 copy-done.1
  34.6 7.9 %shard_map.108 = (bf16[1024,128]{1,0:T(8,128)(2,1)S(1)}, f32[1024,128]{1,0:T(8,128)S(1)}, bf16[1024,128]{1,0:T(8,128)(2,1)}) custom-call(s32[12,2]{1,0:T(8,128)S(1)} %get-tuple-element.122.refs_0_, s32[12,2]{1,0:T(8,128)S(1)} %get-tuple-element.115.refs_1_, s32[12,2]{1,0:T(8,128)S(1)} %get-tuple-element.120.refs_2_, s32[12,2]{1,0:T(8,128)S(1)} %get-tuple-element.111.refs_3_, ...), custom_call_target="tpu_custom_call" | custom-call | flops 402653184 | bytes 4980736 | tf_op jit(solution)/shard_map/pallas_call | solution.py:198
  42.6 4.7 %collective-permute-start.13 = (bf16[1024,128]{1,0:T(8,128)(2,1)S(1)}, bf16[1024,128]{1,0:T(8,128)(2,1)S(1)}, u32[]{:S(2)}, u32[]{:S(2)}) collective-permute-start(bf16[1024,128]{1,0:T(8,128)(2,1)S(1)} %get-tuple-element.75), channel_id=1, source_target_pairs={{4,0},{8,4},{12,8},{16,12},{20,16},{24,20},{28,24},{0,28},{5,1},{9... | collective-permute-start | bytes 786440 | tf_op jit(solution)/shard_map/ppermute | solution.py:410
  47.4 7.2 %collective-permute-done.12 = bf16[1024,128]{1,0:T(8,128)(2,1)S(1)} collective-permute-done((bf16[1024,128]{1,0:T(8,128)(2,1)}, bf16[1024,128]{1,0:T(8,128)(2,1)S(1)}, u32[]{:S(2)}, u32[]{:S(2)}) %collective-permute-start.12) | collective-permute-done | bytes 262176 | tf_op jit(solution)/shard_map/ppermute | solution.py:409
  54.6 2.1 %collective-permute-done.13 = bf16[1024,128]{1,0:T(8,128)(2,1)S(1)} collective-permute-done((bf16[1024,128]{1,0:T(8,128)(2,1)S(1)}, bf16[1024,128]{1,0:T(8,128)(2,1)S(1)}, u32[]{:S(2)}, u32[]{:S(2)}) %collective-permute-start.13) | collective-permute-done | bytes 262176 | tf_op jit(solution)/shard_map/ppermute | solution.py:410
  57.6 2.9 %convolution_bitcast_fusion.3 = f32[1,128,1920]{2,1,0:T(8,128)S(1)} fusion(bf16[1024,128]{1,0:T(8,128)(2,1)S(1)} %add_convert_fusion, bf16[1024,1920]{1,0:T(8,128)(2,1)} %param.15), kind=kOutput, calls=%fused_computation.3 | convolution fusion | flops 503316480 | bytes 5177344 | tf_op jit(solution)/shard_map/dot_general | solution.py:423
  60.5 3.0 %convolution_bitcast_fusion.2 = f32[1,128,1920]{2,1,0:T(8,128)S(1)} fusion(bf16[1024,128]{1,0:T(8,128)(2,1)S(1)} %add_convert_fusion, bf16[1024,1920]{1,0:T(8,128)(2,1)} %collective-permute-done.15), kind=kOutput, calls=%fused_computation.2 | convolution fusion | flops 503316480 | bytes 5177344 | tf_op jit(solution)/shard_map/dot_general | solution.py:423
  65.9 2.9 %convolution_bitcast_fusion = f32[1,128,1920]{2,1,0:T(8,128)S(1)} fusion(bf16[1024,128]{1,0:T(8,128)(2,1)S(1)} %collective-permute-done.14, bf16[1024,1920]{1,0:T(8,128)(2,1)} %collective-permute-done.15), kind=kOutput, calls=%fused_computation | convolution fusion | flops 503316480 | bytes 5177344 | tf_op jit(solution)/shard_map/dot_general | solution.py:423
  68.8 1.5 collective-permute-start.23
  70.4 3.0 %collective-permute-done.16 = bf16[2,64,1920]{2,1,0:T(8,128)(2,1)S(1)} collective-permute-done((bf16[2,64,1920]{2,1,0:T(8,128)(2,1)S(1)}, bf16[2,64,1920]{2,1,0:T(8,128)(2,1)S(1)}, u32[]{:S(2)}, u32[]{:S(2)}) %collective-permute-start.16) | collective-permute-done | bytes 491552 | tf_op jit(solution)/shard_map/ppermute | solution.py:331
  73.5 1.2 collective-permute-start.17
  74.8 8.7 %collective-permute-done.23 = bf16[2,64,1920]{2,1,0:T(8,128)(2,1)S(1)} collective-permute-done((bf16[2,64,1920]{2,1,0:T(8,128)(2,1)S(1)}, bf16[2,64,1920]{2,1,0:T(8,128)(2,1)S(1)}, u32[]{:S(2)}, u32[]{:S(2)}) %collective-permute-start.23) | collective-permute-done | bytes 491552 | tf_op jit(solution)/shard_map/ppermute | solution.py:331
  84.3 2.7 %collective-permute-start.18 = (bf16[2,32,1920]{2,1,0:T(8,128)(2,1)S(1)}, bf16[2,32,1920]{2,1,0:T(8,128)(2,1)}, u32[]{:S(2)}, u32[]{:S(2)}) collective-permute-start(bf16[2,32,1920]{2,1,0:T(8,128)(2,1)S(1)} %fusion.21), channel_id=1, source_target_pairs={{0,16},{1,17},{2,18},{3,19},{4,20},{5,21},{6,22},{7,23},{8,24},{9,... | collective-permute-start | bytes 737288 | tf_op jit(solution)/shard_map/ppermute | solution.py:331
  87.1 6.0 %collective-permute-done.24 = bf16[2,32,1920]{2,1,0:T(8,128)(2,1)S(1)} collective-permute-done((bf16[2,32,1920]{2,1,0:T(8,128)(2,1)S(1)}, bf16[2,32,1920]{2,1,0:T(8,128)(2,1)S(1)}, u32[]{:S(2)}, u32[]{:S(2)}) %collective-permute-start.24) | collective-permute-done | bytes 245792 | tf_op jit(solution)/shard_map/ppermute | solution.py:331
  94.7 7.4 %collective-permute-done.18 = bf16[2,32,1920]{2,1,0:T(8,128)(2,1)} collective-permute-done((bf16[2,32,1920]{2,1,0:T(8,128)(2,1)S(1)}, bf16[2,32,1920]{2,1,0:T(8,128)(2,1)}, u32[]{:S(2)}, u32[]{:S(2)}) %collective-permute-start.18) | collective-permute-done | bytes 245792 | tf_op jit(solution)/shard_map/ppermute | solution.py:331
  102.1 2.7 %collective-permute-done.25 = bf16[2,32,1920]{2,1,0:T(8,128)(2,1)} collective-permute-done((bf16[2,32,1920]{2,1,0:T(8,128)(2,1)}, bf16[2,32,1920]{2,1,0:T(8,128)(2,1)}, u32[]{:S(2)}, u32[]{:S(2)}) %collective-permute-start.25) | collective-permute-done | bytes 245792 | tf_op jit(solution)/shard_map/ppermute | solution.py:331
  104.8 2.2 %divide_convert_fusion = (bf16[2,32,1920]{2,1,0:T(8,128)(2,1)}, bf16[2,32,1920]{2,1,0:T(8,128)(2,1)S(1)}) fusion(bf16[2,32,1920]{2,1,0:T(8,128)(2,1)} %collective-permute-done.25, bf16[2,32,1920]{2,1,0:T(8,128)(2,1)} %copy-done.19, f32[2,64,1920]{2,1,0:T(8,128)S(1)} %fusion.8, s32[]{:T(128)S(6)} %select_n.117, f32[32]{0:T(128)S(1)} %dynamic_slice.54, ...), kind=kLoop, calls=%fused_computation.41 | loop fusion | flops 1720320 | bytes 2473220 | tf_op jit(solution)/shard_map/convert_element_type | solution.py:348
  107.9 1.4 collective-permute-start.22
  109.3 1.7 collective-permute-start.19
  111.0 2.4 %collective-permute-done.26 = bf16[2,32,1920]{2,1,0:T(8,128)(2,1)S(1)} collective-permute-done((bf16[2,32,1920]{2,1,0:T(8,128)(2,1)}, bf16[2,32,1920]{2,1,0:T(8,128)(2,1)S(1)}, u32[]{:S(2)}, u32[]{:S(2)}) %collective-permute-start.26) | collective-permute-done | bytes 245792 | tf_op jit(solution)/shard_map/ppermute | solution.py:331
  113.3 1.0 broadcast_select_fusion.9
  115.1 3.3 %collective-permute-done.19 = bf16[2,32,1920]{2,1,0:T(8,128)(2,1)S(1)} collective-permute-done((bf16[2,32,1920]{2,1,0:T(8,128)(2,1)S(1)}, bf16[2,32,1920]{2,1,0:T(8,128)(2,1)S(1)}, u32[]{:S(2)}, u32[]{:S(2)}) %collective-permute-start.19) | collective-permute-done | bytes 245792 | tf_op jit(solution)/shard_map/ppermute | solution.py:331
  119.4 3.9 %collective-permute-done.27 = bf16[2,64,1920]{2,1,0:T(8,128)(2,1)S(1)} collective-permute-done((bf16[2,64,1920]{2,1,0:T(8,128)(2,1)S(1)}, bf16[2,64,1920]{2,1,0:T(8,128)(2,1)S(1)}, u32[]{:S(2)}, u32[]{:S(2)}) %collective-permute-start.27) | collective-permute-done | bytes 491552 | tf_op jit(solution)/shard_map/ppermute | solution.py:331
  123.5 1.2 fusion.11
  124.6 3.3 %fusion.4 = bf16[1024,128]{1,0:T(8,128)(2,1)S(1)} fusion(f32[128,1024]{0,1:T(8,128)S(1)} %fusion.11, bf16[1024,1920]{1,0:T(8,128)(2,1)} %collective-permute-done.15, bf16[2,64,1920]{2,1,0:T(8,128)(2,1)S(1)} %get-tuple-element.98, bf16[2,64,1920]{2,1,0:T(8,128)(2,1)S(1)} %get-tuple-element.99), kind=kOutput, calls=%fused_computation.15 | convolution fusion | flops 504561664 | bytes 5701632 | tf_op jit(solution)/shard_map/dot_general | solution.py:434
  129.0 1.2 fusion.17
  130.2 4.2 %collective-permute-done.28 = bf16[1024,128]{1,0:T(8,128)(2,1)S(1)} collective-permute-done((bf16[1024,128]{1,0:T(8,128)(2,1)S(1)}, bf16[1024,128]{1,0:T(8,128)(2,1)S(1)}, u32[]{:S(2)}, u32[]{:S(2)}) %collective-permute-start.28) | collective-permute-done | bytes 262176 | tf_op jit(solution)/shard_map/ppermute | solution.py:299
  134.4 3.3 %fusion.2.refs_10_ = bf16[1024,128]{1,0:T(8,128)(2,1)S(1)} fusion(f32[128,1024]{0,1:T(8,128)S(1)} %fusion.17, bf16[1024,1920]{1,0:T(8,128)(2,1)} %collective-permute-done.15, bf16[1024,128]{1,0:T(8,128)(2,1)S(1)} %collective-permute-done.28, bf16[2,128,1920]{2,1,0:T(8,128)(2,1)S(1)} %pad_maximum_fusion.2), kind=kOutput, calls=%fused_computation.13 | convolution fusion | flops 503840768 | bytes 5472256 | tf_op jit(solution)/shard_map/dot_general | solution.py:434
  139.1 4.1 %collective-permute-start.31 = (bf16[1024,128]{1,0:T(8,128)(2,1)S(1)}, bf16[1024,128]{1,0:T(8,128)(2,1)S(1)}, u32[]{:S(2)}, u32[]{:S(2)}) collective-permute-start(bf16[1024,128]{1,0:T(8,128)(2,1)S(1)} %fusion.2.refs_10_), channel_id=1, source_target_pairs={{4,0},{8,4},{12,8},{16,12},{20,16},{24,20},{28,24},{0,28},{5,1},{9... | collective-permute-start | bytes 786440 | tf_op jit(solution)/shard_map/ppermute | solution.py:305
  144.1 3.7 %collective-permute-done.30.refs_8_ = bf16[1024,128]{1,0:T(8,128)(2,1)S(1)} collective-permute-done((bf16[1024,128]{1,0:T(8,128)(2,1)S(1)}, bf16[1024,128]{1,0:T(8,128)(2,1)S(1)}, u32[]{:S(2)}, u32[]{:S(2)}) %collective-permute-start.30) | collective-permute-done | bytes 262176 | tf_op jit(solution)/shard_map/ppermute | solution.py:304
  147.8 2.6 %collective-permute-done.31.refs_12_ = bf16[1024,128]{1,0:T(8,128)(2,1)S(1)} collective-permute-done((bf16[1024,128]{1,0:T(8,128)(2,1)S(1)}, bf16[1024,128]{1,0:T(8,128)(2,1)S(1)}, u32[]{:S(2)}, u32[]{:S(2)}) %collective-permute-start.31) | collective-permute-done | bytes 262176 | tf_op jit(solution)/shard_map/ppermute | solution.py:305
  152.1 1.4 collective-permute-start.33
  154.4 1.4 broadcast_select_fusion.1
  155.7 1.1 pad_maximum_fusion.1
  156.9 4.7 %collective-permute-done.33.refs_9_ = bf16[1024,128]{1,0:T(8,128)(2,1)} collective-permute-done((bf16[1024,128]{1,0:T(8,128)(2,1)}, bf16[1024,128]{1,0:T(8,128)(2,1)}, u32[]{:S(2)}, u32[]{:S(2)}) %collective-permute-start.33) | collective-permute-done | bytes 262176 | tf_op jit(solution)/shard_map/ppermute | solution.py:299
  161.6 5.2 %collective-permute-done.34.refs_13_ = bf16[1024,128]{1,0:T(8,128)(2,1)} collective-permute-done((bf16[1024,128]{1,0:T(8,128)(2,1)}, bf16[1024,128]{1,0:T(8,128)(2,1)}, u32[]{:S(2)}, u32[]{:S(2)}) %collective-permute-start.34) | collective-permute-done | bytes 262176 | tf_op jit(solution)/shard_map/ppermute | solution.py:299
  169.6 4.3 %shard_map.109 = (f32[24,128,128]{2,1,0:T(8,128)S(1)}, bf16[24,128,128]{2,1,0:T(8,128)(2,1)S(1)}) custom-call(s32[24,2]{1,0:T(8,128)S(1)} %copy.19.refs_0_, s32[24,2]{1,0:T(8,128)S(1)} %collective-permute-done.refs_1_, bf16[1024,128]{1,0:T(8,128)(2,1)S(1)} %collective-permute-done.4.refs_16_.refs_2_, bf16[1024,128]{1,0:T(8,128)(2,1)S(1)} %collective-permute-done.21.refs_3_, ...), custom_call_target="tpu_custom_call" | custom-call | flops 402653184 | bytes 5505024 | tf_op jit(solution)/shard_map/pallas_call | solution.py:251
  174.0 2.3 %collective-permute-done.35.second_ref = bf16[24,128,128]{2,1,0:T(8,128)(2,1)S(1)} collective-permute-done((bf16[24,128,128]{2,1,0:T(8,128)(2,1)S(1)}, bf16[24,128,128]{2,1,0:T(8,128)(2,1)S(1)}, u32[]{:S(2)}, u32[]{:S(2)}) %collective-permute-start.35) | collective-permute-done | bytes 786464 | tf_op jit(solution)/shard_map/ppermute | solution.py:299
  176.2 3.1 %shard_map.110 = f32[24,256]{1,0:T(8,128)} custom-call(s32[24]{0:T(128)S(1)} %copy-done.14, bf16[24,256,128]{2,1,0:T(8,128)(2,1)S(1)} %copy-done, f32[24,128,128]{2,1,0:T(8,128)S(1)} %get-tuple-element.92.first_ref, bf16[24,128,128]{2,1,0:T(8,128)(2,1)S(1)} %collective-permute-done.35.second_ref, f32[24,256]{1,0:T(8,128)S(1)} %copy-done.13), custom_call_target="tpu_custom_call" | custom-call | flops 402653184 | bytes 3932160 | tf_op jit(solution)/shard_map/pallas_call | solution.py:284
  (119 shorter events, 28.2 us)
Async XLA Ops:
  0.6 27.5 %copy-start.20 = (s32[24,2]{0,1:T(2,128)S(1)}, s32[24,2]{0,1:T(2,128)}, u32[]{:S(2)}) copy-start(s32[24,2]{0,1:T(2,128)} %param.10) | copy-start | bytes 580
  0.6 27.6 %copy-start.21 = (f32[1920]{0:T(1024)S(1)}, f32[1920]{0:T(1024)}, u32[]{:S(2)}) copy-start(f32[1920]{0:T(1024)} %param.17) | copy-start | bytes 23044
  0.7 59.8 %collective-permute-start.15 = (bf16[1024,1920]{1,0:T(8,128)(2,1)}, bf16[1024,1920]{1,0:T(8,128)(2,1)}, u32[]{:S(2)}, u32[]{:S(2)}) collective-permute-start(bf16[1024,1920]{1,0:T(8,128)(2,1)} %param.15), channel_id=1, source_target_pairs={{0,1},{1,0},{2,3},{3,2},{4,5},{5,4},{6,7},{7,6},{8,9},{9,8},{10,11... | collective-permute-start | bytes 11796488 | tf_op jit(solution)/shard_map/ppermute | solution.py:299
  2.2 24.5 %collective-permute-start.4 = (bf16[1024,128]{1,0:T(8,128)(2,1)S(1)}, bf16[1024,128]{1,0:T(8,128)(2,1)S(1)}, u32[]{:S(2)}, u32[]{:S(2)}) collective-permute-start(bf16[1024,128]{1,0:T(8,128)(2,1)S(1)} %get-tuple-element.70.refs_17_.refs_4_), channel_id=1, source_target_pairs={{0,4},{4,8},{8,12},{12,16},{16,20},{20,24},{24,28},{28,0},{1,5},{5... | collective-permute-start | bytes 786440 | tf_op jit(solution)/shard_map/ppermute | solution.py:304
  4.9 22.4 %collective-permute-start.5 = (bf16[1024,128]{1,0:T(8,128)(2,1)S(1)}, bf16[1024,128]{1,0:T(8,128)(2,1)S(1)}, u32[]{:S(2)}, u32[]{:S(2)}) collective-permute-start(bf16[1024,128]{1,0:T(8,128)(2,1)S(1)} %get-tuple-element.70.refs_17_.refs_4_), channel_id=1, source_target_pairs={{4,0},{8,4},{12,8},{16,12},{20,16},{24,20},{28,24},{0,28},{5,1},{9... | collective-permute-start | bytes 786440 | tf_op jit(solution)/shard_map/ppermute | solution.py:305
  8.7 38.6 %copy-start.22 = (f32[512]{0:T(512)S(1)}, f32[512]{0:T(512)}, u32[]{:S(2)}) copy-start(f32[512]{0:T(512)} %param.16) | copy-start | bytes 6148
  8.7 5.3 %collective-permute-start.1 = (s32[24,2]{1,0:T(8,128)S(1)}, s32[24,2]{1,0:T(8,128)S(1)}, u32[]{:S(2)}, u32[]{:S(2)}) collective-permute-start(s32[24,2]{1,0:T(8,128)S(1)} %copy.11), channel_id=1, source_target_pairs={{0,2},{1,3},{2,0},{3,1},{4,6},{5,7},{6,4},{7,5},{8,10},{9,11},{10,... | collective-permute-start | bytes 584 | tf_op jit(solution)/shard_map/ppermute | solution.py:299
  10.3 4.3 %collective-permute-start = (s32[24,2]{1,0:T(8,128)S(1)}, s32[24,2]{1,0:T(8,128)S(1)}, u32[]{:S(2)}, u32[]{:S(2)}) collective-permute-start(s32[24,2]{1,0:T(8,128)S(1)} %copy.11), channel_id=1, source_target_pairs={{0,1},{1,0},{2,3},{3,2},{4,5},{5,4},{6,7},{7,6},{8,9},{9,8},{10,11... | collective-permute-start | bytes 584 | tf_op jit(solution)/shard_map/ppermute | solution.py:299
  14.1 1.4 collective-permute-start.2
  14.6 7.3 %collective-permute-start.7 = (bf16[800,128]{1,0:T(8,128)(2,1)}, bf16[800,128]{1,0:T(8,128)(2,1)S(1)}, u32[]{:S(2)}, u32[]{:S(2)}) collective-permute-start(bf16[800,128]{1,0:T(8,128)(2,1)} %get-tuple-element.66), channel_id=1, source_target_pairs={{0,2},{1,3},{2,0},{3,1},{4,6},{5,7},{6,4},{7,5},{8,10},{9,11},{10,... | collective-permute-start | bytes 614408 | tf_op jit(solution)/shard_map/ppermute | solution.py:299
  19.2 7.5 %collective-permute-start.3 = (bf16[800,128]{1,0:T(8,128)(2,1)}, bf16[800,128]{1,0:T(8,128)(2,1)S(1)}, u32[]{:S(2)}, u32[]{:S(2)}) collective-permute-start(bf16[800,128]{1,0:T(8,128)(2,1)} %get-tuple-element.60), channel_id=1, source_target_pairs={{0,2},{1,3},{2,0},{3,1},{4,6},{5,7},{6,4},{7,5},{8,10},{9,11},{10,... | collective-permute-start | bytes 614408 | tf_op jit(solution)/shard_map/ppermute | solution.py:299
  21.9 6.4 %collective-permute-start.6 = (bf16[12,128,128]{2,1,0:T(8,128)(2,1)}, bf16[12,128,128]{2,1,0:T(8,128)(2,1)S(1)}, u32[]{:S(2)}, u32[]{:S(2)}) collective-permute-start(bf16[12,128,128]{2,1,0:T(8,128)(2,1)} %get-tuple-element.65.refs_8_), channel_id=1, source_target_pairs={{0,1},{1,0},{2,3},{3,2},{4,5},{5,4},{6,7},{7,6},{8,9},{9,8},{10,11... | collective-permute-start | bytes 1179656 | tf_op jit(solution)/shard_map/ppermute | solution.py:299
  26.7 2.4 %collective-permute-start.9 = (bf16[12,128,128]{2,1,0:T(8,128)(2,1)}, bf16[12,128,128]{2,1,0:T(8,128)(2,1)S(1)}, u32[]{:S(2)}, u32[]{:S(2)}) collective-permute-start(bf16[12,128,128]{2,1,0:T(8,128)(2,1)} %get-tuple-element.67.refs_12_), channel_id=1, source_target_pairs={{0,1},{1,0},{2,3},{3,2},{4,5},{5,4},{6,7},{7,6},{8,9},{9,8},{10,11... | collective-permute-start | bytes 1179656 | tf_op jit(solution)/shard_map/ppermute | solution.py:299
  26.7 3.2 %collective-permute-start.8 = (bf16[12,128,128]{2,1,0:T(8,128)(2,1)S(1)}, bf16[12,128,128]{2,1,0:T(8,128)(2,1)S(1)}, u32[]{:S(2)}, u32[]{:S(2)}) collective-permute-start(bf16[12,128,128]{2,1,0:T(8,128)(2,1)S(1)} %shard_map.106.refs_10_), channel_id=1, source_target_pairs={{0,1},{1,0},{2,3},{3,2},{4,5},{5,4},{6,7},{7,6},{8,9},{9,8},{10,11... | collective-permute-start | bytes 1179656 | tf_op jit(solution)/shard_map/ppermute | solution.py:299
  28.1 2.5 %collective-permute-start.10 = (bf16[12,128,128]{2,1,0:T(8,128)(2,1)S(1)}, bf16[12,128,128]{2,1,0:T(8,128)(2,1)}, u32[]{:S(2)}, u32[]{:S(2)}) collective-permute-start(bf16[12,128,128]{2,1,0:T(8,128)(2,1)S(1)} %shard_map.107.refs_14_), channel_id=1, source_target_pairs={{0,1},{1,0},{2,3},{3,2},{4,5},{5,4},{6,7},{7,6},{8,9},{9,8},{10,11... | collective-permute-start | bytes 1179656 | tf_op jit(solution)/shard_map/ppermute | solution.py:299
  28.3 19.1 %collective-permute-start.11 = (f32[1920]{0:T(1024)S(1)}, f32[1920]{0:T(1024)S(1)}, u32[]{:S(2)}, u32[]{:S(2)}) collective-permute-start(f32[1920]{0:T(1024)S(1)} %copy-done.21), channel_id=1, source_target_pairs={{0,1},{1,0},{2,3},{3,2},{4,5},{5,4},{6,7},{7,6},{8,9},{9,8},{10,11... | collective-permute-start | bytes 23048 | tf_op jit(solution)/shard_map/ppermute | solution.py:299
  42.5 12.1 %collective-permute-start.12 = (bf16[1024,128]{1,0:T(8,128)(2,1)}, bf16[1024,128]{1,0:T(8,128)(2,1)S(1)}, u32[]{:S(2)}, u32[]{:S(2)}) collective-permute-start(bf16[1024,128]{1,0:T(8,128)(2,1)} %get-tuple-element.74), channel_id=1, source_target_pairs={{0,4},{4,8},{8,12},{12,16},{16,20},{20,24},{24,28},{28,0},{1,5},{5... | collective-permute-start | bytes 786440 | tf_op jit(solution)/shard_map/ppermute | solution.py:409
  42.6 14.2 %collective-permute-start.13 = (bf16[1024,128]{1,0:T(8,128)(2,1)S(1)}, bf16[1024,128]{1,0:T(8,128)(2,1)S(1)}, u32[]{:S(2)}, u32[]{:S(2)}) collective-permute-start(bf16[1024,128]{1,0:T(8,128)(2,1)S(1)} %get-tuple-element.75), channel_id=1, source_target_pairs={{4,0},{8,4},{12,8},{16,12},{20,16},{24,20},{28,24},{0,28},{5,1},{9... | collective-permute-start | bytes 786440 | tf_op jit(solution)/shard_map/ppermute | solution.py:410
  56.9 7.6 %collective-permute-start.14 = (bf16[1024,128]{1,0:T(8,128)(2,1)S(1)}, bf16[1024,128]{1,0:T(8,128)(2,1)S(1)}, u32[]{:S(2)}, u32[]{:S(2)}) collective-permute-start(bf16[1024,128]{1,0:T(8,128)(2,1)S(1)} %add_convert_fusion), channel_id=1, source_target_pairs={{0,2},{1,3},{2,0},{3,1},{4,6},{5,7},{6,4},{7,5},{8,10},{9,11},{10,... | collective-permute-start | bytes 786440 | tf_op jit(solution)/shard_map/ppermute | solution.py:299
  60.5 4.7 %copy-start.15 = (bf16[1024,1920]{1,0:T(8,128)(2,1)S(1)}, bf16[1024,1920]{1,0:T(8,128)(2,1)}, u32[]{:S(2)}) copy-start(bf16[1024,1920]{1,0:T(8,128)(2,1)} %param.15) | copy-start | bytes 11796484
  64.5 8.9 %collective-permute-start.16 = (bf16[2,64,1920]{2,1,0:T(8,128)(2,1)S(1)}, bf16[2,64,1920]{2,1,0:T(8,128)(2,1)S(1)}, u32[]{:S(2)}, u32[]{:S(2)}) collective-permute-start(bf16[2,64,1920]{2,1,0:T(8,128)(2,1)S(1)} %dynamic-slice_convert_fusion), channel_id=1, source_target_pairs={{0,4},{1,9},{2,6},{3,11},{4,0},{5,13},{6,2},{7,15},{8,12},{9,1},{1... | collective-permute-start | bytes 1474568 | tf_op jit(solution)/shard_map/ppermute | solution.py:331
  68.8 14.6 %collective-permute-start.23 = (bf16[2,64,1920]{2,1,0:T(8,128)(2,1)S(1)}, bf16[2,64,1920]{2,1,0:T(8,128)(2,1)S(1)}, u32[]{:S(2)}, u32[]{:S(2)}) collective-permute-start(bf16[2,64,1920]{2,1,0:T(8,128)(2,1)S(1)} %fusion.6), channel_id=1, source_target_pairs={{0,4},{1,9},{2,6},{3,11},{4,0},{5,13},{6,2},{7,15},{8,12},{9,1},{1... | collective-permute-start | bytes 1474568 | tf_op jit(solution)/shard_map/ppermute | solution.py:331
  73.5 10.7 %collective-permute-start.17 = (bf16[2,32,1920]{2,1,0:T(8,128)(2,1)S(1)}, bf16[2,32,1920]{2,1,0:T(8,128)(2,1)S(1)}, u32[]{:S(2)}, u32[]{:S(2)}) collective-permute-start(bf16[2,32,1920]{2,1,0:T(8,128)(2,1)S(1)} %dynamic-slice_convert_fusion.2), channel_id=1, source_target_pairs={{0,8},{1,5},{2,10},{3,7},{4,12},{5,1},{6,14},{7,3},{8,0},{9,13},{1... | collective-permute-start | bytes 737288 | tf_op jit(solution)/shard_map/ppermute | solution.py:331
  83.6 9.5 %collective-permute-start.24 = (bf16[2,32,1920]{2,1,0:T(8,128)(2,1)S(1)}, bf16[2,32,1920]{2,1,0:T(8,128)(2,1)S(1)}, u32[]{:S(2)}, u32[]{:S(2)}) collective-permute-start(bf16[2,32,1920]{2,1,0:T(8,128)(2,1)S(1)} %dynamic-slice_convert_fusion.1), channel_id=1, source_target_pairs={{0,8},{1,5},{2,10},{3,7},{4,12},{5,1},{6,14},{7,3},{8,0},{9,13},{1... | collective-permute-start | bytes 737288 | tf_op jit(solution)/shard_map/ppermute | solution.py:331
  84.3 17.7 %collective-permute-start.18 = (bf16[2,32,1920]{2,1,0:T(8,128)(2,1)S(1)}, bf16[2,32,1920]{2,1,0:T(8,128)(2,1)}, u32[]{:S(2)}, u32[]{:S(2)}) collective-permute-start(bf16[2,32,1920]{2,1,0:T(8,128)(2,1)S(1)} %fusion.21), channel_id=1, source_target_pairs={{0,16},{1,17},{2,18},{3,19},{4,20},{5,21},{6,22},{7,23},{8,24},{9,... | collective-permute-start | bytes 737288 | tf_op jit(solution)/shard_map/ppermute | solution.py:331
  94.5 10.2 %collective-permute-start.25 = (bf16[2,32,1920]{2,1,0:T(8,128)(2,1)}, bf16[2,32,1920]{2,1,0:T(8,128)(2,1)}, u32[]{:S(2)}, u32[]{:S(2)}) collective-permute-start(bf16[2,32,1920]{2,1,0:T(8,128)(2,1)} %fusion.22), channel_id=1, source_target_pairs={{0,16},{1,17},{2,18},{3,19},{4,20},{5,21},{6,22},{7,23},{8,24},{9,... | collective-permute-start | bytes 737288 | tf_op jit(solution)/shard_map/ppermute | solution.py:331
  106.9 6.4 %collective-permute-start.26 = (bf16[2,32,1920]{2,1,0:T(8,128)(2,1)}, bf16[2,32,1920]{2,1,0:T(8,128)(2,1)S(1)}, u32[]{:S(2)}, u32[]{:S(2)}) collective-permute-start(bf16[2,32,1920]{2,1,0:T(8,128)(2,1)} %get-tuple-element.108), channel_id=1, source_target_pairs={{0,8},{1,5},{2,10},{3,7},{4,12},{5,1},{6,14},{7,3},{8,0},{9,13},{1... | collective-permute-start | bytes 737288 | tf_op jit(solution)/shard_map/ppermute | solution.py:331
  107.3 16.2 %copy-start.16 = (bf16[1024,1920]{1,0:T(8,128)(2,1)S(1)}, bf16[1024,1920]{1,0:T(8,128)(2,1)}, u32[]{:S(2)}) copy-start(bf16[1024,1920]{1,0:T(8,128)(2,1)} %param.15) | copy-start | bytes 11796484
  107.3 21.7 %collective-permute-start.21 = (bf16[1024,128]{1,0:T(8,128)(2,1)S(1)}, bf16[1024,128]{1,0:T(8,128)(2,1)S(1)}, u32[]{:S(2)}, u32[]{:S(2)}) collective-permute-start(bf16[1024,128]{1,0:T(8,128)(2,1)S(1)} %collective-permute-done.4.refs_16_.refs_2_), channel_id=1, source_target_pairs={{0,2},{1,3},{2,0},{3,1},{4,6},{5,7},{6,4},{7,5},{8,10},{9,11},{10,... | collective-permute-start | bytes 786440 | tf_op jit(solution)/shard_map/ppermute | solution.py:299
  107.9 21.0 %collective-permute-start.22 = (bf16[1024,128]{1,0:T(8,128)(2,1)S(1)}, bf16[1024,128]{1,0:T(8,128)(2,1)S(1)}, u32[]{:S(2)}, u32[]{:S(2)}) collective-permute-start(bf16[1024,128]{1,0:T(8,128)(2,1)S(1)} %collective-permute-done.5.refs_18_.refs_6_), channel_id=1, source_target_pairs={{0,2},{1,3},{2,0},{3,1},{4,6},{5,7},{6,4},{7,5},{8,10},{9,11},{10,... | collective-permute-start | bytes 786440 | tf_op jit(solution)/shard_map/ppermute | solution.py:299
  109.3 9.1 %collective-permute-start.19 = (bf16[2,32,1920]{2,1,0:T(8,128)(2,1)S(1)}, bf16[2,32,1920]{2,1,0:T(8,128)(2,1)S(1)}, u32[]{:S(2)}, u32[]{:S(2)}) collective-permute-start(bf16[2,32,1920]{2,1,0:T(8,128)(2,1)S(1)} %get-tuple-element.109), channel_id=1, source_target_pairs={{0,8},{1,5},{2,10},{3,7},{4,12},{5,1},{6,14},{7,3},{8,0},{9,13},{1... | collective-permute-start | bytes 737288 | tf_op jit(solution)/shard_map/ppermute | solution.py:331
  114.4 8.9 %collective-permute-start.27 = (bf16[2,64,1920]{2,1,0:T(8,128)(2,1)S(1)}, bf16[2,64,1920]{2,1,0:T(8,128)(2,1)S(1)}, u32[]{:S(2)}, u32[]{:S(2)}) collective-permute-start(bf16[2,64,1920]{2,1,0:T(8,128)(2,1)S(1)} %pad_maximum_fusion.6), channel_id=1, source_target_pairs={{0,4},{1,9},{2,6},{3,11},{4,0},{5,13},{6,2},{7,15},{8,12},{9,1},{1... | collective-permute-start | bytes 1474568 | tf_op jit(solution)/shard_map/ppermute | solution.py:331
  118.5 10.2 %collective-permute-start.20 = (bf16[2,64,1920]{2,1,0:T(8,128)(2,1)S(1)}, bf16[2,64,1920]{2,1,0:T(8,128)(2,1)S(1)}, u32[]{:S(2)}, u32[]{:S(2)}) collective-permute-start(bf16[2,64,1920]{2,1,0:T(8,128)(2,1)S(1)} %pad_maximum_fusion.5), channel_id=1, source_target_pairs={{0,4},{1,9},{2,6},{3,11},{4,0},{5,13},{6,2},{7,15},{8,12},{9,1},{1... | collective-permute-start | bytes 1474568 | tf_op jit(solution)/shard_map/ppermute | solution.py:331
  128.0 6.4 %collective-permute-start.28 = (bf16[1024,128]{1,0:T(8,128)(2,1)S(1)}, bf16[1024,128]{1,0:T(8,128)(2,1)S(1)}, u32[]{:S(2)}, u32[]{:S(2)}) collective-permute-start(bf16[1024,128]{1,0:T(8,128)(2,1)S(1)} %fusion.4), channel_id=1, source_target_pairs={{0,2},{1,3},{2,0},{3,1},{4,6},{5,7},{6,4},{7,5},{8,10},{9,11},{10,... | collective-permute-start | bytes 786440 | tf_op jit(solution)/shard_map/ppermute | solution.py:299
  129.0 1.2 copy-start.7
  137.7 6.4 %collective-permute-start.29 = (bf16[1024,128]{1,0:T(8,128)(2,1)S(1)}, bf16[1024,128]{1,0:T(8,128)(2,1)S(1)}, u32[]{:S(2)}, u32[]{:S(2)}) collective-permute-start(bf16[1024,128]{1,0:T(8,128)(2,1)S(1)} %fusion.2.refs_10_), channel_id=1, source_target_pairs={{0,2},{1,3},{2,0},{3,1},{4,6},{5,7},{6,4},{7,5},{8,10},{9,11},{10,... | collective-permute-start | bytes 786440 | tf_op jit(solution)/shard_map/ppermute | solution.py:299
  138.4 9.4 %collective-permute-start.30 = (bf16[1024,128]{1,0:T(8,128)(2,1)S(1)}, bf16[1024,128]{1,0:T(8,128)(2,1)S(1)}, u32[]{:S(2)}, u32[]{:S(2)}) collective-permute-start(bf16[1024,128]{1,0:T(8,128)(2,1)S(1)} %fusion.2.refs_10_), channel_id=1, source_target_pairs={{0,4},{4,8},{8,12},{12,16},{16,20},{20,24},{24,28},{28,0},{1,5},{5... | collective-permute-start | bytes 786440 | tf_op jit(solution)/shard_map/ppermute | solution.py:304
  139.1 11.4 %collective-permute-start.31 = (bf16[1024,128]{1,0:T(8,128)(2,1)S(1)}, bf16[1024,128]{1,0:T(8,128)(2,1)S(1)}, u32[]{:S(2)}, u32[]{:S(2)}) collective-permute-start(bf16[1024,128]{1,0:T(8,128)(2,1)S(1)} %fusion.2.refs_10_), channel_id=1, source_target_pairs={{4,0},{8,4},{12,8},{16,12},{20,16},{24,20},{28,24},{0,28},{5,1},{9... | collective-permute-start | bytes 786440 | tf_op jit(solution)/shard_map/ppermute | solution.py:305
  147.8 2.7 %copy-start.9 = (bf16[1024,128]{1,0:T(8,128)(2,1)}, bf16[1024,128]{1,0:T(8,128)(2,1)S(1)}, u32[]{:S(2)}) copy-start(bf16[1024,128]{1,0:T(8,128)(2,1)S(1)} %collective-permute-done.30.refs_8_) | copy-start | bytes 786436
  150.5 1.5 copy-start.17
  150.5 1.5 copy-start.18
  152.0 24.2 %copy-start = (bf16[24,256,128]{2,1,0:T(8,128)(2,1)S(1)}, bf16[24,256,128]{2,1,0:T(8,128)(2,1)}, u32[]{:S(2)}) copy-start(bf16[24,256,128]{2,1,0:T(8,128)(2,1)} %basis_ref.5) | copy-start | bytes 4718596
  152.0 24.2 %copy-start.13 = (f32[24,256]{1,0:T(8,128)S(1)}, f32[24,256]{1,0:T(8,128)}, u32[]{:S(2)}) copy-start(f32[24,256]{1,0:T(8,128)} %scale_ref.1) | copy-start | bytes 73732
  152.0 24.2 %copy-start.14 = (s32[24]{0:T(128)S(1)}, s32[24]{0:T(128)}, u32[]{:S(2)}) copy-start(s32[24]{0:T(128)} %counts_ref.5) | copy-start | bytes 292
  152.0 2.3 %collective-permute-start.32 = (bf16[1024,256]{1,0:T(8,128)(2,1)}, bf16[1024,256]{1,0:T(8,128)(2,1)}, u32[]{:S(2)}, u32[]{:S(2)}) collective-permute-start(bf16[1024,256]{1,0:T(8,128)(2,1)} %pad_maximum_fusion.3), channel_id=1, source_target_pairs={{0,1},{1,0},{2,3},{3,2},{4,5},{5,4},{6,7},{7,6},{8,9},{9,8},{10,11... | collective-permute-start | bytes 1572872 | tf_op jit(solution)/shard_map/ppermute | solution.py:299
  152.1 9.5 %collective-permute-start.33 = (bf16[1024,128]{1,0:T(8,128)(2,1)}, bf16[1024,128]{1,0:T(8,128)(2,1)}, u32[]{:S(2)}, u32[]{:S(2)}) collective-permute-start(bf16[1024,128]{1,0:T(8,128)(2,1)} %copy-done.9), channel_id=1, source_target_pairs={{0,2},{1,3},{2,0},{3,1},{4,6},{5,7},{6,4},{7,5},{8,10},{9,11},{10,... | collective-permute-start | bytes 786440 | tf_op jit(solution)/shard_map/ppermute | solution.py:299
  153.5 13.2 %collective-permute-start.34 = (bf16[1024,128]{1,0:T(8,128)(2,1)}, bf16[1024,128]{1,0:T(8,128)(2,1)}, u32[]{:S(2)}, u32[]{:S(2)}) collective-permute-start(bf16[1024,128]{1,0:T(8,128)(2,1)} %copy-done.11), channel_id=1, source_target_pairs={{0,2},{1,3},{2,0},{3,1},{4,6},{5,7},{6,4},{7,5},{8,10},{9,11},{10,... | collective-permute-start | bytes 786440 | tf_op jit(solution)/shard_map/ppermute | solution.py:299
  173.9 2.4 %collective-permute-start.35 = (bf16[24,128,128]{2,1,0:T(8,128)(2,1)S(1)}, bf16[24,128,128]{2,1,0:T(8,128)(2,1)S(1)}, u32[]{:S(2)}, u32[]{:S(2)}) collective-permute-start(bf16[24,128,128]{2,1,0:T(8,128)(2,1)S(1)} %get-tuple-element.93), channel_id=1, source_target_pairs={{0,1},{1,0},{2,3},{3,2},{4,5},{5,4},{6,7},{7,6},{8,9},{9,8},{10,11... | collective-permute-start | bytes 2359304 | tf_op jit(solution)/shard_map/ppermute | solution.py:299
  (11 other events, 9.8 us)

commit v5 on v4

--- a/solution.py
+++ b/solution.py
@@ -39,66 +39,52 @@
     return jnp.where(points < counts_ref[b], row, 0.0)
 
 
-def integrate_kernel(start, counts_ref, basis_ref, weights_ref, full_ref, packed_ref, diagonal):
-    steps, here = pl.num_programs(0), basis_ref.shape[0]
+def integrate_kernel(counts_ref, basis_ref, weights_ref, full_ref, *refs):
+    packed_refs, diagonal = refs[:-1], refs[-1]
     half = full_ref.shape[2] // 2
     row, column = triangle(half)
-    now = pl.program_id(0)
-
-    @pl.when(now == 0)
-    def _():
+    start = 0
+    for packed_ref, nbatch in zip(packed_refs, groups(full_ref.shape[0])):
         diagonal[...] = jnp.zeros_like(diagonal)
 
-    for b in range(here):
-        place = now * here + b
-        values = basis_ref[b]
-        weighted = values.astype(F32).T * live_row(weights_ref, counts_ref, start + place)
-        ham = split_dot(weighted, values, (((1,), (0,)), ((), ())))
-        full_ref[b] = ham.astype(BF16)
-        last = ham[half:, half:]
-        mixed = jnp.where(row >= column, ham[:half, :half], last)
-        packed = jnp.concatenate([ham[:half, half:], mixed], axis=1)
-        packed_ref[pl.ds(pl.multiple_of(place * half, half), half), :] = packed.astype(BF16)
-        line = jnp.sum(jnp.where(row == column, last, 0.0), axis=0, keepdims=True)
-        diagonal[pl.ds(place, 1), :] = jnp.concatenate([line, jnp.zeros_like(line)], axis=1)
-
-    @pl.when(now == steps - 1)
-    def _():
-        packed_ref[steps * here * half :, :] = diagonal[...].astype(BF16)
+        def step(b, carry, start=start, packed_ref=packed_ref):
+            values = basis_ref[start + b]
+            weighted = values.astype(F32).T * live_row(weights_ref, counts_ref, start + b)
+            ham = split_dot(weighted, values, (((1,), (0,)), ((), ())))
+            full_ref[start + b] = ham.astype(BF16)
+            last = ham[half:, half:]
+            mixed = jnp.where(row >= column, ham[:half, :half], last)
+            packed = jnp.concatenate([ham[:half, half:], mixed], axis=1)
+            packed_ref[pl.ds(pl.multiple_of(b * half, half), half), :] = packed.astype(BF16)
+            line = jnp.sum(jnp.where(row == column, last, 0.0), axis=0, keepdims=True)
+            diagonal[pl.ds(b, 1), :] = jnp.concatenate([line, jnp.zeros_like(line)], axis=1)
+            return carry
+
+        lax.fori_loop(0, nbatch, step, 0, unroll=4)
+        packed_ref[nbatch * half :, :] = diagonal[: packed_ref.shape[0] - nbatch * half].astype(BF16)
+        start += nbatch
+
+
+def groups(nbatch):
+    first = -(-nbatch // 2)
+    return [first, nbatch - first] if nbatch > first else [first]
 
 
 def padded_rows(nbatch):
     return -(-nbatch // 32) * 32
 
 
-def step_size(nbatch, most):
-    return max(k for k in range(1, most + 1) if nbatch % k == 0)
-
-
-def integrate(basis_values, counts, weights, start, stop):
-    _, points, columns = basis_values.shape
-    nbatch = stop - start
-    here = step_size(nbatch, 4)
-    rows = nbatch * columns // 2 + padded_rows(nbatch)
-    first = start // here
+def integrate(basis_values, counts, weights):
+    nbatch, points, columns = basis_values.shape
+    rows = [count * columns // 2 + padded_rows(count) for count in groups(nbatch)]
     return pl.pallas_call(
-        functools.partial(integrate_kernel, start),
-        grid=(nbatch // here,),
-        out_shape=[
-            jax.ShapeDtypeStruct((nbatch, columns, columns), BF16),
-            jax.ShapeDtypeStruct((rows, columns), BF16),
-        ],
-        in_specs=[
-            SMEM,
-            pl.BlockSpec((here, points, columns), lambda i: (first + i, 0, 0)),
-            pl.BlockSpec(weights.shape, lambda i: (0, 0)),
-        ],
-        out_specs=[
-            pl.BlockSpec((here, columns, columns), lambda i: (i, 0, 0)),
-            pl.BlockSpec((rows, columns), lambda i: (0, 0)),
-        ],
-        scratch_shapes=[pltpu.VMEM((padded_rows(nbatch), columns), F32)],
-        compiler_params=params(60),
+        integrate_kernel,
+        out_shape=[jax.ShapeDtypeStruct((nbatch, columns, columns), BF16)]
+        + [jax.ShapeDtypeStruct((row, columns), BF16) for row in rows],
+        in_specs=[SMEM, VMEM, VMEM],
+        out_specs=[VMEM] * (1 + len(rows)),
+        scratch_shapes=[pltpu.VMEM((padded_rows(groups(nbatch)[0]), columns), F32)],
+        compiler_params=params(),
         cost_estimate=pl.CostEstimate(
             flops=4 * nbatch * points * columns * columns,
             bytes_accessed=nbatch * columns * (points * 2 + columns * 3),
@@ -161,59 +147,62 @@
     ]
 
 
-def apply_kernel(pieces, rows, *refs):
+def apply_kernel(starts, rows, *refs):
+    pieces = len(starts)
     block_refs, ham_refs = refs[:pieces], refs[pieces : 2 * pieces]
     window_refs = refs[2 * pieces : 2 * pieces + 3]
     out_before, out_own, out_after = refs[2 * pieces + 3 : 2 * pieces + 6]
-    hams, window, total, semaphores = refs[2 * pieces + 6 :]
+    window, total = refs[2 * pieces + 6 :]
     region = window_refs[0].shape[0]
-    copies = [(ref, hams.at[p]) for p, ref in enumerate(ham_refs)]
     for side, ref in enumerate(window_refs):
-        copies.append((ref, window.at[pl.ds(side * region, region), :]))
-    fetch(copies, semaphores)
+        window[side * region : (side + 1) * region] = ref[...]
     total[...] = jnp.zeros_like(total)
 
-    def step(b, carry):
-        places, products = [], []
-        for p in range(pieces):
-            place = row_places(block_refs[p], b, rows)
-            picked = jnp.concatenate([window[at, :] for at in place], axis=0)
-            products.append(jnp.dot(hams[p, b], picked, preferred_element_type=F32))
-            places.append(place)
-        for place, product in zip(places, products):
-            for j, at in enumerate(place):
-                total[at, :] += product[j * rows : (j + 1) * rows]
-        return carry
-
-    lax.fori_loop(0, hams.shape[1], step, 0)
+    def steps(members, count):
+        def step(b, carry):
+            places, products = [], []
+            for p in members:
+                place = row_places(block_refs[p], starts[p] + b, rows)
+                picked = jnp.concatenate([window[at, :] for at in place], axis=0)
+                products.append(jnp.dot(ham_refs[p][b], picked, preferred_element_type=F32))
+                places.append(place)
+            for place, product in zip(places, products):
+                for j, at in enumerate(place):
+                    total[at, :] += product[j * rows : (j + 1) * rows]
+            return carry
+
+        lax.fori_loop(0, count, step, 0, unroll=2)
+
+    counts = [ref.shape[0] for ref in ham_refs]
+    for count in sorted(set(counts)):
+        steps([p for p in range(pieces) if counts[p] == count], count)
     out_before[...] = total[:region].astype(BF16)
     out_own[...] = total[region : 2 * region]
     out_after[...] = total[2 * region :].astype(BF16)
 
 
-def apply_window(blocks, hams, before, own, after):
+def apply_window(blocks, hams, starts, before, own, after):
     pieces, per_batch = len(hams), blocks[0].shape[1]
-    nbatch, columns = hams[0].shape[:2]
+    columns = hams[0].shape[1]
     region, width = own.shape
+    work = sum(ham.shape[0] for ham in hams)
     return pl.pallas_call(
-        functools.partial(apply_kernel, pieces, columns // per_batch),
+        functools.partial(apply_kernel, starts, columns // per_batch),
         out_shape=[
             jax.ShapeDtypeStruct((region, width), BF16),
             jax.ShapeDtypeStruct((region, width), F32),
             jax.ShapeDtypeStruct((region, width), BF16),
         ],
-        in_specs=[SMEM] * pieces + [HBM] * (pieces + 3),
+        in_specs=[SMEM] * pieces + [VMEM] * (pieces + 3),
         out_specs=[VMEM] * 3,
         scratch_shapes=[
-            pltpu.VMEM((pieces, nbatch, columns, columns), BF16),
             pltpu.VMEM((3 * region, width), BF16),
             pltpu.VMEM((3 * region, width), F32),
-            pltpu.SemaphoreType.DMA((pieces + 3,)),
         ],
         compiler_params=params(),
         cost_estimate=pl.CostEstimate(
-            flops=2 * pieces * nbatch * columns * columns * width,
-            bytes_accessed=pieces * nbatch * columns * columns * 2 + 14 * region * width,
+            flops=2 * work * columns * columns * width,
+            bytes_accessed=work * columns * columns * 2 + 14 * region * width,
             transcendentals=0,
         ),
     )(*blocks, *hams, before, own, after)
@@ -311,43 +300,38 @@
 
 
 def trade(array, rows, choice):
-    keep = lax.dynamic_slice_in_dim(array, choice * rows, rows, 1)
-    return keep, lax.dynamic_slice_in_dim(array, (1 - choice) * rows, rows, 1).astype(BF16)
+    keep = lax.dynamic_slice_in_dim(array, choice * rows, rows, 0)
+    return keep, lax.dynamic_slice_in_dim(array, (1 - choice) * rows, rows, 0).astype(BF16)
 
 
 def join(own, other, choice):
     low, high = jnp.where(choice == 0, own, other), jnp.where(choice == 0, other, own)
-    return jnp.concatenate([low, high], axis=1)
-
-
-def partners(masks):
-    size, tiles = lax.axis_size("grid"), lax.axis_size("tile")
-    return [
-        (g * tiles + t, (g ^ masks[t % 2]) * tiles + t) for g in range(size) for t in range(tiles)
-    ]
-
-
-def swap(array, masks):
-    return lax.ppermute(array, ("grid", "tile"), partners(masks))
-
-
-def rotate(parts, levels, energies):
+    return jnp.concatenate([low, high], axis=0)
+
+
+def halve(part, order):
+    half = part.shape[0] // 2
+    keep, send = trade(part, half, (lax.axis_index("grid") >> order) & 1)
+    return keep, flip(send, "grid", 1 << order)
+
+
+def rotate(part, level, energy, order, halved):
     if lax.axis_size("grid") != 8:
-        total = lax.psum(parts, "grid")
-        return (total / (levels[None, :, None] - energies[:, None, :])).astype(BF16)
-    grid, core = lax.axis_index("grid"), lax.axis_index("tile") % 2
-    first, second = (grid >> core) & 1, (grid >> (1 - core)) & 1
-    half = parts.shape[1] // 2
+        total = lax.psum(part, "grid")
+        return (total / (level[:, None] - energy[None, :])).astype(BF16)
+    grid = lax.axis_index("grid")
+    first, second = (grid >> order) & 1, (grid >> (1 - order)) & 1
+    half = part.shape[0] // 2
     quarter = half // 2
-    keep, send = trade(parts, half, first)
-    total = keep + swap(send, (1, 2)).astype(F32)
+    keep, coming = halved
+    total = keep + coming.astype(F32)
     keep, send = trade(total, quarter, second)
-    total = keep + swap(send, (2, 1)).astype(F32)
-    total = total + swap(total.astype(BF16), (4, 4)).astype(F32)
-    level = lax.dynamic_slice_in_dim(levels, first * half + second * quarter, quarter, 0)
-    own = (total / (level[None, :, None] - energies[:, None, :])).astype(BF16)
-    own = join(own, swap(own, (2, 1)), second)
-    return join(own, swap(own, (1, 2)), first)
+    total = keep + flip(send, "grid", 2 >> order).astype(F32)
+    total = total + flip(total.astype(BF16), "grid", 4).astype(F32)
+    level = lax.dynamic_slice_in_dim(level, first * half + second * quarter, quarter, 0)
+    own = (total / (level[:, None] - energy[None, :])).astype(BF16)
+    own = join(own, flip(own, "grid", 2 >> order), second)
+    return join(own, flip(own, "grid", 1 << order), first)
 
 
 def per_device(
@@ -369,33 +353,29 @@
     quarter = 2 * core + chip
 
     occ_own = column_part(occ_coef, quarter, width)
+
+    lists = [blocks, flip(blocks, "tile", 1), flip(blocks, "tile", 2)]
+    ham, *packed = integrate(basis_values, counts, weighted_potential)
+    arrived = [flip(array, "tile", 2) for array in packed]
+    occ_own, ham, lists = lax.optimization_barrier((occ_own, ham, lists))
+    lists.append(flip(lists[2], "tile", 1))
     occ_before, occ_after = neighbours(occ_own)
-
-    potential, occ_own = lax.optimization_barrier((weighted_potential, occ_own))
-    middle = -(-nbatch // 2)
-    lists = [blocks, flip(blocks, "tile", 1), flip(blocks, "tile", 2)]
-    lists.append(flip(lists[2], "tile", 1))
-    fulls, arrived = [], []
-    for start, stop in ((0, middle), (middle, nbatch)):
-        full, packed = integrate(basis_values, counts, potential, start, stop)
-        fulls.append(full)
-        arrived.append(flip(packed, "tile", 2))
-        potential, lists = lax.optimization_barrier((potential, lists))
-    lists, arrived[1], occ_before, occ_after = lax.optimization_barrier(
-        (lists, arrived[1], occ_before, occ_after)
-    )
-    hams, places = [], []
-    for i, (start, stop) in enumerate(((0, middle), (middle, nbatch))):
-        far = unpack(arrived[i], stop - start, columns)
-        hams += [fulls[i], flip(fulls[i], "tile", 1), far, flip(far, "tile", 1)]
-        places += [array[start:stop] for array in lists]
+    hams, places, starts, start = [ham, flip(ham, "tile", 1)], lists[:2], [0, 0], 0
+    arrived[-1], occ_before, occ_after = lax.optimization_barrier(
+        (arrived[-1], occ_before, occ_after)
+    )
+    for array, count in zip(arrived, groups(nbatch)):
+        far = unpack(array, count, columns)
+        hams += [far, flip(far, "tile", 1)]
+        places, starts, start = places + lists[2:], starts + [start] * 2, start + count
     blocks_near = lists[1]
     virt_near = flip(virt_coef, "tile", 1)
-    energies = jnp.stack([virt_energy, flip(virt_energy, "tile", 1)])
+    energies = [virt_energy, flip(virt_energy, "tile", 1)]
 
     to_before, own_sum, to_after = apply_window(
         places,
         hams,
+        starts,
         occ_before,
         occ_own,
         occ_after,
@@ -411,38 +391,44 @@
     ham_own = (own_sum + from_before.astype(F32) + from_after.astype(F32)).astype(BF16)
     ham_sums = [ham_own, flip(ham_own, "tile", 2)]
 
+    virtuals = [virt_coef, virt_near]
+    parts, halved, (ham_own, ham_far) = [], [], ham_sums
+    for side in range(2):
+        if side == 1:
+            ham_far, parts, halved = lax.optimization_barrier((ham_far, parts, halved))
+        for order, virt in enumerate(virtuals):
+            ham_sum = (ham_own, ham_far)[side]
+            part = lax.dot_general(
+                ham_sum, virt, (((0,), (0,)), ((), ())), preferred_element_type=F32
+            )
+            parts.append(part)
+            halved.append(halve(part, order))
     occ_far = column_part(occ_coef, quarter ^ 1, width)
-    late_before, late_after, _ = lax.optimization_barrier((occ_before, occ_after, ham_sums[1]))
+    late_before, late_after, _ = lax.optimization_barrier((occ_before, occ_after, parts[3]))
     before_far, after_far = flip(late_before, "tile", 2), flip(late_after, "tile", 2)
 
-    virtuals = [virt_coef, virt_near]
-    parts = []
-    for ham_sum in ham_sums:
-        ham_sum, parts = lax.optimization_barrier((ham_sum, parts))
-        products = [
-            lax.dot_general(ham_sum, virt, (((0,), (0,)), ((), ())), preferred_element_type=F32)
-            for virt in virtuals
-        ]
-        parts.append(jnp.stack(products))
-    rotated = [rotate(part, level, energies) for part, level in zip(parts, levels)]
+    rotated = [
+        rotate(part, levels[i // 2], energies[i % 2], i % 2, halved[i])
+        for i, part in enumerate(parts)
+    ]
     rotated[0], before_far, after_far = lax.optimization_barrier(
         (rotated[0], before_far, after_far)
     )
     coefs = []
-    for rotation in rotated:
+    for i in range(2):
         terms = [
-            lax.dot_general(virt, rotation[i], NT, preferred_element_type=F32)
-            for i, virt in enumerate(virtuals)
+            lax.dot_general(virt, rotation, NT, preferred_element_type=F32)
+            for virt, rotation in zip(virtuals, rotated[2 * i : 2 * i + 2])
         ]
         coefs.append(terms[0] + terms[1])
-    coef_far = flip(coefs[1].astype(BF16), "tile", 2)
-    resp_own = (coefs[0] + coef_far.astype(F32)).astype(BF16)
+    coef_own, coef_far = lax.optimization_barrier(
+        (coefs[0], flip(coefs[1].astype(BF16), "tile", 2))
+    )
+    resp_own = (coef_own + coef_far.astype(F32)).astype(BF16)
 
     resp_before, resp_after = neighbours(resp_own)
-    resp_far, resp_before, resp_after = lax.optimization_barrier(
-        (flip(resp_own, "tile", 2), resp_before, resp_after)
-    )
     resp_before_far, resp_after_far = flip(resp_before, "tile", 2), flip(resp_after, "tile", 2)
+    resp_far, *_ = lax.optimization_barrier((flip(resp_own, "tile", 2), resp_before, resp_after))
     first = chip == 0
     half = jnp.concatenate(
         [jnp.where(first, resp_own, resp_far), jnp.where(first, resp_far, resp_own)], axis=1

time: 180 us -> 185 us (1.028)
  starting transfers between devices: 37.5 us -> 48.3 us
  Pallas kernels: 24.5 us -> 19.1 us
  waiting for transfers between devices: 77.5 us -> 81.2 us
  other arithmetic: 8.35 us -> 5.77 us
    ppermute x10 -> x0, waiting for transfers between devices: 37.4 us -> none  [swap(): return lax.ppermute(array, ('grid', 'tile'), partners(masks))]
    ppermute x20 -> x39, waiting for transfers between devices: 24.4 us -> 60.1 us  [flip(): lax.ppermute(array, axis, [(i, i ^ mask) for i in range(lax.axis_size(axi...]
    ppermute x20 -> x39, starting transfers between devices: 11.9 us -> 34.3 us  [flip(): lax.ppermute(array, axis, [(i, i ^ mask) for i in range(lax.axis_size(axi...]
    ppermute x10 -> x0, starting transfers between devices: 10.4 us -> none  [swap(): return lax.ppermute(array, ('grid', 'tile'), partners(masks))]
    pallas_call x3 -> x2, Pallas kernels: 15.3 us -> 9.96 us  [the longest x1 6.47 us: apply_window(): pl.pallas_call(functools.partial(apply_kernel, starts, columns // per_bat...]
    ppermute x2, waiting for transfers between devices: 3.67 us -> 8.81 us  [neighbours(): lax.ppermute(array, 'grid', [(i, (i + 1) % size) for i in range(size)])]
    ppermute x2, starting transfers between devices: 3.27 us -> 0.01 us  [neighbours(): lax.ppermute(array, 'grid', [(i, (i + 1) % size) for i in range(size)])]
    unnamed x47 -> x39, local copies, waits for them, and re-layouts: 10.5 us -> 7.9 us
  transfers between devices with their start and end apart: 36 -> 45, of which waited for: 23 -> 28; matrix products, arithmetic and copies ran while one was open for 13% -> 12% of each run, Pallas kernels for 10% -> 6%
where the time goes in v5:
time: 185 us; the launch traced here: 184 us
  waiting for transfers between devices  81.2 us (44%)
  starting transfers between devices  48.3 us (26%)
  Pallas kernels  19.1 us (10%)
  matrix products  18.3 us (10%)
  local copies, waits for them, and re-layouts  10.3 us (6%)
  other arithmetic  5.77 us (3%)
    ppermute x39, waiting for transfers between devices, flip(): lax.ppermute(array, axis, [(i, i ^ mask) for i in range(lax.axis_size(axi...  60.1 us
    ppermute x39, starting transfers between devices, flip(): lax.ppermute(array, axis, [(i, i ^ mask) for i in range(lax.axis_size(axi...  34.3 us
    dot_general x4, matrix products, per_device(): lax.dot_general(ham_sum, virt, (((0,), (0,)), ((), ())), preferred_elemen...  9.31 us
    ppermute x2, starting transfers between devices, neighbours(): lax.ppermute(array, 'grid', [((i + 1) % size, i) for i in range(size)])  9.3 us
    dot_general x4, matrix products, per_device(): lax.dot_general(virt, rotation, NT, preferred_element_type=F32)  8.94 us
    ppermute x2, waiting for transfers between devices, neighbours(): lax.ppermute(array, 'grid', [(i, (i + 1) % size) for i in range(size)])  8.81 us
    unnamed x39, local copies, waits for them, and re-layouts  7.9 us
    ppermute x1, waiting for transfers between devices, per_device(): lax.ppermute(to_after, 'grid', [(i, (i + 1) % size) for i in range(size)])  6.88 us
  transfers between devices with their start and end apart: 45, of which 28 were waited for; matrix products, arithmetic and copies ran while one was open for 12% of the time, Pallas kernels for 6%

profile of v5, /device:TPU:0, one launch (start us, length us, event | category | flops | bytes accessed | tf_op | source)
XLA Modules:
  0.0 184.0 jit_solution(4898032438941119770)
XLA Ops:
  1.9 2.5 %collective-permute-start.1 = (s32[24,2]{1,0:T(8,128)S(1)}, s32[24,2]{1,0:T(8,128)S(1)}, u32[]{:S(2)}, u32[]{:S(2)}) collective-permute-start(s32[24,2]{1,0:T(8,128)S(1)} %copy.11), channel_id=1, source_target_pairs={{0,2},{1,3},{2,0},{3,1},{4,6},{5,7},{6,4},{7,5},{8,10},{9,11},{10,... | collective-permute-start | bytes 584 | tf_op jit(solution)/shard_map/ppermute | solution.py:288
  4.7 1.4 copy-done
  7.5 3.5 %shard_map.104 = (bf16[24,128,128]{2,1,0:T(8,128)(2,1)S(1)}, bf16[800,128]{1,0:T(8,128)(2,1)S(1)}, bf16[800,128]{1,0:T(8,128)(2,1)S(1)}) custom-call(s32[24]{0:T(128)S(1)} %copy-done.11, bf16[24,256,128]{2,1,0:T(8,128)(2,1)S(1)} %copy-done, f32[24,256]{1,0:T(8,128)S(1)} %copy-done.10), custom_call_target="tpu_custom_call" | custom-call | flops 402653184 | bytes 2752512 | tf_op jit(solution)/shard_map/pallas_call | solution.py:80
  12.5 4.8 %collective-permute-start.8 = (bf16[1024,128]{1,0:T(8,128)(2,1)S(1)}, bf16[1024,128]{1,0:T(8,128)(2,1)S(1)}, u32[]{:S(2)}, u32[]{:S(2)}) collective-permute-start(bf16[1024,128]{1,0:T(8,128)(2,1)S(1)} %get-tuple-element.46.refs_13_.refs_4_), channel_id=1, source_target_pairs={{4,0},{8,4},{12,8},{16,12},{20,16},{24,20},{28,24},{0,28},{5,1},{9... | collective-permute-start | bytes 786440 | tf_op jit(solution)/shard_map/ppermute | solution.py:294
  19.7 5.0 %collective-permute-done.6.packed_ref = bf16[800,128]{1,0:T(8,128)(2,1)S(1)} collective-permute-done((bf16[800,128]{1,0:T(8,128)(2,1)S(1)}, bf16[800,128]{1,0:T(8,128)(2,1)S(1)}, u32[]{:S(2)}, u32[]{:S(2)}) %collective-permute-start.6) | collective-permute-done | bytes 204832 | tf_op jit(solution)/shard_map/ppermute | solution.py:288
  24.8 3.6 %collective-permute-done.7.refs_12_.refs_2_ = bf16[1024,128]{1,0:T(8,128)(2,1)S(1)} collective-permute-done((bf16[1024,128]{1,0:T(8,128)(2,1)S(1)}, bf16[1024,128]{1,0:T(8,128)(2,1)S(1)}, u32[]{:S(2)}, u32[]{:S(2)}) %collective-permute-start.7) | collective-permute-done | bytes 262176 | tf_op jit(solution)/shard_map/ppermute | solution.py:293
  31.2 6.5 %shard_map.107 = (bf16[1024,128]{1,0:T(8,128)(2,1)S(1)}, f32[1024,128]{1,0:T(8,128)S(1)}, bf16[1024,128]{1,0:T(8,128)(2,1)}) custom-call(s32[24,2]{1,0:T(8,128)S(1)} %copy.13.refs_0_, s32[24,2]{1,0:T(8,128)S(1)} %collective-permute-done.refs_1_, s32[24,2]{1,0:T(8,128)S(1)} %collective-permute-done.1.refs_2_.refs_4_, ...), custom_call_target="tpu_custom_call" | custom-call | flops 402653184 | bytes 4980736 | tf_op jit(solution)/shard_map/pallas_call | solution.py:189
  39.5 3.7 %collective-permute-start.12 = (bf16[1024,128]{1,0:T(8,128)(2,1)S(1)}, bf16[1024,128]{1,0:T(8,128)(2,1)S(1)}, u32[]{:S(2)}, u32[]{:S(2)}) collective-permute-start(bf16[1024,128]{1,0:T(8,128)(2,1)S(1)} %get-tuple-element.53), channel_id=1, source_target_pairs={{4,0},{8,4},{12,8},{16,12},{20,16},{24,20},{28,24},{0,28},{5,1},{9... | collective-permute-start | bytes 786440 | tf_op jit(solution)/shard_map/ppermute | solution.py:390
  44.4 6.9 %collective-permute-done.11 = bf16[1024,128]{1,0:T(8,128)(2,1)S(1)} collective-permute-done((bf16[1024,128]{1,0:T(8,128)(2,1)}, bf16[1024,128]{1,0:T(8,128)(2,1)S(1)}, u32[]{:S(2)}, u32[]{:S(2)}) %collective-permute-start.11) | collective-permute-done | bytes 262176 | tf_op jit(solution)/shard_map/ppermute | solution.py:389
  51.3 1.9 %collective-permute-done.12 = bf16[1024,128]{1,0:T(8,128)(2,1)S(1)} collective-permute-done((bf16[1024,128]{1,0:T(8,128)(2,1)S(1)}, bf16[1024,128]{1,0:T(8,128)(2,1)S(1)}, u32[]{:S(2)}, u32[]{:S(2)}) %collective-permute-start.12) | collective-permute-done | bytes 262176 | tf_op jit(solution)/shard_map/ppermute | solution.py:390
  53.2 1.1 add_convert_fusion.1
  54.3 1.6 collective-permute-start.13
  55.9 2.9 %fusion.24 = f32[128,1920]{1,0:T(8,128)S(1)} fusion(bf16[1024,128]{1,0:T(8,128)(2,1)S(1)} %add_convert_fusion.1, bf16[1024,1920]{1,0:T(8,128)(2,1)} %param.15), kind=kOutput, calls=%fused_computation.79 | convolution fusion | flops 503316480 | bytes 5177344 | tf_op jit(solution)/shard_map/dot_general | solution.py:401
  59.4 2.9 %fusion.25 = f32[128,1920]{1,0:T(8,128)S(1)} fusion(bf16[1024,128]{1,0:T(8,128)(2,1)S(1)} %add_convert_fusion.1, bf16[1024,1920]{1,0:T(8,128)(2,1)} %collective-permute-done.14), kind=kOutput, calls=%fused_computation.80 | convolution fusion | flops 503316480 | bytes 5177344 | tf_op jit(solution)/shard_map/dot_general | solution.py:401
  63.3 2.1 %collective-permute-done.15 = bf16[64,1920]{1,0:T(8,128)(2,1)S(1)} collective-permute-done((bf16[64,1920]{1,0:T(8,128)(2,1)S(1)}, bf16[64,1920]{1,0:T(8,128)(2,1)S(1)}, u32[]{:S(2)}, u32[]{:S(2)}) %collective-permute-start.15) | collective-permute-done | bytes 245792 | tf_op jit(solution)/shard_map/ppermute | solution.py:288
  65.5 3.5 %collective-permute-done.16 = bf16[64,1920]{1,0:T(8,128)(2,1)S(1)} collective-permute-done((bf16[64,1920]{1,0:T(8,128)(2,1)S(1)}, bf16[64,1920]{1,0:T(8,128)(2,1)S(1)}, u32[]{:S(2)}, u32[]{:S(2)}) %collective-permute-start.16) | collective-permute-done | bytes 245792 | tf_op jit(solution)/shard_map/ppermute | solution.py:288
  69.0 2.9 %fusion.26 = f32[128,1920]{1,0:T(8,128)S(1)} fusion(bf16[1024,128]{1,0:T(8,128)(2,1)S(1)} %collective-permute-done.13, bf16[1024,1920]{1,0:T(8,128)(2,1)} %collective-permute-done.14), kind=kOutput, calls=%fused_computation.81 | convolution fusion | flops 503316480 | bytes 5177344 | tf_op jit(solution)/shard_map/dot_general | solution.py:401
  73.9 1.8 collective-permute-start.23
  76.7 1.5 collective-permute-start.22
  79.0 1.2 collective-permute-start.27
  80.2 2.6 %collective-permute-start.18 = (bf16[32,1920]{1,0:T(8,128)(2,1)S(1)}, bf16[32,1920]{1,0:T(8,128)(2,1)S(1)}, u32[]{:S(2)}, u32[]{:S(2)}) collective-permute-start(bf16[32,1920]{1,0:T(8,128)(2,1)S(1)} %fusion.14), channel_id=1, source_target_pairs={{0,16},{4,20},{8,24},{12,28},{16,0},{20,4},{24,8},{28,12},{1,17},{... | collective-permute-start | bytes 368648 | tf_op jit(solution)/shard_map/ppermute | solution.py:288
  82.9 1.3 collective-permute-done.32
  84.2 2.8 %collective-permute-start.24 = (bf16[32,1920]{1,0:T(8,128)(2,1)S(1)}, bf16[32,1920]{1,0:T(8,128)(2,1)S(1)}, u32[]{:S(2)}, u32[]{:S(2)}) collective-permute-start(bf16[32,1920]{1,0:T(8,128)(2,1)S(1)} %fusion.15), channel_id=1, source_target_pairs={{0,16},{4,20},{8,24},{12,28},{16,0},{20,4},{24,8},{28,12},{1,17},{... | collective-permute-start | bytes 368648 | tf_op jit(solution)/shard_map/ppermute | solution.py:288
  88.3 3.7 %collective-permute-done.33 = bf16[32,1920]{1,0:T(8,128)(2,1)S(1)} collective-permute-done((bf16[32,1920]{1,0:T(8,128)(2,1)S(1)}, bf16[32,1920]{1,0:T(8,128)(2,1)S(1)}, u32[]{:S(2)}, u32[]{:S(2)}) %collective-permute-start.33) | collective-permute-done | bytes 122912 | tf_op jit(solution)/shard_map/ppermute | solution.py:288
  92.3 4.6 %collective-permute-done.28 = bf16[32,1920]{1,0:T(8,128)(2,1)S(1)} collective-permute-done((bf16[32,1920]{1,0:T(8,128)(2,1)S(1)}, bf16[32,1920]{1,0:T(8,128)(2,1)S(1)}, u32[]{:S(2)}, u32[]{:S(2)}) %collective-permute-start.28) | collective-permute-done | bytes 122912 | tf_op jit(solution)/shard_map/ppermute | solution.py:288
  96.9 1.8 collective-permute-start.34
  98.8 1.2 collective-permute-start.29
  99.9 4.5 %collective-permute-done.34 = bf16[32,1920]{1,0:T(8,128)(2,1)S(1)} collective-permute-done((bf16[32,1920]{1,0:T(8,128)(2,1)S(1)}, bf16[32,1920]{1,0:T(8,128)(2,1)S(1)}, u32[]{:S(2)}, u32[]{:S(2)}) %collective-permute-start.34) | collective-permute-done | bytes 122912 | tf_op jit(solution)/shard_map/ppermute | solution.py:288
  104.6 1.8 collective-permute-start.35
  107.8 1.7 collective-permute-done.35
  112.1 4.0 %collective-permute-done.19 = bf16[32,1920]{1,0:T(8,128)(2,1)S(1)} collective-permute-done((bf16[32,1920]{1,0:T(8,128)(2,1)S(1)}, bf16[32,1920]{1,0:T(8,128)(2,1)S(1)}, u32[]{:S(2)}, u32[]{:S(2)}) %collective-permute-start.19) | collective-permute-done | bytes 122912 | tf_op jit(solution)/shard_map/ppermute | solution.py:288
  117.8 5.3 %collective-permute-done.20 = bf16[64,1920]{1,0:T(8,128)(2,1)S(1)} collective-permute-done((bf16[64,1920]{1,0:T(8,128)(2,1)S(1)}, bf16[64,1920]{1,0:T(8,128)(2,1)S(1)}, u32[]{:S(2)}, u32[]{:S(2)}) %collective-permute-start.20) | collective-permute-done | bytes 245792 | tf_op jit(solution)/shard_map/ppermute | solution.py:288
  124.2 5.1 %collective-permute-done.31 = bf16[64,1920]{1,0:T(8,128)(2,1)S(1)} collective-permute-done((bf16[64,1920]{1,0:T(8,128)(2,1)S(1)}, bf16[64,1920]{1,0:T(8,128)(2,1)S(1)}, u32[]{:S(2)}, u32[]{:S(2)}) %collective-permute-start.31) | collective-permute-done | bytes 245792 | tf_op jit(solution)/shard_map/ppermute | solution.py:288
  129.4 3.3 %fusion.10 = f32[128,1024]{0,1:T(8,128)S(1)} fusion(bf16[1024,1920]{1,0:T(8,128)(2,1)} %collective-permute-done.14, bf16[64,1920]{1,0:T(8,128)(2,1)S(1)} %get-tuple-element.85, bf16[64,1920]{1,0:T(8,128)(2,1)S(1)} %get-tuple-element.84), kind=kOutput, calls=%fused_computation.19 | convolution fusion | flops 504299520 | bytes 4947968 | tf_op jit(solution)/shard_map/dot_general | solution.py:420
  132.7 1.2 fusion.2
  134.5 3.3 %fusion.3 = f32[128,1024]{0,1:T(8,128)S(1)} fusion(bf16[1024,1920]{1,0:T(8,128)(2,1)} %collective-permute-done.14, bf16[64,1920]{1,0:T(8,128)(2,1)S(1)} %get-tuple-element.89, bf16[64,1920]{1,0:T(8,128)(2,1)S(1)} %get-tuple-element.88), kind=kOutput, calls=%fused_computation.12 | convolution fusion | flops 504299520 | bytes 4947968 | tf_op jit(solution)/shard_map/dot_general | solution.py:420
  137.8 1.2 fusion
  139.0 2.5 %collective-permute-done.37 = bf16[1024,128]{1,0:T(8,128)(2,1)S(1)} collective-permute-done((bf16[1024,128]{1,0:T(8,128)(2,1)S(1)}, bf16[1024,128]{1,0:T(8,128)(2,1)S(1)}, u32[]{:S(2)}, u32[]{:S(2)}) %collective-permute-start.37) | collective-permute-done | bytes 262176 | tf_op jit(solution)/shard_map/ppermute | solution.py:288
  141.6 4.5 %collective-permute-start.40 = (bf16[1024,128]{1,0:T(8,128)(2,1)S(1)}, bf16[1024,128]{1,0:T(8,128)(2,1)S(1)}, u32[]{:S(2)}, u32[]{:S(2)}) collective-permute-start(bf16[1024,128]{1,0:T(8,128)(2,1)S(1)} %add_convert_fusion.refs_10_), channel_id=1, source_target_pairs={{4,0},{8,4},{12,8},{16,12},{20,16},{24,20},{28,24},{0,28},{5,1},{9... | collective-permute-start | bytes 786440 | tf_op jit(solution)/shard_map/ppermute | solution.py:294
  146.5 3.5 %collective-permute-done.40.refs_12_ = bf16[1024,128]{1,0:T(8,128)(2,1)S(1)} collective-permute-done((bf16[1024,128]{1,0:T(8,128)(2,1)S(1)}, bf16[1024,128]{1,0:T(8,128)(2,1)S(1)}, u32[]{:S(2)}, u32[]{:S(2)}) %collective-permute-start.40) | collective-permute-done | bytes 262176 | tf_op jit(solution)/shard_map/ppermute | solution.py:294
  149.9 5.2 %collective-permute-done.39.refs_8_ = bf16[1024,128]{1,0:T(8,128)(2,1)S(1)} collective-permute-done((bf16[1024,128]{1,0:T(8,128)(2,1)S(1)}, bf16[1024,128]{1,0:T(8,128)(2,1)S(1)}, u32[]{:S(2)}, u32[]{:S(2)}) %collective-permute-start.39) | collective-permute-done | bytes 262176 | tf_op jit(solution)/shard_map/ppermute | solution.py:293
  157.2 1.6 collective-permute-start.42
  159.0 1.4 broadcast_select_fusion.1
  161.6 4.7 %collective-permute-done.43.refs_13_ = bf16[1024,128]{1,0:T(8,128)(2,1)} collective-permute-done((bf16[1024,128]{1,0:T(8,128)(2,1)}, bf16[1024,128]{1,0:T(8,128)(2,1)}, u32[]{:S(2)}, u32[]{:S(2)}) %collective-permute-start.43) | collective-permute-done | bytes 262176 | tf_op jit(solution)/shard_map/ppermute | solution.py:288
  166.3 5.2 %collective-permute-done.42.refs_9_ = bf16[1024,128]{1,0:T(8,128)(2,1)} collective-permute-done((bf16[1024,128]{1,0:T(8,128)(2,1)}, bf16[1024,128]{1,0:T(8,128)(2,1)}, u32[]{:S(2)}, u32[]{:S(2)}) %collective-permute-start.42) | collective-permute-done | bytes 262176 | tf_op jit(solution)/shard_map/ppermute | solution.py:288
  174.3 4.3 %shard_map.108 = (f32[24,128,128]{2,1,0:T(8,128)S(1)}, bf16[24,128,128]{2,1,0:T(8,128)(2,1)S(1)}) custom-call(s32[24,2]{1,0:T(8,128)S(1)} %copy.18.refs_0_, s32[24,2]{1,0:T(8,128)S(1)} %collective-permute-done.refs_1_, bf16[1024,128]{1,0:T(8,128)(2,1)S(1)} %collective-permute-done.7.refs_12_.refs_2_, bf16[1024,128]{1,0:T(8,128)(2,1)S(1)} %collective-permute-done.21.refs_3_, ...), custom_call_target="tpu_custom_call" | custom-call | flops 402653184 | bytes 5505024 | tf_op jit(solution)/shard_map/pallas_call | solution.py:240
  178.6 2.3 %collective-permute-done.44.second_ref = bf16[24,128,128]{2,1,0:T(8,128)(2,1)S(1)} collective-permute-done((bf16[24,128,128]{2,1,0:T(8,128)(2,1)S(1)}, bf16[24,128,128]{2,1,0:T(8,128)(2,1)S(1)}, u32[]{:S(2)}, u32[]{:S(2)}) %collective-permute-start.44) | collective-permute-done | bytes 786464 | tf_op jit(solution)/shard_map/ppermute | solution.py:288
  180.9 3.1 %shard_map.109 = f32[24,256]{1,0:T(8,128)} custom-call(s32[24]{0:T(128)S(1)} %copy-done.12, bf16[24,256,128]{2,1,0:T(8,128)(2,1)S(1)} %copy-done.1, f32[24,128,128]{2,1,0:T(8,128)S(1)} %get-tuple-element.74.first_ref, bf16[24,128,128]{2,1,0:T(8,128)(2,1)S(1)} %collective-permute-done.44.second_ref, f32[24,256]{1,0:T(8,128)S(1)} %copy-done.9), custom_call_target="tpu_custom_call" | custom-call | flops 402653184 | bytes 3932160 | tf_op jit(solution)/shard_map/pallas_call | solution.py:273
  (139 shorter events, 34.3 us)
Async XLA Ops:
  0.6 58.7 %collective-permute-start.14 = (bf16[1024,1920]{1,0:T(8,128)(2,1)}, bf16[1024,1920]{1,0:T(8,128)(2,1)}, u32[]{:S(2)}, u32[]{:S(2)}) collective-permute-start(bf16[1024,1920]{1,0:T(8,128)(2,1)} %param.15), channel_id=1, source_target_pairs={{0,1},{1,0},{2,3},{3,2},{4,5},{5,4},{6,7},{7,6},{8,9},{9,8},{10,11... | collective-permute-start | bytes 11796488 | tf_op jit(solution)/shard_map/ppermute | solution.py:288
  1.1 42.0 %copy-start.17 = (f32[1920]{0:T(1024)S(1)}, f32[1920]{0:T(1024)}, u32[]{:S(2)}) copy-start(f32[1920]{0:T(1024)} %param.17) | copy-start | bytes 23044
  1.1 42.0 %copy-start.18 = (f32[512]{0:T(512)S(1)}, f32[512]{0:T(512)}, u32[]{:S(2)}) copy-start(f32[512]{0:T(512)} %param.16) | copy-start | bytes 6148
  1.9 10.4 %collective-permute-start.1 = (s32[24,2]{1,0:T(8,128)S(1)}, s32[24,2]{1,0:T(8,128)S(1)}, u32[]{:S(2)}, u32[]{:S(2)}) collective-permute-start(s32[24,2]{1,0:T(8,128)S(1)} %copy.11), channel_id=1, source_target_pairs={{0,2},{1,3},{2,0},{3,1},{4,6},{5,7},{6,4},{7,5},{8,10},{9,11},{10,... | collective-permute-start | bytes 584 | tf_op jit(solution)/shard_map/ppermute | solution.py:288
  4.4 8.0 %collective-permute-start = (s32[24,2]{1,0:T(8,128)S(1)}, s32[24,2]{1,0:T(8,128)S(1)}, u32[]{:S(2)}, u32[]{:S(2)}) collective-permute-start(s32[24,2]{1,0:T(8,128)S(1)} %copy.11), channel_id=1, source_target_pairs={{0,1},{1,0},{2,3},{3,2},{4,5},{5,4},{6,7},{7,6},{8,9},{9,8},{10,11... | collective-permute-start | bytes 584 | tf_op jit(solution)/shard_map/ppermute | solution.py:288
  11.0 7.3 %collective-permute-start.4 = (bf16[800,128]{1,0:T(8,128)(2,1)S(1)}, bf16[800,128]{1,0:T(8,128)(2,1)S(1)}, u32[]{:S(2)}, u32[]{:S(2)}) collective-permute-start(bf16[800,128]{1,0:T(8,128)(2,1)S(1)} %get-tuple-element.44), channel_id=1, source_target_pairs={{0,2},{1,3},{2,0},{3,1},{4,6},{5,7},{6,4},{7,5},{8,10},{9,11},{10,... | collective-permute-start | bytes 614408 | tf_op jit(solution)/shard_map/ppermute | solution.py:288
  12.4 18.8 %collective-permute-start.3 = (bf16[24,128,128]{2,1,0:T(8,128)(2,1)S(1)}, bf16[24,128,128]{2,1,0:T(8,128)(2,1)}, u32[]{:S(2)}, u32[]{:S(2)}) collective-permute-start(bf16[24,128,128]{2,1,0:T(8,128)(2,1)S(1)} %get-tuple-element.43.refs_6_), channel_id=1, source_target_pairs={{0,1},{1,0},{2,3},{3,2},{4,5},{5,4},{6,7},{7,6},{8,9},{9,8},{10,11... | collective-permute-start | bytes 2359304 | tf_op jit(solution)/shard_map/ppermute | solution.py:288
  12.5 12.2 %collective-permute-start.8 = (bf16[1024,128]{1,0:T(8,128)(2,1)S(1)}, bf16[1024,128]{1,0:T(8,128)(2,1)S(1)}, u32[]{:S(2)}, u32[]{:S(2)}) collective-permute-start(bf16[1024,128]{1,0:T(8,128)(2,1)S(1)} %get-tuple-element.46.refs_13_.refs_4_), channel_id=1, source_target_pairs={{4,0},{8,4},{12,8},{16,12},{20,16},{24,20},{28,24},{0,28},{5,1},{9... | collective-permute-start | bytes 786440 | tf_op jit(solution)/shard_map/ppermute | solution.py:294
  17.3 11.1 %collective-permute-start.7 = (bf16[1024,128]{1,0:T(8,128)(2,1)S(1)}, bf16[1024,128]{1,0:T(8,128)(2,1)S(1)}, u32[]{:S(2)}, u32[]{:S(2)}) collective-permute-start(bf16[1024,128]{1,0:T(8,128)(2,1)S(1)} %get-tuple-element.46.refs_13_.refs_4_), channel_id=1, source_target_pairs={{0,4},{4,8},{8,12},{12,16},{16,20},{20,24},{24,28},{28,0},{1,5},{5... | collective-permute-start | bytes 786440 | tf_op jit(solution)/shard_map/ppermute | solution.py:293
  18.3 6.5 %collective-permute-start.6 = (bf16[800,128]{1,0:T(8,128)(2,1)S(1)}, bf16[800,128]{1,0:T(8,128)(2,1)S(1)}, u32[]{:S(2)}, u32[]{:S(2)}) collective-permute-start(bf16[800,128]{1,0:T(8,128)(2,1)S(1)} %get-tuple-element.45), channel_id=1, source_target_pairs={{0,2},{1,3},{2,0},{3,1},{4,6},{5,7},{6,4},{7,5},{8,10},{9,11},{10,... | collective-permute-start | bytes 614408 | tf_op jit(solution)/shard_map/ppermute | solution.py:288
  24.8 6.3 %collective-permute-start.5 = (bf16[12,128,128]{2,1,0:T(8,128)(2,1)S(1)}, bf16[12,128,128]{2,1,0:T(8,128)(2,1)S(1)}, u32[]{:S(2)}, u32[]{:S(2)}) collective-permute-start(bf16[12,128,128]{2,1,0:T(8,128)(2,1)S(1)} %shard_map.105.refs_8_), channel_id=1, source_target_pairs={{0,1},{1,0},{2,3},{3,2},{4,5},{5,4},{6,7},{7,6},{8,9},{9,8},{10,11... | collective-permute-start | bytes 1179656 | tf_op jit(solution)/shard_map/ppermute | solution.py:288
  29.3 1.9 %collective-permute-start.9 = (bf16[12,128,128]{2,1,0:T(8,128)(2,1)S(1)}, bf16[12,128,128]{2,1,0:T(8,128)(2,1)}, u32[]{:S(2)}, u32[]{:S(2)}) collective-permute-start(bf16[12,128,128]{2,1,0:T(8,128)(2,1)S(1)} %shard_map.106.refs_10_), channel_id=1, source_target_pairs={{0,1},{1,0},{2,3},{3,2},{4,5},{5,4},{6,7},{7,6},{8,9},{9,8},{10,11... | collective-permute-start | bytes 1179656 | tf_op jit(solution)/shard_map/ppermute | solution.py:288
  29.3 1.7 collective-permute-start.2
  38.4 12.9 %collective-permute-start.11 = (bf16[1024,128]{1,0:T(8,128)(2,1)}, bf16[1024,128]{1,0:T(8,128)(2,1)S(1)}, u32[]{:S(2)}, u32[]{:S(2)}) collective-permute-start(bf16[1024,128]{1,0:T(8,128)(2,1)} %get-tuple-element.52), channel_id=1, source_target_pairs={{0,4},{4,8},{8,12},{12,16},{16,20},{20,24},{24,28},{28,0},{1,5},{5... | collective-permute-start | bytes 786440 | tf_op jit(solution)/shard_map/ppermute | solution.py:389
  39.5 13.7 %collective-permute-start.12 = (bf16[1024,128]{1,0:T(8,128)(2,1)S(1)}, bf16[1024,128]{1,0:T(8,128)(2,1)S(1)}, u32[]{:S(2)}, u32[]{:S(2)}) collective-permute-start(bf16[1024,128]{1,0:T(8,128)(2,1)S(1)} %get-tuple-element.53), channel_id=1, source_target_pairs={{4,0},{8,4},{12,8},{16,12},{20,16},{24,20},{28,24},{0,28},{5,1},{9... | collective-permute-start | bytes 786440 | tf_op jit(solution)/shard_map/ppermute | solution.py:390
  43.2 1.2 collective-permute-start.10
  54.3 11.1 %collective-permute-start.13 = (bf16[1024,128]{1,0:T(8,128)(2,1)S(1)}, bf16[1024,128]{1,0:T(8,128)(2,1)S(1)}, u32[]{:S(2)}, u32[]{:S(2)}) collective-permute-start(bf16[1024,128]{1,0:T(8,128)(2,1)S(1)} %add_convert_fusion.1), channel_id=1, source_target_pairs={{0,2},{1,3},{2,0},{3,1},{4,6},{5,7},{6,4},{7,5},{8,10},{9,11},{10,... | collective-permute-start | bytes 786440 | tf_op jit(solution)/shard_map/ppermute | solution.py:288
  58.8 6.6 %collective-permute-start.15 = (bf16[64,1920]{1,0:T(8,128)(2,1)S(1)}, bf16[64,1920]{1,0:T(8,128)(2,1)S(1)}, u32[]{:S(2)}, u32[]{:S(2)}) collective-permute-start(bf16[64,1920]{1,0:T(8,128)(2,1)S(1)} %dynamic-slice_convert_fusion.3), channel_id=1, source_target_pairs={{0,4},{4,0},{8,12},{12,8},{16,20},{20,16},{24,28},{28,24},{1,5},{5... | collective-permute-start | bytes 737288 | tf_op jit(solution)/shard_map/ppermute | solution.py:288
  62.3 6.7 %collective-permute-start.16 = (bf16[64,1920]{1,0:T(8,128)(2,1)S(1)}, bf16[64,1920]{1,0:T(8,128)(2,1)S(1)}, u32[]{:S(2)}, u32[]{:S(2)}) collective-permute-start(bf16[64,1920]{1,0:T(8,128)(2,1)S(1)} %dynamic-slice_convert_fusion.2), channel_id=1, source_target_pairs={{0,8},{4,12},{8,0},{12,4},{16,24},{20,28},{24,16},{28,20},{1,9},{5... | collective-permute-start | bytes 737288 | tf_op jit(solution)/shard_map/ppermute | solution.py:288
  72.7 6.3 %collective-permute-start.17 = (bf16[32,1920]{1,0:T(8,128)(2,1)S(1)}, bf16[32,1920]{1,0:T(8,128)(2,1)S(1)}, u32[]{:S(2)}, u32[]{:S(2)}) collective-permute-start(bf16[32,1920]{1,0:T(8,128)(2,1)S(1)} %dynamic-slice_convert_fusion.7), channel_id=1, source_target_pairs={{0,8},{4,12},{8,0},{12,4},{16,24},{20,28},{24,16},{28,20},{1,9},{5... | collective-permute-start | bytes 368648 | tf_op jit(solution)/shard_map/ppermute | solution.py:288
  73.9 6.3 %collective-permute-start.23 = (bf16[32,1920]{1,0:T(8,128)(2,1)S(1)}, bf16[32,1920]{1,0:T(8,128)(2,1)S(1)}, u32[]{:S(2)}, u32[]{:S(2)}) collective-permute-start(bf16[32,1920]{1,0:T(8,128)(2,1)S(1)} %dynamic-slice_convert_fusion.6), channel_id=1, source_target_pairs={{0,4},{4,0},{8,12},{12,8},{16,20},{20,16},{24,28},{28,24},{1,5},{5... | collective-permute-start | bytes 368648 | tf_op jit(solution)/shard_map/ppermute | solution.py:288
  75.7 8.5 %collective-permute-start.32 = (bf16[64,1920]{1,0:T(8,128)(2,1)S(1)}, bf16[64,1920]{1,0:T(8,128)(2,1)S(1)}, u32[]{:S(2)}, u32[]{:S(2)}) collective-permute-start(bf16[64,1920]{1,0:T(8,128)(2,1)S(1)} %dynamic-slice_convert_fusion), channel_id=1, source_target_pairs={{0,8},{4,12},{8,0},{12,4},{16,24},{20,28},{24,16},{28,20},{1,9},{5... | collective-permute-start | bytes 737288 | tf_op jit(solution)/shard_map/ppermute | solution.py:288
  76.2 47.9 %collective-permute-start.21 = (bf16[1024,128]{1,0:T(8,128)(2,1)S(1)}, bf16[1024,128]{1,0:T(8,128)(2,1)S(1)}, u32[]{:S(2)}, u32[]{:S(2)}) collective-permute-start(bf16[1024,128]{1,0:T(8,128)(2,1)S(1)} %collective-permute-done.7.refs_12_.refs_2_), channel_id=1, source_target_pairs={{0,2},{1,3},{2,0},{3,1},{4,6},{5,7},{6,4},{7,5},{8,10},{9,11},{10,... | collective-permute-start | bytes 786440 | tf_op jit(solution)/shard_map/ppermute | solution.py:288
  76.7 47.4 %collective-permute-start.22 = (bf16[1024,128]{1,0:T(8,128)(2,1)S(1)}, bf16[1024,128]{1,0:T(8,128)(2,1)S(1)}, u32[]{:S(2)}, u32[]{:S(2)}) collective-permute-start(bf16[1024,128]{1,0:T(8,128)(2,1)S(1)} %collective-permute-done.8.refs_14_.refs_6_), channel_id=1, source_target_pairs={{0,2},{1,3},{2,0},{3,1},{4,6},{5,7},{6,4},{7,5},{8,10},{9,11},{10,... | collective-permute-start | bytes 786440 | tf_op jit(solution)/shard_map/ppermute | solution.py:288
  79.0 8.1 %collective-permute-start.27 = (bf16[64,1920]{1,0:T(8,128)(2,1)S(1)}, bf16[64,1920]{1,0:T(8,128)(2,1)S(1)}, u32[]{:S(2)}, u32[]{:S(2)}) collective-permute-start(bf16[64,1920]{1,0:T(8,128)(2,1)S(1)} %dynamic-slice_convert_fusion.1), channel_id=1, source_target_pairs={{0,4},{4,0},{8,12},{12,8},{16,20},{20,16},{24,28},{28,24},{1,5},{5... | collective-permute-start | bytes 737288 | tf_op jit(solution)/shard_map/ppermute | solution.py:288
  80.2 26.1 %collective-permute-start.18 = (bf16[32,1920]{1,0:T(8,128)(2,1)S(1)}, bf16[32,1920]{1,0:T(8,128)(2,1)S(1)}, u32[]{:S(2)}, u32[]{:S(2)}) collective-permute-start(bf16[32,1920]{1,0:T(8,128)(2,1)S(1)} %fusion.14), channel_id=1, source_target_pairs={{0,16},{4,20},{8,24},{12,28},{16,0},{20,4},{24,8},{28,12},{1,17},{... | collective-permute-start | bytes 368648 | tf_op jit(solution)/shard_map/ppermute | solution.py:288
  84.2 14.5 %collective-permute-start.24 = (bf16[32,1920]{1,0:T(8,128)(2,1)S(1)}, bf16[32,1920]{1,0:T(8,128)(2,1)S(1)}, u32[]{:S(2)}, u32[]{:S(2)}) collective-permute-start(bf16[32,1920]{1,0:T(8,128)(2,1)S(1)} %fusion.15), channel_id=1, source_target_pairs={{0,16},{4,20},{8,24},{12,28},{16,0},{20,4},{24,8},{28,12},{1,17},{... | collective-permute-start | bytes 368648 | tf_op jit(solution)/shard_map/ppermute | solution.py:288
  87.1 4.9 %collective-permute-start.33 = (bf16[32,1920]{1,0:T(8,128)(2,1)S(1)}, bf16[32,1920]{1,0:T(8,128)(2,1)S(1)}, u32[]{:S(2)}, u32[]{:S(2)}) collective-permute-start(bf16[32,1920]{1,0:T(8,128)(2,1)S(1)} %dynamic-slice_convert_fusion.4), channel_id=1, source_target_pairs={{0,4},{4,0},{8,12},{12,8},{16,20},{20,16},{24,28},{28,24},{1,5},{5... | collective-permute-start | bytes 368648 | tf_op jit(solution)/shard_map/ppermute | solution.py:288
  92.0 4.9 %collective-permute-start.28 = (bf16[32,1920]{1,0:T(8,128)(2,1)S(1)}, bf16[32,1920]{1,0:T(8,128)(2,1)S(1)}, u32[]{:S(2)}, u32[]{:S(2)}) collective-permute-start(bf16[32,1920]{1,0:T(8,128)(2,1)S(1)} %dynamic-slice_convert_fusion.5), channel_id=1, source_target_pairs={{0,8},{4,12},{8,0},{12,4},{16,24},{20,28},{24,16},{28,20},{1,9},{5... | collective-permute-start | bytes 368648 | tf_op jit(solution)/shard_map/ppermute | solution.py:288
  96.9 7.5 %collective-permute-start.34 = (bf16[32,1920]{1,0:T(8,128)(2,1)S(1)}, bf16[32,1920]{1,0:T(8,128)(2,1)S(1)}, u32[]{:S(2)}, u32[]{:S(2)}) collective-permute-start(bf16[32,1920]{1,0:T(8,128)(2,1)S(1)} %fusion.17), channel_id=1, source_target_pairs={{0,16},{4,20},{8,24},{12,28},{16,0},{20,4},{24,8},{28,12},{1,17},{... | collective-permute-start | bytes 368648 | tf_op jit(solution)/shard_map/ppermute | solution.py:288
  98.8 8.2 %collective-permute-start.29 = (bf16[32,1920]{1,0:T(8,128)(2,1)S(1)}, bf16[32,1920]{1,0:T(8,128)(2,1)S(1)}, u32[]{:S(2)}, u32[]{:S(2)}) collective-permute-start(bf16[32,1920]{1,0:T(8,128)(2,1)S(1)} %fusion.16), channel_id=1, source_target_pairs={{0,16},{4,20},{8,24},{12,28},{16,0},{20,4},{24,8},{28,12},{1,17},{... | collective-permute-start | bytes 368648 | tf_op jit(solution)/shard_map/ppermute | solution.py:288
  104.6 4.9 %collective-permute-start.35 = (bf16[32,1920]{1,0:T(8,128)(2,1)S(1)}, bf16[32,1920]{1,0:T(8,128)(2,1)S(1)}, u32[]{:S(2)}, u32[]{:S(2)}) collective-permute-start(bf16[32,1920]{1,0:T(8,128)(2,1)S(1)} %get-tuple-element.100), channel_id=1, source_target_pairs={{0,4},{4,0},{8,12},{12,8},{16,20},{20,16},{24,28},{28,24},{1,5},{5... | collective-permute-start | bytes 368648 | tf_op jit(solution)/shard_map/ppermute | solution.py:288
  106.3 4.9 %collective-permute-start.25 = (bf16[32,1920]{1,0:T(8,128)(2,1)S(1)}, bf16[32,1920]{1,0:T(8,128)(2,1)S(1)}, u32[]{:S(2)}, u32[]{:S(2)}) collective-permute-start(bf16[32,1920]{1,0:T(8,128)(2,1)S(1)} %get-tuple-element.101), channel_id=1, source_target_pairs={{0,4},{4,0},{8,12},{12,8},{16,20},{20,16},{24,28},{28,24},{1,5},{5... | collective-permute-start | bytes 368648 | tf_op jit(solution)/shard_map/ppermute | solution.py:288
  107.2 9.6 %collective-permute-start.30 = (bf16[32,1920]{1,0:T(8,128)(2,1)S(1)}, bf16[32,1920]{1,0:T(8,128)(2,1)S(1)}, u32[]{:S(2)}, u32[]{:S(2)}) collective-permute-start(bf16[32,1920]{1,0:T(8,128)(2,1)S(1)} %get-tuple-element.98), channel_id=1, source_target_pairs={{0,8},{4,12},{8,0},{12,4},{16,24},{20,28},{24,16},{28,20},{1,9},{5... | collective-permute-start | bytes 368648 | tf_op jit(solution)/shard_map/ppermute | solution.py:288
  109.5 6.6 %collective-permute-start.19 = (bf16[32,1920]{1,0:T(8,128)(2,1)S(1)}, bf16[32,1920]{1,0:T(8,128)(2,1)S(1)}, u32[]{:S(2)}, u32[]{:S(2)}) collective-permute-start(bf16[32,1920]{1,0:T(8,128)(2,1)S(1)} %get-tuple-element.99), channel_id=1, source_target_pairs={{0,8},{4,12},{8,0},{12,4},{16,24},{20,28},{24,16},{28,20},{1,9},{5... | collective-permute-start | bytes 368648 | tf_op jit(solution)/shard_map/ppermute | solution.py:288
  111.2 12.9 %collective-permute-start.36 = (bf16[64,1920]{1,0:T(8,128)(2,1)S(1)}, bf16[64,1920]{1,0:T(8,128)(2,1)S(1)}, u32[]{:S(2)}, u32[]{:S(2)}) collective-permute-start(bf16[64,1920]{1,0:T(8,128)(2,1)S(1)} %pad_maximum_fusion.6), channel_id=1, source_target_pairs={{0,8},{4,12},{8,0},{12,4},{16,24},{20,28},{24,16},{28,20},{1,9},{5... | collective-permute-start | bytes 737288 | tf_op jit(solution)/shard_map/ppermute | solution.py:288
  116.1 18.3 %collective-permute-start.26 = (bf16[64,1920]{1,0:T(8,128)(2,1)S(1)}, bf16[64,1920]{1,0:T(8,128)(2,1)S(1)}, u32[]{:S(2)}, u32[]{:S(2)}) collective-permute-start(bf16[64,1920]{1,0:T(8,128)(2,1)S(1)} %pad_maximum_fusion.4), channel_id=1, source_target_pairs={{0,8},{4,12},{8,0},{12,4},{16,24},{20,28},{24,16},{28,20},{1,9},{5... | collective-permute-start | bytes 737288 | tf_op jit(solution)/shard_map/ppermute | solution.py:288
  116.8 6.3 %collective-permute-start.20 = (bf16[64,1920]{1,0:T(8,128)(2,1)S(1)}, bf16[64,1920]{1,0:T(8,128)(2,1)S(1)}, u32[]{:S(2)}, u32[]{:S(2)}) collective-permute-start(bf16[64,1920]{1,0:T(8,128)(2,1)S(1)} %pad_maximum_fusion.3), channel_id=1, source_target_pairs={{0,4},{4,0},{8,12},{12,8},{16,20},{20,16},{24,28},{28,24},{1,5},{5... | collective-permute-start | bytes 737288 | tf_op jit(solution)/shard_map/ppermute | solution.py:288
  123.1 6.2 %collective-permute-start.31 = (bf16[64,1920]{1,0:T(8,128)(2,1)S(1)}, bf16[64,1920]{1,0:T(8,128)(2,1)S(1)}, u32[]{:S(2)}, u32[]{:S(2)}) collective-permute-start(bf16[64,1920]{1,0:T(8,128)(2,1)S(1)} %pad_maximum_fusion.5), channel_id=1, source_target_pairs={{0,4},{4,0},{8,12},{12,8},{16,20},{20,16},{24,28},{28,24},{1,5},{5... | collective-permute-start | bytes 737288 | tf_op jit(solution)/shard_map/ppermute | solution.py:288
  133.9 7.6 %collective-permute-start.37 = (bf16[1024,128]{1,0:T(8,128)(2,1)S(1)}, bf16[1024,128]{1,0:T(8,128)(2,1)S(1)}, u32[]{:S(2)}, u32[]{:S(2)}) collective-permute-start(bf16[1024,128]{1,0:T(8,128)(2,1)S(1)} %fusion.2), channel_id=1, source_target_pairs={{0,2},{1,3},{2,0},{3,1},{4,6},{5,7},{6,4},{7,5},{8,10},{9,11},{10,... | collective-permute-start | bytes 786440 | tf_op jit(solution)/shard_map/ppermute | solution.py:288
  141.6 8.4 %collective-permute-start.40 = (bf16[1024,128]{1,0:T(8,128)(2,1)S(1)}, bf16[1024,128]{1,0:T(8,128)(2,1)S(1)}, u32[]{:S(2)}, u32[]{:S(2)}) collective-permute-start(bf16[1024,128]{1,0:T(8,128)(2,1)S(1)} %add_convert_fusion.refs_10_), channel_id=1, source_target_pairs={{4,0},{8,4},{12,8},{16,12},{20,16},{24,20},{28,24},{0,28},{5,1},{9... | collective-permute-start | bytes 786440 | tf_op jit(solution)/shard_map/ppermute | solution.py:294
  146.1 9.1 %collective-permute-start.39 = (bf16[1024,128]{1,0:T(8,128)(2,1)S(1)}, bf16[1024,128]{1,0:T(8,128)(2,1)S(1)}, u32[]{:S(2)}, u32[]{:S(2)}) collective-permute-start(bf16[1024,128]{1,0:T(8,128)(2,1)S(1)} %add_convert_fusion.refs_10_), channel_id=1, source_target_pairs={{0,4},{4,8},{8,12},{12,16},{16,20},{20,24},{24,28},{28,0},{1,5},{5... | collective-permute-start | bytes 786440 | tf_op jit(solution)/shard_map/ppermute | solution.py:293
  146.1 9.1 %collective-permute-start.38 = (bf16[1024,128]{1,0:T(8,128)(2,1)S(1)}, bf16[1024,128]{1,0:T(8,128)(2,1)S(1)}, u32[]{:S(2)}, u32[]{:S(2)}) collective-permute-start(bf16[1024,128]{1,0:T(8,128)(2,1)S(1)} %add_convert_fusion.refs_10_), channel_id=1, source_target_pairs={{0,2},{1,3},{2,0},{3,1},{4,6},{5,7},{6,4},{7,5},{8,10},{9,11},{10,... | collective-permute-start | bytes 786440 | tf_op jit(solution)/shard_map/ppermute | solution.py:288
  156.7 24.2 %copy-start.9 = (f32[24,256]{1,0:T(8,128)S(1)}, f32[24,256]{1,0:T(8,128)}, u32[]{:S(2)}) copy-start(f32[24,256]{1,0:T(8,128)} %scale_ref.1) | copy-start | bytes 73732
  156.7 2.3 %collective-permute-start.41 = (bf16[1024,256]{1,0:T(8,128)(2,1)}, bf16[1024,256]{1,0:T(8,128)(2,1)}, u32[]{:S(2)}, u32[]{:S(2)}) collective-permute-start(bf16[1024,256]{1,0:T(8,128)(2,1)} %pad_maximum_fusion.1), channel_id=1, source_target_pairs={{0,1},{1,0},{2,3},{3,2},{4,5},{5,4},{6,7},{7,6},{8,9},{9,8},{10,11... | collective-permute-start | bytes 1572872 | tf_op jit(solution)/shard_map/ppermute | solution.py:288
  156.8 9.5 %collective-permute-start.43 = (bf16[1024,128]{1,0:T(8,128)(2,1)}, bf16[1024,128]{1,0:T(8,128)(2,1)}, u32[]{:S(2)}, u32[]{:S(2)}) collective-permute-start(bf16[1024,128]{1,0:T(8,128)(2,1)} %copy-done.5), channel_id=1, source_target_pairs={{0,2},{1,3},{2,0},{3,1},{4,6},{5,7},{6,4},{7,5},{8,10},{9,11},{10,... | collective-permute-start | bytes 786440 | tf_op jit(solution)/shard_map/ppermute | solution.py:288
  157.2 14.2 %collective-permute-start.42 = (bf16[1024,128]{1,0:T(8,128)(2,1)}, bf16[1024,128]{1,0:T(8,128)(2,1)}, u32[]{:S(2)}, u32[]{:S(2)}) collective-permute-start(bf16[1024,128]{1,0:T(8,128)(2,1)} %copy-done.7), channel_id=1, source_target_pairs={{0,2},{1,3},{2,0},{3,1},{4,6},{5,7},{6,4},{7,5},{8,10},{9,11},{10,... | collective-permute-start | bytes 786440 | tf_op jit(solution)/shard_map/ppermute | solution.py:288
  178.5 2.4 %collective-permute-start.44 = (bf16[24,128,128]{2,1,0:T(8,128)(2,1)S(1)}, bf16[24,128,128]{2,1,0:T(8,128)(2,1)S(1)}, u32[]{:S(2)}, u32[]{:S(2)}) collective-permute-start(bf16[24,128,128]{2,1,0:T(8,128)(2,1)S(1)} %get-tuple-element.75), channel_id=1, source_target_pairs={{0,1},{1,0},{2,3},{3,2},{4,5},{5,4},{6,7},{7,6},{8,9},{9,8},{10,11... | collective-permute-start | bytes 2359304 | tf_op jit(solution)/shard_map/ppermute | solution.py:288
  (16 other events, 105.7 us)

commit v6 on v5

--- a/solution.py
+++ b/solution.py
@@ -20,6 +20,42 @@
     return pltpu.CompilerParams(vmem_limit_bytes=mib * MIB)
 
 
+def place_in(array, space):
+    return pltpu.with_memory_space_constraint(array, space)
+
+
+def fetch(copies, semaphores):
+    started = [
+        pltpu.make_async_copy(source, target, semaphores.at[i])
+        for i, (source, target) in enumerate(copies)
+    ]
+    for copy in started:
+        copy.start()
+    return started
+
+
+def load_kernel(source_ref, out_ref, semaphores):
+    rows = source_ref.shape[0] // semaphores.shape[0]
+    places = [pl.ds(i * rows, rows) for i in range(semaphores.shape[0])]
+    for copy in fetch([(source_ref.at[at], out_ref.at[at]) for at in places], semaphores):
+        copy.wait()
+
+
+def load(array):
+    parts = 4 if array.shape[0] % 64 == 0 else 1
+    return pl.pallas_call(
+        load_kernel,
+        out_shape=pltpu.VMEM(array.shape, array.dtype),
+        in_specs=[HBM],
+        out_specs=VMEM,
+        scratch_shapes=[pltpu.SemaphoreType.DMA((parts,))],
+        compiler_params=params(),
+        cost_estimate=pl.CostEstimate(
+            flops=0, bytes_accessed=2 * array.size * array.dtype.itemsize, transcendentals=0
+        ),
+    )(place_in(array, pltpu.HBM))
+
+
 def split_dot(full, other, dims):
     high = full.astype(BF16)
     low = (full - high.astype(F32)).astype(BF16)
@@ -39,12 +75,19 @@
     return jnp.where(points < counts_ref[b], row, 0.0)
 
 
-def integrate_kernel(counts_ref, basis_ref, weights_ref, full_ref, *refs):
-    packed_refs, diagonal = refs[:-1], refs[-1]
+def integrate_kernel(counts_ref, basis_hbm, weights_hbm, full_ref, *refs):
+    packed_refs, (diagonal, basis_ref, weights_ref, semaphores) = refs[:-4], refs[-4:]
     half = full_ref.shape[2] // 2
     row, column = triangle(half)
-    start = 0
-    for packed_ref, nbatch in zip(packed_refs, groups(full_ref.shape[0])):
+    sizes = groups(full_ref.shape[0])
+    starts = [sum(sizes[:i]) for i in range(len(sizes))]
+    copies = [(weights_hbm, weights_ref)]
+    for start, size in zip(starts, sizes):
+        copies.append((basis_hbm.at[pl.ds(start, size)], basis_ref.at[pl.ds(start, size)]))
+    weights_copy, *basis_copies = fetch(copies, semaphores)
+    weights_copy.wait()
+    for copy, packed_ref, start, size in zip(basis_copies, packed_refs, starts, sizes):
+        copy.wait()
         diagonal[...] = jnp.zeros_like(diagonal)
 
         def step(b, carry, start=start, packed_ref=packed_ref):
@@ -60,9 +103,9 @@
             diagonal[pl.ds(b, 1), :] = jnp.concatenate([line, jnp.zeros_like(line)], axis=1)
             return carry
 
-        lax.fori_loop(0, nbatch, step, 0, unroll=4)
-        packed_ref[nbatch * half :, :] = diagonal[: packed_ref.shape[0] - nbatch * half].astype(BF16)
-        start += nbatch
+        lax.fori_loop(0, size, step, 0, unroll=4)
+        tail = packed_ref.shape[0] - size * half
+        packed_ref[size * half :, :] = diagonal[:tail].astype(BF16)
 
 
 def groups(nbatch):
@@ -76,21 +119,27 @@
 
 def integrate(basis_values, counts, weights):
     nbatch, points, columns = basis_values.shape
-    rows = [count * columns // 2 + padded_rows(count) for count in groups(nbatch)]
+    sizes = groups(nbatch)
+    rows = [size * columns // 2 + padded_rows(size) for size in sizes]
     return pl.pallas_call(
         integrate_kernel,
-        out_shape=[jax.ShapeDtypeStruct((nbatch, columns, columns), BF16)]
+        out_shape=[pltpu.VMEM((nbatch, columns, columns), BF16)]
         + [jax.ShapeDtypeStruct((row, columns), BF16) for row in rows],
-        in_specs=[SMEM, VMEM, VMEM],
+        in_specs=[SMEM, HBM, HBM],
         out_specs=[VMEM] * (1 + len(rows)),
-        scratch_shapes=[pltpu.VMEM((padded_rows(groups(nbatch)[0]), columns), F32)],
+        scratch_shapes=[
+            pltpu.VMEM((padded_rows(sizes[0]), columns), F32),
+            pltpu.VMEM(basis_values.shape, BF16),
+            pltpu.VMEM(weights.shape, F32),
+            pltpu.SemaphoreType.DMA((1 + len(sizes),)),
+        ],
         compiler_params=params(),
         cost_estimate=pl.CostEstimate(
             flops=4 * nbatch * points * columns * columns,
             bytes_accessed=nbatch * columns * (points * 2 + columns * 3),
             transcendentals=0,
         ),
-    )(counts, basis_values, weights)
+    )(counts, place_in(basis_values, pltpu.HBM), place_in(weights, pltpu.HBM))
 
 
 def unpack_kernel(packed_ref, full_ref, diagonal):
@@ -130,17 +179,6 @@
     )(packed)
 
 
-def fetch(copies, semaphores):
-    started = [
-        pltpu.make_async_copy(source, target, semaphores.at[i])
-        for i, (source, target) in enumerate(copies)
-    ]
-    for copy in started:
-        copy.start()
-    for copy in started:
-        copy.wait()
-
-
 def row_places(block_ref, b, rows):
     return [
         pl.ds(pl.multiple_of(block_ref[b, j] * rows, rows), rows) for j in range(block_ref.shape[1])
@@ -161,10 +199,10 @@
     def steps(members, count):
         def step(b, carry):
             places, products = [], []
-            for p in members:
-                place = row_places(block_refs[p], starts[p] + b, rows)
+            for p, first in members:
+                place = row_places(block_refs[p], starts[p] + first + b, rows)
                 picked = jnp.concatenate([window[at, :] for at in place], axis=0)
-                products.append(jnp.dot(ham_refs[p][b], picked, preferred_element_type=F32))
+                products.append(jnp.dot(ham_refs[p][first + b], picked, preferred_element_type=F32))
                 places.append(place)
             for place, product in zip(places, products):
                 for j, at in enumerate(place):
@@ -173,9 +211,14 @@
 
         lax.fori_loop(0, count, step, 0, unroll=2)
 
-    counts = [ref.shape[0] for ref in ham_refs]
-    for count in sorted(set(counts)):
-        steps([p for p in range(pieces) if counts[p] == count], count)
+    shares = {}
+    smallest = min(ref.shape[0] for ref in ham_refs)
+    for p, ref in enumerate(ham_refs):
+        for first in range(0, ref.shape[0], smallest):
+            count = min(smallest, ref.shape[0] - first)
+            shares.setdefault(count, []).append((p, first))
+    for count, members in shares.items():
+        steps(members, count)
     out_before[...] = total[:region].astype(BF16)
     out_own[...] = total[region : 2 * region]
     out_after[...] = total[2 * region :].astype(BF16)
@@ -205,21 +248,18 @@
             bytes_accessed=work * columns * columns * 2 + 14 * region * width,
             transcendentals=0,
         ),
-    )(*blocks, *hams, before, own, after)
+    )(*blocks, *[place_in(array, pltpu.VMEM) for array in (*hams, before, own, after)])
 
 
 def overlap_kernel(pieces, rows, *refs):
     block_refs = refs[:pieces]
     sources = refs[pieces : pieces + 12]
     out_refs = refs[pieces + 12 : 2 * pieces + 12]
-    occ, resp, semaphores = refs[2 * pieces + 12 :]
+    occ, resp = refs[2 * pieces + 12 :]
     region, width = sources[0].shape
-    copies = []
     for i, source in enumerate(sources):
         target, side, part = (occ, resp)[i // 6], i % 6 // 2, i % 2
-        place = (pl.ds(side * region, region), pl.ds(part * width, width))
-        copies.append((source, target.at[place]))
-    fetch(copies, semaphores)
+        target[side * region : (side + 1) * region, part * width : (part + 1) * width] = source[...]
 
     def step(b, carry):
         for p in range(pieces):
@@ -239,21 +279,17 @@
     region, width = occ_parts[0].shape
     return pl.pallas_call(
         functools.partial(overlap_kernel, pieces, columns // per_batch),
-        out_shape=[jax.ShapeDtypeStruct((nbatch, columns, columns), kind) for kind in types],
-        in_specs=[SMEM] * pieces + [HBM] * 12,
+        out_shape=[pltpu.VMEM((nbatch, columns, columns), kind) for kind in types],
+        in_specs=[SMEM] * pieces + [VMEM] * 12,
         out_specs=[VMEM] * pieces,
-        scratch_shapes=[
-            pltpu.VMEM((3 * region, 2 * width), BF16),
-            pltpu.VMEM((3 * region, 2 * width), BF16),
-            pltpu.SemaphoreType.DMA((12,)),
-        ],
+        scratch_shapes=[pltpu.VMEM((3 * region, 2 * width), BF16)] * 2,
         compiler_params=params(),
         cost_estimate=pl.CostEstimate(
             flops=4 * pieces * nbatch * columns * columns * width,
             bytes_accessed=24 * region * width + pieces * nbatch * columns * columns * 3,
             transcendentals=0,
         ),
-    )(*blocks, *occ_parts, *resp_parts)
+    )(*blocks, *[place_in(array, pltpu.VMEM) for array in (*occ_parts, *resp_parts)])
 
 
 def density_kernel(counts_ref, basis_ref, first_ref, second_ref, scale_ref, out_ref):
@@ -300,17 +336,17 @@
 
 
 def trade(array, rows, choice):
-    keep = lax.dynamic_slice_in_dim(array, choice * rows, rows, 0)
-    return keep, lax.dynamic_slice_in_dim(array, (1 - choice) * rows, rows, 0).astype(BF16)
+    keep = lax.dynamic_slice_in_dim(array, choice * rows, rows, 1)
+    return keep, lax.dynamic_slice_in_dim(array, (1 - choice) * rows, rows, 1).astype(BF16)
 
 
 def join(own, other, choice):
     low, high = jnp.where(choice == 0, own, other), jnp.where(choice == 0, other, own)
-    return jnp.concatenate([low, high], axis=0)
+    return jnp.concatenate([low, high], axis=1)
 
 
 def halve(part, order):
-    half = part.shape[0] // 2
+    half = part.shape[1] // 2
     keep, send = trade(part, half, (lax.axis_index("grid") >> order) & 1)
     return keep, flip(send, "grid", 1 << order)
 
@@ -318,10 +354,10 @@
 def rotate(part, level, energy, order, halved):
     if lax.axis_size("grid") != 8:
         total = lax.psum(part, "grid")
-        return (total / (level[:, None] - energy[None, :])).astype(BF16)
+        return (total / (level[None, :, None] - energy[:, None, :])).astype(BF16)
     grid = lax.axis_index("grid")
     first, second = (grid >> order) & 1, (grid >> (1 - order)) & 1
-    half = part.shape[0] // 2
+    half = part.shape[1] // 2
     quarter = half // 2
     keep, coming = halved
     total = keep + coming.astype(F32)
@@ -329,7 +365,7 @@
     total = keep + flip(send, "grid", 2 >> order).astype(F32)
     total = total + flip(total.astype(BF16), "grid", 4).astype(F32)
     level = lax.dynamic_slice_in_dim(level, first * half + second * quarter, quarter, 0)
-    own = (total / (level[:, None] - energy[None, :])).astype(BF16)
+    own = (total / (level[None, :, None] - energy[:, None, :])).astype(BF16)
     own = join(own, flip(own, "grid", 2 >> order), second)
     return join(own, flip(own, "grid", 1 << order), first)
 
@@ -369,8 +405,8 @@
         hams += [far, flip(far, "tile", 1)]
         places, starts, start = places + lists[2:], starts + [start] * 2, start + count
     blocks_near = lists[1]
-    virt_near = flip(virt_coef, "tile", 1)
-    energies = [virt_energy, flip(virt_energy, "tile", 1)]
+    virtuals = [load(virt_coef), load(flip(virt_coef, "tile", 1))]
+    energies = jnp.stack([virt_energy, flip(virt_energy, "tile", 1)])
 
     to_before, own_sum, to_after = apply_window(
         places,
@@ -384,41 +420,42 @@
         lax.dynamic_slice_in_dim(occ_energy, place * width, width, 0)
         for place in (quarter, quarter ^ 1)
     ]
-    own_sum, energies, levels = lax.optimization_barrier((own_sum, energies, levels))
+    own_sum, energies, levels, virtuals = lax.optimization_barrier(
+        (own_sum, energies, levels, virtuals)
+    )
     size = lax.axis_size("grid")
     from_before = lax.ppermute(to_after, "grid", [(i, (i + 1) % size) for i in range(size)])
     from_after = lax.ppermute(to_before, "grid", [((i + 1) % size, i) for i in range(size)])
     ham_own = (own_sum + from_before.astype(F32) + from_after.astype(F32)).astype(BF16)
-    ham_sums = [ham_own, flip(ham_own, "tile", 2)]
-
-    virtuals = [virt_coef, virt_near]
-    parts, halved, (ham_own, ham_far) = [], [], ham_sums
-    for side in range(2):
-        if side == 1:
-            ham_far, parts, halved = lax.optimization_barrier((ham_far, parts, halved))
-        for order, virt in enumerate(virtuals):
-            ham_sum = (ham_own, ham_far)[side]
-            part = lax.dot_general(
-                ham_sum, virt, (((0,), (0,)), ((), ())), preferred_element_type=F32
-            )
-            parts.append(part)
-            halved.append(halve(part, order))
+
+    parts, halved = [], []
+    for order, ham_sum in enumerate((ham_own, ham_own)):
+        if order == 1:
+            ham_sum, parts = lax.optimization_barrier((ham_sum, parts))
+            ham_sum = flip(ham_sum, "tile", 2)
+        products = [
+            lax.dot_general(ham_sum, virt, (((0,), (0,)), ((), ())), preferred_element_type=F32)
+            for virt in virtuals
+        ]
+        parts.append(jnp.stack(products))
+        halved.append(halve(parts[order], order))
+
     occ_far = column_part(occ_coef, quarter ^ 1, width)
-    late_before, late_after, _ = lax.optimization_barrier((occ_before, occ_after, parts[3]))
+    late_before, late_after, _ = lax.optimization_barrier((occ_before, occ_after, parts[1]))
     before_far, after_far = flip(late_before, "tile", 2), flip(late_after, "tile", 2)
 
     rotated = [
-        rotate(part, levels[i // 2], energies[i % 2], i % 2, halved[i])
-        for i, part in enumerate(parts)
+        rotate(part, levels[order], energies, order, halved[order])
+        for order, part in enumerate(parts)
     ]
     rotated[0], before_far, after_far = lax.optimization_barrier(
         (rotated[0], before_far, after_far)
     )
     coefs = []
-    for i in range(2):
+    for rotation in rotated:
         terms = [
-            lax.dot_general(virt, rotation, NT, preferred_element_type=F32)
-            for virt, rotation in zip(virtuals, rotated[2 * i : 2 * i + 2])
+            lax.dot_general(virt, rotation[i], NT, preferred_element_type=F32)
+            for i, virt in enumerate(virtuals)
         ]
         coefs.append(terms[0] + terms[1])
     coef_own, coef_far = lax.optimization_barrier(

time: 185 us -> 176 us (0.951)
  matrix products: 18.3 us -> 7.68 us
  starting transfers between devices: 48.3 us -> 41.5 us
  other arithmetic: 5.77 us -> 9.87 us
  Pallas kernels: 19.1 us -> 22 us
    ppermute x39 -> x29, waiting for transfers between devices: 60.1 us -> 69.3 us  [flip(): lax.ppermute(array, axis, [(i, i ^ mask) for i in range(lax.axis_size(axi...]
    ppermute x39 -> x29, starting transfers between devices: 34.3 us -> 26.8 us  [flip(): lax.ppermute(array, axis, [(i, i ^ mask) for i in range(lax.axis_size(axi...]
    dot_general x4, matrix products: 9.31 us -> 2.98 us  [per_device(): lax.dot_general(ham_sum, virt, (((0,), (0,)), ((), ())), preferred_elemen...]
    ppermute x1, waiting for transfers between devices: 6.88 us -> 1.2 us  [per_device(): lax.ppermute(to_after, 'grid', [(i, (i + 1) % size) for i in range(size)])]
    pallas_call x1 -> x3, Pallas kernels: 3.5 us -> 8.98 us  [the longest x1 4.68 us: integrate(): pl.pallas_call(integrate_kernel, out_shape=[pltpu.VMEM((nbatch, columns,...]
    dot_general x4, matrix products: 8.94 us -> 4.71 us  [per_device(): lax.dot_general(virt, rotation[i], NT, preferred_element_type=F32)]
    ppermute x2, starting transfers between devices: 0.01 us -> 2.88 us  [neighbours(): lax.ppermute(array, 'grid', [(i, (i + 1) % size) for i in range(size)])]
    ppermute x2, waiting for transfers between devices: 8.81 us -> 6.19 us  [neighbours(): lax.ppermute(array, 'grid', [(i, (i + 1) % size) for i in range(size)])]
  transfers between devices with their start and end apart: 45 -> 35, of which waited for: 28 -> 24; matrix products, arithmetic and copies ran while one was open for 12% -> 10% of each run, Pallas kernels for 6% -> 9%
where the time goes in v6:
time: 176 us; the launch traced here: 175 us
  waiting for transfers between devices  83 us (47%)
  starting transfers between devices  41.5 us (24%)
  Pallas kernels  22 us (12%)
  local copies, waits for them, and re-layouts  10 us (6%)
  other arithmetic  9.87 us (6%)
  matrix products  7.68 us (4%)
    ppermute x29, waiting for transfers between devices, flip(): lax.ppermute(array, axis, [(i, i ^ mask) for i in range(lax.axis_size(axi...  69.3 us
    ppermute x29, starting transfers between devices, flip(): lax.ppermute(array, axis, [(i, i ^ mask) for i in range(lax.axis_size(axi...  26.8 us
    unnamed x45, local copies, waits for them, and re-layouts  7.76 us
    ppermute x2, starting transfers between devices, neighbours(): lax.ppermute(array, 'grid', [((i + 1) % size, i) for i in range(size)])  7.01 us
    ppermute x2, waiting for transfers between devices, neighbours(): lax.ppermute(array, 'grid', [(i, (i + 1) % size) for i in range(size)])  6.19 us
    pallas_call x1, Pallas kernels, apply_window(): pl.pallas_call(functools.partial(apply_kernel, starts, columns // per_bat...  4.75 us
    dot_general x4, matrix products, per_device(): lax.dot_general(virt, rotation[i], NT, preferred_element_type=F32)  4.71 us
    pallas_call x1, Pallas kernels, integrate(): pl.pallas_call(integrate_kernel, out_shape=[pltpu.VMEM((nbatch, columns,...  4.68 us
  transfers between devices with their start and end apart: 35, of which 24 were waited for; matrix products, arithmetic and copies ran while one was open for 10% of the time, Pallas kernels for 9%

profile of v6, /device:TPU:0, one launch (start us, length us, event | category | flops | bytes accessed | tf_op | source)
XLA Modules:
  0.0 175.2 jit_solution(14096706277054435338)
XLA Ops:
  2.0 2.9 %collective-permute-start.1 = (s32[24,2]{1,0:T(8,128)S(1)}, s32[24,2]{1,0:T(8,128)S(1)}, u32[]{:S(2)}, u32[]{:S(2)}) collective-permute-start(s32[24,2]{1,0:T(8,128)S(1)} %copy.11), channel_id=1, source_target_pairs={{0,2},{1,3},{2,0},{3,1},{4,6},{5,7},{6,4},{7,5},{8,10},{9,11},{10,... | collective-permute-start | bytes 584 | tf_op jit(solution)/shard_map/ppermute | solution.py:324
  5.6 4.7 %shard_map.104 = (bf16[24,128,128]{2,1,0:T(8,128)(2,1)S(1)}, bf16[800,128]{1,0:T(8,128)(2,1)S(1)}, bf16[800,128]{1,0:T(8,128)(2,1)S(1)}) custom-call(s32[24]{0:T(128)S(1)} %copy-done.15, bf16[24,256,128]{2,1,0:T(8,128)(2,1)} %basis_ref.1, f32[24,256]{1,0:T(8,128)} %weights_hbm.1), custom_call_target="tpu_custom_call" | custom-call | flops 402653184 | bytes 2752512 | tf_op jit(solution)/shard_map/pallas_call | solution.py:124
  11.6 2.1 %collective-permute-start.7 = (bf16[1024,128]{1,0:T(8,128)(2,1)S(1)}, bf16[1024,128]{1,0:T(8,128)(2,1)S(1)}, u32[]{:S(2)}, u32[]{:S(2)}) collective-permute-start(bf16[1024,128]{1,0:T(8,128)(2,1)S(1)} %get-tuple-element.43.refs_13_.refs_4_), channel_id=1, source_target_pairs={{0,4},{4,8},{8,12},{12,16},{16,20},{20,24},{24,28},{28,0},{1,5},{5... | collective-permute-start | bytes 786440 | tf_op jit(solution)/shard_map/ppermute | solution.py:329
  13.6 3.1 %collective-permute-start.8 = (bf16[1024,128]{1,0:T(8,128)(2,1)S(1)}, bf16[1024,128]{1,0:T(8,128)(2,1)S(1)}, u32[]{:S(2)}, u32[]{:S(2)}) collective-permute-start(bf16[1024,128]{1,0:T(8,128)(2,1)S(1)} %get-tuple-element.43.refs_13_.refs_4_), channel_id=1, source_target_pairs={{4,0},{8,4},{12,8},{16,12},{20,16},{24,20},{28,24},{0,28},{5,1},{9... | collective-permute-start | bytes 786440 | tf_op jit(solution)/shard_map/ppermute | solution.py:330
  17.1 1.3 collective-permute-start.6
  19.2 4.6 %collective-permute-done.6.packed_ref = bf16[800,128]{1,0:T(8,128)(2,1)S(1)} collective-permute-done((bf16[800,128]{1,0:T(8,128)(2,1)S(1)}, bf16[800,128]{1,0:T(8,128)(2,1)S(1)}, u32[]{:S(2)}, u32[]{:S(2)}) %collective-permute-start.6) | collective-permute-done | bytes 204832 | tf_op jit(solution)/shard_map/ppermute | solution.py:324
  23.8 1.6 collective-permute-done.7.refs_12_.refs_2_
  25.4 2.2 %collective-permute-done.8.refs_14_.refs_6_ = bf16[1024,128]{1,0:T(8,128)(2,1)S(1)} collective-permute-done((bf16[1024,128]{1,0:T(8,128)(2,1)S(1)}, bf16[1024,128]{1,0:T(8,128)(2,1)S(1)}, u32[]{:S(2)}, u32[]{:S(2)}) %collective-permute-start.8) | collective-permute-done | bytes 262176 | tf_op jit(solution)/shard_map/ppermute | solution.py:330
  30.4 4.7 %shard_map.107 = (bf16[1024,128]{1,0:T(8,128)(2,1)S(1)}, f32[1024,128]{1,0:T(8,128)S(1)}, bf16[1024,128]{1,0:T(8,128)(2,1)}) custom-call(s32[24,2]{1,0:T(8,128)S(1)} %copy.13.refs_0_, s32[24,2]{1,0:T(8,128)S(1)} %collective-permute-done.refs_1_, s32[24,2]{1,0:T(8,128)S(1)} %collective-permute-done.1.refs_2_.refs_4_, ...), custom_call_target="tpu_custom_call" | custom-call | flops 402653184 | bytes 4980736 | tf_op jit(solution)/shard_map/pallas_call | solution.py:232
  35.5 4.4 %collective-permute-start.13 = (bf16[1024,128]{1,0:T(8,128)(2,1)S(1)}, bf16[1024,128]{1,0:T(8,128)(2,1)S(1)}, u32[]{:S(2)}, u32[]{:S(2)}) collective-permute-start(bf16[1024,128]{1,0:T(8,128)(2,1)S(1)} %get-tuple-element.51), channel_id=1, source_target_pairs={{4,0},{8,4},{12,8},{16,12},{20,16},{24,20},{28,24},{0,28},{5,1},{9... | collective-permute-start | bytes 786440 | tf_op jit(solution)/shard_map/ppermute | solution.py:428
  40.0 2.1 %shard_map.108 = bf16[1024,1920]{1,0:T(8,128)(2,1)S(1)} custom-call(bf16[1024,1920]{1,0:T(8,128)(2,1)} %source_ref.1), custom_call_target="tpu_custom_call" | custom-call | bytes 7864320 | tf_op jit(solution)/shard_map/pallas_call | solution.py:46
  42.1 1.9 %copy-done.2 = bf16[1024,1920]{1,0:T(8,128)(2,1)} copy-done((bf16[1024,1920]{1,0:T(8,128)(2,1)}, bf16[1024,1920]{1,0:T(8,128)(2,1)S(1)}, u32[]{:S(2)}) %copy-start.2) | copy-done | bytes 3932184
  44.1 2.2 %shard_map.109 = bf16[1024,1920]{1,0:T(8,128)(2,1)S(1)} custom-call(bf16[1024,1920]{1,0:T(8,128)(2,1)} %collective-permute-done.11.source_ref), custom_call_target="tpu_custom_call" | custom-call | bytes 7864320 | tf_op jit(solution)/shard_map/pallas_call | solution.py:46
  46.3 1.2 collective-permute-done.12
  47.5 2.6 %collective-permute-done.13 = bf16[1024,128]{1,0:T(8,128)(2,1)S(1)} collective-permute-done((bf16[1024,128]{1,0:T(8,128)(2,1)S(1)}, bf16[1024,128]{1,0:T(8,128)(2,1)S(1)}, u32[]{:S(2)}, u32[]{:S(2)}) %collective-permute-start.13) | collective-permute-done | bytes 262176 | tf_op jit(solution)/shard_map/ppermute | solution.py:428
  50.9 1.6 collective-permute-start.19
  53.4 5.4 %collective-permute-done.19 = bf16[1024,128]{1,0:T(8,128)(2,1)S(1)} collective-permute-done((bf16[1024,128]{1,0:T(8,128)(2,1)S(1)}, bf16[1024,128]{1,0:T(8,128)(2,1)S(1)}, u32[]{:S(2)}, u32[]{:S(2)}) %collective-permute-start.19) | collective-permute-done | bytes 262176 | tf_op jit(solution)/shard_map/ppermute | solution.py:324
  60.3 2.0 %collective-permute-start.22 = (bf16[2,64,1920]{2,1,0:T(8,128)(2,1)S(1)}, bf16[2,64,1920]{2,1,0:T(8,128)(2,1)S(1)}, u32[]{:S(2)}, u32[]{:S(2)}) collective-permute-start(bf16[2,64,1920]{2,1,0:T(8,128)(2,1)S(1)} %fusion.4), channel_id=1, source_target_pairs={{0,8},{4,12},{8,0},{12,4},{16,24},{20,28},{24,16},{28,20},{1,9},{5... | collective-permute-start | bytes 1474568 | tf_op jit(solution)/shard_map/ppermute | solution.py:324
  62.3 3.5 %collective-permute-done.14 = bf16[2,64,1920]{2,1,0:T(8,128)(2,1)S(1)} collective-permute-done((bf16[2,64,1920]{2,1,0:T(8,128)(2,1)S(1)}, bf16[2,64,1920]{2,1,0:T(8,128)(2,1)S(1)}, u32[]{:S(2)}, u32[]{:S(2)}) %collective-permute-start.14) | collective-permute-done | bytes 491552 | tf_op jit(solution)/shard_map/ppermute | solution.py:324
  65.9 2.0 %collective-permute-start.15 = (bf16[2,32,1920]{2,1,0:T(8,128)(2,1)S(1)}, bf16[2,32,1920]{2,1,0:T(8,128)(2,1)S(1)}, u32[]{:S(2)}, u32[]{:S(2)}) collective-permute-start(bf16[2,32,1920]{2,1,0:T(8,128)(2,1)S(1)} %dynamic-slice_convert_fusion.1), channel_id=1, source_target_pairs={{0,8},{4,12},{8,0},{12,4},{16,24},{20,28},{24,16},{28,20},{1,9},{5... | collective-permute-start | bytes 737288 | tf_op jit(solution)/shard_map/ppermute | solution.py:324
  67.9 6.7 %collective-permute-done.22 = bf16[2,64,1920]{2,1,0:T(8,128)(2,1)S(1)} collective-permute-done((bf16[2,64,1920]{2,1,0:T(8,128)(2,1)S(1)}, bf16[2,64,1920]{2,1,0:T(8,128)(2,1)S(1)}, u32[]{:S(2)}, u32[]{:S(2)}) %collective-permute-start.22) | collective-permute-done | bytes 491552 | tf_op jit(solution)/shard_map/ppermute | solution.py:324
  74.7 3.2 %collective-permute-done.15 = bf16[2,32,1920]{2,1,0:T(8,128)(2,1)S(1)} collective-permute-done((bf16[2,32,1920]{2,1,0:T(8,128)(2,1)S(1)}, bf16[2,32,1920]{2,1,0:T(8,128)(2,1)S(1)}, u32[]{:S(2)}, u32[]{:S(2)}) %collective-permute-start.15) | collective-permute-done | bytes 245792 | tf_op jit(solution)/shard_map/ppermute | solution.py:324
  78.7 2.8 %collective-permute-start.16 = (bf16[2,32,1920]{2,1,0:T(8,128)(2,1)}, bf16[2,32,1920]{2,1,0:T(8,128)(2,1)}, u32[]{:S(2)}, u32[]{:S(2)}) collective-permute-start(bf16[2,32,1920]{2,1,0:T(8,128)(2,1)} %fusion.21), channel_id=1, source_target_pairs={{0,16},{4,20},{8,24},{12,28},{16,0},{20,4},{24,8},{28,12},{1,17},{... | collective-permute-start | bytes 737288 | tf_op jit(solution)/shard_map/ppermute | solution.py:324
  82.2 2.4 %collective-permute-start.24 = (bf16[2,32,1920]{2,1,0:T(8,128)(2,1)}, bf16[2,32,1920]{2,1,0:T(8,128)(2,1)}, u32[]{:S(2)}, u32[]{:S(2)}) collective-permute-start(bf16[2,32,1920]{2,1,0:T(8,128)(2,1)} %fusion.22), channel_id=1, source_target_pairs={{0,16},{4,20},{8,24},{12,28},{16,0},{20,4},{24,8},{28,12},{1,17},{... | collective-permute-start | bytes 737288 | tf_op jit(solution)/shard_map/ppermute | solution.py:324
  84.8 13.0 %collective-permute-done.16 = bf16[2,32,1920]{2,1,0:T(8,128)(2,1)} collective-permute-done((bf16[2,32,1920]{2,1,0:T(8,128)(2,1)}, bf16[2,32,1920]{2,1,0:T(8,128)(2,1)}, u32[]{:S(2)}, u32[]{:S(2)}) %collective-permute-start.16) | collective-permute-done | bytes 245792 | tf_op jit(solution)/shard_map/ppermute | solution.py:324
  97.8 4.1 %collective-permute-done.24 = bf16[2,32,1920]{2,1,0:T(8,128)(2,1)} collective-permute-done((bf16[2,32,1920]{2,1,0:T(8,128)(2,1)}, bf16[2,32,1920]{2,1,0:T(8,128)(2,1)}, u32[]{:S(2)}, u32[]{:S(2)}) %collective-permute-start.24) | collective-permute-done | bytes 245792 | tf_op jit(solution)/shard_map/ppermute | solution.py:324
  101.9 2.1 %divide_convert_fusion = (bf16[2,32,1920]{2,1,0:T(8,128)(2,1)}, bf16[2,32,1920]{2,1,0:T(8,128)(2,1)}) fusion(bf16[2,32,1920]{2,1,0:T(8,128)(2,1)} %collective-permute-done.24, bf16[2,32,1920]{2,1,0:T(8,128)(2,1)S(1)} %collective-permute-done.23, f32[2,64,1920]{2,1,0:T(8,128)S(1)} %fusion.2, s32[]{:T(128)S(6)} %select_n.138, f32[32]{0:T(128)S(1)} %dynamic_slice.54, ...), kind=kLoop, calls=%fused_computation.45 | loop fusion | flops 1720320 | bytes 2473224 | tf_op jit(solution)/shard_map/convert_element_type | solution.py:368
  104.0 1.5 collective-permute-start.20
  106.1 5.0 %collective-permute-done.25 = bf16[2,32,1920]{2,1,0:T(8,128)(2,1)S(1)} collective-permute-done((bf16[2,32,1920]{2,1,0:T(8,128)(2,1)}, bf16[2,32,1920]{2,1,0:T(8,128)(2,1)S(1)}, u32[]{:S(2)}, u32[]{:S(2)}) %collective-permute-start.25) | collective-permute-done | bytes 245792 | tf_op jit(solution)/shard_map/ppermute | solution.py:324
  113.6 3.1 %collective-permute-start.18 = (bf16[2,64,1920]{2,1,0:T(8,128)(2,1)S(1)}, bf16[2,64,1920]{2,1,0:T(8,128)(2,1)S(1)}, u32[]{:S(2)}, u32[]{:S(2)}) collective-permute-start(bf16[2,64,1920]{2,1,0:T(8,128)(2,1)S(1)} %pad_maximum_fusion.6), channel_id=1, source_target_pairs={{0,4},{4,0},{8,12},{12,8},{16,20},{20,16},{24,28},{28,24},{1,5},{5... | collective-permute-start | bytes 1474568 | tf_op jit(solution)/shard_map/ppermute | solution.py:324
  116.7 6.7 %collective-permute-done.26 = bf16[2,64,1920]{2,1,0:T(8,128)(2,1)S(1)} collective-permute-done((bf16[2,64,1920]{2,1,0:T(8,128)(2,1)S(1)}, bf16[2,64,1920]{2,1,0:T(8,128)(2,1)S(1)}, u32[]{:S(2)}, u32[]{:S(2)}) %collective-permute-start.26) | collective-permute-done | bytes 491552 | tf_op jit(solution)/shard_map/ppermute | solution.py:324
  123.5 1.2 fusion.13
  125.6 1.2 fusion
  126.8 1.5 collective-permute-start.27
  128.6 1.2 fusion.16
  129.8 1.2 convolution_add_fusion.1
  131.0 3.5 %collective-permute-done.27 = bf16[1024,128]{1,0:T(8,128)(2,1)S(1)} collective-permute-done((bf16[1024,128]{1,0:T(8,128)(2,1)S(1)}, bf16[1024,128]{1,0:T(8,128)(2,1)S(1)}, u32[]{:S(2)}, u32[]{:S(2)}) %collective-permute-start.27) | collective-permute-done | bytes 262176 | tf_op jit(solution)/shard_map/ppermute | solution.py:324
  134.6 1.5 collective-permute-start.28
  136.9 3.9 %collective-permute-start.30 = (bf16[1024,128]{1,0:T(8,128)(2,1)S(1)}, bf16[1024,128]{1,0:T(8,128)(2,1)S(1)}, u32[]{:S(2)}, u32[]{:S(2)}) collective-permute-start(bf16[1024,128]{1,0:T(8,128)(2,1)S(1)} %add_convert_fusion.refs_10_), channel_id=1, source_target_pairs={{4,0},{8,4},{12,8},{16,12},{20,16},{24,20},{28,24},{0,28},{5,1},{9... | collective-permute-start | bytes 786440 | tf_op jit(solution)/shard_map/ppermute | solution.py:330
  141.0 4.6 %collective-permute-done.29.refs_8_ = bf16[1024,128]{1,0:T(8,128)(2,1)S(1)} collective-permute-done((bf16[1024,128]{1,0:T(8,128)(2,1)S(1)}, bf16[1024,128]{1,0:T(8,128)(2,1)S(1)}, u32[]{:S(2)}, u32[]{:S(2)}) %collective-permute-start.29) | collective-permute-done | bytes 262176 | tf_op jit(solution)/shard_map/ppermute | solution.py:329
  145.6 1.6 collective-permute-done.30.refs_12_
  149.3 1.6 collective-permute-start.33
  151.0 1.4 broadcast_select_fusion.1
  153.6 4.7 %collective-permute-done.32.refs_9_ = bf16[1024,128]{1,0:T(8,128)(2,1)} collective-permute-done((bf16[1024,128]{1,0:T(8,128)(2,1)}, bf16[1024,128]{1,0:T(8,128)(2,1)}, u32[]{:S(2)}, u32[]{:S(2)}) %collective-permute-start.32) | collective-permute-done | bytes 262176 | tf_op jit(solution)/shard_map/ppermute | solution.py:324
  158.3 5.2 %collective-permute-done.33.refs_13_ = bf16[1024,128]{1,0:T(8,128)(2,1)} collective-permute-done((bf16[1024,128]{1,0:T(8,128)(2,1)}, bf16[1024,128]{1,0:T(8,128)(2,1)}, u32[]{:S(2)}, u32[]{:S(2)}) %collective-permute-start.33) | collective-permute-done | bytes 262176 | tf_op jit(solution)/shard_map/ppermute | solution.py:324
  166.3 3.4 %shard_map.110 = (f32[24,128,128]{2,1,0:T(8,128)S(1)}, bf16[24,128,128]{2,1,0:T(8,128)(2,1)S(1)}) custom-call(s32[24,2]{1,0:T(8,128)S(1)} %copy.14.refs_0_, s32[24,2]{1,0:T(8,128)S(1)} %collective-permute-done.refs_1_, bf16[1024,128]{1,0:T(8,128)(2,1)S(1)} %collective-permute-done.7.refs_12_.refs_2_, bf16[1024,128]{1,0:T(8,128)(2,1)S(1)} %collective-permute-done.20.refs_3_, ...), custom_call_target="tpu_custom_call" | custom-call | flops 402653184 | bytes 5505024 | tf_op jit(solution)/shard_map/pallas_call | solution.py:280
  169.8 2.3 %collective-permute-done.34.second_ref = bf16[24,128,128]{2,1,0:T(8,128)(2,1)S(1)} collective-permute-done((bf16[24,128,128]{2,1,0:T(8,128)(2,1)S(1)}, bf16[24,128,128]{2,1,0:T(8,128)(2,1)S(1)}, u32[]{:S(2)}, u32[]{:S(2)}) %collective-permute-start.34) | collective-permute-done | bytes 786464 | tf_op jit(solution)/shard_map/ppermute | solution.py:324
  172.0 3.1 %shard_map.111 = f32[24,256]{1,0:T(8,128)} custom-call(s32[24]{0:T(128)S(1)} %copy-done.16, bf16[24,256,128]{2,1,0:T(8,128)(2,1)S(1)} %copy-done.5, f32[24,128,128]{2,1,0:T(8,128)S(1)} %get-tuple-element.68.first_ref, bf16[24,128,128]{2,1,0:T(8,128)(2,1)S(1)} %collective-permute-done.34.second_ref, f32[24,256]{1,0:T(8,128)S(1)} %copy-done.14), custom_call_target="tpu_custom_call" | custom-call | flops 402653184 | bytes 3932160 | tf_op jit(solution)/shard_map/pallas_call | solution.py:309
  (114 shorter events, 24.7 us)
Async XLA Ops:
  0.6 29.6 %copy-start.20 = (f32[1920]{0:T(1024)S(1)}, f32[1920]{0:T(1024)}, u32[]{:S(2)}) copy-start(f32[1920]{0:T(1024)} %param.17) | copy-start | bytes 23044
  0.6 43.4 %collective-permute-start.11 = (bf16[1024,1920]{1,0:T(8,128)(2,1)}, bf16[1024,1920]{1,0:T(8,128)(2,1)}, u32[]{:S(2)}, u32[]{:S(2)}) collective-permute-start(bf16[1024,1920]{1,0:T(8,128)(2,1)} %source_ref.1), channel_id=1, source_target_pairs={{0,1},{1,0},{2,3},{3,2},{4,5},{5,4},{6,7},{7,6},{8,9},{9,8},{10,11... | collective-permute-start | bytes 11796488 | tf_op jit(solution)/shard_map/ppermute | solution.py:324
  1.2 38.8 %copy-start.21 = (f32[512]{0:T(512)S(1)}, f32[512]{0:T(512)}, u32[]{:S(2)}) copy-start(f32[512]{0:T(512)} %param.16) | copy-start | bytes 6148
  1.9 9.5 %collective-permute-start = (s32[24,2]{1,0:T(8,128)S(1)}, s32[24,2]{1,0:T(8,128)S(1)}, u32[]{:S(2)}, u32[]{:S(2)}) collective-permute-start(s32[24,2]{1,0:T(8,128)S(1)} %copy.11), channel_id=1, source_target_pairs={{0,1},{1,0},{2,3},{3,2},{4,5},{5,4},{6,7},{7,6},{8,9},{9,8},{10,11... | collective-permute-start | bytes 584 | tf_op jit(solution)/shard_map/ppermute | solution.py:324
  2.0 9.5 %collective-permute-start.1 = (s32[24,2]{1,0:T(8,128)S(1)}, s32[24,2]{1,0:T(8,128)S(1)}, u32[]{:S(2)}, u32[]{:S(2)}) collective-permute-start(s32[24,2]{1,0:T(8,128)S(1)} %copy.11), channel_id=1, source_target_pairs={{0,2},{1,3},{2,0},{3,1},{4,6},{5,7},{6,4},{7,5},{8,10},{9,11},{10,... | collective-permute-start | bytes 584 | tf_op jit(solution)/shard_map/ppermute | solution.py:324
  10.3 6.8 %collective-permute-start.4 = (bf16[800,128]{1,0:T(8,128)(2,1)S(1)}, bf16[800,128]{1,0:T(8,128)(2,1)S(1)}, u32[]{:S(2)}, u32[]{:S(2)}) collective-permute-start(bf16[800,128]{1,0:T(8,128)(2,1)S(1)} %get-tuple-element.41), channel_id=1, source_target_pairs={{0,2},{1,3},{2,0},{3,1},{4,6},{5,7},{6,4},{7,5},{8,10},{9,11},{10,... | collective-permute-start | bytes 614408 | tf_op jit(solution)/shard_map/ppermute | solution.py:324
  11.5 18.9 %collective-permute-start.3 = (bf16[24,128,128]{2,1,0:T(8,128)(2,1)S(1)}, bf16[24,128,128]{2,1,0:T(8,128)(2,1)}, u32[]{:S(2)}, u32[]{:S(2)}) collective-permute-start(bf16[24,128,128]{2,1,0:T(8,128)(2,1)S(1)} %get-tuple-element.40.refs_6_), channel_id=1, source_target_pairs={{0,1},{1,0},{2,3},{3,2},{4,5},{5,4},{6,7},{7,6},{8,9},{9,8},{10,11... | collective-permute-start | bytes 2359304 | tf_op jit(solution)/shard_map/ppermute | solution.py:324
  11.6 13.8 %collective-permute-start.7 = (bf16[1024,128]{1,0:T(8,128)(2,1)S(1)}, bf16[1024,128]{1,0:T(8,128)(2,1)S(1)}, u32[]{:S(2)}, u32[]{:S(2)}) collective-permute-start(bf16[1024,128]{1,0:T(8,128)(2,1)S(1)} %get-tuple-element.43.refs_13_.refs_4_), channel_id=1, source_target_pairs={{0,4},{4,8},{8,12},{12,16},{16,20},{20,24},{24,28},{28,0},{1,5},{5... | collective-permute-start | bytes 786440 | tf_op jit(solution)/shard_map/ppermute | solution.py:329
  13.6 14.0 %collective-permute-start.8 = (bf16[1024,128]{1,0:T(8,128)(2,1)S(1)}, bf16[1024,128]{1,0:T(8,128)(2,1)S(1)}, u32[]{:S(2)}, u32[]{:S(2)}) collective-permute-start(bf16[1024,128]{1,0:T(8,128)(2,1)S(1)} %get-tuple-element.43.refs_13_.refs_4_), channel_id=1, source_target_pairs={{4,0},{8,4},{12,8},{16,12},{20,16},{24,20},{28,24},{0,28},{5,1},{9... | collective-permute-start | bytes 786440 | tf_op jit(solution)/shard_map/ppermute | solution.py:330
  17.1 6.8 %collective-permute-start.6 = (bf16[800,128]{1,0:T(8,128)(2,1)S(1)}, bf16[800,128]{1,0:T(8,128)(2,1)S(1)}, u32[]{:S(2)}, u32[]{:S(2)}) collective-permute-start(bf16[800,128]{1,0:T(8,128)(2,1)S(1)} %get-tuple-element.42), channel_id=1, source_target_pairs={{0,2},{1,3},{2,0},{3,1},{4,6},{5,7},{6,4},{7,5},{8,10},{9,11},{10,... | collective-permute-start | bytes 614408 | tf_op jit(solution)/shard_map/ppermute | solution.py:324
  23.8 6.6 %collective-permute-start.5 = (bf16[12,128,128]{2,1,0:T(8,128)(2,1)S(1)}, bf16[12,128,128]{2,1,0:T(8,128)(2,1)S(1)}, u32[]{:S(2)}, u32[]{:S(2)}) collective-permute-start(bf16[12,128,128]{2,1,0:T(8,128)(2,1)S(1)} %shard_map.105.refs_8_), channel_id=1, source_target_pairs={{0,1},{1,0},{2,3},{3,2},{4,5},{5,4},{6,7},{7,6},{8,9},{9,8},{10,11... | collective-permute-start | bytes 1179656 | tf_op jit(solution)/shard_map/ppermute | solution.py:324
  28.5 1.9 %collective-permute-start.9 = (bf16[12,128,128]{2,1,0:T(8,128)(2,1)S(1)}, bf16[12,128,128]{2,1,0:T(8,128)(2,1)}, u32[]{:S(2)}, u32[]{:S(2)}) collective-permute-start(bf16[12,128,128]{2,1,0:T(8,128)(2,1)S(1)} %shard_map.106.refs_10_), channel_id=1, source_target_pairs={{0,1},{1,0},{2,3},{3,2},{4,5},{5,4},{6,7},{7,6},{8,9},{9,8},{10,11... | collective-permute-start | bytes 1179656 | tf_op jit(solution)/shard_map/ppermute | solution.py:324
  28.5 1.7 collective-permute-start.2
  30.3 13.7 %collective-permute-start.10 = (f32[1920]{0:T(1024)S(1)}, f32[1920]{0:T(1024)S(1)}, u32[]{:S(2)}, u32[]{:S(2)}) collective-permute-start(f32[1920]{0:T(1024)S(1)} %copy-done.20), channel_id=1, source_target_pairs={{0,1},{1,0},{2,3},{3,2},{4,5},{5,4},{6,7},{7,6},{8,9},{9,8},{10,11... | collective-permute-start | bytes 23048 | tf_op jit(solution)/shard_map/ppermute | solution.py:324
  35.2 7.0 %copy-start.6 = (f32[1024,128]{1,0:T(8,128)}, f32[1024,128]{1,0:T(8,128)S(1)}, u32[]{:S(2)}) copy-start(f32[1024,128]{1,0:T(8,128)S(1)} %get-tuple-element.49) | copy-start | bytes 1572868
  35.2 12.3 %collective-permute-start.12 = (bf16[1024,128]{1,0:T(8,128)(2,1)}, bf16[1024,128]{1,0:T(8,128)(2,1)S(1)}, u32[]{:S(2)}, u32[]{:S(2)}) collective-permute-start(bf16[1024,128]{1,0:T(8,128)(2,1)} %get-tuple-element.50), channel_id=1, source_target_pairs={{0,4},{4,8},{8,12},{12,16},{16,20},{20,24},{24,28},{28,0},{1,5},{5... | collective-permute-start | bytes 786440 | tf_op jit(solution)/shard_map/ppermute | solution.py:427
  35.5 14.6 %collective-permute-start.13 = (bf16[1024,128]{1,0:T(8,128)(2,1)S(1)}, bf16[1024,128]{1,0:T(8,128)(2,1)S(1)}, u32[]{:S(2)}, u32[]{:S(2)}) collective-permute-start(bf16[1024,128]{1,0:T(8,128)(2,1)S(1)} %get-tuple-element.51), channel_id=1, source_target_pairs={{4,0},{8,4},{12,8},{16,12},{20,16},{24,20},{28,24},{0,28},{5,1},{9... | collective-permute-start | bytes 786440 | tf_op jit(solution)/shard_map/ppermute | solution.py:428
  44.1 6.0 %copy-start.7 = (f32[1024,128]{1,0:T(8,128)S(1)}, f32[1024,128]{1,0:T(8,128)}, u32[]{:S(2)}) copy-start(f32[1024,128]{1,0:T(8,128)} %copy-done.6) | copy-start | bytes 1572868
  46.3 12.5 %copy-start = (bf16[1024,1920]{1,0:T(8,128)(2,1)}, bf16[1024,1920]{1,0:T(8,128)(2,1)S(1)}, u32[]{:S(2)}) copy-start(bf16[1024,1920]{1,0:T(8,128)(2,1)S(1)} %shard_map.109) | copy-start | bytes 11796484
  46.3 6.2 %copy-start.3 = (bf16[1024,1920]{1,0:T(8,128)(2,1)S(1)}, bf16[1024,1920]{1,0:T(8,128)(2,1)}, u32[]{:S(2)}) copy-start(bf16[1024,1920]{1,0:T(8,128)(2,1)} %copy-done.2) | copy-start | bytes 11796484
  50.9 7.8 %collective-permute-start.19 = (bf16[1024,128]{1,0:T(8,128)(2,1)S(1)}, bf16[1024,128]{1,0:T(8,128)(2,1)S(1)}, u32[]{:S(2)}, u32[]{:S(2)}) collective-permute-start(bf16[1024,128]{1,0:T(8,128)(2,1)S(1)} %add_convert_fusion.1), channel_id=1, source_target_pairs={{0,2},{1,3},{2,0},{3,1},{4,6},{5,7},{6,4},{7,5},{8,10},{9,11},{10,... | collective-permute-start | bytes 786440 | tf_op jit(solution)/shard_map/ppermute | solution.py:324
  53.3 12.5 %collective-permute-start.14 = (bf16[2,64,1920]{2,1,0:T(8,128)(2,1)S(1)}, bf16[2,64,1920]{2,1,0:T(8,128)(2,1)S(1)}, u32[]{:S(2)}, u32[]{:S(2)}) collective-permute-start(bf16[2,64,1920]{2,1,0:T(8,128)(2,1)S(1)} %fusion.8), channel_id=1, source_target_pairs={{0,4},{4,0},{8,12},{12,8},{16,20},{20,16},{24,28},{28,24},{1,5},{5... | collective-permute-start | bytes 1474568 | tf_op jit(solution)/shard_map/ppermute | solution.py:324
  60.3 14.2 %collective-permute-start.22 = (bf16[2,64,1920]{2,1,0:T(8,128)(2,1)S(1)}, bf16[2,64,1920]{2,1,0:T(8,128)(2,1)S(1)}, u32[]{:S(2)}, u32[]{:S(2)}) collective-permute-start(bf16[2,64,1920]{2,1,0:T(8,128)(2,1)S(1)} %fusion.4), channel_id=1, source_target_pairs={{0,8},{4,12},{8,0},{12,4},{16,24},{20,28},{24,16},{28,20},{1,9},{5... | collective-permute-start | bytes 1474568 | tf_op jit(solution)/shard_map/ppermute | solution.py:324
  65.9 12.1 %collective-permute-start.15 = (bf16[2,32,1920]{2,1,0:T(8,128)(2,1)S(1)}, bf16[2,32,1920]{2,1,0:T(8,128)(2,1)S(1)}, u32[]{:S(2)}, u32[]{:S(2)}) collective-permute-start(bf16[2,32,1920]{2,1,0:T(8,128)(2,1)S(1)} %dynamic-slice_convert_fusion.1), channel_id=1, source_target_pairs={{0,8},{4,12},{8,0},{12,4},{16,24},{20,28},{24,16},{28,20},{1,9},{5... | collective-permute-start | bytes 737288 | tf_op jit(solution)/shard_map/ppermute | solution.py:324
  74.7 6.8 %collective-permute-start.23 = (bf16[2,32,1920]{2,1,0:T(8,128)(2,1)S(1)}, bf16[2,32,1920]{2,1,0:T(8,128)(2,1)S(1)}, u32[]{:S(2)}, u32[]{:S(2)}) collective-permute-start(bf16[2,32,1920]{2,1,0:T(8,128)(2,1)S(1)} %dynamic-slice_convert_fusion), channel_id=1, source_target_pairs={{0,4},{4,0},{8,12},{12,8},{16,20},{20,16},{24,28},{28,24},{1,5},{5... | collective-permute-start | bytes 737288 | tf_op jit(solution)/shard_map/ppermute | solution.py:324
  78.7 19.1 %collective-permute-start.16 = (bf16[2,32,1920]{2,1,0:T(8,128)(2,1)}, bf16[2,32,1920]{2,1,0:T(8,128)(2,1)}, u32[]{:S(2)}, u32[]{:S(2)}) collective-permute-start(bf16[2,32,1920]{2,1,0:T(8,128)(2,1)} %fusion.21), channel_id=1, source_target_pairs={{0,16},{4,20},{8,24},{12,28},{16,0},{20,4},{24,8},{28,12},{1,17},{... | collective-permute-start | bytes 737288 | tf_op jit(solution)/shard_map/ppermute | solution.py:324
  82.2 19.7 %collective-permute-start.24 = (bf16[2,32,1920]{2,1,0:T(8,128)(2,1)}, bf16[2,32,1920]{2,1,0:T(8,128)(2,1)}, u32[]{:S(2)}, u32[]{:S(2)}) collective-permute-start(bf16[2,32,1920]{2,1,0:T(8,128)(2,1)} %fusion.22), channel_id=1, source_target_pairs={{0,16},{4,20},{8,24},{12,28},{16,0},{20,4},{24,8},{28,12},{1,17},{... | collective-permute-start | bytes 737288 | tf_op jit(solution)/shard_map/ppermute | solution.py:324
  104.0 7.0 %collective-permute-start.25 = (bf16[2,32,1920]{2,1,0:T(8,128)(2,1)}, bf16[2,32,1920]{2,1,0:T(8,128)(2,1)S(1)}, u32[]{:S(2)}, u32[]{:S(2)}) collective-permute-start(bf16[2,32,1920]{2,1,0:T(8,128)(2,1)} %get-tuple-element.84), channel_id=1, source_target_pairs={{0,4},{4,0},{8,12},{12,8},{16,20},{20,16},{24,28},{28,24},{1,5},{5... | collective-permute-start | bytes 737288 | tf_op jit(solution)/shard_map/ppermute | solution.py:324
  104.0 19.5 %copy-start.1 = (bf16[1024,1920]{1,0:T(8,128)(2,1)S(1)}, bf16[1024,1920]{1,0:T(8,128)(2,1)}, u32[]{:S(2)}) copy-start(bf16[1024,1920]{1,0:T(8,128)(2,1)} %copy-done) | copy-start | bytes 11796484
  104.0 24.5 %collective-permute-start.20 = (bf16[1024,128]{1,0:T(8,128)(2,1)S(1)}, bf16[1024,128]{1,0:T(8,128)(2,1)S(1)}, u32[]{:S(2)}, u32[]{:S(2)}) collective-permute-start(bf16[1024,128]{1,0:T(8,128)(2,1)S(1)} %collective-permute-done.7.refs_12_.refs_2_), channel_id=1, source_target_pairs={{0,2},{1,3},{2,0},{3,1},{4,6},{5,7},{6,4},{7,5},{8,10},{9,11},{10,... | collective-permute-start | bytes 786440 | tf_op jit(solution)/shard_map/ppermute | solution.py:324
  105.5 23.1 %collective-permute-start.21 = (bf16[1024,128]{1,0:T(8,128)(2,1)S(1)}, bf16[1024,128]{1,0:T(8,128)(2,1)S(1)}, u32[]{:S(2)}, u32[]{:S(2)}) collective-permute-start(bf16[1024,128]{1,0:T(8,128)(2,1)S(1)} %collective-permute-done.8.refs_14_.refs_6_), channel_id=1, source_target_pairs={{0,2},{1,3},{2,0},{3,1},{4,6},{5,7},{6,4},{7,5},{8,10},{9,11},{10,... | collective-permute-start | bytes 786440 | tf_op jit(solution)/shard_map/ppermute | solution.py:324
  106.1 6.5 %collective-permute-start.17 = (bf16[2,32,1920]{2,1,0:T(8,128)(2,1)}, bf16[2,32,1920]{2,1,0:T(8,128)(2,1)S(1)}, u32[]{:S(2)}, u32[]{:S(2)}) collective-permute-start(bf16[2,32,1920]{2,1,0:T(8,128)(2,1)} %get-tuple-element.85), channel_id=1, source_target_pairs={{0,8},{4,12},{8,0},{12,4},{16,24},{20,28},{24,16},{28,20},{1,9},{5... | collective-permute-start | bytes 737288 | tf_op jit(solution)/shard_map/ppermute | solution.py:324
  112.1 11.2 %collective-permute-start.26 = (bf16[2,64,1920]{2,1,0:T(8,128)(2,1)S(1)}, bf16[2,64,1920]{2,1,0:T(8,128)(2,1)S(1)}, u32[]{:S(2)}, u32[]{:S(2)}) collective-permute-start(bf16[2,64,1920]{2,1,0:T(8,128)(2,1)S(1)} %pad_maximum_fusion.7), channel_id=1, source_target_pairs={{0,8},{4,12},{8,0},{12,4},{16,24},{20,28},{24,16},{28,20},{1,9},{5... | collective-permute-start | bytes 1474568 | tf_op jit(solution)/shard_map/ppermute | solution.py:324
  113.6 14.7 %collective-permute-start.18 = (bf16[2,64,1920]{2,1,0:T(8,128)(2,1)S(1)}, bf16[2,64,1920]{2,1,0:T(8,128)(2,1)S(1)}, u32[]{:S(2)}, u32[]{:S(2)}) collective-permute-start(bf16[2,64,1920]{2,1,0:T(8,128)(2,1)S(1)} %pad_maximum_fusion.6), channel_id=1, source_target_pairs={{0,4},{4,0},{8,12},{12,8},{16,20},{20,16},{24,28},{28,24},{1,5},{5... | collective-permute-start | bytes 1474568 | tf_op jit(solution)/shard_map/ppermute | solution.py:324
  123.5 2.1 %copy-start.4 = (bf16[1024,1920]{1,0:T(8,128)(2,1)S(1)}, bf16[1024,1920]{1,0:T(8,128)(2,1)}, u32[]{:S(2)}) copy-start(bf16[1024,1920]{1,0:T(8,128)(2,1)} %copy-done.2) | copy-start | bytes 11796484
  126.8 7.7 %collective-permute-start.27 = (bf16[1024,128]{1,0:T(8,128)(2,1)S(1)}, bf16[1024,128]{1,0:T(8,128)(2,1)S(1)}, u32[]{:S(2)}, u32[]{:S(2)}) collective-permute-start(bf16[1024,128]{1,0:T(8,128)(2,1)S(1)} %fusion), channel_id=1, source_target_pairs={{0,2},{1,3},{2,0},{3,1},{4,6},{5,7},{6,4},{7,5},{8,10},{9,11},{10,... | collective-permute-start | bytes 786440 | tf_op jit(solution)/shard_map/ppermute | solution.py:324
  128.6 2.4 %copy-start.8 = (bf16[1024,128]{1,0:T(8,128)(2,1)}, bf16[1024,128]{1,0:T(8,128)(2,1)S(1)}, u32[]{:S(2)}) copy-start(bf16[1024,128]{1,0:T(8,128)(2,1)S(1)} %collective-permute-done.21.refs_7_) | copy-start | bytes 786436
  131.0 22.5 %copy-start.19 = (s32[24,2]{0,1:T(2,128)S(1)}, s32[24,2]{0,1:T(2,128)}, u32[]{:S(2)}) copy-start(s32[24,2]{0,1:T(2,128)} %param.10) | copy-start | bytes 580
  134.6 6.4 %collective-permute-start.28 = (bf16[1024,128]{1,0:T(8,128)(2,1)S(1)}, bf16[1024,128]{1,0:T(8,128)(2,1)S(1)}, u32[]{:S(2)}, u32[]{:S(2)}) collective-permute-start(bf16[1024,128]{1,0:T(8,128)(2,1)S(1)} %add_convert_fusion.refs_10_), channel_id=1, source_target_pairs={{0,2},{1,3},{2,0},{3,1},{4,6},{5,7},{6,4},{7,5},{8,10},{9,11},{10,... | collective-permute-start | bytes 786440 | tf_op jit(solution)/shard_map/ppermute | solution.py:324
  136.1 9.5 %collective-permute-start.29 = (bf16[1024,128]{1,0:T(8,128)(2,1)S(1)}, bf16[1024,128]{1,0:T(8,128)(2,1)S(1)}, u32[]{:S(2)}, u32[]{:S(2)}) collective-permute-start(bf16[1024,128]{1,0:T(8,128)(2,1)S(1)} %add_convert_fusion.refs_10_), channel_id=1, source_target_pairs={{0,4},{4,8},{8,12},{12,16},{16,20},{20,24},{24,28},{28,0},{1,5},{5... | collective-permute-start | bytes 786440 | tf_op jit(solution)/shard_map/ppermute | solution.py:329
  136.9 10.2 %collective-permute-start.30 = (bf16[1024,128]{1,0:T(8,128)(2,1)S(1)}, bf16[1024,128]{1,0:T(8,128)(2,1)S(1)}, u32[]{:S(2)}, u32[]{:S(2)}) collective-permute-start(bf16[1024,128]{1,0:T(8,128)(2,1)S(1)} %add_convert_fusion.refs_10_), channel_id=1, source_target_pairs={{4,0},{8,4},{12,8},{16,12},{20,16},{24,20},{28,24},{0,28},{5,1},{9... | collective-permute-start | bytes 786440 | tf_op jit(solution)/shard_map/ppermute | solution.py:330
  148.7 23.3 %copy-start.5 = (bf16[24,256,128]{2,1,0:T(8,128)(2,1)S(1)}, bf16[24,256,128]{2,1,0:T(8,128)(2,1)}, u32[]{:S(2)}) copy-start(bf16[24,256,128]{2,1,0:T(8,128)(2,1)} %basis_ref.1) | copy-start | bytes 4718596
  148.7 23.3 %copy-start.14 = (f32[24,256]{1,0:T(8,128)S(1)}, f32[24,256]{1,0:T(8,128)}, u32[]{:S(2)}) copy-start(f32[24,256]{1,0:T(8,128)} %scale_ref.1) | copy-start | bytes 73732
  148.7 23.3 %copy-start.16 = (s32[24]{0:T(128)S(1)}, s32[24]{0:T(128)}, u32[]{:S(2)}) copy-start(s32[24]{0:T(128)} %counts_ref.3) | copy-start | bytes 292
  148.7 2.3 %collective-permute-start.31 = (bf16[1024,256]{1,0:T(8,128)(2,1)}, bf16[1024,256]{1,0:T(8,128)(2,1)}, u32[]{:S(2)}, u32[]{:S(2)}) collective-permute-start(bf16[1024,256]{1,0:T(8,128)(2,1)} %pad_maximum_fusion.4), channel_id=1, source_target_pairs={{0,1},{1,0},{2,3},{3,2},{4,5},{5,4},{6,7},{7,6},{8,9},{9,8},{10,11... | collective-permute-start | bytes 1572872 | tf_op jit(solution)/shard_map/ppermute | solution.py:324
  148.8 9.5 %collective-permute-start.32 = (bf16[1024,128]{1,0:T(8,128)(2,1)}, bf16[1024,128]{1,0:T(8,128)(2,1)}, u32[]{:S(2)}, u32[]{:S(2)}) collective-permute-start(bf16[1024,128]{1,0:T(8,128)(2,1)} %copy-done.10), channel_id=1, source_target_pairs={{0,2},{1,3},{2,0},{3,1},{4,6},{5,7},{6,4},{7,5},{8,10},{9,11},{10,... | collective-permute-start | bytes 786440 | tf_op jit(solution)/shard_map/ppermute | solution.py:324
  149.3 14.1 %collective-permute-start.33 = (bf16[1024,128]{1,0:T(8,128)(2,1)}, bf16[1024,128]{1,0:T(8,128)(2,1)}, u32[]{:S(2)}, u32[]{:S(2)}) collective-permute-start(bf16[1024,128]{1,0:T(8,128)(2,1)} %copy-done.12), channel_id=1, source_target_pairs={{0,2},{1,3},{2,0},{3,1},{4,6},{5,7},{6,4},{7,5},{8,10},{9,11},{10,... | collective-permute-start | bytes 786440 | tf_op jit(solution)/shard_map/ppermute | solution.py:324
  169.7 2.4 %collective-permute-start.34 = (bf16[24,128,128]{2,1,0:T(8,128)(2,1)S(1)}, bf16[24,128,128]{2,1,0:T(8,128)(2,1)S(1)}, u32[]{:S(2)}, u32[]{:S(2)}) collective-permute-start(bf16[24,128,128]{2,1,0:T(8,128)(2,1)S(1)} %get-tuple-element.69), channel_id=1, source_target_pairs={{0,1},{1,0},{2,3},{3,2},{4,5},{5,4},{6,7},{7,6},{8,9},{9,8},{10,11... | collective-permute-start | bytes 2359304 | tf_op jit(solution)/shard_map/ppermute | solution.py:324
  (9 other events, 10.7 us)

commit v7 on v6

--- a/solution.py
+++ b/solution.py
@@ -16,7 +16,7 @@
 NT = (((1,), (1,)), ((), ()))
 
 
-def params(mib=20):
+def params(mib=4):
     return pltpu.CompilerParams(vmem_limit_bytes=mib * MIB)
 
 
@@ -70,42 +70,39 @@
 
 
 def live_row(values_ref, counts_ref, b):
-    row = values_ref[pl.ds(b, 1), :]
+    row = values_ref[b : b + 1, :]
     points = lax.broadcasted_iota(jnp.int32, row.shape, 1)
     return jnp.where(points < counts_ref[b], row, 0.0)
 
 
-def integrate_kernel(counts_ref, basis_hbm, weights_hbm, full_ref, *refs):
-    packed_refs, (diagonal, basis_ref, weights_ref, semaphores) = refs[:-4], refs[-4:]
+def integrate_kernel(start, counts_hbm, basis_hbm, weights_hbm, full_ref, packed_ref, *scratch):
+    diagonal, basis_ref, weights_ref, counts_ref, semaphores = scratch
+    size = full_ref.shape[0]
     half = full_ref.shape[2] // 2
     row, column = triangle(half)
-    sizes = groups(full_ref.shape[0])
-    starts = [sum(sizes[:i]) for i in range(len(sizes))]
-    copies = [(weights_hbm, weights_ref)]
-    for start, size in zip(starts, sizes):
-        copies.append((basis_hbm.at[pl.ds(start, size)], basis_ref.at[pl.ds(start, size)]))
-    weights_copy, *basis_copies = fetch(copies, semaphores)
-    weights_copy.wait()
-    for copy, packed_ref, start, size in zip(basis_copies, packed_refs, starts, sizes):
-        copy.wait()
-        diagonal[...] = jnp.zeros_like(diagonal)
-
-        def step(b, carry, start=start, packed_ref=packed_ref):
-            values = basis_ref[start + b]
-            weighted = values.astype(F32).T * live_row(weights_ref, counts_ref, start + b)
-            ham = split_dot(weighted, values, (((1,), (0,)), ((), ())))
-            full_ref[start + b] = ham.astype(BF16)
-            last = ham[half:, half:]
-            mixed = jnp.where(row >= column, ham[:half, :half], last)
-            packed = jnp.concatenate([ham[:half, half:], mixed], axis=1)
-            packed_ref[pl.ds(pl.multiple_of(b * half, half), half), :] = packed.astype(BF16)
-            line = jnp.sum(jnp.where(row == column, last, 0.0), axis=0, keepdims=True)
-            diagonal[pl.ds(b, 1), :] = jnp.concatenate([line, jnp.zeros_like(line)], axis=1)
-            return carry
-
-        lax.fori_loop(0, size, step, 0, unroll=4)
-        tail = packed_ref.shape[0] - size * half
-        packed_ref[size * half :, :] = diagonal[:tail].astype(BF16)
+    cut = -(-size // 2)
+    copies = [(counts_hbm, counts_ref), (weights_hbm, weights_ref)]
+    for place in (pl.ds(0, cut), pl.ds(cut, size - cut)):
+        copies.append((basis_hbm.at[pl.ds(start + place.start, place.size)], basis_ref.at[place]))
+    waits = fetch(copies if cut < size else copies[:3], semaphores)
+    diagonal[...] = jnp.zeros_like(diagonal)
+    for b in range(size):
+        if b == 0:
+            for copy in waits[:3]:
+                copy.wait()
+        elif b == cut:
+            waits[3].wait()
+        values = basis_ref[b]
+        weighted = values.astype(F32).T * live_row(weights_ref, counts_ref, start + b)
+        ham = split_dot(weighted, values, (((1,), (0,)), ((), ())))
+        full_ref[b] = ham.astype(BF16)
+        last = ham[half:, half:]
+        mixed = jnp.where(row >= column, ham[:half, :half], last)
+        packed = jnp.concatenate([ham[:half, half:], mixed], axis=1)
+        packed_ref[b * half : (b + 1) * half, :] = packed.astype(BF16)
+        line = jnp.sum(jnp.where(row == column, last, 0.0), axis=0, keepdims=True)
+        diagonal[b : b + 1, :] = jnp.concatenate([line, jnp.zeros_like(line)], axis=1)
+    packed_ref[size * half :, :] = diagonal[...].astype(BF16)
 
 
 def groups(nbatch):
@@ -117,29 +114,31 @@
     return -(-nbatch // 32) * 32
 
 
-def integrate(basis_values, counts, weights):
-    nbatch, points, columns = basis_values.shape
-    sizes = groups(nbatch)
-    rows = [size * columns // 2 + padded_rows(size) for size in sizes]
+def integrate(basis_values, counts, weights, start, size):
+    _, points, columns = basis_values.shape
+    extra = padded_rows(size)
     return pl.pallas_call(
-        integrate_kernel,
-        out_shape=[pltpu.VMEM((nbatch, columns, columns), BF16)]
-        + [jax.ShapeDtypeStruct((row, columns), BF16) for row in rows],
-        in_specs=[SMEM, HBM, HBM],
-        out_specs=[VMEM] * (1 + len(rows)),
+        functools.partial(integrate_kernel, start),
+        out_shape=[
+            pltpu.VMEM((size, columns, columns), BF16),
+            jax.ShapeDtypeStruct((size * columns // 2 + extra, columns), BF16),
+        ],
+        in_specs=[HBM, HBM, HBM],
+        out_specs=[VMEM, VMEM],
         scratch_shapes=[
-            pltpu.VMEM((padded_rows(sizes[0]), columns), F32),
-            pltpu.VMEM(basis_values.shape, BF16),
+            pltpu.VMEM((extra, columns), F32),
+            pltpu.VMEM((size, points, columns), BF16),
             pltpu.VMEM(weights.shape, F32),
-            pltpu.SemaphoreType.DMA((1 + len(sizes),)),
+            pltpu.SMEM(counts.shape, jnp.int32),
+            pltpu.SemaphoreType.DMA((4,)),
         ],
-        compiler_params=params(),
+        compiler_params=params(6),
         cost_estimate=pl.CostEstimate(
-            flops=4 * nbatch * points * columns * columns,
-            bytes_accessed=nbatch * columns * (points * 2 + columns * 3),
+            flops=4 * size * points * columns * columns,
+            bytes_accessed=size * columns * (points * 2 + columns * 3),
             transcendentals=0,
         ),
-    )(counts, place_in(basis_values, pltpu.HBM), place_in(weights, pltpu.HBM))
+    )(*[place_in(array, pltpu.HBM) for array in (counts, basis_values, weights)])
 
 
 def unpack_kernel(packed_ref, full_ref, diagonal):
@@ -242,7 +241,7 @@
             pltpu.VMEM((3 * region, width), BF16),
             pltpu.VMEM((3 * region, width), F32),
         ],
-        compiler_params=params(),
+        compiler_params=params(6),
         cost_estimate=pl.CostEstimate(
             flops=2 * work * columns * columns * width,
             bytes_accessed=work * columns * columns * 2 + 14 * region * width,
@@ -283,7 +282,7 @@
         in_specs=[SMEM] * pieces + [VMEM] * 12,
         out_specs=[VMEM] * pieces,
         scratch_shapes=[pltpu.VMEM((3 * region, 2 * width), BF16)] * 2,
-        compiler_params=params(),
+        compiler_params=params(8),
         cost_estimate=pl.CostEstimate(
             flops=4 * pieces * nbatch * columns * columns * width,
             bytes_accessed=24 * region * width + pieces * nbatch * columns * columns * 3,
@@ -293,15 +292,12 @@
 
 
 def density_kernel(counts_ref, basis_ref, first_ref, second_ref, scale_ref, out_ref):
-    def step(b, carry):
+    for b in range(basis_ref.shape[0]):
         values = basis_ref[b]
         overlap = first_ref[b] + second_ref[b].astype(F32)
         product = split_dot(overlap, values, NT)
         density = 4.0 * jnp.sum(product * values.astype(F32).T, axis=0, keepdims=True)
-        out_ref[pl.ds(b, 1), :] = live_row(scale_ref, counts_ref, b) * density
-        return carry
-
-    lax.fori_loop(0, basis_ref.shape[0], step, 0, unroll=4)
+        out_ref[b : b + 1, :] = live_row(scale_ref, counts_ref, b) * density
 
 
 def density(basis_values, counts, first, second, scale):
@@ -345,29 +341,48 @@
     return jnp.concatenate([low, high], axis=1)
 
 
-def halve(part, order):
-    half = part.shape[1] // 2
-    keep, send = trade(part, half, (lax.axis_index("grid") >> order) & 1)
-    return keep, flip(send, "grid", 1 << order)
-
-
-def rotate(part, level, energy, order, halved):
-    if lax.axis_size("grid") != 8:
-        total = lax.psum(part, "grid")
-        return (total / (level[None, :, None] - energy[:, None, :])).astype(BF16)
-    grid = lax.axis_index("grid")
-    first, second = (grid >> order) & 1, (grid >> (1 - order)) & 1
-    half = part.shape[1] // 2
-    quarter = half // 2
-    keep, coming = halved
-    total = keep + coming.astype(F32)
-    keep, send = trade(total, quarter, second)
-    total = keep + flip(send, "grid", 2 >> order).astype(F32)
-    total = total + flip(total.astype(BF16), "grid", 4).astype(F32)
-    level = lax.dynamic_slice_in_dim(level, first * half + second * quarter, quarter, 0)
-    own = (total / (level[None, :, None] - energy[:, None, :])).astype(BF16)
-    own = join(own, flip(own, "grid", 2 >> order), second)
-    return join(own, flip(own, "grid", 1 << order), first)
+def swap(array, masks):
+    size, tiles = lax.axis_size("grid"), lax.axis_size("tile")
+    pairs = [
+        (g * tiles + t, (g ^ masks[t % 2]) * tiles + t) for g in range(size) for t in range(tiles)
+    ]
+    return lax.ppermute(array, ("grid", "tile"), pairs)
+
+
+def together(*arrays):
+    return lax.optimization_barrier(arrays)
+
+
+class Reduction:
+    def __init__(self, part, level, energy):
+        grid, core = lax.axis_index("grid"), lax.axis_index("tile") % 2
+        self.masks = (1, 2), (2, 1)
+        self.first, self.second = (grid >> core) & 1, (grid >> (1 - core)) & 1
+        self.level, self.energy = level, energy
+        self.half = part.shape[1] // 2
+        self.keep, send = trade(part, self.half, self.first)
+        self.coming = swap(send, self.masks[0])
+
+    def narrow(self):
+        total = self.keep + self.coming.astype(F32)
+        self.keep, send = trade(total, self.half // 2, self.second)
+        self.total = self.keep + swap(send, self.masks[1]).astype(F32)
+        self.across = self.total.astype(BF16)
+
+    def cross(self):
+        self.coming = flip(self.across, "grid", 4)
+
+    def divide(self):
+        quarter = self.half // 2
+        place = self.first * self.half + self.second * quarter
+        level = lax.dynamic_slice_in_dim(self.level, place, quarter, 0)
+        total = self.total + self.coming.astype(F32)
+        own = (total / (level[None, :, None] - self.energy[:, None, :])).astype(BF16)
+        self.part = join(own, swap(own, self.masks[1]), self.second)
+        self.coming = swap(self.part, self.masks[0])
+
+    def result(self):
+        return join(self.part, self.coming, self.first)
 
 
 def per_device(
@@ -391,19 +406,21 @@
     occ_own = column_part(occ_coef, quarter, width)
 
     lists = [blocks, flip(blocks, "tile", 1), flip(blocks, "tile", 2)]
-    ham, *packed = integrate(basis_values, counts, weighted_potential)
-    arrived = [flip(array, "tile", 2) for array in packed]
-    occ_own, ham, lists = lax.optimization_barrier((occ_own, ham, lists))
+    fulls, arrived, weights = [], [], weighted_potential
+    for i, size in enumerate(groups(nbatch)):
+        full, packed = integrate(basis_values, counts, weights, sum(groups(nbatch)[:i]), size)
+        arrived.append(flip(packed, "tile", 2))
+        if i == 0:
+            occ_own, full = together(occ_own, full)
+            occ_before, occ_after = neighbours(occ_own)
+            weights, lists = together(weights, lists)
+        fulls.append(full)
     lists.append(flip(lists[2], "tile", 1))
-    occ_before, occ_after = neighbours(occ_own)
-    hams, places, starts, start = [ham, flip(ham, "tile", 1)], lists[:2], [0, 0], 0
-    arrived[-1], occ_before, occ_after = lax.optimization_barrier(
-        (arrived[-1], occ_before, occ_after)
-    )
-    for array, count in zip(arrived, groups(nbatch)):
-        far = unpack(array, count, columns)
-        hams += [far, flip(far, "tile", 1)]
-        places, starts, start = places + lists[2:], starts + [start] * 2, start + count
+    hams, places, starts = [], [], []
+    for i, size in enumerate(groups(nbatch)):
+        far = unpack(arrived[i], size, columns)
+        hams += [fulls[i], flip(fulls[i], "tile", 1), far, flip(far, "tile", 1)]
+        places, starts = places + lists, starts + [sum(groups(nbatch)[:i])] * 4
     blocks_near = lists[1]
     virtuals = [load(virt_coef), load(flip(virt_coef, "tile", 1))]
     energies = jnp.stack([virt_energy, flip(virt_energy, "tile", 1)])
@@ -428,29 +445,41 @@
     from_after = lax.ppermute(to_before, "grid", [((i + 1) % size, i) for i in range(size)])
     ham_own = (own_sum + from_before.astype(F32) + from_after.astype(F32)).astype(BF16)
 
-    parts, halved = [], []
-    for order, ham_sum in enumerate((ham_own, ham_own)):
-        if order == 1:
-            ham_sum, parts = lax.optimization_barrier((ham_sum, parts))
-            ham_sum = flip(ham_sum, "tile", 2)
-        products = [
+    occ_far = column_part(occ_coef, quarter ^ 1, width)
+
+    def products(ham_sum):
+        dots = [
             lax.dot_general(ham_sum, virt, (((0,), (0,)), ((), ())), preferred_element_type=F32)
             for virt in virtuals
         ]
-        parts.append(jnp.stack(products))
-        halved.append(halve(parts[order], order))
-
-    occ_far = column_part(occ_coef, quarter ^ 1, width)
-    late_before, late_after, _ = lax.optimization_barrier((occ_before, occ_after, parts[1]))
-    before_far, after_far = flip(late_before, "tile", 2), flip(late_after, "tile", 2)
-
-    rotated = [
-        rotate(part, levels[order], energies, order, halved[order])
-        for order, part in enumerate(parts)
-    ]
-    rotated[0], before_far, after_far = lax.optimization_barrier(
-        (rotated[0], before_far, after_far)
-    )
+        return jnp.stack(dots)
+
+    own_part = products(ham_own)
+    ham_late, _ = together(ham_own, own_part)
+    ham_far = flip(ham_late, "tile", 2)
+    far_part = products(ham_far)
+    if lax.axis_size("grid") == 8:
+        own = Reduction(own_part, levels[0], energies)
+        far = Reduction(far_part, levels[1], energies)
+        own.narrow()
+        far.narrow()
+        far.cross()
+        own.across, occ_before, occ_after = together(own.across, occ_before, occ_after)
+        own.cross()
+        before_far, after_far = flip(occ_before, "tile", 2), flip(occ_after, "tile", 2)
+        own.coming, before_far, after_far = together(own.coming, before_far, after_far)
+        own.divide()
+        far.divide()
+        rotated = [own.result(), far.result()]
+    else:
+        rotated = [
+            (
+                lax.psum(part, "grid") / (level[None, :, None] - energies[:, None, :])
+            ).astype(BF16)
+            for part, level in zip((own_part, far_part), levels)
+        ]
+        before_far, after_far = flip(occ_before, "tile", 2), flip(occ_after, "tile", 2)
+
     coefs = []
     for rotation in rotated:
         terms = [
@@ -464,25 +493,24 @@
     resp_own = (coef_own + coef_far.astype(F32)).astype(BF16)
 
     resp_before, resp_after = neighbours(resp_own)
-    resp_before_far, resp_after_far = flip(resp_before, "tile", 2), flip(resp_after, "tile", 2)
-    resp_far, *_ = lax.optimization_barrier((flip(resp_own, "tile", 2), resp_before, resp_after))
+    resp_before_far = flip(resp_before, "tile", 2)
+    resp_after, resp_far = together(resp_after, flip(resp_own, "tile", 2))
+    resp_after_far = flip(resp_after, "tile", 2)
     first = chip == 0
     half = jnp.concatenate(
         [jnp.where(first, resp_own, resp_far), jnp.where(first, resp_far, resp_own)], axis=1
     )
-    half_near = flip(half, "tile", 1)
-    first = core == 0
-    response_coef = jnp.concatenate(
-        [jnp.where(first, half, half_near), jnp.where(first, half_near, half)], axis=1
-    )
-
-    lists, response_coef = lax.optimization_barrier(([blocks, blocks_near], response_coef))
     overlap_own, overlap_near = overlaps(
-        lists,
+        [blocks, blocks_near],
         columns,
         [occ_before, before_far, occ_own, occ_far, occ_after, after_far],
         [resp_before, resp_before_far, resp_own, resp_far, resp_after, resp_after_far],
         [F32, BF16],
+    )
+    half_near, overlap_own = together(flip(half, "tile", 1), overlap_own)
+    first = core == 0
+    response_coef = jnp.concatenate(
+        [jnp.where(first, half, half_near), jnp.where(first, half_near, half)], axis=1
     )
     response_potential = density(
         basis_values, counts, overlap_own, flip(overlap_near, "tile", 1), xc_kernel

time: 176 us -> 160 us (0.909)
  starting transfers between devices: 41.5 us -> 30.2 us
  waiting for transfers between devices: 83 us -> 78.8 us
    ppermute x29 -> x22, waiting for transfers between devices: 69.3 us -> 33 us  [flip(): lax.ppermute(array, axis, [(i, i ^ mask) for i in range(lax.axis_size(axi...]
    ppermute x0 -> x8, waiting for transfers between devices: none -> 32.4 us  [swap(): return lax.ppermute(array, ('grid', 'tile'), pairs)]
    ppermute x29 -> x22, starting transfers between devices: 26.8 us -> 16.2 us  [flip(): lax.ppermute(array, axis, [(i, i ^ mask) for i in range(lax.axis_size(axi...]
    ppermute x2, waiting for transfers between devices: 6.19 us -> 1.55 us  [neighbours(): lax.ppermute(array, 'grid', [(i, (i + 1) % size) for i in range(size)])]
    ppermute x0 -> x8, starting transfers between devices: none -> 3.71 us  [swap(): return lax.ppermute(array, ('grid', 'tile'), pairs)]
    ppermute x1, waiting for transfers between devices: 2.56 us -> 5.9 us  [per_device(): lax.ppermute(to_before, 'grid', [((i + 1) % size, i) for i in range(size)])]
    ppermute x1, starting transfers between devices: 4.43 us -> 1.87 us  [per_device(): lax.ppermute(to_before, 'grid', [((i + 1) % size, i) for i in range(size)])]
    ppermute x2, waiting for transfers between devices: 3.76 us -> 5.93 us  [neighbours(): lax.ppermute(array, 'grid', [((i + 1) % size, i) for i in range(size)])]
  transfers between devices with their start and end apart: 35 -> 36, of which waited for: 24 -> 22; matrix products, arithmetic and copies ran while one was open for 10% -> 9% of each run, Pallas kernels for 9% -> 12%
where the time goes in v7:
time: 160 us
  waiting for transfers between devices  78.8 us (49%)
  starting transfers between devices  30.2 us (19%)
  Pallas kernels  22.8 us (14%)
  other arithmetic  10.4 us (6%)
  local copies, waits for them, and re-layouts  8.97 us (6%)
  matrix products  7.69 us (5%)
    ppermute x22, waiting for transfers between devices, flip(): lax.ppermute(array, axis, [(i, i ^ mask) for i in range(lax.axis_size(axi...  33 us
    ppermute x8, waiting for transfers between devices, swap(): return lax.ppermute(array, ('grid', 'tile'), pairs)  32.4 us
    ppermute x22, starting transfers between devices, flip(): lax.ppermute(array, axis, [(i, i ^ mask) for i in range(lax.axis_size(axi...  16.2 us
    unnamed x45, local copies, waits for them, and re-layouts  7.5 us
    ppermute x2, waiting for transfers between devices, neighbours(): lax.ppermute(array, 'grid', [((i + 1) % size, i) for i in range(size)])  5.93 us
    ppermute x1, waiting for transfers between devices, per_device(): lax.ppermute(to_before, 'grid', [((i + 1) % size, i) for i in range(size)])  5.9 us
    ppermute x2, starting transfers between devices, neighbours(): lax.ppermute(array, 'grid', [((i + 1) % size, i) for i in range(size)])  5.67 us
    pallas_call x1, Pallas kernels, apply_window(): pl.pallas_call(functools.partial(apply_kernel, starts, columns // per_bat...  5.16 us
  transfers between devices with their start and end apart: 36, of which 22 were waited for; matrix products, arithmetic and copies ran while one was open for 9% of the time, Pallas kernels for 12%

profile of v7, /device:TPU:0, one launch (start us, length us, event | category | flops | bytes accessed | tf_op | source)
XLA Modules:
  0.0 160.0 jit_solution(5873208908045753016)
XLA Ops:
  1.2 2.2 %shard_map.104 = (bf16[12,128,128]{2,1,0:T(8,128)(2,1)S(1)}, bf16[800,128]{1,0:T(8,128)(2,1)S(1)}) custom-call(s32[24]{0:T(128)} %counts_ref.1, bf16[24,256,128]{2,1,0:T(8,128)(2,1)} %basis_ref.1, f32[24,256]{1,0:T(8,128)} %weights_hbm.2), custom_call_target="tpu_custom_call" | custom-call | flops 201326592 | bytes 1376256 | tf_op jit(solution)/shard_map/pallas_call | solution.py:120
  3.4 1.1 constant_dynamic-slice_fusion
  4.5 2.6 %collective-permute-start.9 = (bf16[1024,128]{1,0:T(8,128)(2,1)S(1)}, bf16[1024,128]{1,0:T(8,128)(2,1)S(1)}, u32[]{:S(2)}, u32[]{:S(2)}) collective-permute-start(bf16[1024,128]{1,0:T(8,128)(2,1)S(1)} %get-tuple-element.45.refs_17_.refs_4_), channel_id=1, source_target_pairs={{0,4},{4,8},{8,12},{12,16},{16,20},{20,24},{24,28},{28,0},{1,5},{5... | collective-permute-start | bytes 786440 | tf_op jit(solution)/shard_map/ppermute | solution.py:325
  7.1 3.1 %collective-permute-start.10 = (bf16[1024,128]{1,0:T(8,128)(2,1)S(1)}, bf16[1024,128]{1,0:T(8,128)(2,1)S(1)}, u32[]{:S(2)}, u32[]{:S(2)}) collective-permute-start(bf16[1024,128]{1,0:T(8,128)(2,1)S(1)} %get-tuple-element.45.refs_17_.refs_4_), channel_id=1, source_target_pairs={{4,0},{8,4},{12,8},{16,12},{20,16},{24,20},{28,24},{0,28},{5,1},{9... | collective-permute-start | bytes 786440 | tf_op jit(solution)/shard_map/ppermute | solution.py:326
  11.1 1.5 collective-permute-start.1
  12.6 1.1 collective-permute-start.4
  13.7 1.1 collective-permute-done.1.refs_2_.refs_6_
  14.8 2.2 %shard_map.106 = (bf16[12,128,128]{2,1,0:T(8,128)(2,1)S(1)}, bf16[800,128]{1,0:T(8,128)(2,1)S(1)}) custom-call(s32[24]{0:T(128)} %counts_ref.1, bf16[24,256,128]{2,1,0:T(8,128)(2,1)} %basis_ref.1, f32[24,256]{1,0:T(8,128)} %weights_hbm.2), custom_call_target="tpu_custom_call" | custom-call | flops 201326592 | bytes 1376256 | tf_op jit(solution)/shard_map/pallas_call | solution.py:120
  17.0 1.6 collective-permute-start.7
  18.6 1.7 %collective-permute-done.4.packed_ref = bf16[800,128]{1,0:T(8,128)(2,1)S(1)} collective-permute-done((bf16[800,128]{1,0:T(8,128)(2,1)S(1)}, bf16[800,128]{1,0:T(8,128)(2,1)S(1)}, u32[]{:S(2)}, u32[]{:S(2)}) %collective-permute-start.4) | collective-permute-done | bytes 204832 | tf_op jit(solution)/shard_map/ppermute | solution.py:320
  21.2 2.9 %collective-permute-done.7.packed_ref = bf16[800,128]{1,0:T(8,128)(2,1)S(1)} collective-permute-done((bf16[800,128]{1,0:T(8,128)(2,1)S(1)}, bf16[800,128]{1,0:T(8,128)(2,1)S(1)}, u32[]{:S(2)}, u32[]{:S(2)}) %collective-permute-start.7) | collective-permute-done | bytes 204832 | tf_op jit(solution)/shard_map/ppermute | solution.py:320
  29.2 5.2 %shard_map.108 = (bf16[1024,128]{1,0:T(8,128)(2,1)}, f32[1024,128]{1,0:T(8,128)S(1)}, bf16[1024,128]{1,0:T(8,128)(2,1)}) custom-call(s32[24,2]{1,0:T(8,128)S(1)} %copy.13.refs_0_.refs_4_, s32[24,2]{1,0:T(8,128)S(1)} %collective-permute-done.refs_1_.refs_5_, s32[24,2]{1,0:T(8,128)S(1)} %collective-permute-done.1.refs_2_.refs_6_, ...), custom_call_target="tpu_custom_call" | custom-call | flops 402653184 | bytes 4980736 | tf_op jit(solution)/shard_map/pallas_call | solution.py:231
  34.3 1.9 %collective-permute-start.14 = (bf16[1024,128]{1,0:T(8,128)(2,1)}, bf16[1024,128]{1,0:T(8,128)(2,1)S(1)}, u32[]{:S(2)}, u32[]{:S(2)}) collective-permute-start(bf16[1024,128]{1,0:T(8,128)(2,1)} %get-tuple-element.50), channel_id=1, source_target_pairs={{4,0},{8,4},{12,8},{16,12},{20,16},{24,20},{28,24},{0,28},{5,1},{9... | collective-permute-start | bytes 786440 | tf_op jit(solution)/shard_map/ppermute | solution.py:445
  36.5 2.1 %shard_map.109 = bf16[1024,1920]{1,0:T(8,128)(2,1)S(1)} custom-call(bf16[1024,1920]{1,0:T(8,128)(2,1)} %source_ref.1), custom_call_target="tpu_custom_call" | custom-call | bytes 7864320 | tf_op jit(solution)/shard_map/pallas_call | solution.py:46
  38.6 1.9 %copy-done.2 = bf16[1024,1920]{1,0:T(8,128)(2,1)} copy-done((bf16[1024,1920]{1,0:T(8,128)(2,1)}, bf16[1024,1920]{1,0:T(8,128)(2,1)S(1)}, u32[]{:S(2)}) %copy-start.2) | copy-done | bytes 3932184
  40.6 2.3 %shard_map.110 = bf16[1024,1920]{1,0:T(8,128)(2,1)S(1)} custom-call(bf16[1024,1920]{1,0:T(8,128)(2,1)} %collective-permute-done.12.source_ref), custom_call_target="tpu_custom_call" | custom-call | bytes 7864320 | tf_op jit(solution)/shard_map/pallas_call | solution.py:46
  42.9 5.9 %collective-permute-done.14 = bf16[1024,128]{1,0:T(8,128)(2,1)S(1)} collective-permute-done((bf16[1024,128]{1,0:T(8,128)(2,1)}, bf16[1024,128]{1,0:T(8,128)(2,1)S(1)}, u32[]{:S(2)}, u32[]{:S(2)}) %collective-permute-start.14) | collective-permute-done | bytes 262176 | tf_op jit(solution)/shard_map/ppermute | solution.py:445
  48.9 1.2 collective-permute-start.22
  51.7 5.0 %collective-permute-done.22 = bf16[1024,128]{1,0:T(8,128)(2,1)S(1)} collective-permute-done((bf16[1024,128]{1,0:T(8,128)(2,1)S(1)}, bf16[1024,128]{1,0:T(8,128)(2,1)S(1)}, u32[]{:S(2)}, u32[]{:S(2)}) %collective-permute-start.22) | collective-permute-done | bytes 262176 | tf_op jit(solution)/shard_map/ppermute | solution.py:320
  58.5 2.0 %collective-permute-done.15 = bf16[2,64,1920]{2,1,0:T(8,128)(2,1)S(1)} collective-permute-done((bf16[2,64,1920]{2,1,0:T(8,128)(2,1)S(1)}, bf16[2,64,1920]{2,1,0:T(8,128)(2,1)S(1)}, u32[]{:S(2)}, u32[]{:S(2)}) %collective-permute-start.15) | collective-permute-done | bytes 491552 | tf_op jit(solution)/shard_map/ppermute | solution.py:349
  60.7 10.2 %collective-permute-done.23 = bf16[2,64,1920]{2,1,0:T(8,128)(2,1)S(1)} collective-permute-done((bf16[2,64,1920]{2,1,0:T(8,128)(2,1)S(1)}, bf16[2,64,1920]{2,1,0:T(8,128)(2,1)S(1)}, u32[]{:S(2)}, u32[]{:S(2)}) %collective-permute-start.23) | collective-permute-done | bytes 491552 | tf_op jit(solution)/shard_map/ppermute | solution.py:349
  72.0 2.2 %collective-permute-start.17 = (bf16[2,32,1920]{2,1,0:T(8,128)(2,1)}, bf16[2,32,1920]{2,1,0:T(8,128)(2,1)}, u32[]{:S(2)}, u32[]{:S(2)}) collective-permute-start(bf16[2,32,1920]{2,1,0:T(8,128)(2,1)} %fusion.23), channel_id=1, source_target_pairs={{0,16},{4,20},{8,24},{12,28},{16,0},{20,4},{24,8},{28,12},{1,17},{... | collective-permute-start | bytes 737288 | tf_op jit(solution)/shard_map/ppermute | solution.py:320
  74.8 1.5 collective-permute-start.19
  76.2 3.6 %collective-permute-done.24 = bf16[2,32,1920]{2,1,0:T(8,128)(2,1)S(1)} collective-permute-done((bf16[2,32,1920]{2,1,0:T(8,128)(2,1)S(1)}, bf16[2,32,1920]{2,1,0:T(8,128)(2,1)S(1)}, u32[]{:S(2)}, u32[]{:S(2)}) %collective-permute-start.24) | collective-permute-done | bytes 245792 | tf_op jit(solution)/shard_map/ppermute | solution.py:349
  80.6 9.1 %collective-permute-done.17 = bf16[2,32,1920]{2,1,0:T(8,128)(2,1)} collective-permute-done((bf16[2,32,1920]{2,1,0:T(8,128)(2,1)}, bf16[2,32,1920]{2,1,0:T(8,128)(2,1)}, u32[]{:S(2)}, u32[]{:S(2)}) %collective-permute-start.17) | collective-permute-done | bytes 245792 | tf_op jit(solution)/shard_map/ppermute | solution.py:320
  89.7 3.0 %collective-permute-done.25 = bf16[2,32,1920]{2,1,0:T(8,128)(2,1)} collective-permute-done((bf16[2,32,1920]{2,1,0:T(8,128)(2,1)S(1)}, bf16[2,32,1920]{2,1,0:T(8,128)(2,1)}, u32[]{:S(2)}, u32[]{:S(2)}) %collective-permute-start.25) | collective-permute-done | bytes 245792 | tf_op jit(solution)/shard_map/ppermute | solution.py:320
  92.7 2.2 %divide_convert_fusion = (bf16[2,32,1920]{2,1,0:T(8,128)(2,1)}, bf16[2,32,1920]{2,1,0:T(8,128)(2,1)S(1)}) fusion(bf16[2,32,1920]{2,1,0:T(8,128)(2,1)} %collective-permute-done.25, bf16[2,32,1920]{2,1,0:T(8,128)(2,1)S(1)} %collective-permute-done.24, f32[2,64,1920]{2,1,0:T(8,128)} %copy-done.16, s32[]{:T(128)S(6)} %select_n.117, f32[32]{0:T(128)S(1)} %dynamic_slice.54, ...), kind=kLoop, calls=%fused_computation.48 | loop fusion | flops 1720320 | bytes 2473220 | tf_op jit(solution)/shard_map/convert_element_type | solution.py:380
  94.8 2.0 %collective-permute-start.20 = (bf16[2,32,1920]{2,1,0:T(8,128)(2,1)S(1)}, bf16[2,32,1920]{2,1,0:T(8,128)(2,1)S(1)}, u32[]{:S(2)}, u32[]{:S(2)}) collective-permute-start(bf16[2,32,1920]{2,1,0:T(8,128)(2,1)S(1)} %get-tuple-element.85), channel_id=1, source_target_pairs={{0,8},{1,5},{2,10},{3,7},{4,12},{5,1},{6,14},{7,3},{8,0},{9,13},{1... | collective-permute-start | bytes 737288 | tf_op jit(solution)/shard_map/ppermute | solution.py:349
  96.9 4.4 %collective-permute-done.26 = bf16[2,32,1920]{2,1,0:T(8,128)(2,1)S(1)} collective-permute-done((bf16[2,32,1920]{2,1,0:T(8,128)(2,1)}, bf16[2,32,1920]{2,1,0:T(8,128)(2,1)S(1)}, u32[]{:S(2)}, u32[]{:S(2)}) %collective-permute-start.26) | collective-permute-done | bytes 245792 | tf_op jit(solution)/shard_map/ppermute | solution.py:349
  102.8 3.2 %collective-permute-done.20 = bf16[2,32,1920]{2,1,0:T(8,128)(2,1)S(1)} collective-permute-done((bf16[2,32,1920]{2,1,0:T(8,128)(2,1)S(1)}, bf16[2,32,1920]{2,1,0:T(8,128)(2,1)S(1)}, u32[]{:S(2)}, u32[]{:S(2)}) %collective-permute-start.20) | collective-permute-done | bytes 245792 | tf_op jit(solution)/shard_map/ppermute | solution.py:349
  107.6 3.7 %collective-permute-done.27 = bf16[2,64,1920]{2,1,0:T(8,128)(2,1)} collective-permute-done((bf16[2,64,1920]{2,1,0:T(8,128)(2,1)S(1)}, bf16[2,64,1920]{2,1,0:T(8,128)(2,1)}, u32[]{:S(2)}, u32[]{:S(2)}) %collective-permute-start.27) | collective-permute-done | bytes 491552 | tf_op jit(solution)/shard_map/ppermute | solution.py:349
  111.3 5.3 %collective-permute-done.21 = bf16[2,64,1920]{2,1,0:T(8,128)(2,1)} collective-permute-done((bf16[2,64,1920]{2,1,0:T(8,128)(2,1)}, bf16[2,64,1920]{2,1,0:T(8,128)(2,1)}, u32[]{:S(2)}, u32[]{:S(2)}) %collective-permute-start.21) | collective-permute-done | bytes 491552 | tf_op jit(solution)/shard_map/ppermute | solution.py:349
  116.6 1.5 broadcast_select_fusion.3
  118.1 1.2 fusion.16
  120.2 1.2 fusion
  121.4 1.4 collective-permute-start.28
  122.8 1.2 fusion.20
  124.0 1.2 convolution_add_fusion.1
  125.2 2.7 %collective-permute-done.28 = bf16[1024,128]{1,0:T(8,128)(2,1)S(1)} collective-permute-done((bf16[1024,128]{1,0:T(8,128)(2,1)S(1)}, bf16[1024,128]{1,0:T(8,128)(2,1)S(1)}, u32[]{:S(2)}, u32[]{:S(2)}) %collective-permute-start.28) | collective-permute-done | bytes 262176 | tf_op jit(solution)/shard_map/ppermute | solution.py:320
  127.9 2.6 %collective-permute-start.29 = (bf16[1024,128]{1,0:T(8,128)(2,1)S(1)}, bf16[1024,128]{1,0:T(8,128)(2,1)}, u32[]{:S(2)}, u32[]{:S(2)}) collective-permute-start(bf16[1024,128]{1,0:T(8,128)(2,1)S(1)} %add_convert_fusion.refs_10_), channel_id=1, source_target_pairs={{4,0},{8,4},{12,8},{16,12},{20,16},{24,20},{28,24},{0,28},{5,1},{9... | collective-permute-start | bytes 786440 | tf_op jit(solution)/shard_map/ppermute | solution.py:326
  131.3 5.9 %collective-permute-done.29.refs_12_ = bf16[1024,128]{1,0:T(8,128)(2,1)} collective-permute-done((bf16[1024,128]{1,0:T(8,128)(2,1)S(1)}, bf16[1024,128]{1,0:T(8,128)(2,1)}, u32[]{:S(2)}, u32[]{:S(2)}) %collective-permute-start.29) | collective-permute-done | bytes 262176 | tf_op jit(solution)/shard_map/ppermute | solution.py:326
  139.0 1.5 collective-permute-done.32.refs_8_
  140.5 1.2 collective-permute-start.33
  142.6 5.5 %collective-permute-done.33.refs_9_ = bf16[1024,128]{1,0:T(8,128)(2,1)S(1)} collective-permute-done((bf16[1024,128]{1,0:T(8,128)(2,1)}, bf16[1024,128]{1,0:T(8,128)(2,1)S(1)}, u32[]{:S(2)}, u32[]{:S(2)}) %collective-permute-start.33) | collective-permute-done | bytes 262176 | tf_op jit(solution)/shard_map/ppermute | solution.py:320
  149.1 4.3 %shard_map.111 = (f32[24,128,128]{2,1,0:T(8,128)S(1)}, bf16[24,128,128]{2,1,0:T(8,128)(2,1)}) custom-call(s32[24,2]{1,0:T(8,128)S(1)} %copy-done.13, s32[24,2]{1,0:T(8,128)S(1)} %collective-permute-done.refs_1_.refs_5_, bf16[1024,128]{1,0:T(8,128)(2,1)S(1)} %collective-permute-done.9.refs_16_.refs_2_, bf16[1024,128]{1,0:T(8,128)(2,1)S(1)} %collective-permute-done.18.refs_3_, ...), custom_call_target="tpu_custom_call" | custom-call | flops 402653184 | bytes 5505024 | tf_op jit(solution)/shard_map/pallas_call | solution.py:279
  153.3 1.2 copy-done.6
  154.5 1.5 broadcast_select_fusion.1
  157.2 2.8 %shard_map.112 = f32[24,256]{1,0:T(8,128)} custom-call(s32[24]{0:T(128)S(1)} %copy-done.15, bf16[24,256,128]{2,1,0:T(8,128)(2,1)S(1)} %copy-done.5, f32[24,128,128]{2,1,0:T(8,128)S(1)} %copy-done.7, bf16[24,128,128]{2,1,0:T(8,128)(2,1)} %collective-permute-done.35.second_ref, f32[24,256]{1,0:T(8,128)S(1)} %copy-done.14), custom_call_target="tpu_custom_call" | custom-call | flops 402653184 | bytes 3932160 | tf_op jit(solution)/shard_map/pallas_call | solution.py:305
  (114 shorter events, 23.4 us)
Async XLA Ops:
  0.6 25.5 %copy-start.20 = (s32[24,2]{0,1:T(2,128)S(1)}, s32[24,2]{0,1:T(2,128)}, u32[]{:S(2)}) copy-start(s32[24,2]{0,1:T(2,128)} %param.10) | copy-start | bytes 580
  0.6 26.3 %copy-start.19 = (f32[1920]{0:T(1024)S(1)}, f32[1920]{0:T(1024)}, u32[]{:S(2)}) copy-start(f32[1920]{0:T(1024)} %param.17) | copy-start | bytes 23044
  0.7 39.9 %collective-permute-start.12 = (bf16[1024,1920]{1,0:T(8,128)(2,1)}, bf16[1024,1920]{1,0:T(8,128)(2,1)}, u32[]{:S(2)}, u32[]{:S(2)}) collective-permute-start(bf16[1024,1920]{1,0:T(8,128)(2,1)} %source_ref.1), channel_id=1, source_target_pairs={{0,1},{1,0},{2,3},{3,2},{4,5},{5,4},{6,7},{7,6},{8,9},{9,8},{10,11... | collective-permute-start | bytes 11796488 | tf_op jit(solution)/shard_map/ppermute | solution.py:320
  3.4 33.0 %copy-start.21 = (f32[512]{0:T(512)S(1)}, f32[512]{0:T(512)}, u32[]{:S(2)}) copy-start(f32[512]{0:T(512)} %param.16) | copy-start | bytes 6148
  4.5 21.1 %collective-permute-start.9 = (bf16[1024,128]{1,0:T(8,128)(2,1)S(1)}, bf16[1024,128]{1,0:T(8,128)(2,1)S(1)}, u32[]{:S(2)}, u32[]{:S(2)}) collective-permute-start(bf16[1024,128]{1,0:T(8,128)(2,1)S(1)} %get-tuple-element.45.refs_17_.refs_4_), channel_id=1, source_target_pairs={{0,4},{4,8},{8,12},{12,16},{16,20},{20,24},{24,28},{28,0},{1,5},{5... | collective-permute-start | bytes 786440 | tf_op jit(solution)/shard_map/ppermute | solution.py:325
  7.1 18.6 %collective-permute-start.10 = (bf16[1024,128]{1,0:T(8,128)(2,1)S(1)}, bf16[1024,128]{1,0:T(8,128)(2,1)S(1)}, u32[]{:S(2)}, u32[]{:S(2)}) collective-permute-start(bf16[1024,128]{1,0:T(8,128)(2,1)S(1)} %get-tuple-element.45.refs_17_.refs_4_), channel_id=1, source_target_pairs={{4,0},{8,4},{12,8},{16,12},{20,16},{24,20},{28,24},{0,28},{5,1},{9... | collective-permute-start | bytes 786440 | tf_op jit(solution)/shard_map/ppermute | solution.py:326
  10.9 27.7 %copy-start.12 = (s32[24,2]{1,0:T(8,128)}, s32[24,2]{1,0:T(8,128)S(1)}, u32[]{:S(2)}) copy-start(s32[24,2]{1,0:T(8,128)S(1)} %copy.11.refs_0_) | copy-start | bytes 580
  10.9 1.7 %collective-permute-start = (s32[24,2]{1,0:T(8,128)S(1)}, s32[24,2]{1,0:T(8,128)S(1)}, u32[]{:S(2)}, u32[]{:S(2)}) collective-permute-start(s32[24,2]{1,0:T(8,128)S(1)} %copy.11.refs_0_), channel_id=1, source_target_pairs={{0,1},{1,0},{2,3},{3,2},{4,5},{5,4},{6,7},{7,6},{8,9},{9,8},{10,11... | collective-permute-start | bytes 584 | tf_op jit(solution)/shard_map/ppermute | solution.py:320
  11.1 3.7 %collective-permute-start.1 = (s32[24,2]{1,0:T(8,128)S(1)}, s32[24,2]{1,0:T(8,128)S(1)}, u32[]{:S(2)}, u32[]{:S(2)}) collective-permute-start(s32[24,2]{1,0:T(8,128)S(1)} %copy.11.refs_0_), channel_id=1, source_target_pairs={{0,2},{1,3},{2,0},{3,1},{4,6},{5,7},{6,4},{7,5},{8,10},{9,11},{10,... | collective-permute-start | bytes 584 | tf_op jit(solution)/shard_map/ppermute | solution.py:320
  12.6 7.7 %collective-permute-start.4 = (bf16[800,128]{1,0:T(8,128)(2,1)S(1)}, bf16[800,128]{1,0:T(8,128)(2,1)S(1)}, u32[]{:S(2)}, u32[]{:S(2)}) collective-permute-start(bf16[800,128]{1,0:T(8,128)(2,1)S(1)} %get-tuple-element.41), channel_id=1, source_target_pairs={{0,2},{1,3},{2,0},{3,1},{4,6},{5,7},{6,4},{7,5},{8,10},{9,11},{10,... | collective-permute-start | bytes 614408 | tf_op jit(solution)/shard_map/ppermute | solution.py:320
  17.0 7.1 %collective-permute-start.7 = (bf16[800,128]{1,0:T(8,128)(2,1)S(1)}, bf16[800,128]{1,0:T(8,128)(2,1)S(1)}, u32[]{:S(2)}, u32[]{:S(2)}) collective-permute-start(bf16[800,128]{1,0:T(8,128)(2,1)S(1)} %get-tuple-element.44), channel_id=1, source_target_pairs={{0,2},{1,3},{2,0},{3,1},{4,6},{5,7},{6,4},{7,5},{8,10},{9,11},{10,... | collective-permute-start | bytes 614408 | tf_op jit(solution)/shard_map/ppermute | solution.py:320
  20.3 4.8 %collective-permute-start.2 = (s32[24,2]{1,0:T(8,128)S(1)}, s32[24,2]{1,0:T(8,128)S(1)}, u32[]{:S(2)}, u32[]{:S(2)}) collective-permute-start(s32[24,2]{1,0:T(8,128)S(1)} %collective-permute-done.1.refs_2_.refs_6_), channel_id=1, source_target_pairs={{0,1},{1,0},{2,3},{3,2},{4,5},{5,4},{6,7},{7,6},{8,9},{9,8},{10,11... | collective-permute-start | bytes 584 | tf_op jit(solution)/shard_map/ppermute | solution.py:320
  24.2 2.0 %collective-permute-start.3 = (bf16[12,128,128]{2,1,0:T(8,128)(2,1)S(1)}, bf16[12,128,128]{2,1,0:T(8,128)(2,1)S(1)}, u32[]{:S(2)}, u32[]{:S(2)}) collective-permute-start(bf16[12,128,128]{2,1,0:T(8,128)(2,1)S(1)} %get-tuple-element.40.refs_8_), channel_id=1, source_target_pairs={{0,1},{1,0},{2,3},{3,2},{4,5},{5,4},{6,7},{7,6},{8,9},{9,8},{10,11... | collective-permute-start | bytes 1179656 | tf_op jit(solution)/shard_map/ppermute | solution.py:320
  25.1 2.0 %collective-permute-start.6 = (bf16[12,128,128]{2,1,0:T(8,128)(2,1)S(1)}, bf16[12,128,128]{2,1,0:T(8,128)(2,1)}, u32[]{:S(2)}, u32[]{:S(2)}) collective-permute-start(bf16[12,128,128]{2,1,0:T(8,128)(2,1)S(1)} %get-tuple-element.43.refs_12_), channel_id=1, source_target_pairs={{0,1},{1,0},{2,3},{3,2},{4,5},{5,4},{6,7},{7,6},{8,9},{9,8},{10,11... | collective-permute-start | bytes 1179656 | tf_op jit(solution)/shard_map/ppermute | solution.py:320
  25.6 2.0 %collective-permute-start.5 = (bf16[12,128,128]{2,1,0:T(8,128)(2,1)S(1)}, bf16[12,128,128]{2,1,0:T(8,128)(2,1)}, u32[]{:S(2)}, u32[]{:S(2)}) collective-permute-start(bf16[12,128,128]{2,1,0:T(8,128)(2,1)S(1)} %shard_map.105.refs_10_), channel_id=1, source_target_pairs={{0,1},{1,0},{2,3},{3,2},{4,5},{5,4},{6,7},{7,6},{8,9},{9,8},{10,11... | collective-permute-start | bytes 1179656 | tf_op jit(solution)/shard_map/ppermute | solution.py:320
  25.7 2.5 %collective-permute-start.8 = (bf16[12,128,128]{2,1,0:T(8,128)(2,1)S(1)}, bf16[12,128,128]{2,1,0:T(8,128)(2,1)}, u32[]{:S(2)}, u32[]{:S(2)}) collective-permute-start(bf16[12,128,128]{2,1,0:T(8,128)(2,1)S(1)} %shard_map.107.refs_14_), channel_id=1, source_target_pairs={{0,1},{1,0},{2,3},{3,2},{4,5},{5,4},{6,7},{7,6},{8,9},{9,8},{10,11... | collective-permute-start | bytes 1179656 | tf_op jit(solution)/shard_map/ppermute | solution.py:320
  26.9 13.6 %collective-permute-start.11 = (f32[1920]{0:T(1024)S(1)}, f32[1920]{0:T(1024)S(1)}, u32[]{:S(2)}, u32[]{:S(2)}) collective-permute-start(f32[1920]{0:T(1024)S(1)} %copy-done.19), channel_id=1, source_target_pairs={{0,1},{1,0},{2,3},{3,2},{4,5},{5,4},{6,7},{7,6},{8,9},{9,8},{10,11... | collective-permute-start | bytes 23048 | tf_op jit(solution)/shard_map/ppermute | solution.py:320
  34.3 14.4 %collective-permute-start.14 = (bf16[1024,128]{1,0:T(8,128)(2,1)}, bf16[1024,128]{1,0:T(8,128)(2,1)S(1)}, u32[]{:S(2)}, u32[]{:S(2)}) collective-permute-start(bf16[1024,128]{1,0:T(8,128)(2,1)} %get-tuple-element.50), channel_id=1, source_target_pairs={{4,0},{8,4},{12,8},{16,12},{20,16},{24,20},{28,24},{0,28},{5,1},{9... | collective-permute-start | bytes 786440 | tf_op jit(solution)/shard_map/ppermute | solution.py:445
  36.2 12.6 %collective-permute-start.13 = (bf16[1024,128]{1,0:T(8,128)(2,1)}, bf16[1024,128]{1,0:T(8,128)(2,1)S(1)}, u32[]{:S(2)}, u32[]{:S(2)}) collective-permute-start(bf16[1024,128]{1,0:T(8,128)(2,1)} %get-tuple-element.49), channel_id=1, source_target_pairs={{0,4},{4,8},{8,12},{12,16},{16,20},{20,24},{24,28},{28,0},{1,5},{5... | collective-permute-start | bytes 786440 | tf_op jit(solution)/shard_map/ppermute | solution.py:444
  40.6 9.5 %copy-start.3 = (bf16[1024,1920]{1,0:T(8,128)(2,1)S(1)}, bf16[1024,1920]{1,0:T(8,128)(2,1)}, u32[]{:S(2)}) copy-start(bf16[1024,1920]{1,0:T(8,128)(2,1)} %copy-done.2) | copy-start | bytes 11796484
  42.9 14.6 %copy-start = (bf16[1024,1920]{1,0:T(8,128)(2,1)}, bf16[1024,1920]{1,0:T(8,128)(2,1)S(1)}, u32[]{:S(2)}) copy-start(bf16[1024,1920]{1,0:T(8,128)(2,1)S(1)} %shard_map.110) | copy-start | bytes 11796484
  48.9 7.8 %collective-permute-start.22 = (bf16[1024,128]{1,0:T(8,128)(2,1)S(1)}, bf16[1024,128]{1,0:T(8,128)(2,1)S(1)}, u32[]{:S(2)}, u32[]{:S(2)}) collective-permute-start(bf16[1024,128]{1,0:T(8,128)(2,1)S(1)} %add_convert_fusion.1), channel_id=1, source_target_pairs={{0,2},{1,3},{2,0},{3,1},{4,6},{5,7},{6,4},{7,5},{8,10},{9,11},{10,... | collective-permute-start | bytes 786440 | tf_op jit(solution)/shard_map/ppermute | solution.py:320
  51.6 8.9 %collective-permute-start.15 = (bf16[2,64,1920]{2,1,0:T(8,128)(2,1)S(1)}, bf16[2,64,1920]{2,1,0:T(8,128)(2,1)S(1)}, u32[]{:S(2)}, u32[]{:S(2)}) collective-permute-start(bf16[2,64,1920]{2,1,0:T(8,128)(2,1)S(1)} %fusion.8), channel_id=1, source_target_pairs={{0,4},{1,9},{2,6},{3,11},{4,0},{5,13},{6,2},{7,15},{8,12},{9,1},{1... | collective-permute-start | bytes 1474568 | tf_op jit(solution)/shard_map/ppermute | solution.py:349
  58.3 12.6 %collective-permute-start.23 = (bf16[2,64,1920]{2,1,0:T(8,128)(2,1)S(1)}, bf16[2,64,1920]{2,1,0:T(8,128)(2,1)S(1)}, u32[]{:S(2)}, u32[]{:S(2)}) collective-permute-start(bf16[2,64,1920]{2,1,0:T(8,128)(2,1)S(1)} %fusion.2), channel_id=1, source_target_pairs={{0,4},{1,9},{2,6},{3,11},{4,0},{5,13},{6,2},{7,15},{8,12},{9,1},{1... | collective-permute-start | bytes 1474568 | tf_op jit(solution)/shard_map/ppermute | solution.py:349
  60.6 10.5 %collective-permute-start.16 = (bf16[2,32,1920]{2,1,0:T(8,128)(2,1)S(1)}, bf16[2,32,1920]{2,1,0:T(8,128)(2,1)S(1)}, u32[]{:S(2)}, u32[]{:S(2)}) collective-permute-start(bf16[2,32,1920]{2,1,0:T(8,128)(2,1)S(1)} %dynamic-slice_convert_fusion.1), channel_id=1, source_target_pairs={{0,8},{1,5},{2,10},{3,7},{4,12},{5,1},{6,14},{7,3},{8,0},{9,13},{1... | collective-permute-start | bytes 737288 | tf_op jit(solution)/shard_map/ppermute | solution.py:349
  71.1 8.8 %collective-permute-start.24 = (bf16[2,32,1920]{2,1,0:T(8,128)(2,1)S(1)}, bf16[2,32,1920]{2,1,0:T(8,128)(2,1)S(1)}, u32[]{:S(2)}, u32[]{:S(2)}) collective-permute-start(bf16[2,32,1920]{2,1,0:T(8,128)(2,1)S(1)} %dynamic-slice_convert_fusion), channel_id=1, source_target_pairs={{0,8},{1,5},{2,10},{3,7},{4,12},{5,1},{6,14},{7,3},{8,0},{9,13},{1... | collective-permute-start | bytes 737288 | tf_op jit(solution)/shard_map/ppermute | solution.py:349
  72.0 17.7 %collective-permute-start.17 = (bf16[2,32,1920]{2,1,0:T(8,128)(2,1)}, bf16[2,32,1920]{2,1,0:T(8,128)(2,1)}, u32[]{:S(2)}, u32[]{:S(2)}) collective-permute-start(bf16[2,32,1920]{2,1,0:T(8,128)(2,1)} %fusion.23), channel_id=1, source_target_pairs={{0,16},{4,20},{8,24},{12,28},{16,0},{20,4},{24,8},{28,12},{1,17},{... | collective-permute-start | bytes 737288 | tf_op jit(solution)/shard_map/ppermute | solution.py:320
  74.2 15.5 %collective-permute-start.18 = (bf16[1024,128]{1,0:T(8,128)(2,1)S(1)}, bf16[1024,128]{1,0:T(8,128)(2,1)S(1)}, u32[]{:S(2)}, u32[]{:S(2)}) collective-permute-start(bf16[1024,128]{1,0:T(8,128)(2,1)S(1)} %collective-permute-done.9.refs_16_.refs_2_), channel_id=1, source_target_pairs={{0,2},{1,3},{2,0},{3,1},{4,6},{5,7},{6,4},{7,5},{8,10},{9,11},{10,... | collective-permute-start | bytes 786440 | tf_op jit(solution)/shard_map/ppermute | solution.py:320
  74.8 14.9 %collective-permute-start.19 = (bf16[1024,128]{1,0:T(8,128)(2,1)S(1)}, bf16[1024,128]{1,0:T(8,128)(2,1)S(1)}, u32[]{:S(2)}, u32[]{:S(2)}) collective-permute-start(bf16[1024,128]{1,0:T(8,128)(2,1)S(1)} %collective-permute-done.10.refs_18_.refs_6_), channel_id=1, source_target_pairs={{0,2},{1,3},{2,0},{3,1},{4,6},{5,7},{6,4},{7,5},{8,10},{9,11},{10,... | collective-permute-start | bytes 786440 | tf_op jit(solution)/shard_map/ppermute | solution.py:320
  79.9 12.8 %collective-permute-start.25 = (bf16[2,32,1920]{2,1,0:T(8,128)(2,1)S(1)}, bf16[2,32,1920]{2,1,0:T(8,128)(2,1)}, u32[]{:S(2)}, u32[]{:S(2)}) collective-permute-start(bf16[2,32,1920]{2,1,0:T(8,128)(2,1)S(1)} %fusion.24), channel_id=1, source_target_pairs={{0,16},{4,20},{8,24},{12,28},{16,0},{20,4},{24,8},{28,12},{1,17},{... | collective-permute-start | bytes 737288 | tf_op jit(solution)/shard_map/ppermute | solution.py:320
  89.7 28.4 %copy-start.10 = (bf16[1024,128]{1,0:T(8,128)(2,1)}, bf16[1024,128]{1,0:T(8,128)(2,1)S(1)}, u32[]{:S(2)}) copy-start(bf16[1024,128]{1,0:T(8,128)(2,1)S(1)} %collective-permute-done.19.refs_7_) | copy-start | bytes 786436
  94.8 6.4 %collective-permute-start.26 = (bf16[2,32,1920]{2,1,0:T(8,128)(2,1)}, bf16[2,32,1920]{2,1,0:T(8,128)(2,1)S(1)}, u32[]{:S(2)}, u32[]{:S(2)}) collective-permute-start(bf16[2,32,1920]{2,1,0:T(8,128)(2,1)} %get-tuple-element.84), channel_id=1, source_target_pairs={{0,8},{1,5},{2,10},{3,7},{4,12},{5,1},{6,14},{7,3},{8,0},{9,13},{1... | collective-permute-start | bytes 737288 | tf_op jit(solution)/shard_map/ppermute | solution.py:349
  94.8 11.2 %collective-permute-start.20 = (bf16[2,32,1920]{2,1,0:T(8,128)(2,1)S(1)}, bf16[2,32,1920]{2,1,0:T(8,128)(2,1)S(1)}, u32[]{:S(2)}, u32[]{:S(2)}) collective-permute-start(bf16[2,32,1920]{2,1,0:T(8,128)(2,1)S(1)} %get-tuple-element.85), channel_id=1, source_target_pairs={{0,8},{1,5},{2,10},{3,7},{4,12},{5,1},{6,14},{7,3},{8,0},{9,13},{1... | collective-permute-start | bytes 737288 | tf_op jit(solution)/shard_map/ppermute | solution.py:349
  102.3 9.0 %collective-permute-start.27 = (bf16[2,64,1920]{2,1,0:T(8,128)(2,1)S(1)}, bf16[2,64,1920]{2,1,0:T(8,128)(2,1)}, u32[]{:S(2)}, u32[]{:S(2)}) collective-permute-start(bf16[2,64,1920]{2,1,0:T(8,128)(2,1)S(1)} %pad_maximum_fusion.6), channel_id=1, source_target_pairs={{0,4},{1,9},{2,6},{3,11},{4,0},{5,13},{6,2},{7,15},{8,12},{9,1},{1... | collective-permute-start | bytes 1474568 | tf_op jit(solution)/shard_map/ppermute | solution.py:349
  106.9 9.6 %collective-permute-start.21 = (bf16[2,64,1920]{2,1,0:T(8,128)(2,1)}, bf16[2,64,1920]{2,1,0:T(8,128)(2,1)}, u32[]{:S(2)}, u32[]{:S(2)}) collective-permute-start(bf16[2,64,1920]{2,1,0:T(8,128)(2,1)} %pad_maximum_fusion.5), channel_id=1, source_target_pairs={{0,4},{1,9},{2,6},{3,11},{4,0},{5,13},{6,2},{7,15},{8,12},{9,1},{1... | collective-permute-start | bytes 1474568 | tf_op jit(solution)/shard_map/ppermute | solution.py:349
  107.6 10.5 %copy-start.1 = (bf16[1024,1920]{1,0:T(8,128)(2,1)S(1)}, bf16[1024,1920]{1,0:T(8,128)(2,1)}, u32[]{:S(2)}) copy-start(bf16[1024,1920]{1,0:T(8,128)(2,1)} %copy-done) | copy-start | bytes 11796484
  121.4 6.4 %collective-permute-start.28 = (bf16[1024,128]{1,0:T(8,128)(2,1)S(1)}, bf16[1024,128]{1,0:T(8,128)(2,1)S(1)}, u32[]{:S(2)}, u32[]{:S(2)}) collective-permute-start(bf16[1024,128]{1,0:T(8,128)(2,1)S(1)} %fusion), channel_id=1, source_target_pairs={{0,2},{1,3},{2,0},{3,1},{4,6},{5,7},{6,4},{7,5},{8,10},{9,11},{10,... | collective-permute-start | bytes 786440 | tf_op jit(solution)/shard_map/ppermute | solution.py:320
  124.0 24.1 %copy-start.13 = (s32[24,2]{1,0:T(8,128)S(1)}, s32[24,2]{1,0:T(8,128)}, u32[]{:S(2)}) copy-start(s32[24,2]{1,0:T(8,128)} %copy-done.12) | copy-start | bytes 580
  127.9 9.3 %collective-permute-start.29 = (bf16[1024,128]{1,0:T(8,128)(2,1)S(1)}, bf16[1024,128]{1,0:T(8,128)(2,1)}, u32[]{:S(2)}, u32[]{:S(2)}) collective-permute-start(bf16[1024,128]{1,0:T(8,128)(2,1)S(1)} %add_convert_fusion.refs_10_), channel_id=1, source_target_pairs={{4,0},{8,4},{12,8},{16,12},{20,16},{24,20},{28,24},{0,28},{5,1},{9... | collective-permute-start | bytes 786440 | tf_op jit(solution)/shard_map/ppermute | solution.py:326
  130.5 7.6 %collective-permute-start.30 = (bf16[1024,128]{1,0:T(8,128)(2,1)S(1)}, bf16[1024,128]{1,0:T(8,128)(2,1)S(1)}, u32[]{:S(2)}, u32[]{:S(2)}) collective-permute-start(bf16[1024,128]{1,0:T(8,128)(2,1)S(1)} %add_convert_fusion.refs_10_), channel_id=1, source_target_pairs={{0,2},{1,3},{2,0},{3,1},{4,6},{5,7},{6,4},{7,5},{8,10},{9,11},{10,... | collective-permute-start | bytes 786440 | tf_op jit(solution)/shard_map/ppermute | solution.py:320
  131.3 9.2 %collective-permute-start.32 = (bf16[1024,128]{1,0:T(8,128)(2,1)S(1)}, bf16[1024,128]{1,0:T(8,128)(2,1)}, u32[]{:S(2)}, u32[]{:S(2)}) collective-permute-start(bf16[1024,128]{1,0:T(8,128)(2,1)S(1)} %add_convert_fusion.refs_10_), channel_id=1, source_target_pairs={{0,4},{4,8},{8,12},{12,16},{16,20},{20,24},{24,28},{28,0},{1,5},{5... | collective-permute-start | bytes 786440 | tf_op jit(solution)/shard_map/ppermute | solution.py:325
  138.1 10.0 %collective-permute-start.34 = (bf16[1024,128]{1,0:T(8,128)(2,1)}, bf16[1024,128]{1,0:T(8,128)(2,1)S(1)}, u32[]{:S(2)}, u32[]{:S(2)}) collective-permute-start(bf16[1024,128]{1,0:T(8,128)(2,1)} %collective-permute-done.29.refs_12_), channel_id=1, source_target_pairs={{0,2},{1,3},{2,0},{3,1},{4,6},{5,7},{6,4},{7,5},{8,10},{9,11},{10,... | collective-permute-start | bytes 786440 | tf_op jit(solution)/shard_map/ppermute | solution.py:320
  140.5 7.6 %collective-permute-start.33 = (bf16[1024,128]{1,0:T(8,128)(2,1)}, bf16[1024,128]{1,0:T(8,128)(2,1)S(1)}, u32[]{:S(2)}, u32[]{:S(2)}) collective-permute-start(bf16[1024,128]{1,0:T(8,128)(2,1)} %collective-permute-done.32.refs_8_), channel_id=1, source_target_pairs={{0,2},{1,3},{2,0},{3,1},{4,6},{5,7},{6,4},{7,5},{8,10},{9,11},{10,... | collective-permute-start | bytes 786440 | tf_op jit(solution)/shard_map/ppermute | solution.py:320
  141.7 15.4 %copy-start.14 = (f32[24,256]{1,0:T(8,128)S(1)}, f32[24,256]{1,0:T(8,128)}, u32[]{:S(2)}) copy-start(f32[24,256]{1,0:T(8,128)} %scale_ref.1) | copy-start | bytes 73732
  141.8 15.4 %copy-start.15 = (s32[24]{0:T(128)S(1)}, s32[24]{0:T(128)}, u32[]{:S(2)}) copy-start(s32[24]{0:T(128)} %counts_ref.1) | copy-start | bytes 292
  142.6 14.5 %copy-start.5 = (bf16[24,256,128]{2,1,0:T(8,128)(2,1)S(1)}, bf16[24,256,128]{2,1,0:T(8,128)(2,1)}, u32[]{:S(2)}) copy-start(bf16[24,256,128]{2,1,0:T(8,128)(2,1)} %basis_ref.1) | copy-start | bytes 4718596
  142.6 11.9 %collective-permute-start.31 = (bf16[1024,256]{1,0:T(8,128)(2,1)}, bf16[1024,256]{1,0:T(8,128)(2,1)}, u32[]{:S(2)}, u32[]{:S(2)}) collective-permute-start(bf16[1024,256]{1,0:T(8,128)(2,1)} %pad_maximum_fusion.2), channel_id=1, source_target_pairs={{0,1},{1,0},{2,3},{3,2},{4,5},{5,4},{6,7},{7,6},{8,9},{9,8},{10,11... | collective-permute-start | bytes 1572872 | tf_op jit(solution)/shard_map/ppermute | solution.py:320
  154.5 2.6 %collective-permute-start.35 = (bf16[24,128,128]{2,1,0:T(8,128)(2,1)}, bf16[24,128,128]{2,1,0:T(8,128)(2,1)}, u32[]{:S(2)}, u32[]{:S(2)}) collective-permute-start(bf16[24,128,128]{2,1,0:T(8,128)(2,1)} %get-tuple-element.69), channel_id=1, source_target_pairs={{0,1},{1,0},{2,3},{3,2},{4,5},{5,4},{6,7},{7,6},{8,9},{9,8},{10,11... | collective-permute-start | bytes 2359304 | tf_op jit(solution)/shard_map/ppermute | solution.py:320
  (10 other events, 32.1 us)

commit v8 on v7

--- a/solution.py
+++ b/solution.py
@@ -13,6 +13,7 @@
 MIB = 1024 * 1024
 F32 = jnp.float32
 BF16 = jnp.bfloat16
+LANES = 128
 NT = (((1,), (1,)), ((), ()))
 
 
@@ -32,28 +33,6 @@
     for copy in started:
         copy.start()
     return started
-
-
-def load_kernel(source_ref, out_ref, semaphores):
-    rows = source_ref.shape[0] // semaphores.shape[0]
-    places = [pl.ds(i * rows, rows) for i in range(semaphores.shape[0])]
-    for copy in fetch([(source_ref.at[at], out_ref.at[at]) for at in places], semaphores):
-        copy.wait()
-
-
-def load(array):
-    parts = 4 if array.shape[0] % 64 == 0 else 1
-    return pl.pallas_call(
-        load_kernel,
-        out_shape=pltpu.VMEM(array.shape, array.dtype),
-        in_specs=[HBM],
-        out_specs=VMEM,
-        scratch_shapes=[pltpu.SemaphoreType.DMA((parts,))],
-        compiler_params=params(),
-        cost_estimate=pl.CostEstimate(
-            flops=0, bytes_accessed=2 * array.size * array.dtype.itemsize, transcendentals=0
-        ),
-    )(place_in(array, pltpu.HBM))
 
 
 def split_dot(full, other, dims):
@@ -184,16 +163,21 @@
     ]
 
 
-def apply_kernel(starts, rows, *refs):
+def apply_kernel(starts, far, rows, *refs):
     pieces = len(starts)
-    block_refs, ham_refs = refs[:pieces], refs[pieces : 2 * pieces]
+    block_refs, ham_refs = refs[:pieces], list(refs[pieces : 2 * pieces])
     window_refs = refs[2 * pieces : 2 * pieces + 3]
     out_before, out_own, out_after = refs[2 * pieces + 3 : 2 * pieces + 6]
-    window, total = refs[2 * pieces + 6 :]
+    window, total, semaphores, *held = refs[2 * pieces + 6 :]
+    waits = fetch([(ham_refs[p], target) for p, target in zip(far, held)], semaphores)
+    for p, target in zip(far, held):
+        ham_refs[p] = target
     region = window_refs[0].shape[0]
     for side, ref in enumerate(window_refs):
         window[side * region : (side + 1) * region] = ref[...]
     total[...] = jnp.zeros_like(total)
+    for copy in waits:
+        copy.wait()
 
     def steps(members, count):
         def step(b, carry):
@@ -223,97 +207,246 @@
     out_after[...] = total[2 * region :].astype(BF16)
 
 
-def apply_window(blocks, hams, starts, before, own, after):
+def apply_window(blocks, hams, starts, far, before, own, after):
     pieces, per_batch = len(hams), blocks[0].shape[1]
     columns = hams[0].shape[1]
     region, width = own.shape
     work = sum(ham.shape[0] for ham in hams)
     return pl.pallas_call(
-        functools.partial(apply_kernel, starts, columns // per_batch),
+        functools.partial(apply_kernel, starts, far, columns // per_batch),
         out_shape=[
             jax.ShapeDtypeStruct((region, width), BF16),
             jax.ShapeDtypeStruct((region, width), F32),
             jax.ShapeDtypeStruct((region, width), BF16),
         ],
-        in_specs=[SMEM] * pieces + [VMEM] * (pieces + 3),
+        in_specs=[SMEM] * pieces
+        + [HBM if p in far else VMEM for p in range(pieces)]
+        + [VMEM] * 3,
         out_specs=[VMEM] * 3,
         scratch_shapes=[
             pltpu.VMEM((3 * region, width), BF16),
             pltpu.VMEM((3 * region, width), F32),
-        ],
-        compiler_params=params(6),
+            pltpu.SemaphoreType.DMA((len(far),)),
+        ]
+        + [pltpu.VMEM(hams[p].shape, BF16) for p in far],
+        compiler_params=params(8),
         cost_estimate=pl.CostEstimate(
             flops=2 * work * columns * columns * width,
             bytes_accessed=work * columns * columns * 2 + 14 * region * width,
             transcendentals=0,
         ),
-    )(*blocks, *[place_in(array, pltpu.VMEM) for array in (*hams, before, own, after)])
-
-
-def overlap_kernel(pieces, rows, *refs):
-    block_refs = refs[:pieces]
-    sources = refs[pieces : pieces + 12]
-    out_refs = refs[pieces + 12 : 2 * pieces + 12]
-    occ, resp = refs[2 * pieces + 12 :]
+    )(
+        *blocks,
+        *[ham if p in far else place_in(ham, pltpu.VMEM) for p, ham in enumerate(hams)],
+        *[place_in(array, pltpu.VMEM) for array in (before, own, after)],
+    )
+
+
+def project_kernel(first_ref, ham_ref, *refs):
+    sources, (keep_ref, send_ref, held, semaphores) = refs[:2], refs[2:]
+    blocks = semaphores.shape[0] // 2
+    width = held.shape[2] // blocks
+    copies = []
+    for i in range(blocks):
+        place = (slice(None), pl.ds(i * width, width))
+        for share, source in enumerate(sources):
+            copies.append((source.at[place], held.at[(share, *place)]))
+    waits = fetch(copies, semaphores)
+    turned = ham_ref[...].astype(F32).T.astype(BF16)
+    half = turned.shape[0] // 2
+    low = first_ref[0] == 0
+    for i in range(blocks):
+        at = slice(i * width, (i + 1) * width)
+        for share in range(2):
+            waits[2 * i + share].wait()
+            product = jnp.dot(turned, held[share, :, at], preferred_element_type=F32)
+            keep_ref[share, :, at] = jnp.where(low, product[:half], product[half:])
+            send_ref[share, :, at] = jnp.where(low, product[half:], product[:half]).astype(BF16)
+
+
+def lane_block(size, most):
+    tiles = size // LANES
+    return LANES * max(k for k in range(1, tiles + 1) if tiles % k == 0 and k * LANES <= most)
+
+
+def project(first, ham, virtuals):
+    region, width = ham.shape
+    virt = virtuals[0].shape[1]
+    blocks = virt // lane_block(virt, 512)
+    return pl.pallas_call(
+        project_kernel,
+        out_shape=[
+            jax.ShapeDtypeStruct((2, width // 2, virt), F32),
+            jax.ShapeDtypeStruct((2, width // 2, virt), BF16),
+        ],
+        in_specs=[SMEM, VMEM, HBM, HBM],
+        out_specs=[VMEM, VMEM],
+        scratch_shapes=[
+            pltpu.VMEM((2, region, virt), BF16),
+            pltpu.SemaphoreType.DMA((2 * blocks,)),
+        ],
+        compiler_params=params(14),
+        cost_estimate=pl.CostEstimate(
+            flops=4 * region * width * virt,
+            bytes_accessed=4 * region * virt + 6 * width * virt,
+            transcendentals=0,
+        ),
+    )(first.reshape(1), ham, place_in(virtuals[0], pltpu.HBM), virtuals[1])
+
+
+def expand_kernel(first_ref, part_ref, coming_ref, *refs):
+    sources, (out_ref, held, semaphores) = refs[:2], refs[-3:]
+    blocks = semaphores.shape[0] // 2
+    rows = held.shape[1] // blocks
+    copies = []
+    for i in range(blocks):
+        place = pl.ds(i * rows, rows)
+        for share, source in enumerate(sources):
+            copies.append((source.at[place], held.at[share, place]))
+    waits = fetch(copies, semaphores)
+    low = first_ref[0] == 0
+    rotations = []
+    for share in range(2):
+        part, coming = part_ref[share], coming_ref[share]
+        halves = [jnp.where(low, part, coming), jnp.where(low, coming, part)]
+        rotations.append(jnp.concatenate(halves, axis=0))
+    for i in range(blocks):
+        at = slice(i * rows, (i + 1) * rows)
+        total = None
+        for share in range(2):
+            waits[2 * i + share].wait()
+            product = lax.dot_general(
+                held[share, at], rotations[share], NT, preferred_element_type=F32
+            )
+            total = product if total is None else total + product
+        out_ref[at] = total.astype(out_ref.dtype)
+
+
+def expand(first, part, coming, virtuals, kind, ahead):
+    region, virt = virtuals[0].shape
+    width = 2 * part.shape[1]
+    blocks = 4 if region % 64 == 0 and region > 64 else 1
+    return pl.pallas_call(
+        expand_kernel,
+        out_shape=jax.ShapeDtypeStruct((region, width), kind),
+        in_specs=[SMEM, VMEM, VMEM, HBM, HBM] + [HBM] * len(ahead),
+        out_specs=VMEM,
+        scratch_shapes=[
+            pltpu.VMEM((2, region, virt), BF16),
+            pltpu.SemaphoreType.DMA((2 * blocks,)),
+        ],
+        compiler_params=params(14),
+        cost_estimate=pl.CostEstimate(
+            flops=4 * region * width * virt if kind == BF16 else 0,
+            bytes_accessed=4 * region * virt if kind == BF16 else 0,
+            transcendentals=0,
+        ),
+    )(first.reshape(1), part, coming, place_in(virtuals[0], pltpu.HBM), virtuals[1], *ahead)
+
+
+def overlap_steps(block_ref, occ_ref, resp_ref, out_ref, rows):
+    def step(b, carry):
+        place = row_places(block_ref, b, rows)
+        left = jnp.concatenate([resp_ref[at, :] for at in place], axis=0)
+        right = jnp.concatenate([occ_ref[at, :] for at in place], axis=0)
+        product = lax.dot_general(left, right, NT, preferred_element_type=F32)
+        out_ref[b] = product.astype(out_ref.dtype)
+        return carry
+
+    lax.fori_loop(0, out_ref.shape[0], step, 0, unroll=8)
+
+
+def gather_kernel(rows, block_ref, *refs):
+    sources, (out_ref, occ_ref, resp_ref, semaphores) = refs[:12], refs[12:]
     region, width = sources[0].shape
+    copies = []
     for i, source in enumerate(sources):
-        target, side, part = (occ, resp)[i // 6], i % 6 // 2, i % 2
-        target[side * region : (side + 1) * region, part * width : (part + 1) * width] = source[...]
-
-    def step(b, carry):
-        for p in range(pieces):
-            place = row_places(block_refs[p], b, rows)
-            left = jnp.concatenate([resp[at, :] for at in place], axis=0)
-            right = jnp.concatenate([occ[at, :] for at in place], axis=0)
-            product = lax.dot_general(left, right, NT, preferred_element_type=F32)
-            out_refs[p][b] = product.astype(out_refs[p].dtype)
-        return carry
-
-    lax.fori_loop(0, out_refs[0].shape[0], step, 0, unroll=4)
-
-
-def overlaps(blocks, columns, occ_parts, resp_parts, types):
-    pieces = len(blocks)
-    nbatch, per_batch = blocks[0].shape
+        target, side, part = (occ_ref, resp_ref)[i // 6], i % 6 // 2, i % 2
+        place = (pl.ds(side * region, region), pl.ds(part * width, width))
+        copies.append((source, target.at[place]))
+    for copy in fetch(copies, semaphores):
+        copy.wait()
+    overlap_steps(block_ref, occ_ref, resp_ref, out_ref, rows)
+
+
+def gather_overlaps(blocks, columns, occ_parts, resp_parts):
+    nbatch, per_batch = blocks.shape
     region, width = occ_parts[0].shape
     return pl.pallas_call(
-        functools.partial(overlap_kernel, pieces, columns // per_batch),
-        out_shape=[pltpu.VMEM((nbatch, columns, columns), kind) for kind in types],
-        in_specs=[SMEM] * pieces + [VMEM] * 12,
-        out_specs=[VMEM] * pieces,
-        scratch_shapes=[pltpu.VMEM((3 * region, 2 * width), BF16)] * 2,
-        compiler_params=params(8),
-        cost_estimate=pl.CostEstimate(
-            flops=4 * pieces * nbatch * columns * columns * width,
-            bytes_accessed=24 * region * width + pieces * nbatch * columns * columns * 3,
-            transcendentals=0,
-        ),
-    )(*blocks, *[place_in(array, pltpu.VMEM) for array in (*occ_parts, *resp_parts)])
-
-
-def density_kernel(counts_ref, basis_ref, first_ref, second_ref, scale_ref, out_ref):
+        functools.partial(gather_kernel, columns // per_batch),
+        out_shape=[jax.ShapeDtypeStruct((nbatch, columns, columns), BF16)]
+        + [pltpu.VMEM((3 * region, 2 * width), BF16)] * 2,
+        in_specs=[SMEM] + [HBM] * 12,
+        out_specs=[VMEM] * 3,
+        scratch_shapes=[pltpu.SemaphoreType.DMA((12,))],
+        compiler_params=params(),
+        cost_estimate=pl.CostEstimate(
+            flops=4 * nbatch * columns * columns * width,
+            bytes_accessed=24 * region * width + nbatch * columns * columns * 2,
+            transcendentals=0,
+        ),
+    )(blocks, *occ_parts, *resp_parts)
+
+
+def overlap_kernel(rows, block_ref, occ_ref, resp_ref, out_ref):
+    overlap_steps(block_ref, occ_ref, resp_ref, out_ref, rows)
+
+
+def overlaps(blocks, columns, occ_window, resp_window):
+    nbatch, per_batch = blocks.shape
+    return pl.pallas_call(
+        functools.partial(overlap_kernel, columns // per_batch),
+        out_shape=pltpu.VMEM((nbatch, columns, columns), F32),
+        in_specs=[SMEM, VMEM, VMEM],
+        out_specs=VMEM,
+        compiler_params=params(),
+        cost_estimate=pl.CostEstimate(
+            flops=2 * nbatch * columns * columns * occ_window.shape[1],
+            bytes_accessed=nbatch * columns * columns * 4,
+            transcendentals=0,
+        ),
+    )(blocks, place_in(occ_window, pltpu.VMEM), place_in(resp_window, pltpu.VMEM))
+
+
+def density_kernel(
+    core_ref, counts_ref, basis_ref, first_ref, second_ref, scale_ref, half_ref, near_ref,
+    out_ref, coef_ref, semaphores,
+):
+    width = half_ref.shape[1]
+    copies = []
+    for source, place in ((half_ref, core_ref[0]), (near_ref, 1 - core_ref[0])):
+        columns = pl.ds(pl.multiple_of(place * width, width), width)
+        copies.append((source, coef_ref.at[:, columns]))
+    waits = fetch(copies, semaphores)
     for b in range(basis_ref.shape[0]):
         values = basis_ref[b]
         overlap = first_ref[b] + second_ref[b].astype(F32)
         product = split_dot(overlap, values, NT)
         density = 4.0 * jnp.sum(product * values.astype(F32).T, axis=0, keepdims=True)
         out_ref[b : b + 1, :] = live_row(scale_ref, counts_ref, b) * density
-
-
-def density(basis_values, counts, first, second, scale):
+    for copy in waits:
+        copy.wait()
+
+
+def density(core, basis_values, counts, first, second, scale, half, half_near):
     nbatch, points, columns = basis_values.shape
+    region, width = half.shape
     return pl.pallas_call(
         density_kernel,
-        out_shape=jax.ShapeDtypeStruct((nbatch, points), F32),
-        in_specs=[SMEM] + [VMEM] * 4,
-        out_specs=VMEM,
+        out_shape=[
+            jax.ShapeDtypeStruct((nbatch, points), F32),
+            jax.ShapeDtypeStruct((region, 2 * width), BF16),
+        ],
+        in_specs=[SMEM] * 2 + [VMEM] * 4 + [HBM] * 2,
+        out_specs=[VMEM, HBM],
+        scratch_shapes=[pltpu.SemaphoreType.DMA((2,))],
         compiler_params=params(),
         cost_estimate=pl.CostEstimate(
             flops=4 * nbatch * points * columns * columns,
             bytes_accessed=basis_values.size * 2 + nbatch * columns * columns * 6,
             transcendentals=0,
         ),
-    )(counts, basis_values, first, second, scale)
+    )(core.reshape(1), counts, basis_values, place_in(first, pltpu.VMEM), second, scale, half, half_near)
 
 
 def flip(array, axis, mask):
@@ -354,14 +487,14 @@
 
 
 class Reduction:
-    def __init__(self, part, level, energy):
+    def __init__(self, ham, virtuals, level, energy):
         grid, core = lax.axis_index("grid"), lax.axis_index("tile") % 2
         self.masks = (1, 2), (2, 1)
         self.first, self.second = (grid >> core) & 1, (grid >> (1 - core)) & 1
         self.level, self.energy = level, energy
-        self.half = part.shape[1] // 2
-        self.keep, send = trade(part, self.half, self.first)
-        self.coming = swap(send, self.masks[0])
+        self.half, self.virtuals = ham.shape[1] // 2, virtuals
+        self.keep, self.send = project(self.first, ham, virtuals)
+        self.coming = swap(self.send, self.masks[0])
 
     def narrow(self):
         total = self.keep + self.coming.astype(F32)
@@ -381,8 +514,8 @@
         self.part = join(own, swap(own, self.masks[1]), self.second)
         self.coming = swap(self.part, self.masks[0])
 
-    def result(self):
-        return join(self.part, self.coming, self.first)
+    def result(self, kind, *ahead):
+        return expand(self.first, self.part, self.coming, self.virtuals, kind, ahead)
 
 
 def per_device(
@@ -406,29 +539,29 @@
     occ_own = column_part(occ_coef, quarter, width)
 
     lists = [blocks, flip(blocks, "tile", 1), flip(blocks, "tile", 2)]
-    fulls, arrived, weights = [], [], weighted_potential
-    for i, size in enumerate(groups(nbatch)):
-        full, packed = integrate(basis_values, counts, weights, sum(groups(nbatch)[:i]), size)
+    occ_before, occ_after = neighbours(occ_own)
+    sizes, fulls, arrived = groups(nbatch), [], []
+    for i, size in enumerate(sizes):
+        full, packed = integrate(basis_values, counts, weighted_potential, sum(sizes[:i]), size)
+        fulls.append(full)
         arrived.append(flip(packed, "tile", 2))
-        if i == 0:
-            occ_own, full = together(occ_own, full)
-            occ_before, occ_after = neighbours(occ_own)
-            weights, lists = together(weights, lists)
-        fulls.append(full)
+    arrived[0], occ_before, occ_after = together(arrived[0], occ_before, occ_after)
+    arrived[-1], lists[2] = together(arrived[-1], lists[2])
     lists.append(flip(lists[2], "tile", 1))
     hams, places, starts = [], [], []
-    for i, size in enumerate(groups(nbatch)):
+    for i, size in enumerate(sizes):
         far = unpack(arrived[i], size, columns)
         hams += [fulls[i], flip(fulls[i], "tile", 1), far, flip(far, "tile", 1)]
-        places, starts = places + lists, starts + [sum(groups(nbatch)[:i])] * 4
+        places, starts = places + lists, starts + [sum(sizes[:i])] * 4
     blocks_near = lists[1]
-    virtuals = [load(virt_coef), load(flip(virt_coef, "tile", 1))]
+    virtuals = [virt_coef, flip(virt_coef, "tile", 1)]
     energies = jnp.stack([virt_energy, flip(virt_energy, "tile", 1)])
 
     to_before, own_sum, to_after = apply_window(
         places,
         hams,
         starts,
+        [p for p in range(len(hams)) if p % 2 == 1],
         occ_before,
         occ_own,
         occ_after,
@@ -437,30 +570,17 @@
         lax.dynamic_slice_in_dim(occ_energy, place * width, width, 0)
         for place in (quarter, quarter ^ 1)
     ]
-    own_sum, energies, levels, virtuals = lax.optimization_barrier(
-        (own_sum, energies, levels, virtuals)
-    )
+    own_sum, energies, levels = together(own_sum, energies, levels)
     size = lax.axis_size("grid")
     from_before = lax.ppermute(to_after, "grid", [(i, (i + 1) % size) for i in range(size)])
     from_after = lax.ppermute(to_before, "grid", [((i + 1) % size, i) for i in range(size)])
     ham_own = (own_sum + from_before.astype(F32) + from_after.astype(F32)).astype(BF16)
 
+    ham_far = flip(ham_own, "tile", 2)
     occ_far = column_part(occ_coef, quarter ^ 1, width)
-
-    def products(ham_sum):
-        dots = [
-            lax.dot_general(ham_sum, virt, (((0,), (0,)), ((), ())), preferred_element_type=F32)
-            for virt in virtuals
-        ]
-        return jnp.stack(dots)
-
-    own_part = products(ham_own)
-    ham_late, _ = together(ham_own, own_part)
-    ham_far = flip(ham_late, "tile", 2)
-    far_part = products(ham_far)
     if lax.axis_size("grid") == 8:
-        own = Reduction(own_part, levels[0], energies)
-        far = Reduction(far_part, levels[1], energies)
+        own = Reduction(ham_own, virtuals, levels[0], energies)
+        far = Reduction(ham_far, virtuals, levels[1], energies)
         own.narrow()
         far.narrow()
         far.cross()
@@ -470,26 +590,25 @@
         own.coming, before_far, after_far = together(own.coming, before_far, after_far)
         own.divide()
         far.divide()
-        rotated = [own.result(), far.result()]
+        coef_far = far.result(BF16)
+        coef_own = own.result(F32, coef_far)
     else:
-        rotated = [
-            (
-                lax.psum(part, "grid") / (level[None, :, None] - energies[:, None, :])
-            ).astype(BF16)
-            for part, level in zip((own_part, far_part), levels)
-        ]
         before_far, after_far = flip(occ_before, "tile", 2), flip(occ_after, "tile", 2)
-
-    coefs = []
-    for rotation in rotated:
-        terms = [
-            lax.dot_general(virt, rotation[i], NT, preferred_element_type=F32)
-            for i, virt in enumerate(virtuals)
-        ]
-        coefs.append(terms[0] + terms[1])
-    coef_own, coef_far = lax.optimization_barrier(
-        (coefs[0], flip(coefs[1].astype(BF16), "tile", 2))
-    )
+        coefs = []
+        for ham_sum, level in ((ham_own, levels[0]), (ham_far, levels[1])):
+            products = [
+                lax.dot_general(ham_sum, virt, (((0,), (0,)), ((), ())), preferred_element_type=F32)
+                for virt in virtuals
+            ]
+            total = lax.psum(jnp.stack(products), "grid")
+            rotation = (total / (level[None, :, None] - energies[:, None, :])).astype(BF16)
+            terms = [
+                lax.dot_general(virt, rotation[i], NT, preferred_element_type=F32)
+                for i, virt in enumerate(virtuals)
+            ]
+            coefs.append(terms[0] + terms[1])
+        coef_own, coef_far = coefs[0], coefs[1].astype(BF16)
+    coef_own, coef_far = together(coef_own, flip(coef_far, "tile", 2))
     resp_own = (coef_own + coef_far.astype(F32)).astype(BF16)
 
     resp_before, resp_after = neighbours(resp_own)
@@ -500,20 +619,21 @@
     half = jnp.concatenate(
         [jnp.where(first, resp_own, resp_far), jnp.where(first, resp_far, resp_own)], axis=1
     )
-    overlap_own, overlap_near = overlaps(
-        [blocks, blocks_near],
+    overlap_near, occ_window, resp_window = gather_overlaps(
+        blocks_near,
         columns,
         [occ_before, before_far, occ_own, occ_far, occ_after, after_far],
         [resp_before, resp_before_far, resp_own, resp_far, resp_after, resp_after_far],
-        [F32, BF16],
-    )
-    half_near, overlap_own = together(flip(half, "tile", 1), overlap_own)
-    first = core == 0
-    response_coef = jnp.concatenate(
-        [jnp.where(first, half, half_near), jnp.where(first, half_near, half)], axis=1
-    )
-    response_potential = density(
-        basis_values, counts, overlap_own, flip(overlap_near, "tile", 1), xc_kernel
+    )
+    response_potential, response_coef = density(
+        core,
+        basis_values,
+        counts,
+        overlaps(blocks, columns, occ_window, resp_window),
+        flip(overlap_near, "tile", 1),
+        xc_kernel,
+        half,
+        flip(half, "tile", 1),
     )
     return (response_coef, response_potential)
 

time: 160 us -> 160 us (level)
  Pallas kernels: 22.8 us -> 36.1 us
  matrix products: 7.69 us -> 0 us
  starting transfers between devices: 30.2 us -> 37.5 us
  local copies, waits for them, and re-layouts: 8.97 us -> 2.17 us
  other arithmetic: 10.4 us -> 5.63 us
  waiting for transfers between devices: 78.8 us -> 76.9 us
    pallas_call x5 -> x8, Pallas kernels: 16.7 us -> 30 us  [the longest x2 9.13 us: expand(): pl.pallas_call(expand_kernel, out_shape=jax.ShapeDtypeStruct((region, wid...]
    ppermute x8, waiting for transfers between devices: 32.4 us -> 22 us  [swap(): return lax.ppermute(array, ('grid', 'tile'), pairs)]
    dot_general x8 -> x0, matrix products: 7.69 us -> none  [the longest x4 4.72 us: per_device(): lax.dot_general(virt, rotation[i], NT, preferred_element_type=F32)]
    ppermute x1, waiting for transfers between devices: 0.01 us -> 7 us  [per_device(): lax.ppermute(to_after, 'grid', [(i, (i + 1) % size) for i in range(size)])]
    unnamed x45 -> x13, local copies, waits for them, and re-layouts: 7.5 us -> 0.78 us
    ppermute x22, waiting for transfers between devices: 33 us -> 39.3 us  [flip(): lax.ppermute(array, axis, [(i, i ^ mask) for i in range(lax.axis_size(axi...]
    ppermute x8, starting transfers between devices: 3.71 us -> 7.58 us  [swap(): return lax.ppermute(array, ('grid', 'tile'), pairs)]
    ppermute x1, waiting for transfers between devices: 5.9 us -> 2.44 us  [per_device(): lax.ppermute(to_before, 'grid', [((i + 1) % size, i) for i in range(size)])]
  transfers between devices with their start and end apart: 36 -> 36, of which waited for: 22 -> 22; matrix products, arithmetic and copies ran while one was open for 9% -> 3% of each run, Pallas kernels for 12% -> 17%
where the time goes in v8:
time: 160 us; the launch traced here: 159 us
  waiting for transfers between devices  76.9 us (48%)
  starting transfers between devices  37.5 us (23%)
  Pallas kernels  36.1 us (23%)
  other arithmetic  5.63 us (4%)
  local copies, waits for them, and re-layouts  2.17 us (1%)
    ppermute x22, waiting for transfers between devices, flip(): lax.ppermute(array, axis, [(i, i ^ mask) for i in range(lax.axis_size(axi...  39.3 us
    ppermute x8, waiting for transfers between devices, swap(): return lax.ppermute(array, ('grid', 'tile'), pairs)  22 us
    ppermute x22, starting transfers between devices, flip(): lax.ppermute(array, axis, [(i, i ^ mask) for i in range(lax.axis_size(axi...  16.8 us
    pallas_call x2, Pallas kernels, expand(): pl.pallas_call(expand_kernel, out_shape=jax.ShapeDtypeStruct((region, wid...  9.13 us
    pallas_call x2, Pallas kernels, project(): pl.pallas_call(project_kernel, out_shape=[jax.ShapeDtypeStruct((2, width...  8.48 us
    ppermute x2, starting transfers between devices, neighbours(): lax.ppermute(array, 'grid', [((i + 1) % size, i) for i in range(size)])  8.36 us
    ppermute x8, starting transfers between devices, swap(): return lax.ppermute(array, ('grid', 'tile'), pairs)  7.58 us
    ppermute x1, waiting for transfers between devices, per_device(): lax.ppermute(to_after, 'grid', [(i, (i + 1) % size) for i in range(size)])  7 us
  transfers between devices with their start and end apart: 36, of which 22 were waited for; matrix products, arithmetic and copies ran while one was open for 3% of the time, Pallas kernels for 17%

profile of v8, /device:TPU:0, one launch (start us, length us, event | category | flops | bytes accessed | tf_op | source)
XLA Modules:
  0.0 159.4 jit_solution(6131578851505645234)
XLA Ops:
  1.1 1.1 constant_dynamic-slice_fusion
  2.2 5.7 %collective-permute-start.7 = (bf16[1024,128]{1,0:T(8,128)(2,1)S(1)}, bf16[1024,128]{1,0:T(8,128)(2,1)S(1)}, u32[]{:S(2)}, u32[]{:S(2)}) collective-permute-start(bf16[1024,128]{1,0:T(8,128)(2,1)S(1)} %get-tuple-element.73.refs_17_.refs_2_), channel_id=1, source_target_pairs={{4,0},{8,4},{12,8},{16,12},{20,16},{24,20},{28,24},{0,28},{5,1},{9... | collective-permute-start | bytes 786440 | tf_op jit(solution)/shard_map/ppermute | solution.py:459
  7.9 0.8 copy.15.refs_0_.refs_4_.block_ref
  8.6 1.5 collective-permute-start.2
  10.1 2.2 %shard_map.104 = (bf16[12,128,128]{2,1,0:T(8,128)(2,1)S(1)}, bf16[800,128]{1,0:T(8,128)(2,1)S(1)}) custom-call(s32[24]{0:T(128)} %counts_ref.1, bf16[24,256,128]{2,1,0:T(8,128)(2,1)} %basis_ref.1, f32[24,256]{1,0:T(8,128)} %weights_hbm.3), custom_call_target="tpu_custom_call" | custom-call | flops 201326592 | bytes 1376256 | tf_op jit(solution)/shard_map/pallas_call | solution.py:99
  12.9 2.2 %shard_map.105 = (bf16[12,128,128]{2,1,0:T(8,128)(2,1)S(1)}, bf16[800,128]{1,0:T(8,128)(2,1)S(1)}) custom-call(s32[24]{0:T(128)} %counts_ref.1, bf16[24,256,128]{2,1,0:T(8,128)(2,1)} %basis_ref.1, f32[24,256]{1,0:T(8,128)} %weights_hbm.3), custom_call_target="tpu_custom_call" | custom-call | flops 201326592 | bytes 1376256 | tf_op jit(solution)/shard_map/pallas_call | solution.py:99
  15.1 1.5 collective-permute-start.5
  16.7 3.7 %collective-permute-done.1.packed_ref = bf16[800,128]{1,0:T(8,128)(2,1)S(1)} collective-permute-done((bf16[800,128]{1,0:T(8,128)(2,1)S(1)}, bf16[800,128]{1,0:T(8,128)(2,1)S(1)}, u32[]{:S(2)}, u32[]{:S(2)}) %collective-permute-start.1) | collective-permute-done | bytes 204832 | tf_op jit(solution)/shard_map/ppermute | solution.py:453
  20.4 0.9 shard_map.107.refs_14_
  21.3 2.4 %collective-permute-done.5.packed_ref = bf16[800,128]{1,0:T(8,128)(2,1)S(1)} collective-permute-done((bf16[800,128]{1,0:T(8,128)(2,1)S(1)}, bf16[800,128]{1,0:T(8,128)(2,1)S(1)}, u32[]{:S(2)}, u32[]{:S(2)}) %collective-permute-start.5) | collective-permute-done | bytes 204832 | tf_op jit(solution)/shard_map/ppermute | solution.py:453
  24.3 0.9 shard_map.106.refs_10_
  27.7 5.2 %shard_map.108 = (bf16[1024,128]{1,0:T(8,128)(2,1)S(1)}, f32[1024,128]{1,0:T(8,128)S(1)}, bf16[1024,128]{1,0:T(8,128)(2,1)S(1)}) custom-call(s32[24,2]{1,0:T(8,128)S(1)} %copy.15.refs_0_.refs_4_.block_ref, s32[24,2]{1,0:T(8,128)S(1)} %collective-permute-done.refs_1_.refs_5_.block_ref, s32[24,2]{1,0:T(8,128)S(1)} %collective-permute-done.2.refs_2_.refs_6_, ...), custom_call_target="tpu_custom_call" | custom-call | flops 402653184 | bytes 4980736 | tf_op jit(solution)/shard_map/pallas_call | solution.py:215
  33.0 4.7 %collective-permute-start.13 = (bf16[1024,128]{1,0:T(8,128)(2,1)S(1)}, bf16[1024,128]{1,0:T(8,128)(2,1)S(1)}, u32[]{:S(2)}, u32[]{:S(2)}) collective-permute-start(bf16[1024,128]{1,0:T(8,128)(2,1)S(1)} %get-tuple-element.49), channel_id=1, source_target_pairs={{4,0},{8,4},{12,8},{16,12},{20,16},{24,20},{28,24},{0,28},{5,1},{9... | collective-permute-start | bytes 786440 | tf_op jit(solution)/shard_map/ppermute | solution.py:576
  37.9 7.0 %collective-permute-done.12 = bf16[1024,128]{1,0:T(8,128)(2,1)S(1)} collective-permute-done((bf16[1024,128]{1,0:T(8,128)(2,1)S(1)}, bf16[1024,128]{1,0:T(8,128)(2,1)S(1)}, u32[]{:S(2)}, u32[]{:S(2)}) %collective-permute-start.12) | collective-permute-done | bytes 262176 | tf_op jit(solution)/shard_map/ppermute | solution.py:575
  44.9 2.4 %collective-permute-done.13 = bf16[1024,128]{1,0:T(8,128)(2,1)S(1)} collective-permute-done((bf16[1024,128]{1,0:T(8,128)(2,1)S(1)}, bf16[1024,128]{1,0:T(8,128)(2,1)S(1)}, u32[]{:S(2)}, u32[]{:S(2)}) %collective-permute-start.13) | collective-permute-done | bytes 262176 | tf_op jit(solution)/shard_map/ppermute | solution.py:576
  47.4 4.2 %shard_map.109 = (f32[2,64,1920]{2,1,0:T(8,128)S(1)}, bf16[2,64,1920]{2,1,0:T(8,128)(2,1)S(1)}) custom-call(s32[1]{0:T(128)} %bitcast.1.first_ref, bf16[1024,128]{1,0:T(8,128)(2,1)S(1)} %add_convert_fusion.1.ham_ref, bf16[1024,1920]{1,0:T(8,128)(2,1)} %refs_0_.8, bf16[1024,1920]{1,0:T(8,128)(2,1)} %collective-permute-done.14.refs_1_), custom_call_target="tpu_custom_call" | custom-call | flops 1006632960 | bytes 9338880 | tf_op jit(solution)/shard_map/pallas_call | solution.py:276
  52.3 7.1 %collective-permute-done.22.ham_ref = bf16[1024,128]{1,0:T(8,128)(2,1)S(1)} collective-permute-done((bf16[1024,128]{1,0:T(8,128)(2,1)S(1)}, bf16[1024,128]{1,0:T(8,128)(2,1)S(1)}, u32[]{:S(2)}, u32[]{:S(2)}) %collective-permute-start.22) | collective-permute-done | bytes 262176 | tf_op jit(solution)/shard_map/ppermute | solution.py:453
  59.4 4.2 %shard_map.110 = (f32[2,64,1920]{2,1,0:T(8,128)S(1)}, bf16[2,64,1920]{2,1,0:T(8,128)(2,1)S(1)}) custom-call(s32[1]{0:T(128)} %bitcast.1.first_ref, bf16[1024,128]{1,0:T(8,128)(2,1)S(1)} %collective-permute-done.22.ham_ref, bf16[1024,1920]{1,0:T(8,128)(2,1)} %refs_0_.8, bf16[1024,1920]{1,0:T(8,128)(2,1)} %collective-permute-done.14.refs_1_), custom_call_target="tpu_custom_call" | custom-call | flops 1006632960 | bytes 9338880 | tf_op jit(solution)/shard_map/pallas_call | solution.py:276
  63.7 0.8 collective-permute-start.23
  64.4 1.1 convert_add_fusion.1
  65.6 1.4 collective-permute-start.16
  67.0 8.2 %collective-permute-done.23 = bf16[2,64,1920]{2,1,0:T(8,128)(2,1)S(1)} collective-permute-done((bf16[2,64,1920]{2,1,0:T(8,128)(2,1)S(1)}, bf16[2,64,1920]{2,1,0:T(8,128)(2,1)S(1)}, u32[]{:S(2)}, u32[]{:S(2)}) %collective-permute-start.23) | collective-permute-done | bytes 491552 | tf_op jit(solution)/shard_map/ppermute | solution.py:482
  75.3 1.4 collective-permute-start.24
  76.8 3.7 %collective-permute-start.17 = (bf16[2,32,1920]{2,1,0:T(8,128)(2,1)S(1)}, bf16[2,32,1920]{2,1,0:T(8,128)(2,1)}, u32[]{:S(2)}, u32[]{:S(2)}) collective-permute-start(bf16[2,32,1920]{2,1,0:T(8,128)(2,1)S(1)} %fusion), channel_id=1, source_target_pairs={{0,16},{4,20},{8,24},{12,28},{16,0},{20,4},{24,8},{28,12},{1,17},{... | collective-permute-start | bytes 737288 | tf_op jit(solution)/shard_map/ppermute | solution.py:453
  81.0 1.5 collective-permute-start.19
  82.5 2.5 %collective-permute-done.24 = bf16[2,32,1920]{2,1,0:T(8,128)(2,1)S(1)} collective-permute-done((bf16[2,32,1920]{2,1,0:T(8,128)(2,1)S(1)}, bf16[2,32,1920]{2,1,0:T(8,128)(2,1)S(1)}, u32[]{:S(2)}, u32[]{:S(2)}) %collective-permute-start.24) | collective-permute-done | bytes 245792 | tf_op jit(solution)/shard_map/ppermute | solution.py:482
  86.6 8.8 %collective-permute-done.17 = bf16[2,32,1920]{2,1,0:T(8,128)(2,1)} collective-permute-done((bf16[2,32,1920]{2,1,0:T(8,128)(2,1)S(1)}, bf16[2,32,1920]{2,1,0:T(8,128)(2,1)}, u32[]{:S(2)}, u32[]{:S(2)}) %collective-permute-start.17) | collective-permute-done | bytes 245792 | tf_op jit(solution)/shard_map/ppermute | solution.py:453
  95.4 3.8 %collective-permute-done.25 = bf16[2,32,1920]{2,1,0:T(8,128)(2,1)} collective-permute-done((bf16[2,32,1920]{2,1,0:T(8,128)(2,1)}, bf16[2,32,1920]{2,1,0:T(8,128)(2,1)}, u32[]{:S(2)}, u32[]{:S(2)}) %collective-permute-start.25) | collective-permute-done | bytes 245792 | tf_op jit(solution)/shard_map/ppermute | solution.py:453
  99.2 2.2 %divide_convert_fusion = (bf16[2,32,1920]{2,1,0:T(8,128)(2,1)}, bf16[2,32,1920]{2,1,0:T(8,128)(2,1)S(1)}) fusion(bf16[2,32,1920]{2,1,0:T(8,128)(2,1)} %collective-permute-done.25, bf16[2,32,1920]{2,1,0:T(8,128)(2,1)S(1)} %collective-permute-done.24, f32[2,64,1920]{2,1,0:T(8,128)} %copy-done.3, s32[]{:T(128)S(6)} %select_n.71, f32[32]{0:T(128)S(1)} %dynamic_slice.39, ...), kind=kLoop, calls=%fused_computation.7 | loop fusion | flops 1720320 | bytes 2473220 | tf_op jit(solution)/shard_map/convert_element_type | solution.py:513
  101.4 2.0 %collective-permute-start.20 = (bf16[2,32,1920]{2,1,0:T(8,128)(2,1)S(1)}, bf16[2,32,1920]{2,1,0:T(8,128)(2,1)S(1)}, u32[]{:S(2)}, u32[]{:S(2)}) collective-permute-start(bf16[2,32,1920]{2,1,0:T(8,128)(2,1)S(1)} %get-tuple-element.81), channel_id=1, source_target_pairs={{0,8},{1,5},{2,10},{3,7},{4,12},{5,1},{6,14},{7,3},{8,0},{9,13},{1... | collective-permute-start | bytes 737288 | tf_op jit(solution)/shard_map/ppermute | solution.py:482
  103.4 4.4 %collective-permute-done.26 = bf16[2,32,1920]{2,1,0:T(8,128)(2,1)S(1)} collective-permute-done((bf16[2,32,1920]{2,1,0:T(8,128)(2,1)}, bf16[2,32,1920]{2,1,0:T(8,128)(2,1)S(1)}, u32[]{:S(2)}, u32[]{:S(2)}) %collective-permute-start.26) | collective-permute-done | bytes 245792 | tf_op jit(solution)/shard_map/ppermute | solution.py:482
  107.8 1.0 broadcast_select_fusion.3
  108.9 0.9 collective-permute-start.27
  109.8 1.7 %collective-permute-done.20 = bf16[2,32,1920]{2,1,0:T(8,128)(2,1)S(1)} collective-permute-done((bf16[2,32,1920]{2,1,0:T(8,128)(2,1)S(1)}, bf16[2,32,1920]{2,1,0:T(8,128)(2,1)S(1)}, u32[]{:S(2)}, u32[]{:S(2)}) %collective-permute-start.20) | collective-permute-done | bytes 245792 | tf_op jit(solution)/shard_map/ppermute | solution.py:482
  111.6 1.0 collective-permute-start.21
  112.6 5.2 %collective-permute-done.27.coming_ref = bf16[2,64,1920]{2,1,0:T(8,128)(2,1)S(1)} collective-permute-done((bf16[2,64,1920]{2,1,0:T(8,128)(2,1)S(1)}, bf16[2,64,1920]{2,1,0:T(8,128)(2,1)S(1)}, u32[]{:S(2)}, u32[]{:S(2)}) %collective-permute-start.27) | collective-permute-done | bytes 491552 | tf_op jit(solution)/shard_map/ppermute | solution.py:482
  117.8 4.5 %shard_map.111.refs_2_ = bf16[1024,128]{1,0:T(8,128)(2,1)S(1)} custom-call(s32[1]{0:T(128)} %bitcast.1.first_ref, bf16[2,64,1920]{2,1,0:T(8,128)(2,1)S(1)} %pad_maximum_fusion.2.part_ref, bf16[2,64,1920]{2,1,0:T(8,128)(2,1)S(1)} %collective-permute-done.27.coming_ref, bf16[1024,1920]{1,0:T(8,128)(2,1)} %refs_0_.8, ...), custom_call_target="tpu_custom_call" | custom-call | flops 1006632960 | bytes 7864320 | tf_op jit(solution)/shard_map/pallas_call | solution.py:329
  123.0 4.7 %shard_map.112 = f32[1024,128]{1,0:T(8,128)S(1)} custom-call(s32[1]{0:T(128)} %bitcast.1.first_ref, bf16[2,64,1920]{2,1,0:T(8,128)(2,1)S(1)} %pad_maximum_fusion.1.part_ref, bf16[2,64,1920]{2,1,0:T(8,128)(2,1)S(1)} %collective-permute-done.21.coming_ref, bf16[1024,1920]{1,0:T(8,128)(2,1)} %refs_0_.8, bf16[1024,1920]{1,0:T(8,128)(2,1)} %collective-permute-done.14.refs_1_, ...), custom_call_target="tpu_custom_call" | custom-call | tf_op jit(solution)/shard_map/pallas_call | solution.py:329
  127.7 1.0 collective-permute-done.28
  129.5 2.7 %collective-permute-start.31 = (bf16[1024,128]{1,0:T(8,128)(2,1)S(1)}, bf16[1024,128]{1,0:T(8,128)(2,1)S(1)}, u32[]{:S(2)}, u32[]{:S(2)}) collective-permute-start(bf16[1024,128]{1,0:T(8,128)(2,1)S(1)} %add_convert_fusion.refs_8_), channel_id=1, source_target_pairs={{4,0},{8,4},{12,8},{16,12},{20,16},{24,20},{28,24},{0,28},{5,1},{9... | collective-permute-start | bytes 786440 | tf_op jit(solution)/shard_map/ppermute | solution.py:459
  132.2 3.1 %collective-permute-done.32.refs_9_ = bf16[1024,128]{1,0:T(8,128)(2,1)S(1)} collective-permute-done((bf16[1024,128]{1,0:T(8,128)(2,1)S(1)}, bf16[1024,128]{1,0:T(8,128)(2,1)S(1)}, u32[]{:S(2)}, u32[]{:S(2)}) %collective-permute-start.32) | collective-permute-done | bytes 262176 | tf_op jit(solution)/shard_map/ppermute | solution.py:453
  135.3 6.2 %collective-permute-done.31.refs_10_ = bf16[1024,128]{1,0:T(8,128)(2,1)S(1)} collective-permute-done((bf16[1024,128]{1,0:T(8,128)(2,1)S(1)}, bf16[1024,128]{1,0:T(8,128)(2,1)S(1)}, u32[]{:S(2)}, u32[]{:S(2)}) %collective-permute-start.31) | collective-permute-done | bytes 262176 | tf_op jit(solution)/shard_map/ppermute | solution.py:459
  141.5 2.0 %collective-permute-start.30 = (bf16[1024,128]{1,0:T(8,128)(2,1)S(1)}, bf16[1024,128]{1,0:T(8,128)(2,1)S(1)}, u32[]{:S(2)}, u32[]{:S(2)}) collective-permute-start(bf16[1024,128]{1,0:T(8,128)(2,1)S(1)} %collective-permute-done.29.refs_6_), channel_id=1, source_target_pairs={{0,2},{1,3},{2,0},{3,1},{4,6},{5,7},{6,4},{7,5},{8,10},{9,11},{10,... | collective-permute-start | bytes 786440 | tf_op jit(solution)/shard_map/ppermute | solution.py:453
  143.5 4.3 %collective-permute-done.33.refs_11_ = bf16[1024,128]{1,0:T(8,128)(2,1)S(1)} collective-permute-done((bf16[1024,128]{1,0:T(8,128)(2,1)S(1)}, bf16[1024,128]{1,0:T(8,128)(2,1)S(1)}, u32[]{:S(2)}, u32[]{:S(2)}) %collective-permute-start.33) | collective-permute-done | bytes 262176 | tf_op jit(solution)/shard_map/ppermute | solution.py:453
  147.8 2.8 %collective-permute-done.30.refs_7_ = bf16[1024,128]{1,0:T(8,128)(2,1)S(1)} collective-permute-done((bf16[1024,128]{1,0:T(8,128)(2,1)S(1)}, bf16[1024,128]{1,0:T(8,128)(2,1)S(1)}, u32[]{:S(2)}, u32[]{:S(2)}) %collective-permute-start.30) | collective-permute-done | bytes 262176 | tf_op jit(solution)/shard_map/ppermute | solution.py:453
  150.7 2.3 %shard_map.113 = (bf16[24,128,128]{2,1,0:T(8,128)(2,1)S(1)}, bf16[3072,256]{1,0:T(8,128)(2,1)S(1)}, bf16[3072,256]{1,0:T(8,128)(2,1)S(1)}) custom-call(s32[24,2]{1,0:T(8,128)S(1)} %collective-permute-done.refs_1_.refs_5_.block_ref, bf16[1024,128]{1,0:T(8,128)(2,1)S(1)} %collective-permute-done.6.refs_16_.refs_0_, ...), custom_call_target="tpu_custom_call" | custom-call | flops 201326592 | bytes 3932160 | tf_op jit(solution)/shard_map/pallas_call | solution.py:375
  153.7 1.6 %shard_map.114.first_ref = f32[24,128,128]{2,1,0:T(8,128)S(1)} custom-call(s32[24,2]{1,0:T(8,128)S(1)} %copy.15.refs_0_.refs_4_.block_ref, bf16[3072,256]{1,0:T(8,128)(2,1)S(1)} %get-tuple-element.67.occ_ref, bf16[3072,256]{1,0:T(8,128)(2,1)S(1)} %get-tuple-element.68.resp_ref), custom_call_target="tpu_custom_call" | custom-call | flops 201326592 | bytes 1572864 | tf_op jit(solution)/shard_map/pallas_call | solution.py:397
  156.1 3.2 %shard_map.115 = (f32[24,256]{1,0:T(8,128)}, bf16[1024,512]{1,0:T(8,128)(2,1)}) custom-call(s32[1]{0:T(128)} %bitcast.core_ref, s32[24]{0:T(128)S(1)} %copy-done.2, bf16[24,256,128]{2,1,0:T(8,128)(2,1)S(1)} %copy-done, f32[24,128,128]{2,1,0:T(8,128)S(1)} %shard_map.114.first_ref, bf16[24,128,128]{2,1,0:T(8,128)(2,1)S(1)} %collective-permute-done.34.second_ref, ...), custom_call_target="tpu_custom_call" | custom-call | flops 402653184 | bytes 3932160 | tf_op jit(solution)/shard_map/pallas_call | solution.py:434
  (71 shorter events, 10.7 us)
Async XLA Ops:
  0.6 46.8 %collective-permute-start.14 = (bf16[1024,1920]{1,0:T(8,128)(2,1)}, bf16[1024,1920]{1,0:T(8,128)(2,1)}, u32[]{:S(2)}, u32[]{:S(2)}) collective-permute-start(bf16[1024,1920]{1,0:T(8,128)(2,1)} %refs_0_.8), channel_id=1, source_target_pairs={{0,1},{1,0},{2,3},{3,2},{4,5},{5,4},{6,7},{7,6},{8,9},{9,8},{10,11... | collective-permute-start | bytes 11796488 | tf_op jit(solution)/shard_map/ppermute | solution.py:453
  2.2 21.5 %collective-permute-start.7 = (bf16[1024,128]{1,0:T(8,128)(2,1)S(1)}, bf16[1024,128]{1,0:T(8,128)(2,1)S(1)}, u32[]{:S(2)}, u32[]{:S(2)}) collective-permute-start(bf16[1024,128]{1,0:T(8,128)(2,1)S(1)} %get-tuple-element.73.refs_17_.refs_2_), channel_id=1, source_target_pairs={{4,0},{8,4},{12,8},{16,12},{20,16},{24,20},{28,24},{0,28},{5,1},{9... | collective-permute-start | bytes 786440 | tf_op jit(solution)/shard_map/ppermute | solution.py:459
  7.9 16.3 %collective-permute-start.6 = (bf16[1024,128]{1,0:T(8,128)(2,1)S(1)}, bf16[1024,128]{1,0:T(8,128)(2,1)S(1)}, u32[]{:S(2)}, u32[]{:S(2)}) collective-permute-start(bf16[1024,128]{1,0:T(8,128)(2,1)S(1)} %get-tuple-element.73.refs_17_.refs_2_), channel_id=1, source_target_pairs={{0,4},{4,8},{8,12},{12,16},{16,20},{20,24},{24,28},{28,0},{1,5},{5... | collective-permute-start | bytes 786440 | tf_op jit(solution)/shard_map/ppermute | solution.py:458
  8.6 6.5 %collective-permute-start.2 = (s32[24,2]{1,0:T(8,128)S(1)}, s32[24,2]{1,0:T(8,128)S(1)}, u32[]{:S(2)}, u32[]{:S(2)}) collective-permute-start(s32[24,2]{1,0:T(8,128)S(1)} %copy.15.refs_0_.refs_4_.block_ref), channel_id=1, source_target_pairs={{0,2},{1,3},{2,0},{3,1},{4,6},{5,7},{6,4},{7,5},{8,10},{9,11},{10,... | collective-permute-start | bytes 584 | tf_op jit(solution)/shard_map/ppermute | solution.py:453
  12.3 13.8 %copy-start.4 = (f32[1920]{0:T(1024)S(1)}, f32[1920]{0:T(1024)}, u32[]{:S(2)}) copy-start(f32[1920]{0:T(1024)} %param.17) | copy-start | bytes 23044
  12.3 8.0 %collective-permute-start.1 = (bf16[800,128]{1,0:T(8,128)(2,1)S(1)}, bf16[800,128]{1,0:T(8,128)(2,1)S(1)}, u32[]{:S(2)}, u32[]{:S(2)}) collective-permute-start(bf16[800,128]{1,0:T(8,128)(2,1)S(1)} %get-tuple-element.37), channel_id=1, source_target_pairs={{0,2},{1,3},{2,0},{3,1},{4,6},{5,7},{6,4},{7,5},{8,10},{9,11},{10,... | collective-permute-start | bytes 614408 | tf_op jit(solution)/shard_map/ppermute | solution.py:453
  15.1 8.5 %collective-permute-start.5 = (bf16[800,128]{1,0:T(8,128)(2,1)S(1)}, bf16[800,128]{1,0:T(8,128)(2,1)S(1)}, u32[]{:S(2)}, u32[]{:S(2)}) collective-permute-start(bf16[800,128]{1,0:T(8,128)(2,1)S(1)} %get-tuple-element.40), channel_id=1, source_target_pairs={{0,2},{1,3},{2,0},{3,1},{4,6},{5,7},{6,4},{7,5},{8,10},{9,11},{10,... | collective-permute-start | bytes 614408 | tf_op jit(solution)/shard_map/ppermute | solution.py:453
  20.4 4.8 %collective-permute-start = (s32[24,2]{1,0:T(8,128)S(1)}, s32[24,2]{1,0:T(8,128)S(1)}, u32[]{:S(2)}, u32[]{:S(2)}) collective-permute-start(s32[24,2]{1,0:T(8,128)S(1)} %copy.15.refs_0_.refs_4_.block_ref), channel_id=1, source_target_pairs={{0,1},{1,0},{2,3},{3,2},{4,5},{5,4},{6,7},{7,6},{8,9},{9,8},{10,11... | collective-permute-start | bytes 584 | tf_op jit(solution)/shard_map/ppermute | solution.py:453
  23.7 2.4 %collective-permute-start.4 = (bf16[12,128,128]{2,1,0:T(8,128)(2,1)S(1)}, bf16[12,128,128]{2,1,0:T(8,128)(2,1)S(1)}, u32[]{:S(2)}, u32[]{:S(2)}) collective-permute-start(bf16[12,128,128]{2,1,0:T(8,128)(2,1)S(1)} %get-tuple-element.39.refs_8_), channel_id=1, source_target_pairs={{0,1},{1,0},{2,3},{3,2},{4,5},{5,4},{6,7},{7,6},{8,9},{9,8},{10,11... | collective-permute-start | bytes 1179656 | tf_op jit(solution)/shard_map/ppermute | solution.py:453
  23.7 2.8 %collective-permute-start.9 = (bf16[12,128,128]{2,1,0:T(8,128)(2,1)S(1)}, bf16[12,128,128]{2,1,0:T(8,128)(2,1)S(1)}, u32[]{:S(2)}, u32[]{:S(2)}) collective-permute-start(bf16[12,128,128]{2,1,0:T(8,128)(2,1)S(1)} %get-tuple-element.42.refs_12_), channel_id=1, source_target_pairs={{0,1},{1,0},{2,3},{3,2},{4,5},{5,4},{6,7},{7,6},{8,9},{9,8},{10,11... | collective-permute-start | bytes 1179656 | tf_op jit(solution)/shard_map/ppermute | solution.py:453
  24.2 1.8 %collective-permute-start.3 = (s32[24,2]{1,0:T(8,128)S(1)}, s32[24,2]{1,0:T(8,128)S(1)}, u32[]{:S(2)}, u32[]{:S(2)}) collective-permute-start(s32[24,2]{1,0:T(8,128)S(1)} %collective-permute-done.2.refs_2_.refs_6_), channel_id=1, source_target_pairs={{0,1},{1,0},{2,3},{3,2},{4,5},{5,4},{6,7},{7,6},{8,9},{9,8},{10,11... | collective-permute-start | bytes 584 | tf_op jit(solution)/shard_map/ppermute | solution.py:453
  25.2 12.6 %copy-start.5 = (f32[512]{0:T(512)S(1)}, f32[512]{0:T(512)}, u32[]{:S(2)}) copy-start(f32[512]{0:T(512)} %param.16) | copy-start | bytes 6148
  25.2 1.8 %collective-permute-start.10 = (bf16[12,128,128]{2,1,0:T(8,128)(2,1)S(1)}, bf16[12,128,128]{2,1,0:T(8,128)(2,1)S(1)}, u32[]{:S(2)}, u32[]{:S(2)}) collective-permute-start(bf16[12,128,128]{2,1,0:T(8,128)(2,1)S(1)} %shard_map.107.refs_14_), channel_id=1, source_target_pairs={{0,1},{1,0},{2,3},{3,2},{4,5},{5,4},{6,7},{7,6},{8,9},{9,8},{10,11... | collective-permute-start | bytes 1179656 | tf_op jit(solution)/shard_map/ppermute | solution.py:453
  26.0 1.7 %collective-permute-start.8 = (bf16[12,128,128]{2,1,0:T(8,128)(2,1)S(1)}, bf16[12,128,128]{2,1,0:T(8,128)(2,1)S(1)}, u32[]{:S(2)}, u32[]{:S(2)}) collective-permute-start(bf16[12,128,128]{2,1,0:T(8,128)(2,1)S(1)} %shard_map.106.refs_10_), channel_id=1, source_target_pairs={{0,1},{1,0},{2,3},{3,2},{4,5},{5,4},{6,7},{7,6},{8,9},{9,8},{10,11... | collective-permute-start | bytes 1179656 | tf_op jit(solution)/shard_map/ppermute | solution.py:453
  26.1 11.7 %collective-permute-start.11 = (f32[1920]{0:T(1024)S(1)}, f32[1920]{0:T(1024)S(1)}, u32[]{:S(2)}, u32[]{:S(2)}) collective-permute-start(f32[1920]{0:T(1024)S(1)} %copy-done.4), channel_id=1, source_target_pairs={{0,1},{1,0},{2,3},{3,2},{4,5},{5,4},{6,7},{7,6},{8,9},{9,8},{10,11... | collective-permute-start | bytes 23048 | tf_op jit(solution)/shard_map/ppermute | solution.py:453
  32.9 11.9 %collective-permute-start.12 = (bf16[1024,128]{1,0:T(8,128)(2,1)S(1)}, bf16[1024,128]{1,0:T(8,128)(2,1)S(1)}, u32[]{:S(2)}, u32[]{:S(2)}) collective-permute-start(bf16[1024,128]{1,0:T(8,128)(2,1)S(1)} %get-tuple-element.48), channel_id=1, source_target_pairs={{0,4},{4,8},{8,12},{12,16},{16,20},{20,24},{24,28},{28,0},{1,5},{5... | collective-permute-start | bytes 786440 | tf_op jit(solution)/shard_map/ppermute | solution.py:575
  33.0 14.3 %collective-permute-start.13 = (bf16[1024,128]{1,0:T(8,128)(2,1)S(1)}, bf16[1024,128]{1,0:T(8,128)(2,1)S(1)}, u32[]{:S(2)}, u32[]{:S(2)}) collective-permute-start(bf16[1024,128]{1,0:T(8,128)(2,1)S(1)} %get-tuple-element.49), channel_id=1, source_target_pairs={{4,0},{8,4},{12,8},{16,12},{20,16},{24,20},{28,24},{0,28},{5,1},{9... | collective-permute-start | bytes 786440 | tf_op jit(solution)/shard_map/ppermute | solution.py:576
  51.7 12.8 %collective-permute-start.15 = (bf16[2,64,1920]{2,1,0:T(8,128)(2,1)S(1)}, bf16[2,64,1920]{2,1,0:T(8,128)(2,1)}, u32[]{:S(2)}, u32[]{:S(2)}) collective-permute-start(bf16[2,64,1920]{2,1,0:T(8,128)(2,1)S(1)} %get-tuple-element.51), channel_id=1, source_target_pairs={{0,4},{1,9},{2,6},{3,11},{4,0},{5,13},{6,2},{7,15},{8,12},{9,1},{1... | collective-permute-start | bytes 1474568 | tf_op jit(solution)/shard_map/ppermute | solution.py:482
  51.8 7.7 %collective-permute-start.22 = (bf16[1024,128]{1,0:T(8,128)(2,1)S(1)}, bf16[1024,128]{1,0:T(8,128)(2,1)S(1)}, u32[]{:S(2)}, u32[]{:S(2)}) collective-permute-start(bf16[1024,128]{1,0:T(8,128)(2,1)S(1)} %add_convert_fusion.1.ham_ref), channel_id=1, source_target_pairs={{0,2},{1,3},{2,0},{3,1},{4,6},{5,7},{6,4},{7,5},{8,10},{9,11},{10,... | collective-permute-start | bytes 786440 | tf_op jit(solution)/shard_map/ppermute | solution.py:453
  63.7 11.5 %collective-permute-start.23 = (bf16[2,64,1920]{2,1,0:T(8,128)(2,1)S(1)}, bf16[2,64,1920]{2,1,0:T(8,128)(2,1)S(1)}, u32[]{:S(2)}, u32[]{:S(2)}) collective-permute-start(bf16[2,64,1920]{2,1,0:T(8,128)(2,1)S(1)} %get-tuple-element.61), channel_id=1, source_target_pairs={{0,4},{1,9},{2,6},{3,11},{4,0},{5,13},{6,2},{7,15},{8,12},{9,1},{1... | collective-permute-start | bytes 1474568 | tf_op jit(solution)/shard_map/ppermute | solution.py:482
  65.6 11.1 %collective-permute-start.16 = (bf16[2,32,1920]{2,1,0:T(8,128)(2,1)S(1)}, bf16[2,32,1920]{2,1,0:T(8,128)(2,1)S(1)}, u32[]{:S(2)}, u32[]{:S(2)}) collective-permute-start(bf16[2,32,1920]{2,1,0:T(8,128)(2,1)S(1)} %dynamic-slice_convert_fusion.1), channel_id=1, source_target_pairs={{0,8},{1,5},{2,10},{3,7},{4,12},{5,1},{6,14},{7,3},{8,0},{9,13},{1... | collective-permute-start | bytes 737288 | tf_op jit(solution)/shard_map/ppermute | solution.py:482
  75.3 9.7 %copy-start.3 = (f32[2,64,1920]{2,1,0:T(8,128)}, f32[2,64,1920]{2,1,0:T(8,128)S(1)}, u32[]{:S(2)}) copy-start(f32[2,64,1920]{2,1,0:T(8,128)S(1)} %convert_add_fusion) | copy-start | bytes 2949124
  75.3 9.6 %collective-permute-start.24 = (bf16[2,32,1920]{2,1,0:T(8,128)(2,1)S(1)}, bf16[2,32,1920]{2,1,0:T(8,128)(2,1)S(1)}, u32[]{:S(2)}, u32[]{:S(2)}) collective-permute-start(bf16[2,32,1920]{2,1,0:T(8,128)(2,1)S(1)} %dynamic-slice_convert_fusion), channel_id=1, source_target_pairs={{0,8},{1,5},{2,10},{3,7},{4,12},{5,1},{6,14},{7,3},{8,0},{9,13},{1... | collective-permute-start | bytes 737288 | tf_op jit(solution)/shard_map/ppermute | solution.py:482
  76.8 18.6 %collective-permute-start.17 = (bf16[2,32,1920]{2,1,0:T(8,128)(2,1)S(1)}, bf16[2,32,1920]{2,1,0:T(8,128)(2,1)}, u32[]{:S(2)}, u32[]{:S(2)}) collective-permute-start(bf16[2,32,1920]{2,1,0:T(8,128)(2,1)S(1)} %fusion), channel_id=1, source_target_pairs={{0,16},{4,20},{8,24},{12,28},{16,0},{20,4},{24,8},{28,12},{1,17},{... | collective-permute-start | bytes 737288 | tf_op jit(solution)/shard_map/ppermute | solution.py:453
  80.5 14.9 %collective-permute-start.18 = (bf16[1024,128]{1,0:T(8,128)(2,1)S(1)}, bf16[1024,128]{1,0:T(8,128)(2,1)S(1)}, u32[]{:S(2)}, u32[]{:S(2)}) collective-permute-start(bf16[1024,128]{1,0:T(8,128)(2,1)S(1)} %collective-permute-done.6.refs_16_.refs_0_), channel_id=1, source_target_pairs={{0,2},{1,3},{2,0},{3,1},{4,6},{5,7},{6,4},{7,5},{8,10},{9,11},{10,... | collective-permute-start | bytes 786440 | tf_op jit(solution)/shard_map/ppermute | solution.py:453
  81.0 14.3 %collective-permute-start.19 = (bf16[1024,128]{1,0:T(8,128)(2,1)S(1)}, bf16[1024,128]{1,0:T(8,128)(2,1)S(1)}, u32[]{:S(2)}, u32[]{:S(2)}) collective-permute-start(bf16[1024,128]{1,0:T(8,128)(2,1)S(1)} %collective-permute-done.7.refs_18_.refs_4_), channel_id=1, source_target_pairs={{0,2},{1,3},{2,0},{3,1},{4,6},{5,7},{6,4},{7,5},{8,10},{9,11},{10,... | collective-permute-start | bytes 786440 | tf_op jit(solution)/shard_map/ppermute | solution.py:453
  85.7 13.5 %collective-permute-start.25 = (bf16[2,32,1920]{2,1,0:T(8,128)(2,1)}, bf16[2,32,1920]{2,1,0:T(8,128)(2,1)}, u32[]{:S(2)}, u32[]{:S(2)}) collective-permute-start(bf16[2,32,1920]{2,1,0:T(8,128)(2,1)} %fusion.1), channel_id=1, source_target_pairs={{0,16},{4,20},{8,24},{12,28},{16,0},{20,4},{24,8},{28,12},{1,17},{... | collective-permute-start | bytes 737288 | tf_op jit(solution)/shard_map/ppermute | solution.py:453
  101.4 6.4 %collective-permute-start.26 = (bf16[2,32,1920]{2,1,0:T(8,128)(2,1)}, bf16[2,32,1920]{2,1,0:T(8,128)(2,1)S(1)}, u32[]{:S(2)}, u32[]{:S(2)}) collective-permute-start(bf16[2,32,1920]{2,1,0:T(8,128)(2,1)} %get-tuple-element.80), channel_id=1, source_target_pairs={{0,8},{1,5},{2,10},{3,7},{4,12},{5,1},{6,14},{7,3},{8,0},{9,13},{1... | collective-permute-start | bytes 737288 | tf_op jit(solution)/shard_map/ppermute | solution.py:482
  101.4 10.1 %collective-permute-start.20 = (bf16[2,32,1920]{2,1,0:T(8,128)(2,1)S(1)}, bf16[2,32,1920]{2,1,0:T(8,128)(2,1)S(1)}, u32[]{:S(2)}, u32[]{:S(2)}) collective-permute-start(bf16[2,32,1920]{2,1,0:T(8,128)(2,1)S(1)} %get-tuple-element.81), channel_id=1, source_target_pairs={{0,8},{1,5},{2,10},{3,7},{4,12},{5,1},{6,14},{7,3},{8,0},{9,13},{1... | collective-permute-start | bytes 737288 | tf_op jit(solution)/shard_map/ppermute | solution.py:482
  108.9 8.9 %collective-permute-start.27 = (bf16[2,64,1920]{2,1,0:T(8,128)(2,1)S(1)}, bf16[2,64,1920]{2,1,0:T(8,128)(2,1)S(1)}, u32[]{:S(2)}, u32[]{:S(2)}) collective-permute-start(bf16[2,64,1920]{2,1,0:T(8,128)(2,1)S(1)} %pad_maximum_fusion.2.part_ref), channel_id=1, source_target_pairs={{0,4},{1,9},{2,6},{3,11},{4,0},{5,13},{6,2},{7,15},{8,12},{9,1},{1... | collective-permute-start | bytes 1474568 | tf_op jit(solution)/shard_map/ppermute | solution.py:482
  111.6 11.4 %collective-permute-start.21 = (bf16[2,64,1920]{2,1,0:T(8,128)(2,1)S(1)}, bf16[2,64,1920]{2,1,0:T(8,128)(2,1)S(1)}, u32[]{:S(2)}, u32[]{:S(2)}) collective-permute-start(bf16[2,64,1920]{2,1,0:T(8,128)(2,1)S(1)} %pad_maximum_fusion.1.part_ref), channel_id=1, source_target_pairs={{0,4},{1,9},{2,6},{3,11},{4,0},{5,13},{6,2},{7,15},{8,12},{9,1},{1... | collective-permute-start | bytes 1474568 | tf_op jit(solution)/shard_map/ppermute | solution.py:482
  122.2 6.5 %collective-permute-start.28 = (bf16[1024,128]{1,0:T(8,128)(2,1)S(1)}, bf16[1024,128]{1,0:T(8,128)(2,1)S(1)}, u32[]{:S(2)}, u32[]{:S(2)}) collective-permute-start(bf16[1024,128]{1,0:T(8,128)(2,1)S(1)} %shard_map.111.refs_2_), channel_id=1, source_target_pairs={{0,2},{1,3},{2,0},{3,1},{4,6},{5,7},{6,4},{7,5},{8,10},{9,11},{10,... | collective-permute-start | bytes 786440 | tf_op jit(solution)/shard_map/ppermute | solution.py:453
  128.8 6.5 %collective-permute-start.32 = (bf16[1024,128]{1,0:T(8,128)(2,1)S(1)}, bf16[1024,128]{1,0:T(8,128)(2,1)S(1)}, u32[]{:S(2)}, u32[]{:S(2)}) collective-permute-start(bf16[1024,128]{1,0:T(8,128)(2,1)S(1)} %add_convert_fusion.refs_8_), channel_id=1, source_target_pairs={{0,2},{1,3},{2,0},{3,1},{4,6},{5,7},{6,4},{7,5},{8,10},{9,11},{10,... | collective-permute-start | bytes 786440 | tf_op jit(solution)/shard_map/ppermute | solution.py:453
  129.5 12.0 %collective-permute-start.31 = (bf16[1024,128]{1,0:T(8,128)(2,1)S(1)}, bf16[1024,128]{1,0:T(8,128)(2,1)S(1)}, u32[]{:S(2)}, u32[]{:S(2)}) collective-permute-start(bf16[1024,128]{1,0:T(8,128)(2,1)S(1)} %add_convert_fusion.refs_8_), channel_id=1, source_target_pairs={{4,0},{8,4},{12,8},{16,12},{20,16},{24,20},{28,24},{0,28},{5,1},{9... | collective-permute-start | bytes 786440 | tf_op jit(solution)/shard_map/ppermute | solution.py:459
  132.2 9.3 %collective-permute-start.29 = (bf16[1024,128]{1,0:T(8,128)(2,1)S(1)}, bf16[1024,128]{1,0:T(8,128)(2,1)S(1)}, u32[]{:S(2)}, u32[]{:S(2)}) collective-permute-start(bf16[1024,128]{1,0:T(8,128)(2,1)S(1)} %add_convert_fusion.refs_8_), channel_id=1, source_target_pairs={{0,4},{4,8},{8,12},{12,16},{16,20},{20,24},{24,28},{28,0},{1,5},{5... | collective-permute-start | bytes 786440 | tf_op jit(solution)/shard_map/ppermute | solution.py:458
  141.5 6.4 %collective-permute-start.33 = (bf16[1024,128]{1,0:T(8,128)(2,1)S(1)}, bf16[1024,128]{1,0:T(8,128)(2,1)S(1)}, u32[]{:S(2)}, u32[]{:S(2)}) collective-permute-start(bf16[1024,128]{1,0:T(8,128)(2,1)S(1)} %collective-permute-done.31.refs_10_), channel_id=1, source_target_pairs={{0,2},{1,3},{2,0},{3,1},{4,6},{5,7},{6,4},{7,5},{8,10},{9,11},{10,... | collective-permute-start | bytes 786440 | tf_op jit(solution)/shard_map/ppermute | solution.py:453
  141.5 9.2 %collective-permute-start.30 = (bf16[1024,128]{1,0:T(8,128)(2,1)S(1)}, bf16[1024,128]{1,0:T(8,128)(2,1)S(1)}, u32[]{:S(2)}, u32[]{:S(2)}) collective-permute-start(bf16[1024,128]{1,0:T(8,128)(2,1)S(1)} %collective-permute-done.29.refs_6_), channel_id=1, source_target_pairs={{0,2},{1,3},{2,0},{3,1},{4,6},{5,7},{6,4},{7,5},{8,10},{9,11},{10,... | collective-permute-start | bytes 786440 | tf_op jit(solution)/shard_map/ppermute | solution.py:453
  153.0 3.1 %collective-permute-start.34 = (bf16[24,128,128]{2,1,0:T(8,128)(2,1)S(1)}, bf16[24,128,128]{2,1,0:T(8,128)(2,1)S(1)}, u32[]{:S(2)}, u32[]{:S(2)}) collective-permute-start(bf16[24,128,128]{2,1,0:T(8,128)(2,1)S(1)} %get-tuple-element.69), channel_id=1, source_target_pairs={{0,1},{1,0},{2,3},{3,2},{4,5},{5,4},{6,7},{7,6},{8,9},{9,8},{10,11... | collective-permute-start | bytes 2359304 | tf_op jit(solution)/shard_map/ppermute | solution.py:453
  153.2 2.9 %collective-permute-start.35 = (bf16[1024,256]{1,0:T(8,128)(2,1)S(1)}, bf16[1024,256]{1,0:T(8,128)(2,1)S(1)}, u32[]{:S(2)}, u32[]{:S(2)}) collective-permute-start(bf16[1024,256]{1,0:T(8,128)(2,1)S(1)} %pad_maximum_fusion.half_ref), channel_id=1, source_target_pairs={{0,1},{1,0},{2,3},{3,2},{4,5},{5,4},{6,7},{7,6},{8,9},{9,8},{10,11... | collective-permute-start | bytes 1572872 | tf_op jit(solution)/shard_map/ppermute | solution.py:453
  153.7 2.4 %copy-start = (bf16[24,256,128]{2,1,0:T(8,128)(2,1)S(1)}, bf16[24,256,128]{2,1,0:T(8,128)(2,1)}, u32[]{:S(2)}) copy-start(bf16[24,256,128]{2,1,0:T(8,128)(2,1)} %basis_ref.1) | copy-start | bytes 4718596
  153.7 2.4 %copy-start.1 = (f32[24,256]{1,0:T(8,128)S(1)}, f32[24,256]{1,0:T(8,128)}, u32[]{:S(2)}) copy-start(f32[24,256]{1,0:T(8,128)} %scale_ref.1) | copy-start | bytes 73732
  153.7 2.4 %copy-start.2 = (s32[24]{0:T(128)S(1)}, s32[24]{0:T(128)}, u32[]{:S(2)}) copy-start(s32[24]{0:T(128)} %counts_ref.1) | copy-start | bytes 292

commit v9 on v8

--- a/solution.py
+++ b/solution.py
@@ -1,4 +1,5 @@
 import functools
+import math
 
 import jax
 import jax.numpy as jnp
@@ -13,7 +14,6 @@
 MIB = 1024 * 1024
 F32 = jnp.float32
 BF16 = jnp.bfloat16
-LANES = 128
 NT = (((1,), (1,)), ((), ()))
 
 
@@ -33,6 +33,28 @@
     for copy in started:
         copy.start()
     return started
+
+
+def load_kernel(source_ref, out_ref, semaphores):
+    rows = source_ref.shape[0] // semaphores.shape[0]
+    places = [pl.ds(i * rows, rows) for i in range(semaphores.shape[0])]
+    for copy in fetch([(source_ref.at[at], out_ref.at[at]) for at in places], semaphores):
+        copy.wait()
+
+
+def load(array):
+    parts = 4 if array.shape[0] % 64 == 0 else 1
+    return pl.pallas_call(
+        load_kernel,
+        out_shape=pltpu.VMEM(array.shape, array.dtype),
+        in_specs=[HBM],
+        out_specs=VMEM,
+        scratch_shapes=[pltpu.SemaphoreType.DMA((parts,))],
+        compiler_params=params(),
+        cost_estimate=pl.CostEstimate(
+            flops=0, bytes_accessed=2 * array.size * array.dtype.itemsize, transcendentals=0
+        ),
+    )(place_in(array, pltpu.HBM))
 
 
 def split_dot(full, other, dims):
@@ -163,21 +185,16 @@
     ]
 
 
-def apply_kernel(starts, far, rows, *refs):
+def apply_kernel(starts, rows, *refs):
     pieces = len(starts)
-    block_refs, ham_refs = refs[:pieces], list(refs[pieces : 2 * pieces])
+    block_refs, ham_refs = refs[:pieces], refs[pieces : 2 * pieces]
     window_refs = refs[2 * pieces : 2 * pieces + 3]
     out_before, out_own, out_after = refs[2 * pieces + 3 : 2 * pieces + 6]
-    window, total, semaphores, *held = refs[2 * pieces + 6 :]
-    waits = fetch([(ham_refs[p], target) for p, target in zip(far, held)], semaphores)
-    for p, target in zip(far, held):
-        ham_refs[p] = target
+    window, total = refs[2 * pieces + 6 :]
     region = window_refs[0].shape[0]
     for side, ref in enumerate(window_refs):
         window[side * region : (side + 1) * region] = ref[...]
     total[...] = jnp.zeros_like(total)
-    for copy in waits:
-        copy.wait()
 
     def steps(members, count):
         def step(b, carry):
@@ -207,29 +224,25 @@
     out_after[...] = total[2 * region :].astype(BF16)
 
 
-def apply_window(blocks, hams, starts, far, before, own, after):
+def apply_window(blocks, hams, starts, before, own, after):
     pieces, per_batch = len(hams), blocks[0].shape[1]
     columns = hams[0].shape[1]
     region, width = own.shape
     work = sum(ham.shape[0] for ham in hams)
     return pl.pallas_call(
-        functools.partial(apply_kernel, starts, far, columns // per_batch),
+        functools.partial(apply_kernel, starts, columns // per_batch),
         out_shape=[
             jax.ShapeDtypeStruct((region, width), BF16),
             jax.ShapeDtypeStruct((region, width), F32),
             jax.ShapeDtypeStruct((region, width), BF16),
         ],
-        in_specs=[SMEM] * pieces
-        + [HBM if p in far else VMEM for p in range(pieces)]
-        + [VMEM] * 3,
+        in_specs=[SMEM] * pieces + [VMEM] * (pieces + 3),
         out_specs=[VMEM] * 3,
         scratch_shapes=[
             pltpu.VMEM((3 * region, width), BF16),
             pltpu.VMEM((3 * region, width), F32),
-            pltpu.SemaphoreType.DMA((len(far),)),
-        ]
-        + [pltpu.VMEM(hams[p].shape, BF16) for p in far],
-        compiler_params=params(8),
+        ],
+        compiler_params=params(6),
         cost_estimate=pl.CostEstimate(
             flops=2 * work * columns * columns * width,
             bytes_accessed=work * columns * columns * 2 + 14 * region * width,
@@ -237,61 +250,9 @@
         ),
     )(
         *blocks,
-        *[ham if p in far else place_in(ham, pltpu.VMEM) for p, ham in enumerate(hams)],
+        *hams,
         *[place_in(array, pltpu.VMEM) for array in (before, own, after)],
     )
-
-
-def project_kernel(first_ref, ham_ref, *refs):
-    sources, (keep_ref, send_ref, held, semaphores) = refs[:2], refs[2:]
-    blocks = semaphores.shape[0] // 2
-    width = held.shape[2] // blocks
-    copies = []
-    for i in range(blocks):
-        place = (slice(None), pl.ds(i * width, width))
-        for share, source in enumerate(sources):
-            copies.append((source.at[place], held.at[(share, *place)]))
-    waits = fetch(copies, semaphores)
-    turned = ham_ref[...].astype(F32).T.astype(BF16)
-    half = turned.shape[0] // 2
-    low = first_ref[0] == 0
-    for i in range(blocks):
-        at = slice(i * width, (i + 1) * width)
-        for share in range(2):
-            waits[2 * i + share].wait()
-            product = jnp.dot(turned, held[share, :, at], preferred_element_type=F32)
-            keep_ref[share, :, at] = jnp.where(low, product[:half], product[half:])
-            send_ref[share, :, at] = jnp.where(low, product[half:], product[:half]).astype(BF16)
-
-
-def lane_block(size, most):
-    tiles = size // LANES
-    return LANES * max(k for k in range(1, tiles + 1) if tiles % k == 0 and k * LANES <= most)
-
-
-def project(first, ham, virtuals):
-    region, width = ham.shape
-    virt = virtuals[0].shape[1]
-    blocks = virt // lane_block(virt, 512)
-    return pl.pallas_call(
-        project_kernel,
-        out_shape=[
-            jax.ShapeDtypeStruct((2, width // 2, virt), F32),
-            jax.ShapeDtypeStruct((2, width // 2, virt), BF16),
-        ],
-        in_specs=[SMEM, VMEM, HBM, HBM],
-        out_specs=[VMEM, VMEM],
-        scratch_shapes=[
-            pltpu.VMEM((2, region, virt), BF16),
-            pltpu.SemaphoreType.DMA((2 * blocks,)),
-        ],
-        compiler_params=params(14),
-        cost_estimate=pl.CostEstimate(
-            flops=4 * region * width * virt,
-            bytes_accessed=4 * region * virt + 6 * width * virt,
-            transcendentals=0,
-        ),
-    )(first.reshape(1), ham, place_in(virtuals[0], pltpu.HBM), virtuals[1])
 
 
 def expand_kernel(first_ref, part_ref, coming_ref, *refs):
@@ -486,36 +447,64 @@
     return lax.optimization_barrier(arrays)
 
 
+def divide_kernel(place_ref, energy_ref, *refs):
+    chunks = len(refs) // 4
+    rows = refs[0].shape[1]
+    place = pl.multiple_of(place_ref[0], rows)
+    for c in range(chunks):
+        total_ref, coming_ref, level_ref, out_ref = refs[3 * c : 3 * c + 3] + (refs[3 * chunks + c],)
+        level = level_ref[pl.ds(place, rows), :]
+        for share in range(total_ref.shape[0]):
+            total = total_ref[share] + coming_ref[share].astype(F32)
+            gap = level - energy_ref[share : share + 1, :]
+            out_ref[share] = (total / gap).astype(out_ref.dtype)
+
+
+def divide(place, energies, chunks):
+    shape = chunks[0].total.shape
+    operands = []
+    for chunk in chunks:
+        operands += [chunk.total, chunk.coming, chunk.level[:, None]]
+    return pl.pallas_call(
+        divide_kernel,
+        out_shape=[pltpu.VMEM(shape, BF16)] * len(chunks),
+        in_specs=[SMEM] + [VMEM] * (1 + len(operands)),
+        out_specs=[VMEM] * len(chunks),
+        compiler_params=params(),
+        cost_estimate=pl.CostEstimate(
+            flops=len(chunks) * math.prod(shape) * 8, bytes_accessed=0, transcendentals=0
+        ),
+    )(place.reshape(1), energies, *operands)
+
+
 class Reduction:
-    def __init__(self, ham, virtuals, level, energy):
+    def __init__(self, part, level):
         grid, core = lax.axis_index("grid"), lax.axis_index("tile") % 2
         self.masks = (1, 2), (2, 1)
         self.first, self.second = (grid >> core) & 1, (grid >> (1 - core)) & 1
-        self.level, self.energy = level, energy
-        self.half, self.virtuals = ham.shape[1] // 2, virtuals
-        self.keep, self.send = project(self.first, ham, virtuals)
-        self.coming = swap(self.send, self.masks[0])
+        self.level = level
+        self.half = part.shape[1] // 2
+        self.keep, send = trade(part, self.half, self.first)
+        self.coming = swap(send, self.masks[0])
 
     def narrow(self):
         total = self.keep + self.coming.astype(F32)
         self.keep, send = trade(total, self.half // 2, self.second)
         self.total = self.keep + swap(send, self.masks[1]).astype(F32)
-        self.across = self.total.astype(BF16)
+        self.total, self.across = together(self.total, self.total.astype(BF16))
 
     def cross(self):
         self.coming = flip(self.across, "grid", 4)
 
-    def divide(self):
-        quarter = self.half // 2
-        place = self.first * self.half + self.second * quarter
-        level = lax.dynamic_slice_in_dim(self.level, place, quarter, 0)
-        total = self.total + self.coming.astype(F32)
-        own = (total / (level[None, :, None] - self.energy[:, None, :])).astype(BF16)
+    def place(self):
+        return self.first * self.half + self.second * (self.half // 2)
+
+    def widen(self, own):
         self.part = join(own, swap(own, self.masks[1]), self.second)
         self.coming = swap(self.part, self.masks[0])
 
-    def result(self, kind, *ahead):
-        return expand(self.first, self.part, self.coming, self.virtuals, kind, ahead)
+    def result(self, virtuals, kind, *ahead):
+        return expand(self.first, self.part, self.coming, virtuals, kind, ahead)
 
 
 def per_device(
@@ -546,14 +535,14 @@
         fulls.append(full)
         arrived.append(flip(packed, "tile", 2))
     arrived[0], occ_before, occ_after = together(arrived[0], occ_before, occ_after)
-    arrived[-1], lists[2] = together(arrived[-1], lists[2])
+    far = [unpack(array, size, columns) for array, size in zip(arrived, sizes)]
+    far[-1], lists[2] = together(far[-1], lists[2])
     lists.append(flip(lists[2], "tile", 1))
-    hams, places, starts = [], [], []
-    for i, size in enumerate(sizes):
-        far = unpack(arrived[i], size, columns)
-        hams += [fulls[i], flip(fulls[i], "tile", 1), far, flip(far, "tile", 1)]
-        places, starts = places + lists, starts + [sum(sizes[:i])] * 4
-    blocks_near = lists[1]
+    hams = []
+    for full, other in zip(fulls, far):
+        hams += [full, flip(full, "tile", 1), other, flip(other, "tile", 1)]
+    places, blocks_near = lists * len(sizes), lists[1]
+    starts = [sum(sizes[:i]) for i in range(len(sizes)) for _ in range(4)]
     virtuals = [virt_coef, flip(virt_coef, "tile", 1)]
     energies = jnp.stack([virt_energy, flip(virt_energy, "tile", 1)])
 
@@ -561,7 +550,6 @@
         places,
         hams,
         starts,
-        [p for p in range(len(hams)) if p % 2 == 1],
         occ_before,
         occ_own,
         occ_after,
@@ -570,17 +558,25 @@
         lax.dynamic_slice_in_dim(occ_energy, place * width, width, 0)
         for place in (quarter, quarter ^ 1)
     ]
-    own_sum, energies, levels = together(own_sum, energies, levels)
+    loaded = [load(array) for array in virtuals]
+    own_sum, energies, levels, loaded = together(own_sum, energies, levels, loaded)
     size = lax.axis_size("grid")
     from_before = lax.ppermute(to_after, "grid", [(i, (i + 1) % size) for i in range(size)])
     from_after = lax.ppermute(to_before, "grid", [((i + 1) % size, i) for i in range(size)])
     ham_own = (own_sum + from_before.astype(F32) + from_after.astype(F32)).astype(BF16)
 
-    ham_far = flip(ham_own, "tile", 2)
+    def products(ham_sum):
+        dots = [
+            lax.dot_general(ham_sum, virt, (((0,), (0,)), ((), ())), preferred_element_type=F32)
+            for virt in loaded
+        ]
+        return jnp.stack(dots)
+
+    own_part, far_part = products(ham_own), products(flip(ham_own, "tile", 2))
     occ_far = column_part(occ_coef, quarter ^ 1, width)
     if lax.axis_size("grid") == 8:
-        own = Reduction(ham_own, virtuals, levels[0], energies)
-        far = Reduction(ham_far, virtuals, levels[1], energies)
+        own = Reduction(own_part, levels[0])
+        far = Reduction(far_part, levels[1])
         own.narrow()
         far.narrow()
         far.cross()
@@ -588,19 +584,16 @@
         own.cross()
         before_far, after_far = flip(occ_before, "tile", 2), flip(occ_after, "tile", 2)
         own.coming, before_far, after_far = together(own.coming, before_far, after_far)
-        own.divide()
-        far.divide()
-        coef_far = far.result(BF16)
-        coef_own = own.result(F32, coef_far)
+        own_rotation, far_rotation = divide(own.place(), energies, [own, far])
+        own.widen(own_rotation)
+        far.widen(far_rotation)
+        coef_far = far.result(virtuals, BF16)
+        coef_own = own.result(virtuals, F32, coef_far)
     else:
         before_far, after_far = flip(occ_before, "tile", 2), flip(occ_after, "tile", 2)
         coefs = []
-        for ham_sum, level in ((ham_own, levels[0]), (ham_far, levels[1])):
-            products = [
-                lax.dot_general(ham_sum, virt, (((0,), (0,)), ((), ())), preferred_element_type=F32)
-                for virt in virtuals
-            ]
-            total = lax.psum(jnp.stack(products), "grid")
+        for part, level in ((own_part, levels[0]), (far_part, levels[1])):
+            total = lax.psum(part, "grid")
             rotation = (total / (level[None, :, None] - energies[:, None, :])).astype(BF16)
             terms = [
                 lax.dot_general(virt, rotation[i], NT, preferred_element_type=F32)

time: 160 us -> 148 us (0.925)
  waiting for transfers between devices: 76.9 us -> 66.9 us
  Pallas kernels: 36.1 us -> 31.8 us
  other arithmetic: 5.63 us -> 2.49 us
  matrix products: 0 us -> 2.96 us
    ppermute x22, waiting for transfers between devices: 39.3 us -> 31.1 us  [flip(): lax.ppermute(array, axis, [(i, i ^ mask) for i in range(lax.axis_size(axi...]
    ppermute x1, waiting for transfers between devices: 7 us -> 0.81 us  [per_device(): lax.ppermute(to_after, 'grid', [(i, (i + 1) % size) for i in range(size)])]
    ppermute x8, waiting for transfers between devices: 22 us -> 27.2 us  [swap(): return lax.ppermute(array, ('grid', 'tile'), pairs)]
    pallas_call x3 -> x4, Pallas kernels: 13.7 us -> 9.63 us  [the longest x1 4.45 us: apply_window(): pl.pallas_call(functools.partial(apply_kernel, starts, columns // per_bat...]
    dot_general x0 -> x4, matrix products: none -> 2.96 us  [products(): lax.dot_general(ham_sum, virt, (((0,), (0,)), ((), ())), preferred_elemen...]
    ppermute x2, waiting for transfers between devices: 6.17 us -> 3.54 us  [neighbours(): lax.ppermute(array, 'grid', [((i + 1) % size, i) for i in range(size)])]
    ppermute x8, starting transfers between devices: 7.58 us -> 5.41 us  [swap(): return lax.ppermute(array, ('grid', 'tile'), pairs)]
    convert_element_type x3 -> x4, other arithmetic: 3 us -> 0.93 us  [the longest x2 0.81 us: narrow(): self.total, self.across = together(self.total, self.total.astype(BF16))]
  transfers between devices with their start and end apart: 36 -> 36, of which waited for: 22 -> 23; matrix products, arithmetic and copies ran while one was open for 3% -> 5% of each run, Pallas kernels for 17% -> 17%
where the time goes in v9:
time: 148 us; the launch traced here: 146 us
  waiting for transfers between devices  66.9 us (45%)
  starting transfers between devices  37.2 us (25%)
  Pallas kernels  31.8 us (21%)
  local copies, waits for them, and re-layouts  3.55 us (2%)
  matrix products  2.96 us (2%)
  other arithmetic  2.49 us (2%)
    ppermute x22, waiting for transfers between devices, flip(): lax.ppermute(array, axis, [(i, i ^ mask) for i in range(lax.axis_size(axi...  31.1 us
    ppermute x8, waiting for transfers between devices, swap(): return lax.ppermute(array, ('grid', 'tile'), pairs)  27.2 us
    ppermute x22, starting transfers between devices, flip(): lax.ppermute(array, axis, [(i, i ^ mask) for i in range(lax.axis_size(axi...  18.3 us
    pallas_call x2, Pallas kernels, expand(): pl.pallas_call(expand_kernel, out_shape=jax.ShapeDtypeStruct((region, wid...  8.91 us
    ppermute x2, starting transfers between devices, neighbours(): lax.ppermute(array, 'grid', [((i + 1) % size, i) for i in range(size)])  8.79 us
    ppermute x8, starting transfers between devices, swap(): return lax.ppermute(array, ('grid', 'tile'), pairs)  5.41 us
    ppermute x1, starting transfers between devices, per_device(): lax.ppermute(to_before, 'grid', [((i + 1) % size, i) for i in range(size)])  4.71 us
    pallas_call x1, Pallas kernels, apply_window(): pl.pallas_call(functools.partial(apply_kernel, starts, columns // per_bat...  4.45 us
  transfers between devices with their start and end apart: 36, of which 23 were waited for; matrix products, arithmetic and copies ran while one was open for 5% of the time, Pallas kernels for 17%

profile of v9, /device:TPU:0, one launch (start us, length us, event | category | flops | bytes accessed | tf_op | source)
XLA Modules:
  0.0 146.1 jit_solution(2969677181635525647)
XLA Ops:
  1.2 1.1 constant_dynamic-slice_fusion
  2.3 5.7 %collective-permute-start.7 = (bf16[1024,128]{1,0:T(8,128)(2,1)S(1)}, bf16[1024,128]{1,0:T(8,128)(2,1)S(1)}, u32[]{:S(2)}, u32[]{:S(2)}) collective-permute-start(bf16[1024,128]{1,0:T(8,128)(2,1)S(1)} %get-tuple-element.85.refs_17_.refs_2_), channel_id=1, source_target_pairs={{4,0},{8,4},{12,8},{16,12},{20,16},{24,20},{28,24},{0,28},{5,1},{9... | collective-permute-start | bytes 786440 | tf_op jit(solution)/shard_map/ppermute | solution.py:420
  7.9 2.2 %shard_map.104 = (bf16[12,128,128]{2,1,0:T(8,128)(2,1)S(1)}, bf16[800,128]{1,0:T(8,128)(2,1)S(1)}) custom-call(s32[24]{0:T(128)} %counts_ref.1, bf16[24,256,128]{2,1,0:T(8,128)(2,1)} %basis_ref.1, f32[24,256]{1,0:T(8,128)} %weights_hbm.3), custom_call_target="tpu_custom_call" | custom-call | flops 201326592 | bytes 1376256 | tf_op jit(solution)/shard_map/pallas_call | solution.py:121
  10.1 1.6 %collective-permute-start.1 = (bf16[800,128]{1,0:T(8,128)(2,1)S(1)}, bf16[800,128]{1,0:T(8,128)(2,1)S(1)}, u32[]{:S(2)}, u32[]{:S(2)}) collective-permute-start(bf16[800,128]{1,0:T(8,128)(2,1)S(1)} %get-tuple-element.41), channel_id=1, source_target_pairs={{0,2},{1,3},{2,0},{3,1},{4,6},{5,7},{6,4},{7,5},{8,10},{9,11},{10,... | collective-permute-start | bytes 614408 | tf_op jit(solution)/shard_map/ppermute | solution.py:414
  11.7 2.2 %shard_map.106 = (bf16[12,128,128]{2,1,0:T(8,128)(2,1)S(1)}, bf16[800,128]{1,0:T(8,128)(2,1)S(1)}) custom-call(s32[24]{0:T(128)} %counts_ref.1, bf16[24,256,128]{2,1,0:T(8,128)(2,1)} %basis_ref.1, f32[24,256]{1,0:T(8,128)} %weights_hbm.3), custom_call_target="tpu_custom_call" | custom-call | flops 201326592 | bytes 1376256 | tf_op jit(solution)/shard_map/pallas_call | solution.py:121
  14.5 3.5 %collective-permute-done.1.packed_ref = bf16[800,128]{1,0:T(8,128)(2,1)S(1)} collective-permute-done((bf16[800,128]{1,0:T(8,128)(2,1)S(1)}, bf16[800,128]{1,0:T(8,128)(2,1)S(1)}, u32[]{:S(2)}, u32[]{:S(2)}) %collective-permute-start.1) | collective-permute-done | bytes 204832 | tf_op jit(solution)/shard_map/ppermute | solution.py:414
  18.1 1.5 %collective-permute-start.2 = (s32[24,2]{1,0:T(8,128)S(1)}, s32[24,2]{1,0:T(8,128)S(1)}, u32[]{:S(2)}, u32[]{:S(2)}) collective-permute-start(s32[24,2]{1,0:T(8,128)S(1)} %copy.17.refs_0_.refs_4_.block_ref), channel_id=1, source_target_pairs={{0,2},{1,3},{2,0},{3,1},{4,6},{5,7},{6,4},{7,5},{8,10},{9,11},{10,... | collective-permute-start | bytes 584 | tf_op jit(solution)/shard_map/ppermute | solution.py:414
  19.6 0.9 shard_map.105.refs_14_
  20.5 1.5 %collective-permute-done.2.refs_2_.refs_6_ = s32[24,2]{1,0:T(8,128)S(1)} collective-permute-done((s32[24,2]{1,0:T(8,128)S(1)}, s32[24,2]{1,0:T(8,128)S(1)}, u32[]{:S(2)}, u32[]{:S(2)}) %collective-permute-start.2) | collective-permute-done | bytes 224 | tf_op jit(solution)/shard_map/ppermute | solution.py:414
  23.0 0.9 shard_map.107.refs_10_
  26.2 4.4 %shard_map.108 = (bf16[1024,128]{1,0:T(8,128)(2,1)S(1)}, f32[1024,128]{1,0:T(8,128)S(1)}, bf16[1024,128]{1,0:T(8,128)(2,1)S(1)}) custom-call(s32[24,2]{1,0:T(8,128)S(1)} %copy.17.refs_0_.refs_4_.block_ref, s32[24,2]{1,0:T(8,128)S(1)} %collective-permute-done.refs_1_.refs_5_.block_ref, s32[24,2]{1,0:T(8,128)S(1)} %collective-permute-done.2.refs_2_.refs_6_, ...), custom_call_target="tpu_custom_call" | custom-call | flops 402653184 | bytes 4980736 | tf_op jit(solution)/shard_map/pallas_call | solution.py:232
  30.8 4.7 %collective-permute-start.14 = (bf16[1024,128]{1,0:T(8,128)(2,1)S(1)}, bf16[1024,128]{1,0:T(8,128)(2,1)S(1)}, u32[]{:S(2)}, u32[]{:S(2)}) collective-permute-start(bf16[1024,128]{1,0:T(8,128)(2,1)S(1)} %get-tuple-element.53), channel_id=1, source_target_pairs={{4,0},{8,4},{12,8},{16,12},{20,16},{24,20},{28,24},{0,28},{5,1},{9... | collective-permute-start | bytes 786440 | tf_op jit(solution)/shard_map/ppermute | solution.py:565
  35.6 2.1 %shard_map.109 = bf16[1024,1920]{1,0:T(8,128)(2,1)S(1)} custom-call(bf16[1024,1920]{1,0:T(8,128)(2,1)} %refs_0_.4), custom_call_target="tpu_custom_call" | custom-call | bytes 7864320 | tf_op jit(solution)/shard_map/pallas_call | solution.py:47
  37.7 1.9 %copy-done = bf16[1024,1920]{1,0:T(8,128)(2,1)} copy-done((bf16[1024,1920]{1,0:T(8,128)(2,1)}, bf16[1024,1920]{1,0:T(8,128)(2,1)S(1)}, u32[]{:S(2)}) %copy-start) | copy-done | bytes 3932184
  39.7 2.1 %shard_map.110 = bf16[1024,1920]{1,0:T(8,128)(2,1)S(1)} custom-call(bf16[1024,1920]{1,0:T(8,128)(2,1)} %collective-permute-done.12.source_ref.refs_1_), custom_call_target="tpu_custom_call" | custom-call | bytes 7864320 | tf_op jit(solution)/shard_map/pallas_call | solution.py:47
  42.7 2.4 %collective-permute-done.14 = bf16[1024,128]{1,0:T(8,128)(2,1)S(1)} collective-permute-done((bf16[1024,128]{1,0:T(8,128)(2,1)S(1)}, bf16[1024,128]{1,0:T(8,128)(2,1)S(1)}, u32[]{:S(2)}, u32[]{:S(2)}) %collective-permute-start.14) | collective-permute-done | bytes 262176 | tf_op jit(solution)/shard_map/ppermute | solution.py:565
  45.2 1.6 %collective-permute-start.20 = (bf16[1024,128]{1,0:T(8,128)(2,1)S(1)}, bf16[1024,128]{1,0:T(8,128)(2,1)S(1)}, u32[]{:S(2)}, u32[]{:S(2)}) collective-permute-start(bf16[1024,128]{1,0:T(8,128)(2,1)S(1)} %add_convert_fusion.1), channel_id=1, source_target_pairs={{0,2},{1,3},{2,0},{3,1},{4,6},{5,7},{6,4},{7,5},{8,10},{9,11},{10,... | collective-permute-start | bytes 786440 | tf_op jit(solution)/shard_map/ppermute | solution.py:414
  48.5 4.5 %collective-permute-done.20 = bf16[1024,128]{1,0:T(8,128)(2,1)S(1)} collective-permute-done((bf16[1024,128]{1,0:T(8,128)(2,1)S(1)}, bf16[1024,128]{1,0:T(8,128)(2,1)S(1)}, u32[]{:S(2)}, u32[]{:S(2)}) %collective-permute-start.20) | collective-permute-done | bytes 262176 | tf_op jit(solution)/shard_map/ppermute | solution.py:414
  54.9 2.3 %collective-permute-done.15 = bf16[2,64,1920]{2,1,0:T(8,128)(2,1)S(1)} collective-permute-done((bf16[2,64,1920]{2,1,0:T(8,128)(2,1)S(1)}, bf16[2,64,1920]{2,1,0:T(8,128)(2,1)S(1)}, u32[]{:S(2)}, u32[]{:S(2)}) %collective-permute-start.15) | collective-permute-done | bytes 491552 | tf_op jit(solution)/shard_map/ppermute | solution.py:443
  57.5 10.7 %collective-permute-done.21 = bf16[2,64,1920]{2,1,0:T(8,128)(2,1)S(1)} collective-permute-done((bf16[2,64,1920]{2,1,0:T(8,128)(2,1)S(1)}, bf16[2,64,1920]{2,1,0:T(8,128)(2,1)S(1)}, u32[]{:S(2)}, u32[]{:S(2)}) %collective-permute-start.21) | collective-permute-done | bytes 491552 | tf_op jit(solution)/shard_map/ppermute | solution.py:443
  68.4 3.1 %collective-permute-start.17 = (bf16[2,32,1920]{2,1,0:T(8,128)(2,1)S(1)}, bf16[2,32,1920]{2,1,0:T(8,128)(2,1)S(1)}, u32[]{:S(2)}, u32[]{:S(2)}) collective-permute-start(bf16[2,32,1920]{2,1,0:T(8,128)(2,1)S(1)} %get-tuple-element.58), channel_id=1, source_target_pairs={{0,16},{4,20},{8,24},{12,28},{16,0},{20,4},{24,8},{28,12},{1,17},{... | collective-permute-start | bytes 737288 | tf_op jit(solution)/shard_map/ppermute | solution.py:414
  71.5 2.0 %collective-permute-start.19 = (bf16[1024,128]{1,0:T(8,128)(2,1)S(1)}, bf16[1024,128]{1,0:T(8,128)(2,1)S(1)}, u32[]{:S(2)}, u32[]{:S(2)}) collective-permute-start(bf16[1024,128]{1,0:T(8,128)(2,1)S(1)} %collective-permute-done.7.refs_18_.refs_4_), channel_id=1, source_target_pairs={{0,2},{1,3},{2,0},{3,1},{4,6},{5,7},{6,4},{7,5},{8,10},{9,11},{10,... | collective-permute-start | bytes 786440 | tf_op jit(solution)/shard_map/ppermute | solution.py:414
  73.5 3.8 %collective-permute-done.22 = bf16[2,32,1920]{2,1,0:T(8,128)(2,1)S(1)} collective-permute-done((bf16[2,32,1920]{2,1,0:T(8,128)(2,1)S(1)}, bf16[2,32,1920]{2,1,0:T(8,128)(2,1)S(1)}, u32[]{:S(2)}, u32[]{:S(2)}) %collective-permute-start.22) | collective-permute-done | bytes 245792 | tf_op jit(solution)/shard_map/ppermute | solution.py:443
  78.5 7.6 %collective-permute-done.17.refs_1_ = bf16[2,32,1920]{2,1,0:T(8,128)(2,1)S(1)} collective-permute-done((bf16[2,32,1920]{2,1,0:T(8,128)(2,1)S(1)}, bf16[2,32,1920]{2,1,0:T(8,128)(2,1)S(1)}, u32[]{:S(2)}, u32[]{:S(2)}) %collective-permute-start.17) | collective-permute-done | bytes 245792 | tf_op jit(solution)/shard_map/ppermute | solution.py:414
  86.1 2.6 %collective-permute-done.23.refs_4_ = bf16[2,32,1920]{2,1,0:T(8,128)(2,1)S(1)} collective-permute-done((bf16[2,32,1920]{2,1,0:T(8,128)(2,1)}, bf16[2,32,1920]{2,1,0:T(8,128)(2,1)S(1)}, u32[]{:S(2)}, u32[]{:S(2)}) %collective-permute-start.23) | collective-permute-done | bytes 245792 | tf_op jit(solution)/shard_map/ppermute | solution.py:414
  88.7 0.9 shard_map.111
  89.7 2.0 %collective-permute-start.24 = (bf16[2,32,1920]{2,1,0:T(8,128)(2,1)S(1)}, bf16[2,32,1920]{2,1,0:T(8,128)(2,1)S(1)}, u32[]{:S(2)}, u32[]{:S(2)}) collective-permute-start(bf16[2,32,1920]{2,1,0:T(8,128)(2,1)S(1)} %get-tuple-element.69), channel_id=1, source_target_pairs={{0,8},{1,5},{2,10},{3,7},{4,12},{5,1},{6,14},{7,3},{8,0},{9,13},{1... | collective-permute-start | bytes 737288 | tf_op jit(solution)/shard_map/ppermute | solution.py:443
  91.7 4.4 %collective-permute-done.26 = bf16[2,32,1920]{2,1,0:T(8,128)(2,1)S(1)} collective-permute-done((bf16[2,32,1920]{2,1,0:T(8,128)(2,1)}, bf16[2,32,1920]{2,1,0:T(8,128)(2,1)S(1)}, u32[]{:S(2)}, u32[]{:S(2)}) %collective-permute-start.26) | collective-permute-done | bytes 245792 | tf_op jit(solution)/shard_map/ppermute | solution.py:443
  96.1 1.0 broadcast_select_fusion.3
  97.1 1.3 collective-permute-start.27
  98.5 2.9 %collective-permute-done.24 = bf16[2,32,1920]{2,1,0:T(8,128)(2,1)S(1)} collective-permute-done((bf16[2,32,1920]{2,1,0:T(8,128)(2,1)S(1)}, bf16[2,32,1920]{2,1,0:T(8,128)(2,1)S(1)}, u32[]{:S(2)}, u32[]{:S(2)}) %collective-permute-start.24) | collective-permute-done | bytes 245792 | tf_op jit(solution)/shard_map/ppermute | solution.py:443
  101.5 1.3 collective-permute-start.25
  102.8 3.2 %collective-permute-done.27.coming_ref = bf16[2,64,1920]{2,1,0:T(8,128)(2,1)S(1)} collective-permute-done((bf16[2,64,1920]{2,1,0:T(8,128)(2,1)S(1)}, bf16[2,64,1920]{2,1,0:T(8,128)(2,1)S(1)}, u32[]{:S(2)}, u32[]{:S(2)}) %collective-permute-start.27) | collective-permute-done | bytes 491552 | tf_op jit(solution)/shard_map/ppermute | solution.py:443
  106.0 4.5 %shard_map.112.refs_2_ = bf16[1024,128]{1,0:T(8,128)(2,1)S(1)} custom-call(s32[1]{0:T(128)} %bitcast.3.first_ref, bf16[2,64,1920]{2,1,0:T(8,128)(2,1)S(1)} %pad_maximum_fusion.2.part_ref, bf16[2,64,1920]{2,1,0:T(8,128)(2,1)S(1)} %collective-permute-done.27.coming_ref, bf16[1024,1920]{1,0:T(8,128)(2,1)} %refs_0_.4, ...), custom_call_target="tpu_custom_call" | custom-call | flops 1006632960 | bytes 7864320 | tf_op jit(solution)/shard_map/pallas_call | solution.py:290
  110.5 0.9 collective-permute-start.28
  111.4 4.5 %shard_map.113 = f32[1024,128]{1,0:T(8,128)S(1)} custom-call(s32[1]{0:T(128)} %bitcast.3.first_ref, bf16[2,64,1920]{2,1,0:T(8,128)(2,1)S(1)} %pad_maximum_fusion.1.part_ref, bf16[2,64,1920]{2,1,0:T(8,128)(2,1)S(1)} %collective-permute-done.25.coming_ref, bf16[1024,1920]{1,0:T(8,128)(2,1)} %refs_0_.4, ...), custom_call_target="tpu_custom_call" | custom-call | tf_op jit(solution)/shard_map/pallas_call | solution.py:290
  115.9 1.3 collective-permute-done.28
  118.1 3.1 %collective-permute-start.31 = (bf16[1024,128]{1,0:T(8,128)(2,1)S(1)}, bf16[1024,128]{1,0:T(8,128)(2,1)S(1)}, u32[]{:S(2)}, u32[]{:S(2)}) collective-permute-start(bf16[1024,128]{1,0:T(8,128)(2,1)S(1)} %add_convert_fusion.refs_8_), channel_id=1, source_target_pairs={{4,0},{8,4},{12,8},{16,12},{20,16},{24,20},{28,24},{0,28},{5,1},{9... | collective-permute-start | bytes 786440 | tf_op jit(solution)/shard_map/ppermute | solution.py:420
  121.2 2.5 %collective-permute-done.32.refs_9_ = bf16[1024,128]{1,0:T(8,128)(2,1)S(1)} collective-permute-done((bf16[1024,128]{1,0:T(8,128)(2,1)S(1)}, bf16[1024,128]{1,0:T(8,128)(2,1)S(1)}, u32[]{:S(2)}, u32[]{:S(2)}) %collective-permute-start.32) | collective-permute-done | bytes 262176 | tf_op jit(solution)/shard_map/ppermute | solution.py:414
  123.7 3.5 %collective-permute-done.31.refs_10_ = bf16[1024,128]{1,0:T(8,128)(2,1)S(1)} collective-permute-done((bf16[1024,128]{1,0:T(8,128)(2,1)S(1)}, bf16[1024,128]{1,0:T(8,128)(2,1)S(1)}, u32[]{:S(2)}, u32[]{:S(2)}) %collective-permute-start.31) | collective-permute-done | bytes 262176 | tf_op jit(solution)/shard_map/ppermute | solution.py:420
  127.3 1.3 collective-permute-start.33
  128.6 1.7 %collective-permute-done.29.refs_6_ = bf16[1024,128]{1,0:T(8,128)(2,1)S(1)} collective-permute-done((bf16[1024,128]{1,0:T(8,128)(2,1)S(1)}, bf16[1024,128]{1,0:T(8,128)(2,1)S(1)}, u32[]{:S(2)}, u32[]{:S(2)}) %collective-permute-start.29) | collective-permute-done | bytes 262176 | tf_op jit(solution)/shard_map/ppermute | solution.py:419
  130.3 2.0 %collective-permute-start.30 = (bf16[1024,128]{1,0:T(8,128)(2,1)S(1)}, bf16[1024,128]{1,0:T(8,128)(2,1)S(1)}, u32[]{:S(2)}, u32[]{:S(2)}) collective-permute-start(bf16[1024,128]{1,0:T(8,128)(2,1)S(1)} %collective-permute-done.29.refs_6_), channel_id=1, source_target_pairs={{0,2},{1,3},{2,0},{3,1},{4,6},{5,7},{6,4},{7,5},{8,10},{9,11},{10,... | collective-permute-start | bytes 786440 | tf_op jit(solution)/shard_map/ppermute | solution.py:414
  132.2 2.2 %collective-permute-done.33.refs_11_ = bf16[1024,128]{1,0:T(8,128)(2,1)S(1)} collective-permute-done((bf16[1024,128]{1,0:T(8,128)(2,1)S(1)}, bf16[1024,128]{1,0:T(8,128)(2,1)S(1)}, u32[]{:S(2)}, u32[]{:S(2)}) %collective-permute-start.33) | collective-permute-done | bytes 262176 | tf_op jit(solution)/shard_map/ppermute | solution.py:414
  134.5 2.8 %collective-permute-done.30.refs_7_ = bf16[1024,128]{1,0:T(8,128)(2,1)S(1)} collective-permute-done((bf16[1024,128]{1,0:T(8,128)(2,1)S(1)}, bf16[1024,128]{1,0:T(8,128)(2,1)S(1)}, u32[]{:S(2)}, u32[]{:S(2)}) %collective-permute-start.30) | collective-permute-done | bytes 262176 | tf_op jit(solution)/shard_map/ppermute | solution.py:414
  137.3 2.3 %shard_map.114 = (bf16[24,128,128]{2,1,0:T(8,128)(2,1)S(1)}, bf16[3072,256]{1,0:T(8,128)(2,1)S(1)}, bf16[3072,256]{1,0:T(8,128)(2,1)S(1)}) custom-call(s32[24,2]{1,0:T(8,128)S(1)} %copy-done.6, bf16[1024,128]{1,0:T(8,128)(2,1)S(1)} %collective-permute-done.6.refs_16_.refs_0_, bf16[1024,128]{1,0:T(8,128)(2,1)S(1)} %collective-permute-done.18.refs_1_, ...), custom_call_target="tpu_custom_call" | custom-call | flops 201326592 | bytes 3932160 | tf_op jit(solution)/shard_map/pallas_call | solution.py:336
  140.4 1.6 %shard_map.115.first_ref = f32[24,128,128]{2,1,0:T(8,128)S(1)} custom-call(s32[24,2]{1,0:T(8,128)S(1)} %copy-done.4, bf16[3072,256]{1,0:T(8,128)(2,1)S(1)} %get-tuple-element.75.occ_ref, bf16[3072,256]{1,0:T(8,128)(2,1)S(1)} %get-tuple-element.76.resp_ref), custom_call_target="tpu_custom_call" | custom-call | flops 201326592 | bytes 1572864 | tf_op jit(solution)/shard_map/pallas_call | solution.py:358
  142.8 3.2 %shard_map.116 = (f32[24,256]{1,0:T(8,128)}, bf16[1024,512]{1,0:T(8,128)(2,1)}) custom-call(s32[1]{0:T(128)} %bitcast.core_ref, s32[24]{0:T(128)S(1)} %copy-done.8, bf16[24,256,128]{2,1,0:T(8,128)(2,1)S(1)} %copy-done.2, f32[24,128,128]{2,1,0:T(8,128)S(1)} %shard_map.115.first_ref, bf16[24,128,128]{2,1,0:T(8,128)(2,1)S(1)} %collective-permute-done.34.second_ref, ...), custom_call_target="tpu_custom_call" | custom-call | flops 402653184 | bytes 3932160 | tf_op jit(solution)/shard_map/pallas_call | solution.py:395
  (89 shorter events, 13.3 us)
Async XLA Ops:
  0.6 13.8 %copy-start.10 = (s32[24,2]{0,1:T(2,128)S(1)}, s32[24,2]{0,1:T(2,128)}, u32[]{:S(2)}) copy-start(s32[24,2]{0,1:T(2,128)} %param.10) | copy-start | bytes 580
  0.6 24.2 %copy-start.9 = (f32[1920]{0:T(1024)S(1)}, f32[1920]{0:T(1024)}, u32[]{:S(2)}) copy-start(f32[1920]{0:T(1024)} %param.17) | copy-start | bytes 23044
  0.7 39.1 %collective-permute-start.12 = (bf16[1024,1920]{1,0:T(8,128)(2,1)}, bf16[1024,1920]{1,0:T(8,128)(2,1)}, u32[]{:S(2)}, u32[]{:S(2)}) collective-permute-start(bf16[1024,1920]{1,0:T(8,128)(2,1)} %refs_0_.4), channel_id=1, source_target_pairs={{0,1},{1,0},{2,3},{3,2},{4,5},{5,4},{6,7},{7,6},{8,9},{9,8},{10,11... | collective-permute-start | bytes 11796488 | tf_op jit(solution)/shard_map/ppermute | solution.py:414
  2.2 33.2 %copy-start.11 = (f32[512]{0:T(512)S(1)}, f32[512]{0:T(512)}, u32[]{:S(2)}) copy-start(f32[512]{0:T(512)} %param.16) | copy-start | bytes 6148
  2.3 20.2 %collective-permute-start.7 = (bf16[1024,128]{1,0:T(8,128)(2,1)S(1)}, bf16[1024,128]{1,0:T(8,128)(2,1)S(1)}, u32[]{:S(2)}, u32[]{:S(2)}) collective-permute-start(bf16[1024,128]{1,0:T(8,128)(2,1)S(1)} %get-tuple-element.85.refs_17_.refs_2_), channel_id=1, source_target_pairs={{4,0},{8,4},{12,8},{16,12},{20,16},{24,20},{28,24},{0,28},{5,1},{9... | collective-permute-start | bytes 786440 | tf_op jit(solution)/shard_map/ppermute | solution.py:420
  7.9 14.7 %collective-permute-start.6 = (bf16[1024,128]{1,0:T(8,128)(2,1)S(1)}, bf16[1024,128]{1,0:T(8,128)(2,1)S(1)}, u32[]{:S(2)}, u32[]{:S(2)}) collective-permute-start(bf16[1024,128]{1,0:T(8,128)(2,1)S(1)} %get-tuple-element.85.refs_17_.refs_2_), channel_id=1, source_target_pairs={{0,4},{4,8},{8,12},{12,16},{16,20},{20,24},{24,28},{28,0},{1,5},{5... | collective-permute-start | bytes 786440 | tf_op jit(solution)/shard_map/ppermute | solution.py:419
  10.1 8.0 %collective-permute-start.1 = (bf16[800,128]{1,0:T(8,128)(2,1)S(1)}, bf16[800,128]{1,0:T(8,128)(2,1)S(1)}, u32[]{:S(2)}, u32[]{:S(2)}) collective-permute-start(bf16[800,128]{1,0:T(8,128)(2,1)S(1)} %get-tuple-element.41), channel_id=1, source_target_pairs={{0,2},{1,3},{2,0},{3,1},{4,6},{5,7},{6,4},{7,5},{8,10},{9,11},{10,... | collective-permute-start | bytes 614408 | tf_op jit(solution)/shard_map/ppermute | solution.py:414
  13.9 8.1 %collective-permute-start.5 = (bf16[800,128]{1,0:T(8,128)(2,1)S(1)}, bf16[800,128]{1,0:T(8,128)(2,1)S(1)}, u32[]{:S(2)}, u32[]{:S(2)}) collective-permute-start(bf16[800,128]{1,0:T(8,128)(2,1)S(1)} %get-tuple-element.44), channel_id=1, source_target_pairs={{0,2},{1,3},{2,0},{3,1},{4,6},{5,7},{6,4},{7,5},{8,10},{9,11},{10,... | collective-permute-start | bytes 614408 | tf_op jit(solution)/shard_map/ppermute | solution.py:414
  14.5 23.2 %copy-start.3 = (s32[24,2]{1,0:T(8,128)}, s32[24,2]{1,0:T(8,128)S(1)}, u32[]{:S(2)}) copy-start(s32[24,2]{1,0:T(8,128)S(1)} %copy.17.refs_0_.refs_4_.block_ref) | copy-start | bytes 580
  18.1 3.9 %collective-permute-start.2 = (s32[24,2]{1,0:T(8,128)S(1)}, s32[24,2]{1,0:T(8,128)S(1)}, u32[]{:S(2)}, u32[]{:S(2)}) collective-permute-start(s32[24,2]{1,0:T(8,128)S(1)} %copy.17.refs_0_.refs_4_.block_ref), channel_id=1, source_target_pairs={{0,2},{1,3},{2,0},{3,1},{4,6},{5,7},{6,4},{7,5},{8,10},{9,11},{10,... | collective-permute-start | bytes 584 | tf_op jit(solution)/shard_map/ppermute | solution.py:414
  22.0 1.9 %collective-permute-start = (s32[24,2]{1,0:T(8,128)S(1)}, s32[24,2]{1,0:T(8,128)S(1)}, u32[]{:S(2)}, u32[]{:S(2)}) collective-permute-start(s32[24,2]{1,0:T(8,128)S(1)} %copy.17.refs_0_.refs_4_.block_ref), channel_id=1, source_target_pairs={{0,1},{1,0},{2,3},{3,2},{4,5},{5,4},{6,7},{7,6},{8,9},{9,8},{10,11... | collective-permute-start | bytes 584 | tf_op jit(solution)/shard_map/ppermute | solution.py:414
  22.0 2.8 %collective-permute-start.4 = (bf16[12,128,128]{2,1,0:T(8,128)(2,1)S(1)}, bf16[12,128,128]{2,1,0:T(8,128)(2,1)S(1)}, u32[]{:S(2)}, u32[]{:S(2)}) collective-permute-start(bf16[12,128,128]{2,1,0:T(8,128)(2,1)S(1)} %get-tuple-element.43.refs_8_), channel_id=1, source_target_pairs={{0,1},{1,0},{2,3},{3,2},{4,5},{5,4},{6,7},{7,6},{8,9},{9,8},{10,11... | collective-permute-start | bytes 1179656 | tf_op jit(solution)/shard_map/ppermute | solution.py:414
  22.5 2.4 %collective-permute-start.9 = (bf16[12,128,128]{2,1,0:T(8,128)(2,1)S(1)}, bf16[12,128,128]{2,1,0:T(8,128)(2,1)S(1)}, u32[]{:S(2)}, u32[]{:S(2)}) collective-permute-start(bf16[12,128,128]{2,1,0:T(8,128)(2,1)S(1)} %get-tuple-element.46.refs_12_), channel_id=1, source_target_pairs={{0,1},{1,0},{2,3},{3,2},{4,5},{5,4},{6,7},{7,6},{8,9},{9,8},{10,11... | collective-permute-start | bytes 1179656 | tf_op jit(solution)/shard_map/ppermute | solution.py:414
  22.6 1.9 %collective-permute-start.3 = (s32[24,2]{1,0:T(8,128)S(1)}, s32[24,2]{1,0:T(8,128)S(1)}, u32[]{:S(2)}, u32[]{:S(2)}) collective-permute-start(s32[24,2]{1,0:T(8,128)S(1)} %collective-permute-done.2.refs_2_.refs_6_), channel_id=1, source_target_pairs={{0,1},{1,0},{2,3},{3,2},{4,5},{5,4},{6,7},{7,6},{8,9},{9,8},{10,11... | collective-permute-start | bytes 584 | tf_op jit(solution)/shard_map/ppermute | solution.py:414
  23.9 6.8 %copy-start.5 = (s32[24,2]{1,0:T(8,128)}, s32[24,2]{1,0:T(8,128)S(1)}, u32[]{:S(2)}) copy-start(s32[24,2]{1,0:T(8,128)S(1)} %collective-permute-done.refs_1_.refs_5_.block_ref) | copy-start | bytes 580
  23.9 1.8 %collective-permute-start.10 = (bf16[12,128,128]{2,1,0:T(8,128)(2,1)S(1)}, bf16[12,128,128]{2,1,0:T(8,128)(2,1)S(1)}, u32[]{:S(2)}, u32[]{:S(2)}) collective-permute-start(bf16[12,128,128]{2,1,0:T(8,128)(2,1)S(1)} %shard_map.105.refs_14_), channel_id=1, source_target_pairs={{0,1},{1,0},{2,3},{3,2},{4,5},{5,4},{6,7},{7,6},{8,9},{9,8},{10,11... | collective-permute-start | bytes 1179656 | tf_op jit(solution)/shard_map/ppermute | solution.py:414
  24.4 1.8 %collective-permute-start.8 = (bf16[12,128,128]{2,1,0:T(8,128)(2,1)S(1)}, bf16[12,128,128]{2,1,0:T(8,128)(2,1)S(1)}, u32[]{:S(2)}, u32[]{:S(2)}) collective-permute-start(bf16[12,128,128]{2,1,0:T(8,128)(2,1)S(1)} %shard_map.107.refs_10_), channel_id=1, source_target_pairs={{0,1},{1,0},{2,3},{3,2},{4,5},{5,4},{6,7},{7,6},{8,9},{9,8},{10,11... | collective-permute-start | bytes 1179656 | tf_op jit(solution)/shard_map/ppermute | solution.py:414
  24.8 14.9 %collective-permute-start.11 = (f32[1920]{0:T(1024)S(1)}, f32[1920]{0:T(1024)S(1)}, u32[]{:S(2)}, u32[]{:S(2)}) collective-permute-start(f32[1920]{0:T(1024)S(1)} %copy-done.9), channel_id=1, source_target_pairs={{0,1},{1,0},{2,3},{3,2},{4,5},{5,4},{6,7},{7,6},{8,9},{9,8},{10,11... | collective-permute-start | bytes 23048 | tf_op jit(solution)/shard_map/ppermute | solution.py:414
  30.7 12.0 %collective-permute-start.13 = (bf16[1024,128]{1,0:T(8,128)(2,1)S(1)}, bf16[1024,128]{1,0:T(8,128)(2,1)S(1)}, u32[]{:S(2)}, u32[]{:S(2)}) collective-permute-start(bf16[1024,128]{1,0:T(8,128)(2,1)S(1)} %get-tuple-element.52), channel_id=1, source_target_pairs={{0,4},{4,8},{8,12},{12,16},{16,20},{20,24},{24,28},{28,0},{1,5},{5... | collective-permute-start | bytes 786440 | tf_op jit(solution)/shard_map/ppermute | solution.py:564
  30.8 14.3 %collective-permute-start.14 = (bf16[1024,128]{1,0:T(8,128)(2,1)S(1)}, bf16[1024,128]{1,0:T(8,128)(2,1)S(1)}, u32[]{:S(2)}, u32[]{:S(2)}) collective-permute-start(bf16[1024,128]{1,0:T(8,128)(2,1)S(1)} %get-tuple-element.53), channel_id=1, source_target_pairs={{4,0},{8,4},{12,8},{16,12},{20,16},{24,20},{28,24},{0,28},{5,1},{9... | collective-permute-start | bytes 786440 | tf_op jit(solution)/shard_map/ppermute | solution.py:565
  37.7 2.0 %copy-start = (bf16[1024,1920]{1,0:T(8,128)(2,1)}, bf16[1024,1920]{1,0:T(8,128)(2,1)S(1)}, u32[]{:S(2)}) copy-start(bf16[1024,1920]{1,0:T(8,128)(2,1)S(1)} %shard_map.109) | copy-start | bytes 11796484
  41.8 5.7 %copy-start.1 = (bf16[1024,1920]{1,0:T(8,128)(2,1)S(1)}, bf16[1024,1920]{1,0:T(8,128)(2,1)}, u32[]{:S(2)}) copy-start(bf16[1024,1920]{1,0:T(8,128)(2,1)} %copy-done) | copy-start | bytes 11796484
  45.2 7.7 %collective-permute-start.20 = (bf16[1024,128]{1,0:T(8,128)(2,1)S(1)}, bf16[1024,128]{1,0:T(8,128)(2,1)S(1)}, u32[]{:S(2)}, u32[]{:S(2)}) collective-permute-start(bf16[1024,128]{1,0:T(8,128)(2,1)S(1)} %add_convert_fusion.1), channel_id=1, source_target_pairs={{0,2},{1,3},{2,0},{3,1},{4,6},{5,7},{6,4},{7,5},{8,10},{9,11},{10,... | collective-permute-start | bytes 786440 | tf_op jit(solution)/shard_map/ppermute | solution.py:414
  48.3 8.9 %collective-permute-start.15 = (bf16[2,64,1920]{2,1,0:T(8,128)(2,1)S(1)}, bf16[2,64,1920]{2,1,0:T(8,128)(2,1)S(1)}, u32[]{:S(2)}, u32[]{:S(2)}) collective-permute-start(bf16[2,64,1920]{2,1,0:T(8,128)(2,1)S(1)} %fusion.5), channel_id=1, source_target_pairs={{0,4},{1,9},{2,6},{3,11},{4,0},{5,13},{6,2},{7,15},{8,12},{9,1},{1... | collective-permute-start | bytes 1474568 | tf_op jit(solution)/shard_map/ppermute | solution.py:443
  54.5 13.6 %collective-permute-start.21 = (bf16[2,64,1920]{2,1,0:T(8,128)(2,1)S(1)}, bf16[2,64,1920]{2,1,0:T(8,128)(2,1)S(1)}, u32[]{:S(2)}, u32[]{:S(2)}) collective-permute-start(bf16[2,64,1920]{2,1,0:T(8,128)(2,1)S(1)} %fusion.1), channel_id=1, source_target_pairs={{0,4},{1,9},{2,6},{3,11},{4,0},{5,13},{6,2},{7,15},{8,12},{9,1},{1... | collective-permute-start | bytes 1474568 | tf_op jit(solution)/shard_map/ppermute | solution.py:443
  57.4 11.0 %collective-permute-start.16 = (bf16[2,32,1920]{2,1,0:T(8,128)(2,1)S(1)}, bf16[2,32,1920]{2,1,0:T(8,128)(2,1)S(1)}, u32[]{:S(2)}, u32[]{:S(2)}) collective-permute-start(bf16[2,32,1920]{2,1,0:T(8,128)(2,1)S(1)} %dynamic-slice_convert_fusion.1), channel_id=1, source_target_pairs={{0,8},{1,5},{2,10},{3,7},{4,12},{5,1},{6,14},{7,3},{8,0},{9,13},{1... | collective-permute-start | bytes 737288 | tf_op jit(solution)/shard_map/ppermute | solution.py:443
  68.3 9.1 %collective-permute-start.22 = (bf16[2,32,1920]{2,1,0:T(8,128)(2,1)S(1)}, bf16[2,32,1920]{2,1,0:T(8,128)(2,1)S(1)}, u32[]{:S(2)}, u32[]{:S(2)}) collective-permute-start(bf16[2,32,1920]{2,1,0:T(8,128)(2,1)S(1)} %dynamic-slice_convert_fusion), channel_id=1, source_target_pairs={{0,8},{1,5},{2,10},{3,7},{4,12},{5,1},{6,14},{7,3},{8,0},{9,13},{1... | collective-permute-start | bytes 737288 | tf_op jit(solution)/shard_map/ppermute | solution.py:443
  68.4 17.7 %collective-permute-start.17 = (bf16[2,32,1920]{2,1,0:T(8,128)(2,1)S(1)}, bf16[2,32,1920]{2,1,0:T(8,128)(2,1)S(1)}, u32[]{:S(2)}, u32[]{:S(2)}) collective-permute-start(bf16[2,32,1920]{2,1,0:T(8,128)(2,1)S(1)} %get-tuple-element.58), channel_id=1, source_target_pairs={{0,16},{4,20},{8,24},{12,28},{16,0},{20,4},{24,8},{28,12},{1,17},{... | collective-permute-start | bytes 737288 | tf_op jit(solution)/shard_map/ppermute | solution.py:414
  71.5 14.6 %collective-permute-start.18 = (bf16[1024,128]{1,0:T(8,128)(2,1)S(1)}, bf16[1024,128]{1,0:T(8,128)(2,1)S(1)}, u32[]{:S(2)}, u32[]{:S(2)}) collective-permute-start(bf16[1024,128]{1,0:T(8,128)(2,1)S(1)} %collective-permute-done.6.refs_16_.refs_0_), channel_id=1, source_target_pairs={{0,2},{1,3},{2,0},{3,1},{4,6},{5,7},{6,4},{7,5},{8,10},{9,11},{10,... | collective-permute-start | bytes 786440 | tf_op jit(solution)/shard_map/ppermute | solution.py:414
  71.5 14.6 %collective-permute-start.19 = (bf16[1024,128]{1,0:T(8,128)(2,1)S(1)}, bf16[1024,128]{1,0:T(8,128)(2,1)S(1)}, u32[]{:S(2)}, u32[]{:S(2)}) collective-permute-start(bf16[1024,128]{1,0:T(8,128)(2,1)S(1)} %collective-permute-done.7.refs_18_.refs_4_), channel_id=1, source_target_pairs={{0,2},{1,3},{2,0},{3,1},{4,6},{5,7},{6,4},{7,5},{8,10},{9,11},{10,... | collective-permute-start | bytes 786440 | tf_op jit(solution)/shard_map/ppermute | solution.py:414
  78.1 10.7 %collective-permute-start.23 = (bf16[2,32,1920]{2,1,0:T(8,128)(2,1)}, bf16[2,32,1920]{2,1,0:T(8,128)(2,1)S(1)}, u32[]{:S(2)}, u32[]{:S(2)}) collective-permute-start(bf16[2,32,1920]{2,1,0:T(8,128)(2,1)} %get-tuple-element.67), channel_id=1, source_target_pairs={{0,16},{4,20},{8,24},{12,28},{16,0},{20,4},{24,8},{28,12},{1,17},{... | collective-permute-start | bytes 737288 | tf_op jit(solution)/shard_map/ppermute | solution.py:414
  89.7 6.4 %collective-permute-start.26 = (bf16[2,32,1920]{2,1,0:T(8,128)(2,1)}, bf16[2,32,1920]{2,1,0:T(8,128)(2,1)S(1)}, u32[]{:S(2)}, u32[]{:S(2)}) collective-permute-start(bf16[2,32,1920]{2,1,0:T(8,128)(2,1)} %get-tuple-element.70), channel_id=1, source_target_pairs={{0,8},{1,5},{2,10},{3,7},{4,12},{5,1},{6,14},{7,3},{8,0},{9,13},{1... | collective-permute-start | bytes 737288 | tf_op jit(solution)/shard_map/ppermute | solution.py:443
  89.7 11.7 %collective-permute-start.24 = (bf16[2,32,1920]{2,1,0:T(8,128)(2,1)S(1)}, bf16[2,32,1920]{2,1,0:T(8,128)(2,1)S(1)}, u32[]{:S(2)}, u32[]{:S(2)}) collective-permute-start(bf16[2,32,1920]{2,1,0:T(8,128)(2,1)S(1)} %get-tuple-element.69), channel_id=1, source_target_pairs={{0,8},{1,5},{2,10},{3,7},{4,12},{5,1},{6,14},{7,3},{8,0},{9,13},{1... | collective-permute-start | bytes 737288 | tf_op jit(solution)/shard_map/ppermute | solution.py:443
  97.1 8.9 %collective-permute-start.27 = (bf16[2,64,1920]{2,1,0:T(8,128)(2,1)S(1)}, bf16[2,64,1920]{2,1,0:T(8,128)(2,1)S(1)}, u32[]{:S(2)}, u32[]{:S(2)}) collective-permute-start(bf16[2,64,1920]{2,1,0:T(8,128)(2,1)S(1)} %pad_maximum_fusion.2.part_ref), channel_id=1, source_target_pairs={{0,4},{1,9},{2,6},{3,11},{4,0},{5,13},{6,2},{7,15},{8,12},{9,1},{1... | collective-permute-start | bytes 1474568 | tf_op jit(solution)/shard_map/ppermute | solution.py:443
  101.5 10.0 %collective-permute-start.25 = (bf16[2,64,1920]{2,1,0:T(8,128)(2,1)S(1)}, bf16[2,64,1920]{2,1,0:T(8,128)(2,1)S(1)}, u32[]{:S(2)}, u32[]{:S(2)}) collective-permute-start(bf16[2,64,1920]{2,1,0:T(8,128)(2,1)S(1)} %pad_maximum_fusion.1.part_ref), channel_id=1, source_target_pairs={{0,4},{1,9},{2,6},{3,11},{4,0},{5,13},{6,2},{7,15},{8,12},{9,1},{1... | collective-permute-start | bytes 1474568 | tf_op jit(solution)/shard_map/ppermute | solution.py:443
  110.5 26.8 %copy-start.6 = (s32[24,2]{1,0:T(8,128)S(1)}, s32[24,2]{1,0:T(8,128)}, u32[]{:S(2)}) copy-start(s32[24,2]{1,0:T(8,128)} %copy-done.5) | copy-start | bytes 580
  110.5 6.7 %collective-permute-start.28 = (bf16[1024,128]{1,0:T(8,128)(2,1)S(1)}, bf16[1024,128]{1,0:T(8,128)(2,1)S(1)}, u32[]{:S(2)}, u32[]{:S(2)}) collective-permute-start(bf16[1024,128]{1,0:T(8,128)(2,1)S(1)} %shard_map.112.refs_2_), channel_id=1, source_target_pairs={{0,2},{1,3},{2,0},{3,1},{4,6},{5,7},{6,4},{7,5},{8,10},{9,11},{10,... | collective-permute-start | bytes 786440 | tf_op jit(solution)/shard_map/ppermute | solution.py:414
  115.9 24.5 %copy-start.4 = (s32[24,2]{1,0:T(8,128)S(1)}, s32[24,2]{1,0:T(8,128)}, u32[]{:S(2)}) copy-start(s32[24,2]{1,0:T(8,128)} %copy-done.3) | copy-start | bytes 580
  117.3 6.4 %collective-permute-start.32 = (bf16[1024,128]{1,0:T(8,128)(2,1)S(1)}, bf16[1024,128]{1,0:T(8,128)(2,1)S(1)}, u32[]{:S(2)}, u32[]{:S(2)}) collective-permute-start(bf16[1024,128]{1,0:T(8,128)(2,1)S(1)} %add_convert_fusion.refs_8_), channel_id=1, source_target_pairs={{0,2},{1,3},{2,0},{3,1},{4,6},{5,7},{6,4},{7,5},{8,10},{9,11},{10,... | collective-permute-start | bytes 786440 | tf_op jit(solution)/shard_map/ppermute | solution.py:414
  118.1 9.2 %collective-permute-start.31 = (bf16[1024,128]{1,0:T(8,128)(2,1)S(1)}, bf16[1024,128]{1,0:T(8,128)(2,1)S(1)}, u32[]{:S(2)}, u32[]{:S(2)}) collective-permute-start(bf16[1024,128]{1,0:T(8,128)(2,1)S(1)} %add_convert_fusion.refs_8_), channel_id=1, source_target_pairs={{4,0},{8,4},{12,8},{16,12},{20,16},{24,20},{28,24},{0,28},{5,1},{9... | collective-permute-start | bytes 786440 | tf_op jit(solution)/shard_map/ppermute | solution.py:420
  121.2 9.1 %collective-permute-start.29 = (bf16[1024,128]{1,0:T(8,128)(2,1)S(1)}, bf16[1024,128]{1,0:T(8,128)(2,1)S(1)}, u32[]{:S(2)}, u32[]{:S(2)}) collective-permute-start(bf16[1024,128]{1,0:T(8,128)(2,1)S(1)} %add_convert_fusion.refs_8_), channel_id=1, source_target_pairs={{0,4},{4,8},{8,12},{12,16},{16,20},{20,24},{24,28},{28,0},{1,5},{5... | collective-permute-start | bytes 786440 | tf_op jit(solution)/shard_map/ppermute | solution.py:419
  127.3 7.2 %collective-permute-start.33 = (bf16[1024,128]{1,0:T(8,128)(2,1)S(1)}, bf16[1024,128]{1,0:T(8,128)(2,1)S(1)}, u32[]{:S(2)}, u32[]{:S(2)}) collective-permute-start(bf16[1024,128]{1,0:T(8,128)(2,1)S(1)} %collective-permute-done.31.refs_10_), channel_id=1, source_target_pairs={{0,2},{1,3},{2,0},{3,1},{4,6},{5,7},{6,4},{7,5},{8,10},{9,11},{10,... | collective-permute-start | bytes 786440 | tf_op jit(solution)/shard_map/ppermute | solution.py:414
  130.3 7.0 %collective-permute-start.30 = (bf16[1024,128]{1,0:T(8,128)(2,1)S(1)}, bf16[1024,128]{1,0:T(8,128)(2,1)S(1)}, u32[]{:S(2)}, u32[]{:S(2)}) collective-permute-start(bf16[1024,128]{1,0:T(8,128)(2,1)S(1)} %collective-permute-done.29.refs_6_), channel_id=1, source_target_pairs={{0,2},{1,3},{2,0},{3,1},{4,6},{5,7},{6,4},{7,5},{8,10},{9,11},{10,... | collective-permute-start | bytes 786440 | tf_op jit(solution)/shard_map/ppermute | solution.py:414
  139.6 3.1 %copy-start.2 = (bf16[24,256,128]{2,1,0:T(8,128)(2,1)S(1)}, bf16[24,256,128]{2,1,0:T(8,128)(2,1)}, u32[]{:S(2)}) copy-start(bf16[24,256,128]{2,1,0:T(8,128)(2,1)} %basis_ref.1) | copy-start | bytes 4718596
  139.6 3.1 %copy-start.7 = (f32[24,256]{1,0:T(8,128)S(1)}, f32[24,256]{1,0:T(8,128)}, u32[]{:S(2)}) copy-start(f32[24,256]{1,0:T(8,128)} %scale_ref.1) | copy-start | bytes 73732
  139.6 3.1 %copy-start.8 = (s32[24]{0:T(128)S(1)}, s32[24]{0:T(128)}, u32[]{:S(2)}) copy-start(s32[24]{0:T(128)} %counts_ref.1) | copy-start | bytes 292
  139.6 3.1 %collective-permute-start.34 = (bf16[24,128,128]{2,1,0:T(8,128)(2,1)S(1)}, bf16[24,128,128]{2,1,0:T(8,128)(2,1)S(1)}, u32[]{:S(2)}, u32[]{:S(2)}) collective-permute-start(bf16[24,128,128]{2,1,0:T(8,128)(2,1)S(1)} %get-tuple-element.77), channel_id=1, source_target_pairs={{0,1},{1,0},{2,3},{3,2},{4,5},{5,4},{6,7},{7,6},{8,9},{9,8},{10,11... | collective-permute-start | bytes 2359304 | tf_op jit(solution)/shard_map/ppermute | solution.py:414
  139.8 2.9 %collective-permute-start.35 = (bf16[1024,256]{1,0:T(8,128)(2,1)S(1)}, bf16[1024,256]{1,0:T(8,128)(2,1)S(1)}, u32[]{:S(2)}, u32[]{:S(2)}) collective-permute-start(bf16[1024,256]{1,0:T(8,128)(2,1)S(1)} %pad_maximum_fusion.half_ref), channel_id=1, source_target_pairs={{0,1},{1,0},{2,3},{3,2},{4,5},{5,4},{6,7},{7,6},{8,9},{9,8},{10,11... | collective-permute-start | bytes 1572872 | tf_op jit(solution)/shard_map/ppermute | solution.py:414

commit v10 on v9

--- a/solution.py
+++ b/solution.py
@@ -186,11 +186,10 @@
 
 
 def apply_kernel(starts, rows, *refs):
-    pieces = len(starts)
-    block_refs, ham_refs = refs[:pieces], refs[pieces : 2 * pieces]
-    window_refs = refs[2 * pieces : 2 * pieces + 3]
-    out_before, out_own, out_after = refs[2 * pieces + 3 : 2 * pieces + 6]
-    window, total = refs[2 * pieces + 6 :]
+    pieces, lists = len(starts), len(refs) - len(starts) - 8
+    block_refs, refs = refs[:lists] * (pieces // lists), refs[lists:]
+    ham_refs, window_refs = refs[:pieces], refs[pieces : pieces + 3]
+    out_before, out_own, out_after, window, total = refs[pieces + 3 :]
     region = window_refs[0].shape[0]
     for side, ref in enumerate(window_refs):
         window[side * region : (side + 1) * region] = ref[...]
@@ -209,7 +208,7 @@
                     total[at, :] += product[j * rows : (j + 1) * rows]
             return carry
 
-        lax.fori_loop(0, count, step, 0, unroll=2)
+        lax.fori_loop(0, count, step, 0, unroll=6)
 
     shares = {}
     smallest = min(ref.shape[0] for ref in ham_refs)
@@ -236,7 +235,7 @@
             jax.ShapeDtypeStruct((region, width), F32),
             jax.ShapeDtypeStruct((region, width), BF16),
         ],
-        in_specs=[SMEM] * pieces + [VMEM] * (pieces + 3),
+        in_specs=[SMEM] * len(blocks) + [VMEM] * (pieces + 3),
         out_specs=[VMEM] * 3,
         scratch_shapes=[
             pltpu.VMEM((3 * region, width), BF16),
@@ -370,7 +369,7 @@
 
 
 def density_kernel(
-    core_ref, counts_ref, basis_ref, first_ref, second_ref, scale_ref, half_ref, near_ref,
+    core_ref, basis_ref, first_ref, second_ref, scale_ref, half_ref, near_ref,
     out_ref, coef_ref, semaphores,
 ):
     width = half_ref.shape[1]
@@ -383,13 +382,13 @@
         values = basis_ref[b]
         overlap = first_ref[b] + second_ref[b].astype(F32)
         product = split_dot(overlap, values, NT)
-        density = 4.0 * jnp.sum(product * values.astype(F32).T, axis=0, keepdims=True)
-        out_ref[b : b + 1, :] = live_row(scale_ref, counts_ref, b) * density
+        density = jnp.sum(product * values.astype(F32).T, axis=0, keepdims=True)
+        out_ref[b : b + 1, :] = scale_ref[b : b + 1, :] * density
     for copy in waits:
         copy.wait()
 
 
-def density(core, basis_values, counts, first, second, scale, half, half_near):
+def density(core, basis_values, first, second, scale, half, half_near):
     nbatch, points, columns = basis_values.shape
     region, width = half.shape
     return pl.pallas_call(
@@ -398,7 +397,7 @@
             jax.ShapeDtypeStruct((nbatch, points), F32),
             jax.ShapeDtypeStruct((region, 2 * width), BF16),
         ],
-        in_specs=[SMEM] * 2 + [VMEM] * 4 + [HBM] * 2,
+        in_specs=[SMEM] + [VMEM] * 4 + [HBM] * 2,
         out_specs=[VMEM, HBM],
         scratch_shapes=[pltpu.SemaphoreType.DMA((2,))],
         compiler_params=params(),
@@ -407,7 +406,7 @@
             bytes_accessed=basis_values.size * 2 + nbatch * columns * columns * 6,
             transcendentals=0,
         ),
-    )(core.reshape(1), counts, basis_values, place_in(first, pltpu.VMEM), second, scale, half, half_near)
+    )(core.reshape(1), basis_values, place_in(first, pltpu.VMEM), second, scale, half, half_near)
 
 
 def flip(array, axis, mask):
@@ -536,18 +535,18 @@
         arrived.append(flip(packed, "tile", 2))
     arrived[0], occ_before, occ_after = together(arrived[0], occ_before, occ_after)
     far = [unpack(array, size, columns) for array, size in zip(arrived, sizes)]
-    far[-1], lists[2] = together(far[-1], lists[2])
+    far[0], lists[2] = together(far[0], lists[2])
     lists.append(flip(lists[2], "tile", 1))
     hams = []
     for full, other in zip(fulls, far):
         hams += [full, flip(full, "tile", 1), other, flip(other, "tile", 1)]
-    places, blocks_near = lists * len(sizes), lists[1]
+    blocks_near = lists[1]
     starts = [sum(sizes[:i]) for i in range(len(sizes)) for _ in range(4)]
     virtuals = [virt_coef, flip(virt_coef, "tile", 1)]
     energies = jnp.stack([virt_energy, flip(virt_energy, "tile", 1)])
 
     to_before, own_sum, to_after = apply_window(
-        places,
+        lists,
         hams,
         starts,
         occ_before,
@@ -559,7 +558,9 @@
         for place in (quarter, quarter ^ 1)
     ]
     loaded = [load(array) for array in virtuals]
-    own_sum, energies, levels, loaded = together(own_sum, energies, levels, loaded)
+    points = lax.broadcasted_iota(jnp.int32, xc_kernel.shape, 1)
+    scale = jnp.where(points < counts[:, None], 4.0 * xc_kernel, 0.0)
+    own_sum, energies, levels, loaded, scale = together(own_sum, energies, levels, loaded, scale)
     size = lax.axis_size("grid")
     from_before = lax.ppermute(to_after, "grid", [(i, (i + 1) % size) for i in range(size)])
     from_after = lax.ppermute(to_before, "grid", [((i + 1) % size, i) for i in range(size)])
@@ -606,7 +607,7 @@
 
     resp_before, resp_after = neighbours(resp_own)
     resp_before_far = flip(resp_before, "tile", 2)
-    resp_after, resp_far = together(resp_after, flip(resp_own, "tile", 2))
+    resp_far, resp_after = together(flip(resp_own, "tile", 2), resp_after)
     resp_after_far = flip(resp_after, "tile", 2)
     first = chip == 0
     half = jnp.concatenate(
@@ -621,10 +622,9 @@
     response_potential, response_coef = density(
         core,
         basis_values,
-        counts,
         overlaps(blocks, columns, occ_window, resp_window),
         flip(overlap_near, "tile", 1),
-        xc_kernel,
+        scale,
         half,
         flip(half, "tile", 1),
     )

time: 148 us -> 145 us (0.980)
  Pallas kernels: 31.8 us -> 29.7 us
  starting transfers between devices: 37.2 us -> 35.2 us
  waiting for transfers between devices: 66.9 us -> 68.5 us
    ppermute x22, starting transfers between devices: 18.3 us -> 15.7 us  [flip(): lax.ppermute(array, axis, [(i, i ^ mask) for i in range(lax.axis_size(axi...]
  transfers between devices with their start and end apart: 36 -> 36, of which waited for: 23 -> 24; matrix products, arithmetic and copies ran while one was open for 5% -> 5% of each run, Pallas kernels for 17% -> 17%
where the time goes in v10:
time: 145 us; the launch traced here: 144 us
  waiting for transfers between devices  68.5 us (47%)
  starting transfers between devices  35.2 us (24%)
  Pallas kernels  29.7 us (20%)
  local copies, waits for them, and re-layouts  3.54 us (2%)
  other arithmetic  3.17 us (2%)
  matrix products  2.97 us (2%)
    ppermute x22, waiting for transfers between devices, flip(): lax.ppermute(array, axis, [(i, i ^ mask) for i in range(lax.axis_size(axi...  32.4 us
    ppermute x8, waiting for transfers between devices, swap(): return lax.ppermute(array, ('grid', 'tile'), pairs)  28 us
    ppermute x22, starting transfers between devices, flip(): lax.ppermute(array, axis, [(i, i ^ mask) for i in range(lax.axis_size(axi...  15.7 us
    ppermute x2, starting transfers between devices, neighbours(): lax.ppermute(array, 'grid', [((i + 1) % size, i) for i in range(size)])  9.4 us
    pallas_call x2, Pallas kernels, expand(): pl.pallas_call(expand_kernel, out_shape=jax.ShapeDtypeStruct((region, wid...  8.9 us
    ppermute x8, starting transfers between devices, swap(): return lax.ppermute(array, ('grid', 'tile'), pairs)  5.32 us
    ppermute x1, starting transfers between devices, per_device(): lax.ppermute(to_before, 'grid', [((i + 1) % size, i) for i in range(size)])  4.71 us
    pallas_call x2, Pallas kernels, integrate(): pl.pallas_call(functools.partial(integrate_kernel, start), out_shape=[plt...  4.37 us
  transfers between devices with their start and end apart: 36, of which 24 were waited for; matrix products, arithmetic and copies ran while one was open for 5% of the time, Pallas kernels for 17%

profile of v10, /device:TPU:0, one launch (start us, length us, event | category | flops | bytes accessed | tf_op | source)
XLA Modules:
  0.0 144.3 jit_solution(10621470043389178347)
XLA Ops:
  1.2 1.1 constant_dynamic-slice_fusion
  2.3 5.7 %collective-permute-start.3 = (bf16[1024,128]{1,0:T(8,128)(2,1)S(1)}, bf16[1024,128]{1,0:T(8,128)(2,1)S(1)}, u32[]{:S(2)}, u32[]{:S(2)}) collective-permute-start(bf16[1024,128]{1,0:T(8,128)(2,1)S(1)} %get-tuple-element.87.refs_13_.refs_2_), channel_id=1, source_target_pairs={{4,0},{8,4},{12,8},{16,12},{20,16},{24,20},{28,24},{0,28},{5,1},{9... | collective-permute-start | bytes 786440 | tf_op jit(solution)/shard_map/ppermute | solution.py:419
  7.9 2.2 %shard_map.104 = (bf16[12,128,128]{2,1,0:T(8,128)(2,1)S(1)}, bf16[800,128]{1,0:T(8,128)(2,1)S(1)}) custom-call(s32[24]{0:T(128)} %counts_hbm.3, bf16[24,256,128]{2,1,0:T(8,128)(2,1)} %basis_ref.1, f32[24,256]{1,0:T(8,128)} %weights_hbm.3), custom_call_target="tpu_custom_call" | custom-call | flops 201326592 | bytes 1376256 | tf_op jit(solution)/shard_map/pallas_call | solution.py:121
  10.1 1.6 %collective-permute-start.1 = (bf16[800,128]{1,0:T(8,128)(2,1)S(1)}, bf16[800,128]{1,0:T(8,128)(2,1)S(1)}, u32[]{:S(2)}, u32[]{:S(2)}) collective-permute-start(bf16[800,128]{1,0:T(8,128)(2,1)S(1)} %get-tuple-element.42), channel_id=1, source_target_pairs={{0,2},{1,3},{2,0},{3,1},{4,6},{5,7},{6,4},{7,5},{8,10},{9,11},{10,... | collective-permute-start | bytes 614408 | tf_op jit(solution)/shard_map/ppermute | solution.py:413
  11.7 2.2 %shard_map.106 = (bf16[12,128,128]{2,1,0:T(8,128)(2,1)S(1)}, bf16[800,128]{1,0:T(8,128)(2,1)S(1)}) custom-call(s32[24]{0:T(128)} %counts_hbm.3, bf16[24,256,128]{2,1,0:T(8,128)(2,1)} %basis_ref.1, f32[24,256]{1,0:T(8,128)} %weights_hbm.3), custom_call_target="tpu_custom_call" | custom-call | flops 201326592 | bytes 1376256 | tf_op jit(solution)/shard_map/pallas_call | solution.py:121
  14.6 3.5 %collective-permute-done.1.packed_ref = bf16[800,128]{1,0:T(8,128)(2,1)S(1)} collective-permute-done((bf16[800,128]{1,0:T(8,128)(2,1)S(1)}, bf16[800,128]{1,0:T(8,128)(2,1)S(1)}, u32[]{:S(2)}, u32[]{:S(2)}) %collective-permute-start.1) | collective-permute-done | bytes 204832 | tf_op jit(solution)/shard_map/ppermute | solution.py:413
  18.1 1.5 %collective-permute-start.4 = (s32[24,2]{1,0:T(8,128)S(1)}, s32[24,2]{1,0:T(8,128)S(1)}, u32[]{:S(2)}, u32[]{:S(2)}) collective-permute-start(s32[24,2]{1,0:T(8,128)S(1)} %copy.16.refs_0_.block_ref), channel_id=1, source_target_pairs={{0,2},{1,3},{2,0},{3,1},{4,6},{5,7},{6,4},{7,5},{8,10},{9,11},{10,... | collective-permute-start | bytes 584 | tf_op jit(solution)/shard_map/ppermute | solution.py:413
  20.1 0.9 shard_map.105.refs_6_
  21.0 1.0 collective-permute-done.4.refs_2_
  22.5 0.9 shard_map.107.refs_10_
  25.8 3.1 %shard_map.108 = (bf16[1024,128]{1,0:T(8,128)(2,1)S(1)}, f32[1024,128]{1,0:T(8,128)S(1)}, bf16[1024,128]{1,0:T(8,128)(2,1)S(1)}) custom-call(s32[24,2]{1,0:T(8,128)S(1)} %copy.16.refs_0_.block_ref, s32[24,2]{1,0:T(8,128)S(1)} %collective-permute-done.refs_1_.block_ref, s32[24,2]{1,0:T(8,128)S(1)} %collective-permute-done.4.refs_2_, ...), custom_call_target="tpu_custom_call" | custom-call | flops 402653184 | bytes 4980736 | tf_op jit(solution)/shard_map/pallas_call | solution.py:231
  28.9 4.7 %collective-permute-start.14 = (bf16[1024,128]{1,0:T(8,128)(2,1)S(1)}, bf16[1024,128]{1,0:T(8,128)(2,1)S(1)}, u32[]{:S(2)}, u32[]{:S(2)}) collective-permute-start(bf16[1024,128]{1,0:T(8,128)(2,1)S(1)} %get-tuple-element.54), channel_id=1, source_target_pairs={{4,0},{8,4},{12,8},{16,12},{20,16},{24,20},{28,24},{0,28},{5,1},{9... | collective-permute-start | bytes 786440 | tf_op jit(solution)/shard_map/ppermute | solution.py:566
  33.7 2.1 %shard_map.109 = bf16[1024,1920]{1,0:T(8,128)(2,1)S(1)} custom-call(bf16[1024,1920]{1,0:T(8,128)(2,1)} %refs_0_.4), custom_call_target="tpu_custom_call" | custom-call | bytes 7864320 | tf_op jit(solution)/shard_map/pallas_call | solution.py:47
  35.9 1.9 %copy-done = bf16[1024,1920]{1,0:T(8,128)(2,1)} copy-done((bf16[1024,1920]{1,0:T(8,128)(2,1)}, bf16[1024,1920]{1,0:T(8,128)(2,1)S(1)}, u32[]{:S(2)}) %copy-start) | copy-done | bytes 3932184
  37.9 2.1 %shard_map.110 = bf16[1024,1920]{1,0:T(8,128)(2,1)S(1)} custom-call(bf16[1024,1920]{1,0:T(8,128)(2,1)} %collective-permute-done.12.source_ref.refs_1_), custom_call_target="tpu_custom_call" | custom-call | bytes 7864320 | tf_op jit(solution)/shard_map/pallas_call | solution.py:47
  40.7 2.4 %collective-permute-done.14 = bf16[1024,128]{1,0:T(8,128)(2,1)S(1)} collective-permute-done((bf16[1024,128]{1,0:T(8,128)(2,1)S(1)}, bf16[1024,128]{1,0:T(8,128)(2,1)S(1)}, u32[]{:S(2)}, u32[]{:S(2)}) %collective-permute-start.14) | collective-permute-done | bytes 262176 | tf_op jit(solution)/shard_map/ppermute | solution.py:566
  43.2 1.6 %collective-permute-start.20 = (bf16[1024,128]{1,0:T(8,128)(2,1)S(1)}, bf16[1024,128]{1,0:T(8,128)(2,1)S(1)}, u32[]{:S(2)}, u32[]{:S(2)}) collective-permute-start(bf16[1024,128]{1,0:T(8,128)(2,1)S(1)} %add_convert_fusion.1), channel_id=1, source_target_pairs={{0,2},{1,3},{2,0},{3,1},{4,6},{5,7},{6,4},{7,5},{8,10},{9,11},{10,... | collective-permute-start | bytes 786440 | tf_op jit(solution)/shard_map/ppermute | solution.py:413
  45.5 0.7 convolution_bitcast_fusion.3
  46.5 4.3 %collective-permute-done.20 = bf16[1024,128]{1,0:T(8,128)(2,1)S(1)} collective-permute-done((bf16[1024,128]{1,0:T(8,128)(2,1)S(1)}, bf16[1024,128]{1,0:T(8,128)(2,1)S(1)}, u32[]{:S(2)}, u32[]{:S(2)}) %collective-permute-start.20) | collective-permute-done | bytes 262176 | tf_op jit(solution)/shard_map/ppermute | solution.py:413
  52.8 2.5 %collective-permute-done.15 = bf16[2,64,1920]{2,1,0:T(8,128)(2,1)S(1)} collective-permute-done((bf16[2,64,1920]{2,1,0:T(8,128)(2,1)S(1)}, bf16[2,64,1920]{2,1,0:T(8,128)(2,1)S(1)}, u32[]{:S(2)}, u32[]{:S(2)}) %collective-permute-start.15) | collective-permute-done | bytes 491552 | tf_op jit(solution)/shard_map/ppermute | solution.py:442
  55.5 10.7 %collective-permute-done.21 = bf16[2,64,1920]{2,1,0:T(8,128)(2,1)S(1)} collective-permute-done((bf16[2,64,1920]{2,1,0:T(8,128)(2,1)S(1)}, bf16[2,64,1920]{2,1,0:T(8,128)(2,1)S(1)}, u32[]{:S(2)}, u32[]{:S(2)}) %collective-permute-start.21) | collective-permute-done | bytes 491552 | tf_op jit(solution)/shard_map/ppermute | solution.py:442
  66.4 3.0 %collective-permute-start.17 = (bf16[2,32,1920]{2,1,0:T(8,128)(2,1)S(1)}, bf16[2,32,1920]{2,1,0:T(8,128)(2,1)S(1)}, u32[]{:S(2)}, u32[]{:S(2)}) collective-permute-start(bf16[2,32,1920]{2,1,0:T(8,128)(2,1)S(1)} %get-tuple-element.59), channel_id=1, source_target_pairs={{0,16},{4,20},{8,24},{12,28},{16,0},{20,4},{24,8},{28,12},{1,17},{... | collective-permute-start | bytes 737288 | tf_op jit(solution)/shard_map/ppermute | solution.py:413
  69.5 2.0 %collective-permute-start.19 = (bf16[1024,128]{1,0:T(8,128)(2,1)S(1)}, bf16[1024,128]{1,0:T(8,128)(2,1)S(1)}, u32[]{:S(2)}, u32[]{:S(2)}) collective-permute-start(bf16[1024,128]{1,0:T(8,128)(2,1)S(1)} %collective-permute-done.3.refs_14_.refs_4_), channel_id=1, source_target_pairs={{0,2},{1,3},{2,0},{3,1},{4,6},{5,7},{6,4},{7,5},{8,10},{9,11},{10,... | collective-permute-start | bytes 786440 | tf_op jit(solution)/shard_map/ppermute | solution.py:413
  71.5 3.8 %collective-permute-done.22 = bf16[2,32,1920]{2,1,0:T(8,128)(2,1)S(1)} collective-permute-done((bf16[2,32,1920]{2,1,0:T(8,128)(2,1)S(1)}, bf16[2,32,1920]{2,1,0:T(8,128)(2,1)S(1)}, u32[]{:S(2)}, u32[]{:S(2)}) %collective-permute-start.22) | collective-permute-done | bytes 245792 | tf_op jit(solution)/shard_map/ppermute | solution.py:442
  75.3 0.7 fusion.8
  76.6 7.4 %collective-permute-done.17.refs_1_ = bf16[2,32,1920]{2,1,0:T(8,128)(2,1)S(1)} collective-permute-done((bf16[2,32,1920]{2,1,0:T(8,128)(2,1)S(1)}, bf16[2,32,1920]{2,1,0:T(8,128)(2,1)S(1)}, u32[]{:S(2)}, u32[]{:S(2)}) %collective-permute-start.17) | collective-permute-done | bytes 245792 | tf_op jit(solution)/shard_map/ppermute | solution.py:413
  84.0 2.6 %collective-permute-done.23.refs_4_ = bf16[2,32,1920]{2,1,0:T(8,128)(2,1)S(1)} collective-permute-done((bf16[2,32,1920]{2,1,0:T(8,128)(2,1)}, bf16[2,32,1920]{2,1,0:T(8,128)(2,1)S(1)}, u32[]{:S(2)}, u32[]{:S(2)}) %collective-permute-start.23) | collective-permute-done | bytes 245792 | tf_op jit(solution)/shard_map/ppermute | solution.py:413
  86.6 0.9 shard_map.111
  87.5 2.0 %collective-permute-start.24 = (bf16[2,32,1920]{2,1,0:T(8,128)(2,1)S(1)}, bf16[2,32,1920]{2,1,0:T(8,128)(2,1)S(1)}, u32[]{:S(2)}, u32[]{:S(2)}) collective-permute-start(bf16[2,32,1920]{2,1,0:T(8,128)(2,1)S(1)} %get-tuple-element.70), channel_id=1, source_target_pairs={{0,8},{1,5},{2,10},{3,7},{4,12},{5,1},{6,14},{7,3},{8,0},{9,13},{1... | collective-permute-start | bytes 737288 | tf_op jit(solution)/shard_map/ppermute | solution.py:442
  89.6 4.5 %collective-permute-done.26 = bf16[2,32,1920]{2,1,0:T(8,128)(2,1)S(1)} collective-permute-done((bf16[2,32,1920]{2,1,0:T(8,128)(2,1)}, bf16[2,32,1920]{2,1,0:T(8,128)(2,1)S(1)}, u32[]{:S(2)}, u32[]{:S(2)}) %collective-permute-start.26) | collective-permute-done | bytes 245792 | tf_op jit(solution)/shard_map/ppermute | solution.py:442
  94.0 1.0 broadcast_select_fusion.3
  95.1 1.3 collective-permute-start.27
  96.4 2.9 %collective-permute-done.24 = bf16[2,32,1920]{2,1,0:T(8,128)(2,1)S(1)} collective-permute-done((bf16[2,32,1920]{2,1,0:T(8,128)(2,1)S(1)}, bf16[2,32,1920]{2,1,0:T(8,128)(2,1)S(1)}, u32[]{:S(2)}, u32[]{:S(2)}) %collective-permute-start.24) | collective-permute-done | bytes 245792 | tf_op jit(solution)/shard_map/ppermute | solution.py:442
  99.4 1.3 collective-permute-start.25
  100.7 3.3 %collective-permute-done.27.coming_ref = bf16[2,64,1920]{2,1,0:T(8,128)(2,1)S(1)} collective-permute-done((bf16[2,64,1920]{2,1,0:T(8,128)(2,1)S(1)}, bf16[2,64,1920]{2,1,0:T(8,128)(2,1)S(1)}, u32[]{:S(2)}, u32[]{:S(2)}) %collective-permute-start.27) | collective-permute-done | bytes 491552 | tf_op jit(solution)/shard_map/ppermute | solution.py:442
  104.0 4.5 %shard_map.112.refs_2_ = bf16[1024,128]{1,0:T(8,128)(2,1)S(1)} custom-call(s32[1]{0:T(128)} %bitcast.3.first_ref, bf16[2,64,1920]{2,1,0:T(8,128)(2,1)S(1)} %pad_maximum_fusion.2.part_ref, bf16[2,64,1920]{2,1,0:T(8,128)(2,1)S(1)} %collective-permute-done.27.coming_ref, bf16[1024,1920]{1,0:T(8,128)(2,1)} %refs_0_.4, ...), custom_call_target="tpu_custom_call" | custom-call | flops 1006632960 | bytes 7864320 | tf_op jit(solution)/shard_map/pallas_call | solution.py:289
  109.2 4.5 %shard_map.113 = f32[1024,128]{1,0:T(8,128)S(1)} custom-call(s32[1]{0:T(128)} %bitcast.3.first_ref, bf16[2,64,1920]{2,1,0:T(8,128)(2,1)S(1)} %pad_maximum_fusion.1.part_ref, bf16[2,64,1920]{2,1,0:T(8,128)(2,1)S(1)} %collective-permute-done.25.coming_ref, bf16[1024,1920]{1,0:T(8,128)(2,1)} %refs_0_.4, ...), custom_call_target="tpu_custom_call" | custom-call | tf_op jit(solution)/shard_map/pallas_call | solution.py:289
  113.7 1.2 collective-permute-done.28
  114.9 3.7 %collective-permute-start.32 = (bf16[1024,128]{1,0:T(8,128)(2,1)S(1)}, bf16[1024,128]{1,0:T(8,128)(2,1)S(1)}, u32[]{:S(2)}, u32[]{:S(2)}) collective-permute-start(bf16[1024,128]{1,0:T(8,128)(2,1)S(1)} %add_convert_fusion.refs_8_), channel_id=1, source_target_pairs={{4,0},{8,4},{12,8},{16,12},{20,16},{24,20},{28,24},{0,28},{5,1},{9... | collective-permute-start | bytes 786440 | tf_op jit(solution)/shard_map/ppermute | solution.py:419
  118.9 3.7 %collective-permute-done.32.refs_10_ = bf16[1024,128]{1,0:T(8,128)(2,1)S(1)} collective-permute-done((bf16[1024,128]{1,0:T(8,128)(2,1)S(1)}, bf16[1024,128]{1,0:T(8,128)(2,1)S(1)}, u32[]{:S(2)}, u32[]{:S(2)}) %collective-permute-start.32) | collective-permute-done | bytes 262176 | tf_op jit(solution)/shard_map/ppermute | solution.py:419
  122.6 4.1 %collective-permute-done.31.refs_9_ = bf16[1024,128]{1,0:T(8,128)(2,1)S(1)} collective-permute-done((bf16[1024,128]{1,0:T(8,128)(2,1)S(1)}, bf16[1024,128]{1,0:T(8,128)(2,1)S(1)}, u32[]{:S(2)}, u32[]{:S(2)}) %collective-permute-start.31) | collective-permute-done | bytes 262176 | tf_op jit(solution)/shard_map/ppermute | solution.py:413
  126.7 1.3 collective-permute-done.29.refs_6_
  128.0 1.8 %collective-permute-start.30 = (bf16[1024,128]{1,0:T(8,128)(2,1)S(1)}, bf16[1024,128]{1,0:T(8,128)(2,1)S(1)}, u32[]{:S(2)}, u32[]{:S(2)}) collective-permute-start(bf16[1024,128]{1,0:T(8,128)(2,1)S(1)} %collective-permute-done.29.refs_6_), channel_id=1, source_target_pairs={{0,2},{1,3},{2,0},{3,1},{4,6},{5,7},{6,4},{7,5},{8,10},{9,11},{10,... | collective-permute-start | bytes 786440 | tf_op jit(solution)/shard_map/ppermute | solution.py:413
  129.8 3.7 %collective-permute-done.33.refs_11_ = bf16[1024,128]{1,0:T(8,128)(2,1)S(1)} collective-permute-done((bf16[1024,128]{1,0:T(8,128)(2,1)S(1)}, bf16[1024,128]{1,0:T(8,128)(2,1)S(1)}, u32[]{:S(2)}, u32[]{:S(2)}) %collective-permute-start.33) | collective-permute-done | bytes 262176 | tf_op jit(solution)/shard_map/ppermute | solution.py:413
  133.5 2.8 %collective-permute-done.30.refs_7_ = bf16[1024,128]{1,0:T(8,128)(2,1)S(1)} collective-permute-done((bf16[1024,128]{1,0:T(8,128)(2,1)S(1)}, bf16[1024,128]{1,0:T(8,128)(2,1)S(1)}, u32[]{:S(2)}, u32[]{:S(2)}) %collective-permute-start.30) | collective-permute-done | bytes 262176 | tf_op jit(solution)/shard_map/ppermute | solution.py:413
  136.3 2.3 %shard_map.114 = (bf16[24,128,128]{2,1,0:T(8,128)(2,1)S(1)}, bf16[3072,256]{1,0:T(8,128)(2,1)S(1)}, bf16[3072,256]{1,0:T(8,128)(2,1)S(1)}) custom-call(s32[24,2]{1,0:T(8,128)S(1)} %copy-done.7, bf16[1024,128]{1,0:T(8,128)(2,1)S(1)} %collective-permute-done.2.refs_12_.refs_0_, bf16[1024,128]{1,0:T(8,128)(2,1)S(1)} %collective-permute-done.18.refs_1_, ...), custom_call_target="tpu_custom_call" | custom-call | flops 201326592 | bytes 3932160 | tf_op jit(solution)/shard_map/pallas_call | solution.py:335
  139.4 1.6 %shard_map.115.first_ref = f32[24,128,128]{2,1,0:T(8,128)S(1)} custom-call(s32[24,2]{1,0:T(8,128)S(1)} %copy-done.4, bf16[3072,256]{1,0:T(8,128)(2,1)S(1)} %get-tuple-element.76.occ_ref, bf16[3072,256]{1,0:T(8,128)(2,1)S(1)} %get-tuple-element.77.resp_ref), custom_call_target="tpu_custom_call" | custom-call | flops 201326592 | bytes 1572864 | tf_op jit(solution)/shard_map/pallas_call | solution.py:357
  141.7 2.4 %shard_map.116 = (f32[24,256]{1,0:T(8,128)}, bf16[1024,512]{1,0:T(8,128)(2,1)}) custom-call(s32[1]{0:T(128)} %bitcast.core_ref, bf16[24,256,128]{2,1,0:T(8,128)(2,1)S(1)} %copy-done.2, f32[24,128,128]{2,1,0:T(8,128)S(1)} %shard_map.115.first_ref, bf16[24,128,128]{2,1,0:T(8,128)(2,1)S(1)} %collective-permute-done.34.second_ref, f32[24,256]{1,0:T(8,128)S(1)} %copy-done.5, ...), custom_call_target="tpu_custom_call" | custom-call | flops 402653184 | bytes 3932160 | tf_op jit(solution)/shard_map/pallas_call | solution.py:394
  (92 shorter events, 12.1 us)
Async XLA Ops:
  0.6 23.4 %copy-start.10 = (s32[24]{0:T(128)S(1)}, s32[24]{0:T(128)}, u32[]{:S(2)}) copy-start(s32[24]{0:T(128)} %counts_hbm.3) | copy-start | bytes 292
  0.6 13.8 %copy-start.11 = (s32[24,2]{0,1:T(2,128)S(1)}, s32[24,2]{0,1:T(2,128)}, u32[]{:S(2)}) copy-start(s32[24,2]{0,1:T(2,128)} %param.10) | copy-start | bytes 580
  0.7 23.3 %copy-start.8 = (f32[24,256]{1,0:T(8,128)S(1)}, f32[24,256]{1,0:T(8,128)}, u32[]{:S(2)}) copy-start(f32[24,256]{1,0:T(8,128)} %param.13) | copy-start | bytes 73732
  0.7 24.0 %copy-start.9 = (f32[1920]{0:T(1024)S(1)}, f32[1920]{0:T(1024)}, u32[]{:S(2)}) copy-start(f32[1920]{0:T(1024)} %param.17) | copy-start | bytes 23044
  0.7 37.2 %collective-permute-start.12 = (bf16[1024,1920]{1,0:T(8,128)(2,1)}, bf16[1024,1920]{1,0:T(8,128)(2,1)}, u32[]{:S(2)}, u32[]{:S(2)}) collective-permute-start(bf16[1024,1920]{1,0:T(8,128)(2,1)} %refs_0_.4), channel_id=1, source_target_pairs={{0,1},{1,0},{2,3},{3,2},{4,5},{5,4},{6,7},{7,6},{8,9},{9,8},{10,11... | collective-permute-start | bytes 11796488 | tf_op jit(solution)/shard_map/ppermute | solution.py:413
  2.3 31.4 %copy-start.12 = (f32[512]{0:T(512)S(1)}, f32[512]{0:T(512)}, u32[]{:S(2)}) copy-start(f32[512]{0:T(512)} %param.16) | copy-start | bytes 6148
  2.3 17.3 %collective-permute-start.3 = (bf16[1024,128]{1,0:T(8,128)(2,1)S(1)}, bf16[1024,128]{1,0:T(8,128)(2,1)S(1)}, u32[]{:S(2)}, u32[]{:S(2)}) collective-permute-start(bf16[1024,128]{1,0:T(8,128)(2,1)S(1)} %get-tuple-element.87.refs_13_.refs_2_), channel_id=1, source_target_pairs={{4,0},{8,4},{12,8},{16,12},{20,16},{24,20},{28,24},{0,28},{5,1},{9... | collective-permute-start | bytes 786440 | tf_op jit(solution)/shard_map/ppermute | solution.py:419
  7.9 11.7 %collective-permute-start.2 = (bf16[1024,128]{1,0:T(8,128)(2,1)S(1)}, bf16[1024,128]{1,0:T(8,128)(2,1)S(1)}, u32[]{:S(2)}, u32[]{:S(2)}) collective-permute-start(bf16[1024,128]{1,0:T(8,128)(2,1)S(1)} %get-tuple-element.87.refs_13_.refs_2_), channel_id=1, source_target_pairs={{0,4},{4,8},{8,12},{12,16},{16,20},{20,24},{24,28},{28,0},{1,5},{5... | collective-permute-start | bytes 786440 | tf_op jit(solution)/shard_map/ppermute | solution.py:418
  10.1 8.0 %collective-permute-start.1 = (bf16[800,128]{1,0:T(8,128)(2,1)S(1)}, bf16[800,128]{1,0:T(8,128)(2,1)S(1)}, u32[]{:S(2)}, u32[]{:S(2)}) collective-permute-start(bf16[800,128]{1,0:T(8,128)(2,1)S(1)} %get-tuple-element.42), channel_id=1, source_target_pairs={{0,2},{1,3},{2,0},{3,1},{4,6},{5,7},{6,4},{7,5},{8,10},{9,11},{10,... | collective-permute-start | bytes 614408 | tf_op jit(solution)/shard_map/ppermute | solution.py:413
  13.9 8.1 %collective-permute-start.9 = (bf16[800,128]{1,0:T(8,128)(2,1)S(1)}, bf16[800,128]{1,0:T(8,128)(2,1)S(1)}, u32[]{:S(2)}, u32[]{:S(2)}) collective-permute-start(bf16[800,128]{1,0:T(8,128)(2,1)S(1)} %get-tuple-element.48), channel_id=1, source_target_pairs={{0,2},{1,3},{2,0},{3,1},{4,6},{5,7},{6,4},{7,5},{8,10},{9,11},{10,... | collective-permute-start | bytes 614408 | tf_op jit(solution)/shard_map/ppermute | solution.py:413
  14.6 21.3 %copy-start.3 = (s32[24,2]{1,0:T(8,128)}, s32[24,2]{1,0:T(8,128)S(1)}, u32[]{:S(2)}) copy-start(s32[24,2]{1,0:T(8,128)S(1)} %copy.16.refs_0_.block_ref) | copy-start | bytes 580
  18.1 3.9 %collective-permute-start.4 = (s32[24,2]{1,0:T(8,128)S(1)}, s32[24,2]{1,0:T(8,128)S(1)}, u32[]{:S(2)}, u32[]{:S(2)}) collective-permute-start(s32[24,2]{1,0:T(8,128)S(1)} %copy.16.refs_0_.block_ref), channel_id=1, source_target_pairs={{0,2},{1,3},{2,0},{3,1},{4,6},{5,7},{6,4},{7,5},{8,10},{9,11},{10,... | collective-permute-start | bytes 584 | tf_op jit(solution)/shard_map/ppermute | solution.py:413
  19.6 3.8 %collective-permute-start = (s32[24,2]{1,0:T(8,128)S(1)}, s32[24,2]{1,0:T(8,128)S(1)}, u32[]{:S(2)}, u32[]{:S(2)}) collective-permute-start(s32[24,2]{1,0:T(8,128)S(1)} %copy.16.refs_0_.block_ref), channel_id=1, source_target_pairs={{0,1},{1,0},{2,3},{3,2},{4,5},{5,4},{6,7},{7,6},{8,9},{9,8},{10,11... | collective-permute-start | bytes 584 | tf_op jit(solution)/shard_map/ppermute | solution.py:413
  19.6 5.0 %collective-permute-start.8 = (bf16[12,128,128]{2,1,0:T(8,128)(2,1)S(1)}, bf16[12,128,128]{2,1,0:T(8,128)(2,1)S(1)}, u32[]{:S(2)}, u32[]{:S(2)}) collective-permute-start(bf16[12,128,128]{2,1,0:T(8,128)(2,1)S(1)} %get-tuple-element.47.refs_8_), channel_id=1, source_target_pairs={{0,1},{1,0},{2,3},{3,2},{4,5},{5,4},{6,7},{7,6},{8,9},{9,8},{10,11... | collective-permute-start | bytes 1179656 | tf_op jit(solution)/shard_map/ppermute | solution.py:413
  22.0 2.9 %collective-permute-start.6 = (bf16[12,128,128]{2,1,0:T(8,128)(2,1)S(1)}, bf16[12,128,128]{2,1,0:T(8,128)(2,1)S(1)}, u32[]{:S(2)}, u32[]{:S(2)}) collective-permute-start(bf16[12,128,128]{2,1,0:T(8,128)(2,1)S(1)} %get-tuple-element.45.refs_4_), channel_id=1, source_target_pairs={{0,1},{1,0},{2,3},{3,2},{4,5},{5,4},{6,7},{7,6},{8,9},{9,8},{10,11... | collective-permute-start | bytes 1179656 | tf_op jit(solution)/shard_map/ppermute | solution.py:413
  22.0 1.7 %collective-permute-start.5 = (s32[24,2]{1,0:T(8,128)S(1)}, s32[24,2]{1,0:T(8,128)S(1)}, u32[]{:S(2)}, u32[]{:S(2)}) collective-permute-start(s32[24,2]{1,0:T(8,128)S(1)} %collective-permute-done.4.refs_2_), channel_id=1, source_target_pairs={{0,1},{1,0},{2,3},{3,2},{4,5},{5,4},{6,7},{7,6},{8,9},{9,8},{10,11... | collective-permute-start | bytes 584 | tf_op jit(solution)/shard_map/ppermute | solution.py:413
  23.4 12.4 %copy-start.6 = (s32[24,2]{1,0:T(8,128)}, s32[24,2]{1,0:T(8,128)S(1)}, u32[]{:S(2)}) copy-start(s32[24,2]{1,0:T(8,128)S(1)} %collective-permute-done.refs_1_.block_ref) | copy-start | bytes 580
  23.4 1.8 %collective-permute-start.10 = (bf16[12,128,128]{2,1,0:T(8,128)(2,1)S(1)}, bf16[12,128,128]{2,1,0:T(8,128)(2,1)S(1)}, u32[]{:S(2)}, u32[]{:S(2)}) collective-permute-start(bf16[12,128,128]{2,1,0:T(8,128)(2,1)S(1)} %shard_map.107.refs_10_), channel_id=1, source_target_pairs={{0,1},{1,0},{2,3},{3,2},{4,5},{5,4},{6,7},{7,6},{8,9},{9,8},{10,11... | collective-permute-start | bytes 1179656 | tf_op jit(solution)/shard_map/ppermute | solution.py:413
  23.8 2.0 %collective-permute-start.7 = (bf16[12,128,128]{2,1,0:T(8,128)(2,1)S(1)}, bf16[12,128,128]{2,1,0:T(8,128)(2,1)S(1)}, u32[]{:S(2)}, u32[]{:S(2)}) collective-permute-start(bf16[12,128,128]{2,1,0:T(8,128)(2,1)S(1)} %shard_map.105.refs_6_), channel_id=1, source_target_pairs={{0,1},{1,0},{2,3},{3,2},{4,5},{5,4},{6,7},{7,6},{8,9},{9,8},{10,11... | collective-permute-start | bytes 1179656 | tf_op jit(solution)/shard_map/ppermute | solution.py:413
  24.7 13.2 %collective-permute-start.11 = (f32[1920]{0:T(1024)S(1)}, f32[1920]{0:T(1024)S(1)}, u32[]{:S(2)}, u32[]{:S(2)}) collective-permute-start(f32[1920]{0:T(1024)S(1)} %copy-done.9), channel_id=1, source_target_pairs={{0,1},{1,0},{2,3},{3,2},{4,5},{5,4},{6,7},{7,6},{8,9},{9,8},{10,11... | collective-permute-start | bytes 23048 | tf_op jit(solution)/shard_map/ppermute | solution.py:413
  28.9 11.8 %collective-permute-start.13 = (bf16[1024,128]{1,0:T(8,128)(2,1)S(1)}, bf16[1024,128]{1,0:T(8,128)(2,1)S(1)}, u32[]{:S(2)}, u32[]{:S(2)}) collective-permute-start(bf16[1024,128]{1,0:T(8,128)(2,1)S(1)} %get-tuple-element.53), channel_id=1, source_target_pairs={{0,4},{4,8},{8,12},{12,16},{16,20},{20,24},{24,28},{28,0},{1,5},{5... | collective-permute-start | bytes 786440 | tf_op jit(solution)/shard_map/ppermute | solution.py:565
  28.9 14.2 %collective-permute-start.14 = (bf16[1024,128]{1,0:T(8,128)(2,1)S(1)}, bf16[1024,128]{1,0:T(8,128)(2,1)S(1)}, u32[]{:S(2)}, u32[]{:S(2)}) collective-permute-start(bf16[1024,128]{1,0:T(8,128)(2,1)S(1)} %get-tuple-element.54), channel_id=1, source_target_pairs={{4,0},{8,4},{12,8},{16,12},{20,16},{24,20},{28,24},{0,28},{5,1},{9... | collective-permute-start | bytes 786440 | tf_op jit(solution)/shard_map/ppermute | solution.py:566
  40.0 5.5 %copy-start.1 = (bf16[1024,1920]{1,0:T(8,128)(2,1)S(1)}, bf16[1024,1920]{1,0:T(8,128)(2,1)}, u32[]{:S(2)}) copy-start(bf16[1024,1920]{1,0:T(8,128)(2,1)} %copy-done) | copy-start | bytes 11796484
  43.2 7.6 %collective-permute-start.20 = (bf16[1024,128]{1,0:T(8,128)(2,1)S(1)}, bf16[1024,128]{1,0:T(8,128)(2,1)S(1)}, u32[]{:S(2)}, u32[]{:S(2)}) collective-permute-start(bf16[1024,128]{1,0:T(8,128)(2,1)S(1)} %add_convert_fusion.1), channel_id=1, source_target_pairs={{0,2},{1,3},{2,0},{3,1},{4,6},{5,7},{6,4},{7,5},{8,10},{9,11},{10,... | collective-permute-start | bytes 786440 | tf_op jit(solution)/shard_map/ppermute | solution.py:413
  46.4 8.9 %collective-permute-start.15 = (bf16[2,64,1920]{2,1,0:T(8,128)(2,1)S(1)}, bf16[2,64,1920]{2,1,0:T(8,128)(2,1)S(1)}, u32[]{:S(2)}, u32[]{:S(2)}) collective-permute-start(bf16[2,64,1920]{2,1,0:T(8,128)(2,1)S(1)} %fusion.5), channel_id=1, source_target_pairs={{0,4},{1,9},{2,6},{3,11},{4,0},{5,13},{6,2},{7,15},{8,12},{9,1},{1... | collective-permute-start | bytes 1474568 | tf_op jit(solution)/shard_map/ppermute | solution.py:442
  52.4 13.8 %collective-permute-start.21 = (bf16[2,64,1920]{2,1,0:T(8,128)(2,1)S(1)}, bf16[2,64,1920]{2,1,0:T(8,128)(2,1)S(1)}, u32[]{:S(2)}, u32[]{:S(2)}) collective-permute-start(bf16[2,64,1920]{2,1,0:T(8,128)(2,1)S(1)} %fusion.1), channel_id=1, source_target_pairs={{0,4},{1,9},{2,6},{3,11},{4,0},{5,13},{6,2},{7,15},{8,12},{9,1},{1... | collective-permute-start | bytes 1474568 | tf_op jit(solution)/shard_map/ppermute | solution.py:442
  55.4 11.0 %collective-permute-start.16 = (bf16[2,32,1920]{2,1,0:T(8,128)(2,1)S(1)}, bf16[2,32,1920]{2,1,0:T(8,128)(2,1)S(1)}, u32[]{:S(2)}, u32[]{:S(2)}) collective-permute-start(bf16[2,32,1920]{2,1,0:T(8,128)(2,1)S(1)} %dynamic-slice_convert_fusion.1), channel_id=1, source_target_pairs={{0,8},{1,5},{2,10},{3,7},{4,12},{5,1},{6,14},{7,3},{8,0},{9,13},{1... | collective-permute-start | bytes 737288 | tf_op jit(solution)/shard_map/ppermute | solution.py:442
  66.3 9.0 %collective-permute-start.22 = (bf16[2,32,1920]{2,1,0:T(8,128)(2,1)S(1)}, bf16[2,32,1920]{2,1,0:T(8,128)(2,1)S(1)}, u32[]{:S(2)}, u32[]{:S(2)}) collective-permute-start(bf16[2,32,1920]{2,1,0:T(8,128)(2,1)S(1)} %dynamic-slice_convert_fusion), channel_id=1, source_target_pairs={{0,8},{1,5},{2,10},{3,7},{4,12},{5,1},{6,14},{7,3},{8,0},{9,13},{1... | collective-permute-start | bytes 737288 | tf_op jit(solution)/shard_map/ppermute | solution.py:442
  66.4 17.5 %collective-permute-start.17 = (bf16[2,32,1920]{2,1,0:T(8,128)(2,1)S(1)}, bf16[2,32,1920]{2,1,0:T(8,128)(2,1)S(1)}, u32[]{:S(2)}, u32[]{:S(2)}) collective-permute-start(bf16[2,32,1920]{2,1,0:T(8,128)(2,1)S(1)} %get-tuple-element.59), channel_id=1, source_target_pairs={{0,16},{4,20},{8,24},{12,28},{16,0},{20,4},{24,8},{28,12},{1,17},{... | collective-permute-start | bytes 737288 | tf_op jit(solution)/shard_map/ppermute | solution.py:413
  69.5 14.5 %collective-permute-start.18 = (bf16[1024,128]{1,0:T(8,128)(2,1)S(1)}, bf16[1024,128]{1,0:T(8,128)(2,1)S(1)}, u32[]{:S(2)}, u32[]{:S(2)}) collective-permute-start(bf16[1024,128]{1,0:T(8,128)(2,1)S(1)} %collective-permute-done.2.refs_12_.refs_0_), channel_id=1, source_target_pairs={{0,2},{1,3},{2,0},{3,1},{4,6},{5,7},{6,4},{7,5},{8,10},{9,11},{10,... | collective-permute-start | bytes 786440 | tf_op jit(solution)/shard_map/ppermute | solution.py:413
  69.5 14.5 %collective-permute-start.19 = (bf16[1024,128]{1,0:T(8,128)(2,1)S(1)}, bf16[1024,128]{1,0:T(8,128)(2,1)S(1)}, u32[]{:S(2)}, u32[]{:S(2)}) collective-permute-start(bf16[1024,128]{1,0:T(8,128)(2,1)S(1)} %collective-permute-done.3.refs_14_.refs_4_), channel_id=1, source_target_pairs={{0,2},{1,3},{2,0},{3,1},{4,6},{5,7},{6,4},{7,5},{8,10},{9,11},{10,... | collective-permute-start | bytes 786440 | tf_op jit(solution)/shard_map/ppermute | solution.py:413
  76.0 10.6 %collective-permute-start.23 = (bf16[2,32,1920]{2,1,0:T(8,128)(2,1)}, bf16[2,32,1920]{2,1,0:T(8,128)(2,1)S(1)}, u32[]{:S(2)}, u32[]{:S(2)}) collective-permute-start(bf16[2,32,1920]{2,1,0:T(8,128)(2,1)} %get-tuple-element.68), channel_id=1, source_target_pairs={{0,16},{4,20},{8,24},{12,28},{16,0},{20,4},{24,8},{28,12},{1,17},{... | collective-permute-start | bytes 737288 | tf_op jit(solution)/shard_map/ppermute | solution.py:413
  87.5 6.5 %collective-permute-start.26 = (bf16[2,32,1920]{2,1,0:T(8,128)(2,1)}, bf16[2,32,1920]{2,1,0:T(8,128)(2,1)S(1)}, u32[]{:S(2)}, u32[]{:S(2)}) collective-permute-start(bf16[2,32,1920]{2,1,0:T(8,128)(2,1)} %get-tuple-element.71), channel_id=1, source_target_pairs={{0,8},{1,5},{2,10},{3,7},{4,12},{5,1},{6,14},{7,3},{8,0},{9,13},{1... | collective-permute-start | bytes 737288 | tf_op jit(solution)/shard_map/ppermute | solution.py:442
  87.5 11.8 %collective-permute-start.24 = (bf16[2,32,1920]{2,1,0:T(8,128)(2,1)S(1)}, bf16[2,32,1920]{2,1,0:T(8,128)(2,1)S(1)}, u32[]{:S(2)}, u32[]{:S(2)}) collective-permute-start(bf16[2,32,1920]{2,1,0:T(8,128)(2,1)S(1)} %get-tuple-element.70), channel_id=1, source_target_pairs={{0,8},{1,5},{2,10},{3,7},{4,12},{5,1},{6,14},{7,3},{8,0},{9,13},{1... | collective-permute-start | bytes 737288 | tf_op jit(solution)/shard_map/ppermute | solution.py:442
  95.1 8.9 %collective-permute-start.27 = (bf16[2,64,1920]{2,1,0:T(8,128)(2,1)S(1)}, bf16[2,64,1920]{2,1,0:T(8,128)(2,1)S(1)}, u32[]{:S(2)}, u32[]{:S(2)}) collective-permute-start(bf16[2,64,1920]{2,1,0:T(8,128)(2,1)S(1)} %pad_maximum_fusion.2.part_ref), channel_id=1, source_target_pairs={{0,4},{1,9},{2,6},{3,11},{4,0},{5,13},{6,2},{7,15},{8,12},{9,1},{1... | collective-permute-start | bytes 1474568 | tf_op jit(solution)/shard_map/ppermute | solution.py:442
  99.4 9.8 %collective-permute-start.25 = (bf16[2,64,1920]{2,1,0:T(8,128)(2,1)S(1)}, bf16[2,64,1920]{2,1,0:T(8,128)(2,1)S(1)}, u32[]{:S(2)}, u32[]{:S(2)}) collective-permute-start(bf16[2,64,1920]{2,1,0:T(8,128)(2,1)S(1)} %pad_maximum_fusion.1.part_ref), channel_id=1, source_target_pairs={{0,4},{1,9},{2,6},{3,11},{4,0},{5,13},{6,2},{7,15},{8,12},{9,1},{1... | collective-permute-start | bytes 1474568 | tf_op jit(solution)/shard_map/ppermute | solution.py:442
  108.4 27.9 %copy-start.7 = (s32[24,2]{1,0:T(8,128)S(1)}, s32[24,2]{1,0:T(8,128)}, u32[]{:S(2)}) copy-start(s32[24,2]{1,0:T(8,128)} %copy-done.6) | copy-start | bytes 580
  108.5 6.4 %collective-permute-start.28 = (bf16[1024,128]{1,0:T(8,128)(2,1)S(1)}, bf16[1024,128]{1,0:T(8,128)(2,1)S(1)}, u32[]{:S(2)}, u32[]{:S(2)}) collective-permute-start(bf16[1024,128]{1,0:T(8,128)(2,1)S(1)} %shard_map.112.refs_2_), channel_id=1, source_target_pairs={{0,2},{1,3},{2,0},{3,1},{4,6},{5,7},{6,4},{7,5},{8,10},{9,11},{10,... | collective-permute-start | bytes 786440 | tf_op jit(solution)/shard_map/ppermute | solution.py:413
  113.7 25.7 %copy-start.4 = (s32[24,2]{1,0:T(8,128)S(1)}, s32[24,2]{1,0:T(8,128)}, u32[]{:S(2)}) copy-start(s32[24,2]{1,0:T(8,128)} %copy-done.3) | copy-start | bytes 580
  114.9 7.6 %collective-permute-start.32 = (bf16[1024,128]{1,0:T(8,128)(2,1)S(1)}, bf16[1024,128]{1,0:T(8,128)(2,1)S(1)}, u32[]{:S(2)}, u32[]{:S(2)}) collective-permute-start(bf16[1024,128]{1,0:T(8,128)(2,1)S(1)} %add_convert_fusion.refs_8_), channel_id=1, source_target_pairs={{4,0},{8,4},{12,8},{16,12},{20,16},{24,20},{28,24},{0,28},{5,1},{9... | collective-permute-start | bytes 786440 | tf_op jit(solution)/shard_map/ppermute | solution.py:419
  118.7 8.0 %collective-permute-start.31 = (bf16[1024,128]{1,0:T(8,128)(2,1)S(1)}, bf16[1024,128]{1,0:T(8,128)(2,1)S(1)}, u32[]{:S(2)}, u32[]{:S(2)}) collective-permute-start(bf16[1024,128]{1,0:T(8,128)(2,1)S(1)} %add_convert_fusion.refs_8_), channel_id=1, source_target_pairs={{0,2},{1,3},{2,0},{3,1},{4,6},{5,7},{6,4},{7,5},{8,10},{9,11},{10,... | collective-permute-start | bytes 786440 | tf_op jit(solution)/shard_map/ppermute | solution.py:413
  118.9 9.1 %collective-permute-start.29 = (bf16[1024,128]{1,0:T(8,128)(2,1)S(1)}, bf16[1024,128]{1,0:T(8,128)(2,1)S(1)}, u32[]{:S(2)}, u32[]{:S(2)}) collective-permute-start(bf16[1024,128]{1,0:T(8,128)(2,1)S(1)} %add_convert_fusion.refs_8_), channel_id=1, source_target_pairs={{0,4},{4,8},{8,12},{12,16},{16,20},{20,24},{24,28},{28,0},{1,5},{5... | collective-permute-start | bytes 786440 | tf_op jit(solution)/shard_map/ppermute | solution.py:418
  126.7 6.8 %collective-permute-start.33 = (bf16[1024,128]{1,0:T(8,128)(2,1)S(1)}, bf16[1024,128]{1,0:T(8,128)(2,1)S(1)}, u32[]{:S(2)}, u32[]{:S(2)}) collective-permute-start(bf16[1024,128]{1,0:T(8,128)(2,1)S(1)} %collective-permute-done.32.refs_10_), channel_id=1, source_target_pairs={{0,2},{1,3},{2,0},{3,1},{4,6},{5,7},{6,4},{7,5},{8,10},{9,11},{10,... | collective-permute-start | bytes 786440 | tf_op jit(solution)/shard_map/ppermute | solution.py:413
  128.0 8.3 %collective-permute-start.30 = (bf16[1024,128]{1,0:T(8,128)(2,1)S(1)}, bf16[1024,128]{1,0:T(8,128)(2,1)S(1)}, u32[]{:S(2)}, u32[]{:S(2)}) collective-permute-start(bf16[1024,128]{1,0:T(8,128)(2,1)S(1)} %collective-permute-done.29.refs_6_), channel_id=1, source_target_pairs={{0,2},{1,3},{2,0},{3,1},{4,6},{5,7},{6,4},{7,5},{8,10},{9,11},{10,... | collective-permute-start | bytes 786440 | tf_op jit(solution)/shard_map/ppermute | solution.py:413
  138.6 3.1 %copy-start.2 = (bf16[24,256,128]{2,1,0:T(8,128)(2,1)S(1)}, bf16[24,256,128]{2,1,0:T(8,128)(2,1)}, u32[]{:S(2)}) copy-start(bf16[24,256,128]{2,1,0:T(8,128)(2,1)} %basis_ref.1) | copy-start | bytes 4718596
  138.6 3.1 %copy-start.5 = (f32[24,256]{1,0:T(8,128)S(1)}, f32[24,256]{1,0:T(8,128)}, u32[]{:S(2)}) copy-start(f32[24,256]{1,0:T(8,128)} %multiply_select_fusion.scale_ref) | copy-start | bytes 73732
  138.6 3.1 %collective-permute-start.34 = (bf16[24,128,128]{2,1,0:T(8,128)(2,1)S(1)}, bf16[24,128,128]{2,1,0:T(8,128)(2,1)S(1)}, u32[]{:S(2)}, u32[]{:S(2)}) collective-permute-start(bf16[24,128,128]{2,1,0:T(8,128)(2,1)S(1)} %get-tuple-element.78), channel_id=1, source_target_pairs={{0,1},{1,0},{2,3},{3,2},{4,5},{5,4},{6,7},{7,6},{8,9},{9,8},{10,11... | collective-permute-start | bytes 2359304 | tf_op jit(solution)/shard_map/ppermute | solution.py:413
  138.8 2.9 %collective-permute-start.35 = (bf16[1024,256]{1,0:T(8,128)(2,1)S(1)}, bf16[1024,256]{1,0:T(8,128)(2,1)S(1)}, u32[]{:S(2)}, u32[]{:S(2)}) collective-permute-start(bf16[1024,256]{1,0:T(8,128)(2,1)S(1)} %pad_maximum_fusion.half_ref), channel_id=1, source_target_pairs={{0,1},{1,0},{2,3},{3,2},{4,5},{5,4},{6,7},{7,6},{8,9},{9,8},{10,11... | collective-permute-start | bytes 1572872 | tf_op jit(solution)/shard_map/ppermute | solution.py:413
  (1 other events, 1.9 us)

commit v11 on v10

--- a/solution.py
+++ b/solution.py
@@ -208,7 +208,7 @@
                     total[at, :] += product[j * rows : (j + 1) * rows]
             return carry
 
-        lax.fori_loop(0, count, step, 0, unroll=6)
+        lax.fori_loop(0, count, step, 0, unroll=12)
 
     shares = {}
     smallest = min(ref.shape[0] for ref in ham_refs)
@@ -254,16 +254,17 @@
     )
 
 
-def expand_kernel(first_ref, part_ref, coming_ref, *refs):
+def expand_kernel(fetched, first_ref, part_ref, coming_ref, *refs):
     sources, (out_ref, held, semaphores) = refs[:2], refs[-3:]
-    blocks = semaphores.shape[0] // 2
+    blocks = semaphores.shape[0] // fetched
     rows = held.shape[1] // blocks
     copies = []
     for i in range(blocks):
         place = pl.ds(i * rows, rows)
-        for share, source in enumerate(sources):
-            copies.append((source.at[place], held.at[share, place]))
+        for share in range(fetched):
+            copies.append((sources[share].at[place], held.at[share, place]))
     waits = fetch(copies, semaphores)
+    places = [held.at[share] if share < fetched else sources[share] for share in range(2)]
     low = first_ref[0] == 0
     rotations = []
     for share in range(2):
@@ -273,35 +274,37 @@
     for i in range(blocks):
         at = slice(i * rows, (i + 1) * rows)
         total = None
-        for share in range(2):
-            waits[2 * i + share].wait()
+        for share in reversed(range(2)):
+            if share < fetched:
+                waits[fetched * i + share].wait()
             product = lax.dot_general(
-                held[share, at], rotations[share], NT, preferred_element_type=F32
+                places[share][at], rotations[share], NT, preferred_element_type=F32
             )
             total = product if total is None else total + product
         out_ref[at] = total.astype(out_ref.dtype)
 
 
-def expand(first, part, coming, virtuals, kind, ahead):
+def expand(first, part, coming, virtuals, kind, ahead, fetched):
     region, virt = virtuals[0].shape
     width = 2 * part.shape[1]
     blocks = 4 if region % 64 == 0 and region > 64 else 1
-    return pl.pallas_call(
-        expand_kernel,
+    near = virtuals[1] if fetched == 2 else place_in(virtuals[1], pltpu.VMEM)
+    return pl.pallas_call(
+        functools.partial(expand_kernel, fetched),
         out_shape=jax.ShapeDtypeStruct((region, width), kind),
-        in_specs=[SMEM, VMEM, VMEM, HBM, HBM] + [HBM] * len(ahead),
+        in_specs=[SMEM, VMEM, VMEM, HBM, HBM if fetched == 2 else VMEM] + [HBM] * len(ahead),
         out_specs=VMEM,
         scratch_shapes=[
-            pltpu.VMEM((2, region, virt), BF16),
-            pltpu.SemaphoreType.DMA((2 * blocks,)),
+            pltpu.VMEM((fetched, region, virt), BF16),
+            pltpu.SemaphoreType.DMA((fetched * blocks,)),
         ],
-        compiler_params=params(14),
+        compiler_params=params(6 + 4 * fetched),
         cost_estimate=pl.CostEstimate(
             flops=4 * region * width * virt if kind == BF16 else 0,
             bytes_accessed=4 * region * virt if kind == BF16 else 0,
             transcendentals=0,
         ),
-    )(first.reshape(1), part, coming, place_in(virtuals[0], pltpu.HBM), virtuals[1], *ahead)
+    )(first.reshape(1), part, coming, place_in(virtuals[0], pltpu.HBM), near, *ahead)
 
 
 def overlap_steps(block_ref, occ_ref, resp_ref, out_ref, rows):
@@ -313,7 +316,7 @@
         out_ref[b] = product.astype(out_ref.dtype)
         return carry
 
-    lax.fori_loop(0, out_ref.shape[0], step, 0, unroll=8)
+    lax.fori_loop(0, out_ref.shape[0], step, 0, unroll=24)
 
 
 def gather_kernel(rows, block_ref, *refs):
@@ -502,8 +505,8 @@
         self.part = join(own, swap(own, self.masks[1]), self.second)
         self.coming = swap(self.part, self.masks[0])
 
-    def result(self, virtuals, kind, *ahead):
-        return expand(self.first, self.part, self.coming, virtuals, kind, ahead)
+    def result(self, virtuals, kind, *ahead, fetched=2):
+        return expand(self.first, self.part, self.coming, virtuals, kind, ahead, fetched)
 
 
 def per_device(
@@ -588,7 +591,8 @@
         own_rotation, far_rotation = divide(own.place(), energies, [own, far])
         own.widen(own_rotation)
         far.widen(far_rotation)
-        coef_far = far.result(virtuals, BF16)
+        far.part, near = together(far.part, virtuals[1])
+        coef_far = far.result([virt_coef, load(near)], BF16, fetched=1)
         coef_own = own.result(virtuals, F32, coef_far)
     else:
         before_far, after_far = flip(occ_before, "tile", 2), flip(occ_after, "tile", 2)

time: 145 us -> 144 us (level)
  waiting for transfers between devices: 68.5 us -> 66.6 us
    pallas_call x2 -> x3, Pallas kernels: 4.25 us -> 6.37 us  [load(): pl.pallas_call(load_kernel, out_shape=pltpu.VMEM(array.shape, array.dtype...]
    ppermute x8, waiting for transfers between devices: 28 us -> 26.2 us  [swap(): return lax.ppermute(array, ('grid', 'tile'), pairs)]
  transfers between devices with their start and end apart: 36 -> 36, of which waited for: 24 -> 24; matrix products, arithmetic and copies ran while one was open for 5% -> 5% of each run, Pallas kernels for 17% -> 18%
where the time goes in v11:
time: 144 us; the launch traced here: 143 us
  waiting for transfers between devices  66.6 us (46%)
  starting transfers between devices  35.3 us (25%)
  Pallas kernels  30.7 us (21%)
  local copies, waits for them, and re-layouts  3.54 us (2%)
  other arithmetic  3.17 us (2%)
  matrix products  2.96 us (2%)
    ppermute x22, waiting for transfers between devices, flip(): lax.ppermute(array, axis, [(i, i ^ mask) for i in range(lax.axis_size(axi...  31.9 us
    ppermute x8, waiting for transfers between devices, swap(): return lax.ppermute(array, ('grid', 'tile'), pairs)  26.2 us
    ppermute x22, starting transfers between devices, flip(): lax.ppermute(array, axis, [(i, i ^ mask) for i in range(lax.axis_size(axi...  15.7 us
    ppermute x2, starting transfers between devices, neighbours(): lax.ppermute(array, 'grid', [((i + 1) % size, i) for i in range(size)])  9.41 us
    pallas_call x2, Pallas kernels, expand(): pl.pallas_call(functools.partial(expand_kernel, fetched), out_shape=jax.S...  8.62 us
    pallas_call x3, Pallas kernels, load(): pl.pallas_call(load_kernel, out_shape=pltpu.VMEM(array.shape, array.dtype...  6.37 us
    ppermute x8, starting transfers between devices, swap(): return lax.ppermute(array, ('grid', 'tile'), pairs)  5.33 us
    ppermute x1, starting transfers between devices, per_device(): lax.ppermute(to_before, 'grid', [((i + 1) % size, i) for i in range(size)])  4.71 us
  transfers between devices with their start and end apart: 36, of which 24 were waited for; matrix products, arithmetic and copies ran while one was open for 5% of the time, Pallas kernels for 18%

profile of v11, /device:TPU:0, one launch (start us, length us, event | category | flops | bytes accessed | tf_op | source)
XLA Modules:
  0.0 143.4 jit_solution(5897349460169945767)
XLA Ops:
  1.2 1.1 constant_dynamic-slice_fusion
  2.3 5.7 %collective-permute-start.3 = (bf16[1024,128]{1,0:T(8,128)(2,1)S(1)}, bf16[1024,128]{1,0:T(8,128)(2,1)S(1)}, u32[]{:S(2)}, u32[]{:S(2)}) collective-permute-start(bf16[1024,128]{1,0:T(8,128)(2,1)S(1)} %get-tuple-element.91.refs_13_.refs_2_), channel_id=1, source_target_pairs={{4,0},{8,4},{12,8},{16,12},{20,16},{24,20},{28,24},{0,28},{5,1},{9... | collective-permute-start | bytes 786440 | tf_op jit(solution)/shard_map/ppermute | solution.py:422
  7.9 2.2 %shard_map.104 = (bf16[12,128,128]{2,1,0:T(8,128)(2,1)S(1)}, bf16[800,128]{1,0:T(8,128)(2,1)S(1)}) custom-call(s32[24]{0:T(128)} %counts_hbm.3, bf16[24,256,128]{2,1,0:T(8,128)(2,1)} %basis_ref.1, f32[24,256]{1,0:T(8,128)} %weights_hbm.3), custom_call_target="tpu_custom_call" | custom-call | flops 201326592 | bytes 1376256 | tf_op jit(solution)/shard_map/pallas_call | solution.py:121
  10.1 1.6 %collective-permute-start.1 = (bf16[800,128]{1,0:T(8,128)(2,1)S(1)}, bf16[800,128]{1,0:T(8,128)(2,1)S(1)}, u32[]{:S(2)}, u32[]{:S(2)}) collective-permute-start(bf16[800,128]{1,0:T(8,128)(2,1)S(1)} %get-tuple-element.44), channel_id=1, source_target_pairs={{0,2},{1,3},{2,0},{3,1},{4,6},{5,7},{6,4},{7,5},{8,10},{9,11},{10,... | collective-permute-start | bytes 614408 | tf_op jit(solution)/shard_map/ppermute | solution.py:416
  11.7 2.2 %shard_map.106 = (bf16[12,128,128]{2,1,0:T(8,128)(2,1)S(1)}, bf16[800,128]{1,0:T(8,128)(2,1)S(1)}) custom-call(s32[24]{0:T(128)} %counts_hbm.3, bf16[24,256,128]{2,1,0:T(8,128)(2,1)} %basis_ref.1, f32[24,256]{1,0:T(8,128)} %weights_hbm.3), custom_call_target="tpu_custom_call" | custom-call | flops 201326592 | bytes 1376256 | tf_op jit(solution)/shard_map/pallas_call | solution.py:121
  14.6 3.5 %collective-permute-done.1.packed_ref = bf16[800,128]{1,0:T(8,128)(2,1)S(1)} collective-permute-done((bf16[800,128]{1,0:T(8,128)(2,1)S(1)}, bf16[800,128]{1,0:T(8,128)(2,1)S(1)}, u32[]{:S(2)}, u32[]{:S(2)}) %collective-permute-start.1) | collective-permute-done | bytes 204832 | tf_op jit(solution)/shard_map/ppermute | solution.py:416
  18.1 1.5 %collective-permute-start.4 = (s32[24,2]{1,0:T(8,128)S(1)}, s32[24,2]{1,0:T(8,128)S(1)}, u32[]{:S(2)}, u32[]{:S(2)}) collective-permute-start(s32[24,2]{1,0:T(8,128)S(1)} %copy.16.refs_0_.block_ref), channel_id=1, source_target_pairs={{0,2},{1,3},{2,0},{3,1},{4,6},{5,7},{6,4},{7,5},{8,10},{9,11},{10,... | collective-permute-start | bytes 584 | tf_op jit(solution)/shard_map/ppermute | solution.py:416
  20.1 0.9 shard_map.105.refs_6_
  21.0 1.0 collective-permute-done.4.refs_2_
  22.5 0.9 shard_map.107.refs_10_
  25.8 2.9 %shard_map.108 = (bf16[1024,128]{1,0:T(8,128)(2,1)S(1)}, f32[1024,128]{1,0:T(8,128)S(1)}, bf16[1024,128]{1,0:T(8,128)(2,1)S(1)}) custom-call(s32[24,2]{1,0:T(8,128)S(1)} %copy.16.refs_0_.block_ref, s32[24,2]{1,0:T(8,128)S(1)} %collective-permute-done.refs_1_.block_ref, s32[24,2]{1,0:T(8,128)S(1)} %collective-permute-done.4.refs_2_, ...), custom_call_target="tpu_custom_call" | custom-call | flops 402653184 | bytes 4980736 | tf_op jit(solution)/shard_map/pallas_call | solution.py:231
  28.7 4.7 %collective-permute-start.14 = (bf16[1024,128]{1,0:T(8,128)(2,1)S(1)}, bf16[1024,128]{1,0:T(8,128)(2,1)S(1)}, u32[]{:S(2)}, u32[]{:S(2)}) collective-permute-start(bf16[1024,128]{1,0:T(8,128)(2,1)S(1)} %get-tuple-element.56), channel_id=1, source_target_pairs={{4,0},{8,4},{12,8},{16,12},{20,16},{24,20},{28,24},{0,28},{5,1},{9... | collective-permute-start | bytes 786440 | tf_op jit(solution)/shard_map/ppermute | solution.py:569
  33.5 2.1 %shard_map.109 = bf16[1024,1920]{1,0:T(8,128)(2,1)S(1)} custom-call(bf16[1024,1920]{1,0:T(8,128)(2,1)} %refs_0_.4), custom_call_target="tpu_custom_call" | custom-call | bytes 7864320 | tf_op jit(solution)/shard_map/pallas_call | solution.py:47
  35.7 1.9 %copy-done = bf16[1024,1920]{1,0:T(8,128)(2,1)} copy-done((bf16[1024,1920]{1,0:T(8,128)(2,1)}, bf16[1024,1920]{1,0:T(8,128)(2,1)S(1)}, u32[]{:S(2)}) %copy-start) | copy-done | bytes 3932184
  37.7 2.1 %shard_map.110 = bf16[1024,1920]{1,0:T(8,128)(2,1)S(1)} custom-call(bf16[1024,1920]{1,0:T(8,128)(2,1)} %collective-permute-done.12.source_ref.refs_1_), custom_call_target="tpu_custom_call" | custom-call | bytes 7864320 | tf_op jit(solution)/shard_map/pallas_call | solution.py:47
  40.5 2.4 %collective-permute-done.14 = bf16[1024,128]{1,0:T(8,128)(2,1)S(1)} collective-permute-done((bf16[1024,128]{1,0:T(8,128)(2,1)S(1)}, bf16[1024,128]{1,0:T(8,128)(2,1)S(1)}, u32[]{:S(2)}, u32[]{:S(2)}) %collective-permute-start.14) | collective-permute-done | bytes 262176 | tf_op jit(solution)/shard_map/ppermute | solution.py:569
  43.0 1.5 %collective-permute-start.20 = (bf16[1024,128]{1,0:T(8,128)(2,1)S(1)}, bf16[1024,128]{1,0:T(8,128)(2,1)S(1)}, u32[]{:S(2)}, u32[]{:S(2)}) collective-permute-start(bf16[1024,128]{1,0:T(8,128)(2,1)S(1)} %add_convert_fusion.1), channel_id=1, source_target_pairs={{0,2},{1,3},{2,0},{3,1},{4,6},{5,7},{6,4},{7,5},{8,10},{9,11},{10,... | collective-permute-start | bytes 786440 | tf_op jit(solution)/shard_map/ppermute | solution.py:416
  46.3 4.4 %collective-permute-done.20 = bf16[1024,128]{1,0:T(8,128)(2,1)S(1)} collective-permute-done((bf16[1024,128]{1,0:T(8,128)(2,1)S(1)}, bf16[1024,128]{1,0:T(8,128)(2,1)S(1)}, u32[]{:S(2)}, u32[]{:S(2)}) %collective-permute-start.20) | collective-permute-done | bytes 262176 | tf_op jit(solution)/shard_map/ppermute | solution.py:416
  52.6 2.4 %collective-permute-done.15 = bf16[2,64,1920]{2,1,0:T(8,128)(2,1)S(1)} collective-permute-done((bf16[2,64,1920]{2,1,0:T(8,128)(2,1)S(1)}, bf16[2,64,1920]{2,1,0:T(8,128)(2,1)S(1)}, u32[]{:S(2)}, u32[]{:S(2)}) %collective-permute-start.15) | collective-permute-done | bytes 491552 | tf_op jit(solution)/shard_map/ppermute | solution.py:445
  55.3 10.7 %collective-permute-done.21 = bf16[2,64,1920]{2,1,0:T(8,128)(2,1)S(1)} collective-permute-done((bf16[2,64,1920]{2,1,0:T(8,128)(2,1)S(1)}, bf16[2,64,1920]{2,1,0:T(8,128)(2,1)S(1)}, u32[]{:S(2)}, u32[]{:S(2)}) %collective-permute-start.21) | collective-permute-done | bytes 491552 | tf_op jit(solution)/shard_map/ppermute | solution.py:445
  66.2 3.0 %collective-permute-start.17 = (bf16[2,32,1920]{2,1,0:T(8,128)(2,1)S(1)}, bf16[2,32,1920]{2,1,0:T(8,128)(2,1)S(1)}, u32[]{:S(2)}, u32[]{:S(2)}) collective-permute-start(bf16[2,32,1920]{2,1,0:T(8,128)(2,1)S(1)} %get-tuple-element.61), channel_id=1, source_target_pairs={{0,16},{4,20},{8,24},{12,28},{16,0},{20,4},{24,8},{28,12},{1,17},{... | collective-permute-start | bytes 737288 | tf_op jit(solution)/shard_map/ppermute | solution.py:416
  69.3 2.0 %collective-permute-start.19 = (bf16[1024,128]{1,0:T(8,128)(2,1)S(1)}, bf16[1024,128]{1,0:T(8,128)(2,1)S(1)}, u32[]{:S(2)}, u32[]{:S(2)}) collective-permute-start(bf16[1024,128]{1,0:T(8,128)(2,1)S(1)} %collective-permute-done.3.refs_14_.refs_4_), channel_id=1, source_target_pairs={{0,2},{1,3},{2,0},{3,1},{4,6},{5,7},{6,4},{7,5},{8,10},{9,11},{10,... | collective-permute-start | bytes 786440 | tf_op jit(solution)/shard_map/ppermute | solution.py:416
  71.3 3.7 %collective-permute-done.22 = bf16[2,32,1920]{2,1,0:T(8,128)(2,1)S(1)} collective-permute-done((bf16[2,32,1920]{2,1,0:T(8,128)(2,1)S(1)}, bf16[2,32,1920]{2,1,0:T(8,128)(2,1)S(1)}, u32[]{:S(2)}, u32[]{:S(2)}) %collective-permute-start.22) | collective-permute-done | bytes 245792 | tf_op jit(solution)/shard_map/ppermute | solution.py:445
  76.4 7.4 %collective-permute-done.17.refs_1_ = bf16[2,32,1920]{2,1,0:T(8,128)(2,1)S(1)} collective-permute-done((bf16[2,32,1920]{2,1,0:T(8,128)(2,1)S(1)}, bf16[2,32,1920]{2,1,0:T(8,128)(2,1)S(1)}, u32[]{:S(2)}, u32[]{:S(2)}) %collective-permute-start.17) | collective-permute-done | bytes 245792 | tf_op jit(solution)/shard_map/ppermute | solution.py:416
  83.8 2.6 %collective-permute-done.23.refs_4_ = bf16[2,32,1920]{2,1,0:T(8,128)(2,1)S(1)} collective-permute-done((bf16[2,32,1920]{2,1,0:T(8,128)(2,1)}, bf16[2,32,1920]{2,1,0:T(8,128)(2,1)S(1)}, u32[]{:S(2)}, u32[]{:S(2)}) %collective-permute-start.23) | collective-permute-done | bytes 245792 | tf_op jit(solution)/shard_map/ppermute | solution.py:416
  86.4 0.9 shard_map.111
  87.4 2.0 %collective-permute-start.24 = (bf16[2,32,1920]{2,1,0:T(8,128)(2,1)S(1)}, bf16[2,32,1920]{2,1,0:T(8,128)(2,1)S(1)}, u32[]{:S(2)}, u32[]{:S(2)}) collective-permute-start(bf16[2,32,1920]{2,1,0:T(8,128)(2,1)S(1)} %get-tuple-element.72), channel_id=1, source_target_pairs={{0,8},{1,5},{2,10},{3,7},{4,12},{5,1},{6,14},{7,3},{8,0},{9,13},{1... | collective-permute-start | bytes 737288 | tf_op jit(solution)/shard_map/ppermute | solution.py:445
  89.4 4.5 %collective-permute-done.26 = bf16[2,32,1920]{2,1,0:T(8,128)(2,1)S(1)} collective-permute-done((bf16[2,32,1920]{2,1,0:T(8,128)(2,1)}, bf16[2,32,1920]{2,1,0:T(8,128)(2,1)S(1)}, u32[]{:S(2)}, u32[]{:S(2)}) %collective-permute-start.26) | collective-permute-done | bytes 245792 | tf_op jit(solution)/shard_map/ppermute | solution.py:445
  93.8 1.0 broadcast_select_fusion.3
  94.9 1.3 collective-permute-start.27
  96.2 2.9 %collective-permute-done.24 = bf16[2,32,1920]{2,1,0:T(8,128)(2,1)S(1)} collective-permute-done((bf16[2,32,1920]{2,1,0:T(8,128)(2,1)S(1)}, bf16[2,32,1920]{2,1,0:T(8,128)(2,1)S(1)}, u32[]{:S(2)}, u32[]{:S(2)}) %collective-permute-start.24) | collective-permute-done | bytes 245792 | tf_op jit(solution)/shard_map/ppermute | solution.py:445
  99.2 1.3 collective-permute-start.25
  100.5 2.1 %shard_map.112.refs_1_ = bf16[1024,1920]{1,0:T(8,128)(2,1)S(1)} custom-call(bf16[1024,1920]{1,0:T(8,128)(2,1)} %collective-permute-done.12.source_ref.refs_1_), custom_call_target="tpu_custom_call" | custom-call | bytes 7864320 | tf_op jit(solution)/shard_map/pallas_call | solution.py:47
  102.7 1.1 collective-permute-done.27.coming_ref
  103.8 4.1 %shard_map.113.refs_2_ = bf16[1024,128]{1,0:T(8,128)(2,1)S(1)} custom-call(s32[1]{0:T(128)} %bitcast.3.first_ref, bf16[2,64,1920]{2,1,0:T(8,128)(2,1)S(1)} %pad_maximum_fusion.2.part_ref, bf16[2,64,1920]{2,1,0:T(8,128)(2,1)S(1)} %collective-permute-done.27.coming_ref, bf16[1024,1920]{1,0:T(8,128)(2,1)} %refs_0_.4, bf16[1024,1920]{1,0:T(8,128)(2,1)S(1)} %shard_map.112.refs_1_), custom_call_target="tpu_custom_call" | custom-call | flops 1006632960 | bytes 7864320 | tf_op jit(solution)/shard_map/pallas_call | solution.py:292
  108.3 0.8 collective-permute-done.25.coming_ref
  109.1 4.5 %shard_map.114 = f32[1024,128]{1,0:T(8,128)S(1)} custom-call(s32[1]{0:T(128)} %bitcast.3.first_ref, bf16[2,64,1920]{2,1,0:T(8,128)(2,1)S(1)} %pad_maximum_fusion.1.part_ref, bf16[2,64,1920]{2,1,0:T(8,128)(2,1)S(1)} %collective-permute-done.25.coming_ref, bf16[1024,1920]{1,0:T(8,128)(2,1)} %refs_0_.4, ...), custom_call_target="tpu_custom_call" | custom-call | tf_op jit(solution)/shard_map/pallas_call | solution.py:292
  114.4 3.7 %collective-permute-start.32 = (bf16[1024,128]{1,0:T(8,128)(2,1)S(1)}, bf16[1024,128]{1,0:T(8,128)(2,1)S(1)}, u32[]{:S(2)}, u32[]{:S(2)}) collective-permute-start(bf16[1024,128]{1,0:T(8,128)(2,1)S(1)} %add_convert_fusion.refs_8_), channel_id=1, source_target_pairs={{4,0},{8,4},{12,8},{16,12},{20,16},{24,20},{28,24},{0,28},{5,1},{9... | collective-permute-start | bytes 786440 | tf_op jit(solution)/shard_map/ppermute | solution.py:422
  118.4 3.7 %collective-permute-done.32.refs_10_ = bf16[1024,128]{1,0:T(8,128)(2,1)S(1)} collective-permute-done((bf16[1024,128]{1,0:T(8,128)(2,1)S(1)}, bf16[1024,128]{1,0:T(8,128)(2,1)S(1)}, u32[]{:S(2)}, u32[]{:S(2)}) %collective-permute-start.32) | collective-permute-done | bytes 262176 | tf_op jit(solution)/shard_map/ppermute | solution.py:422
  122.0 3.6 %collective-permute-done.31.refs_9_ = bf16[1024,128]{1,0:T(8,128)(2,1)S(1)} collective-permute-done((bf16[1024,128]{1,0:T(8,128)(2,1)S(1)}, bf16[1024,128]{1,0:T(8,128)(2,1)S(1)}, u32[]{:S(2)}, u32[]{:S(2)}) %collective-permute-start.31) | collective-permute-done | bytes 262176 | tf_op jit(solution)/shard_map/ppermute | solution.py:416
  125.7 1.8 %collective-permute-done.29.refs_6_ = bf16[1024,128]{1,0:T(8,128)(2,1)S(1)} collective-permute-done((bf16[1024,128]{1,0:T(8,128)(2,1)S(1)}, bf16[1024,128]{1,0:T(8,128)(2,1)S(1)}, u32[]{:S(2)}, u32[]{:S(2)}) %collective-permute-start.29) | collective-permute-done | bytes 262176 | tf_op jit(solution)/shard_map/ppermute | solution.py:421
  127.4 1.8 %collective-permute-start.30 = (bf16[1024,128]{1,0:T(8,128)(2,1)S(1)}, bf16[1024,128]{1,0:T(8,128)(2,1)S(1)}, u32[]{:S(2)}, u32[]{:S(2)}) collective-permute-start(bf16[1024,128]{1,0:T(8,128)(2,1)S(1)} %collective-permute-done.29.refs_6_), channel_id=1, source_target_pairs={{0,2},{1,3},{2,0},{3,1},{4,6},{5,7},{6,4},{7,5},{8,10},{9,11},{10,... | collective-permute-start | bytes 786440 | tf_op jit(solution)/shard_map/ppermute | solution.py:416
  129.2 3.7 %collective-permute-done.33.refs_11_ = bf16[1024,128]{1,0:T(8,128)(2,1)S(1)} collective-permute-done((bf16[1024,128]{1,0:T(8,128)(2,1)S(1)}, bf16[1024,128]{1,0:T(8,128)(2,1)S(1)}, u32[]{:S(2)}, u32[]{:S(2)}) %collective-permute-start.33) | collective-permute-done | bytes 262176 | tf_op jit(solution)/shard_map/ppermute | solution.py:416
  132.9 2.8 %collective-permute-done.30.refs_7_ = bf16[1024,128]{1,0:T(8,128)(2,1)S(1)} collective-permute-done((bf16[1024,128]{1,0:T(8,128)(2,1)S(1)}, bf16[1024,128]{1,0:T(8,128)(2,1)S(1)}, u32[]{:S(2)}, u32[]{:S(2)}) %collective-permute-start.30) | collective-permute-done | bytes 262176 | tf_op jit(solution)/shard_map/ppermute | solution.py:416
  135.8 2.0 %shard_map.115 = (bf16[24,128,128]{2,1,0:T(8,128)(2,1)S(1)}, bf16[3072,256]{1,0:T(8,128)(2,1)S(1)}, bf16[3072,256]{1,0:T(8,128)(2,1)S(1)}) custom-call(s32[24,2]{1,0:T(8,128)S(1)} %copy-done.7, bf16[1024,128]{1,0:T(8,128)(2,1)S(1)} %collective-permute-done.2.refs_12_.refs_0_, bf16[1024,128]{1,0:T(8,128)(2,1)S(1)} %collective-permute-done.18.refs_1_, ...), custom_call_target="tpu_custom_call" | custom-call | flops 201326592 | bytes 3932160 | tf_op jit(solution)/shard_map/pallas_call | solution.py:338
  138.5 1.3 shard_map.116.first_ref
  139.8 1.0 collective-permute-done.35.near_ref
  140.9 2.4 %shard_map.117 = (f32[24,256]{1,0:T(8,128)}, bf16[1024,512]{1,0:T(8,128)(2,1)}) custom-call(s32[1]{0:T(128)} %bitcast.core_ref, bf16[24,256,128]{2,1,0:T(8,128)(2,1)S(1)} %copy-done.2, f32[24,128,128]{2,1,0:T(8,128)S(1)} %shard_map.116.first_ref, bf16[24,128,128]{2,1,0:T(8,128)(2,1)S(1)} %collective-permute-done.34.second_ref, f32[24,256]{1,0:T(8,128)S(1)} %copy-done.5, ...), custom_call_target="tpu_custom_call" | custom-call | flops 402653184 | bytes 3932160 | tf_op jit(solution)/shard_map/pallas_call | solution.py:397
  (93 shorter events, 13.2 us)
Async XLA Ops:
  0.6 23.4 %copy-start.10 = (s32[24]{0:T(128)S(1)}, s32[24]{0:T(128)}, u32[]{:S(2)}) copy-start(s32[24]{0:T(128)} %counts_hbm.3) | copy-start | bytes 292
  0.6 13.8 %copy-start.11 = (s32[24,2]{0,1:T(2,128)S(1)}, s32[24,2]{0,1:T(2,128)}, u32[]{:S(2)}) copy-start(s32[24,2]{0,1:T(2,128)} %param.10) | copy-start | bytes 580
  0.7 23.3 %copy-start.8 = (f32[24,256]{1,0:T(8,128)S(1)}, f32[24,256]{1,0:T(8,128)}, u32[]{:S(2)}) copy-start(f32[24,256]{1,0:T(8,128)} %param.13) | copy-start | bytes 73732
  0.7 24.0 %copy-start.9 = (f32[1920]{0:T(1024)S(1)}, f32[1920]{0:T(1024)}, u32[]{:S(2)}) copy-start(f32[1920]{0:T(1024)} %param.17) | copy-start | bytes 23044
  0.7 37.0 %collective-permute-start.12 = (bf16[1024,1920]{1,0:T(8,128)(2,1)}, bf16[1024,1920]{1,0:T(8,128)(2,1)}, u32[]{:S(2)}, u32[]{:S(2)}) collective-permute-start(bf16[1024,1920]{1,0:T(8,128)(2,1)} %refs_0_.4), channel_id=1, source_target_pairs={{0,1},{1,0},{2,3},{3,2},{4,5},{5,4},{6,7},{7,6},{8,9},{9,8},{10,11... | collective-permute-start | bytes 11796488 | tf_op jit(solution)/shard_map/ppermute | solution.py:416
  2.3 31.2 %copy-start.12 = (f32[512]{0:T(512)S(1)}, f32[512]{0:T(512)}, u32[]{:S(2)}) copy-start(f32[512]{0:T(512)} %param.16) | copy-start | bytes 6148
  2.3 17.3 %collective-permute-start.3 = (bf16[1024,128]{1,0:T(8,128)(2,1)S(1)}, bf16[1024,128]{1,0:T(8,128)(2,1)S(1)}, u32[]{:S(2)}, u32[]{:S(2)}) collective-permute-start(bf16[1024,128]{1,0:T(8,128)(2,1)S(1)} %get-tuple-element.91.refs_13_.refs_2_), channel_id=1, source_target_pairs={{4,0},{8,4},{12,8},{16,12},{20,16},{24,20},{28,24},{0,28},{5,1},{9... | collective-permute-start | bytes 786440 | tf_op jit(solution)/shard_map/ppermute | solution.py:422
  7.9 11.7 %collective-permute-start.2 = (bf16[1024,128]{1,0:T(8,128)(2,1)S(1)}, bf16[1024,128]{1,0:T(8,128)(2,1)S(1)}, u32[]{:S(2)}, u32[]{:S(2)}) collective-permute-start(bf16[1024,128]{1,0:T(8,128)(2,1)S(1)} %get-tuple-element.91.refs_13_.refs_2_), channel_id=1, source_target_pairs={{0,4},{4,8},{8,12},{12,16},{16,20},{20,24},{24,28},{28,0},{1,5},{5... | collective-permute-start | bytes 786440 | tf_op jit(solution)/shard_map/ppermute | solution.py:421
  10.1 8.0 %collective-permute-start.1 = (bf16[800,128]{1,0:T(8,128)(2,1)S(1)}, bf16[800,128]{1,0:T(8,128)(2,1)S(1)}, u32[]{:S(2)}, u32[]{:S(2)}) collective-permute-start(bf16[800,128]{1,0:T(8,128)(2,1)S(1)} %get-tuple-element.44), channel_id=1, source_target_pairs={{0,2},{1,3},{2,0},{3,1},{4,6},{5,7},{6,4},{7,5},{8,10},{9,11},{10,... | collective-permute-start | bytes 614408 | tf_op jit(solution)/shard_map/ppermute | solution.py:416
  13.9 8.1 %collective-permute-start.9 = (bf16[800,128]{1,0:T(8,128)(2,1)S(1)}, bf16[800,128]{1,0:T(8,128)(2,1)S(1)}, u32[]{:S(2)}, u32[]{:S(2)}) collective-permute-start(bf16[800,128]{1,0:T(8,128)(2,1)S(1)} %get-tuple-element.50), channel_id=1, source_target_pairs={{0,2},{1,3},{2,0},{3,1},{4,6},{5,7},{6,4},{7,5},{8,10},{9,11},{10,... | collective-permute-start | bytes 614408 | tf_op jit(solution)/shard_map/ppermute | solution.py:416
  14.6 21.1 %copy-start.3 = (s32[24,2]{1,0:T(8,128)}, s32[24,2]{1,0:T(8,128)S(1)}, u32[]{:S(2)}) copy-start(s32[24,2]{1,0:T(8,128)S(1)} %copy.16.refs_0_.block_ref) | copy-start | bytes 580
  18.1 3.9 %collective-permute-start.4 = (s32[24,2]{1,0:T(8,128)S(1)}, s32[24,2]{1,0:T(8,128)S(1)}, u32[]{:S(2)}, u32[]{:S(2)}) collective-permute-start(s32[24,2]{1,0:T(8,128)S(1)} %copy.16.refs_0_.block_ref), channel_id=1, source_target_pairs={{0,2},{1,3},{2,0},{3,1},{4,6},{5,7},{6,4},{7,5},{8,10},{9,11},{10,... | collective-permute-start | bytes 584 | tf_op jit(solution)/shard_map/ppermute | solution.py:416
  19.6 3.8 %collective-permute-start = (s32[24,2]{1,0:T(8,128)S(1)}, s32[24,2]{1,0:T(8,128)S(1)}, u32[]{:S(2)}, u32[]{:S(2)}) collective-permute-start(s32[24,2]{1,0:T(8,128)S(1)} %copy.16.refs_0_.block_ref), channel_id=1, source_target_pairs={{0,1},{1,0},{2,3},{3,2},{4,5},{5,4},{6,7},{7,6},{8,9},{9,8},{10,11... | collective-permute-start | bytes 584 | tf_op jit(solution)/shard_map/ppermute | solution.py:416
  19.6 5.0 %collective-permute-start.8 = (bf16[12,128,128]{2,1,0:T(8,128)(2,1)S(1)}, bf16[12,128,128]{2,1,0:T(8,128)(2,1)S(1)}, u32[]{:S(2)}, u32[]{:S(2)}) collective-permute-start(bf16[12,128,128]{2,1,0:T(8,128)(2,1)S(1)} %get-tuple-element.49.refs_8_), channel_id=1, source_target_pairs={{0,1},{1,0},{2,3},{3,2},{4,5},{5,4},{6,7},{7,6},{8,9},{9,8},{10,11... | collective-permute-start | bytes 1179656 | tf_op jit(solution)/shard_map/ppermute | solution.py:416
  22.0 2.9 %collective-permute-start.6 = (bf16[12,128,128]{2,1,0:T(8,128)(2,1)S(1)}, bf16[12,128,128]{2,1,0:T(8,128)(2,1)S(1)}, u32[]{:S(2)}, u32[]{:S(2)}) collective-permute-start(bf16[12,128,128]{2,1,0:T(8,128)(2,1)S(1)} %get-tuple-element.47.refs_4_), channel_id=1, source_target_pairs={{0,1},{1,0},{2,3},{3,2},{4,5},{5,4},{6,7},{7,6},{8,9},{9,8},{10,11... | collective-permute-start | bytes 1179656 | tf_op jit(solution)/shard_map/ppermute | solution.py:416
  22.0 1.7 %collective-permute-start.5 = (s32[24,2]{1,0:T(8,128)S(1)}, s32[24,2]{1,0:T(8,128)S(1)}, u32[]{:S(2)}, u32[]{:S(2)}) collective-permute-start(s32[24,2]{1,0:T(8,128)S(1)} %collective-permute-done.4.refs_2_), channel_id=1, source_target_pairs={{0,1},{1,0},{2,3},{3,2},{4,5},{5,4},{6,7},{7,6},{8,9},{9,8},{10,11... | collective-permute-start | bytes 584 | tf_op jit(solution)/shard_map/ppermute | solution.py:416
  23.4 12.2 %copy-start.6 = (s32[24,2]{1,0:T(8,128)}, s32[24,2]{1,0:T(8,128)S(1)}, u32[]{:S(2)}) copy-start(s32[24,2]{1,0:T(8,128)S(1)} %collective-permute-done.refs_1_.block_ref) | copy-start | bytes 580
  23.4 1.8 %collective-permute-start.10 = (bf16[12,128,128]{2,1,0:T(8,128)(2,1)S(1)}, bf16[12,128,128]{2,1,0:T(8,128)(2,1)S(1)}, u32[]{:S(2)}, u32[]{:S(2)}) collective-permute-start(bf16[12,128,128]{2,1,0:T(8,128)(2,1)S(1)} %shard_map.107.refs_10_), channel_id=1, source_target_pairs={{0,1},{1,0},{2,3},{3,2},{4,5},{5,4},{6,7},{7,6},{8,9},{9,8},{10,11... | collective-permute-start | bytes 1179656 | tf_op jit(solution)/shard_map/ppermute | solution.py:416
  23.8 2.0 %collective-permute-start.7 = (bf16[12,128,128]{2,1,0:T(8,128)(2,1)S(1)}, bf16[12,128,128]{2,1,0:T(8,128)(2,1)S(1)}, u32[]{:S(2)}, u32[]{:S(2)}) collective-permute-start(bf16[12,128,128]{2,1,0:T(8,128)(2,1)S(1)} %shard_map.105.refs_6_), channel_id=1, source_target_pairs={{0,1},{1,0},{2,3},{3,2},{4,5},{5,4},{6,7},{7,6},{8,9},{9,8},{10,11... | collective-permute-start | bytes 1179656 | tf_op jit(solution)/shard_map/ppermute | solution.py:416
  24.7 13.0 %collective-permute-start.11 = (f32[1920]{0:T(1024)S(1)}, f32[1920]{0:T(1024)S(1)}, u32[]{:S(2)}, u32[]{:S(2)}) collective-permute-start(f32[1920]{0:T(1024)S(1)} %copy-done.9), channel_id=1, source_target_pairs={{0,1},{1,0},{2,3},{3,2},{4,5},{5,4},{6,7},{7,6},{8,9},{9,8},{10,11... | collective-permute-start | bytes 23048 | tf_op jit(solution)/shard_map/ppermute | solution.py:416
  28.7 11.8 %collective-permute-start.13 = (bf16[1024,128]{1,0:T(8,128)(2,1)S(1)}, bf16[1024,128]{1,0:T(8,128)(2,1)S(1)}, u32[]{:S(2)}, u32[]{:S(2)}) collective-permute-start(bf16[1024,128]{1,0:T(8,128)(2,1)S(1)} %get-tuple-element.55), channel_id=1, source_target_pairs={{0,4},{4,8},{8,12},{12,16},{16,20},{20,24},{24,28},{28,0},{1,5},{5... | collective-permute-start | bytes 786440 | tf_op jit(solution)/shard_map/ppermute | solution.py:568
  28.7 14.2 %collective-permute-start.14 = (bf16[1024,128]{1,0:T(8,128)(2,1)S(1)}, bf16[1024,128]{1,0:T(8,128)(2,1)S(1)}, u32[]{:S(2)}, u32[]{:S(2)}) collective-permute-start(bf16[1024,128]{1,0:T(8,128)(2,1)S(1)} %get-tuple-element.56), channel_id=1, source_target_pairs={{4,0},{8,4},{12,8},{16,12},{20,16},{24,20},{28,24},{0,28},{5,1},{9... | collective-permute-start | bytes 786440 | tf_op jit(solution)/shard_map/ppermute | solution.py:569
  39.8 5.5 %copy-start.1 = (bf16[1024,1920]{1,0:T(8,128)(2,1)S(1)}, bf16[1024,1920]{1,0:T(8,128)(2,1)}, u32[]{:S(2)}) copy-start(bf16[1024,1920]{1,0:T(8,128)(2,1)} %copy-done) | copy-start | bytes 11796484
  43.0 7.6 %collective-permute-start.20 = (bf16[1024,128]{1,0:T(8,128)(2,1)S(1)}, bf16[1024,128]{1,0:T(8,128)(2,1)S(1)}, u32[]{:S(2)}, u32[]{:S(2)}) collective-permute-start(bf16[1024,128]{1,0:T(8,128)(2,1)S(1)} %add_convert_fusion.1), channel_id=1, source_target_pairs={{0,2},{1,3},{2,0},{3,1},{4,6},{5,7},{6,4},{7,5},{8,10},{9,11},{10,... | collective-permute-start | bytes 786440 | tf_op jit(solution)/shard_map/ppermute | solution.py:416
  46.1 8.9 %collective-permute-start.15 = (bf16[2,64,1920]{2,1,0:T(8,128)(2,1)S(1)}, bf16[2,64,1920]{2,1,0:T(8,128)(2,1)S(1)}, u32[]{:S(2)}, u32[]{:S(2)}) collective-permute-start(bf16[2,64,1920]{2,1,0:T(8,128)(2,1)S(1)} %fusion.5), channel_id=1, source_target_pairs={{0,4},{1,9},{2,6},{3,11},{4,0},{5,13},{6,2},{7,15},{8,12},{9,1},{1... | collective-permute-start | bytes 1474568 | tf_op jit(solution)/shard_map/ppermute | solution.py:445
  52.2 13.8 %collective-permute-start.21 = (bf16[2,64,1920]{2,1,0:T(8,128)(2,1)S(1)}, bf16[2,64,1920]{2,1,0:T(8,128)(2,1)S(1)}, u32[]{:S(2)}, u32[]{:S(2)}) collective-permute-start(bf16[2,64,1920]{2,1,0:T(8,128)(2,1)S(1)} %fusion.1), channel_id=1, source_target_pairs={{0,4},{1,9},{2,6},{3,11},{4,0},{5,13},{6,2},{7,15},{8,12},{9,1},{1... | collective-permute-start | bytes 1474568 | tf_op jit(solution)/shard_map/ppermute | solution.py:445
  55.2 11.0 %collective-permute-start.16 = (bf16[2,32,1920]{2,1,0:T(8,128)(2,1)S(1)}, bf16[2,32,1920]{2,1,0:T(8,128)(2,1)S(1)}, u32[]{:S(2)}, u32[]{:S(2)}) collective-permute-start(bf16[2,32,1920]{2,1,0:T(8,128)(2,1)S(1)} %dynamic-slice_convert_fusion.1), channel_id=1, source_target_pairs={{0,8},{1,5},{2,10},{3,7},{4,12},{5,1},{6,14},{7,3},{8,0},{9,13},{1... | collective-permute-start | bytes 737288 | tf_op jit(solution)/shard_map/ppermute | solution.py:445
  66.1 9.0 %collective-permute-start.22 = (bf16[2,32,1920]{2,1,0:T(8,128)(2,1)S(1)}, bf16[2,32,1920]{2,1,0:T(8,128)(2,1)S(1)}, u32[]{:S(2)}, u32[]{:S(2)}) collective-permute-start(bf16[2,32,1920]{2,1,0:T(8,128)(2,1)S(1)} %dynamic-slice_convert_fusion), channel_id=1, source_target_pairs={{0,8},{1,5},{2,10},{3,7},{4,12},{5,1},{6,14},{7,3},{8,0},{9,13},{1... | collective-permute-start | bytes 737288 | tf_op jit(solution)/shard_map/ppermute | solution.py:445
  66.2 17.5 %collective-permute-start.17 = (bf16[2,32,1920]{2,1,0:T(8,128)(2,1)S(1)}, bf16[2,32,1920]{2,1,0:T(8,128)(2,1)S(1)}, u32[]{:S(2)}, u32[]{:S(2)}) collective-permute-start(bf16[2,32,1920]{2,1,0:T(8,128)(2,1)S(1)} %get-tuple-element.61), channel_id=1, source_target_pairs={{0,16},{4,20},{8,24},{12,28},{16,0},{20,4},{24,8},{28,12},{1,17},{... | collective-permute-start | bytes 737288 | tf_op jit(solution)/shard_map/ppermute | solution.py:416
  69.3 14.5 %collective-permute-start.18 = (bf16[1024,128]{1,0:T(8,128)(2,1)S(1)}, bf16[1024,128]{1,0:T(8,128)(2,1)S(1)}, u32[]{:S(2)}, u32[]{:S(2)}) collective-permute-start(bf16[1024,128]{1,0:T(8,128)(2,1)S(1)} %collective-permute-done.2.refs_12_.refs_0_), channel_id=1, source_target_pairs={{0,2},{1,3},{2,0},{3,1},{4,6},{5,7},{6,4},{7,5},{8,10},{9,11},{10,... | collective-permute-start | bytes 786440 | tf_op jit(solution)/shard_map/ppermute | solution.py:416
  69.3 14.5 %collective-permute-start.19 = (bf16[1024,128]{1,0:T(8,128)(2,1)S(1)}, bf16[1024,128]{1,0:T(8,128)(2,1)S(1)}, u32[]{:S(2)}, u32[]{:S(2)}) collective-permute-start(bf16[1024,128]{1,0:T(8,128)(2,1)S(1)} %collective-permute-done.3.refs_14_.refs_4_), channel_id=1, source_target_pairs={{0,2},{1,3},{2,0},{3,1},{4,6},{5,7},{6,4},{7,5},{8,10},{9,11},{10,... | collective-permute-start | bytes 786440 | tf_op jit(solution)/shard_map/ppermute | solution.py:416
  75.8 10.6 %collective-permute-start.23 = (bf16[2,32,1920]{2,1,0:T(8,128)(2,1)}, bf16[2,32,1920]{2,1,0:T(8,128)(2,1)S(1)}, u32[]{:S(2)}, u32[]{:S(2)}) collective-permute-start(bf16[2,32,1920]{2,1,0:T(8,128)(2,1)} %get-tuple-element.70), channel_id=1, source_target_pairs={{0,16},{4,20},{8,24},{12,28},{16,0},{20,4},{24,8},{28,12},{1,17},{... | collective-permute-start | bytes 737288 | tf_op jit(solution)/shard_map/ppermute | solution.py:416
  87.3 6.5 %collective-permute-start.26 = (bf16[2,32,1920]{2,1,0:T(8,128)(2,1)}, bf16[2,32,1920]{2,1,0:T(8,128)(2,1)S(1)}, u32[]{:S(2)}, u32[]{:S(2)}) collective-permute-start(bf16[2,32,1920]{2,1,0:T(8,128)(2,1)} %get-tuple-element.73), channel_id=1, source_target_pairs={{0,8},{1,5},{2,10},{3,7},{4,12},{5,1},{6,14},{7,3},{8,0},{9,13},{1... | collective-permute-start | bytes 737288 | tf_op jit(solution)/shard_map/ppermute | solution.py:445
  87.4 11.8 %collective-permute-start.24 = (bf16[2,32,1920]{2,1,0:T(8,128)(2,1)S(1)}, bf16[2,32,1920]{2,1,0:T(8,128)(2,1)S(1)}, u32[]{:S(2)}, u32[]{:S(2)}) collective-permute-start(bf16[2,32,1920]{2,1,0:T(8,128)(2,1)S(1)} %get-tuple-element.72), channel_id=1, source_target_pairs={{0,8},{1,5},{2,10},{3,7},{4,12},{5,1},{6,14},{7,3},{8,0},{9,13},{1... | collective-permute-start | bytes 737288 | tf_op jit(solution)/shard_map/ppermute | solution.py:445
  94.9 8.9 %collective-permute-start.27 = (bf16[2,64,1920]{2,1,0:T(8,128)(2,1)S(1)}, bf16[2,64,1920]{2,1,0:T(8,128)(2,1)S(1)}, u32[]{:S(2)}, u32[]{:S(2)}) collective-permute-start(bf16[2,64,1920]{2,1,0:T(8,128)(2,1)S(1)} %pad_maximum_fusion.2.part_ref), channel_id=1, source_target_pairs={{0,4},{1,9},{2,6},{3,11},{4,0},{5,13},{6,2},{7,15},{8,12},{9,1},{1... | collective-permute-start | bytes 1474568 | tf_op jit(solution)/shard_map/ppermute | solution.py:445
  99.2 9.8 %collective-permute-start.25 = (bf16[2,64,1920]{2,1,0:T(8,128)(2,1)S(1)}, bf16[2,64,1920]{2,1,0:T(8,128)(2,1)S(1)}, u32[]{:S(2)}, u32[]{:S(2)}) collective-permute-start(bf16[2,64,1920]{2,1,0:T(8,128)(2,1)S(1)} %pad_maximum_fusion.1.part_ref), channel_id=1, source_target_pairs={{0,4},{1,9},{2,6},{3,11},{4,0},{5,13},{6,2},{7,15},{8,12},{9,1},{1... | collective-permute-start | bytes 1474568 | tf_op jit(solution)/shard_map/ppermute | solution.py:445
  107.9 27.9 %copy-start.7 = (s32[24,2]{1,0:T(8,128)S(1)}, s32[24,2]{1,0:T(8,128)}, u32[]{:S(2)}) copy-start(s32[24,2]{1,0:T(8,128)} %copy-done.6) | copy-start | bytes 580
  107.9 6.4 %collective-permute-start.28 = (bf16[1024,128]{1,0:T(8,128)(2,1)S(1)}, bf16[1024,128]{1,0:T(8,128)(2,1)S(1)}, u32[]{:S(2)}, u32[]{:S(2)}) collective-permute-start(bf16[1024,128]{1,0:T(8,128)(2,1)S(1)} %shard_map.113.refs_2_), channel_id=1, source_target_pairs={{0,2},{1,3},{2,0},{3,1},{4,6},{5,7},{6,4},{7,5},{8,10},{9,11},{10,... | collective-permute-start | bytes 786440 | tf_op jit(solution)/shard_map/ppermute | solution.py:416
  113.6 24.9 %copy-start.4 = (s32[24,2]{1,0:T(8,128)S(1)}, s32[24,2]{1,0:T(8,128)}, u32[]{:S(2)}) copy-start(s32[24,2]{1,0:T(8,128)} %copy-done.3) | copy-start | bytes 580
  114.4 7.6 %collective-permute-start.32 = (bf16[1024,128]{1,0:T(8,128)(2,1)S(1)}, bf16[1024,128]{1,0:T(8,128)(2,1)S(1)}, u32[]{:S(2)}, u32[]{:S(2)}) collective-permute-start(bf16[1024,128]{1,0:T(8,128)(2,1)S(1)} %add_convert_fusion.refs_8_), channel_id=1, source_target_pairs={{4,0},{8,4},{12,8},{16,12},{20,16},{24,20},{28,24},{0,28},{5,1},{9... | collective-permute-start | bytes 786440 | tf_op jit(solution)/shard_map/ppermute | solution.py:422
  118.1 7.5 %collective-permute-start.31 = (bf16[1024,128]{1,0:T(8,128)(2,1)S(1)}, bf16[1024,128]{1,0:T(8,128)(2,1)S(1)}, u32[]{:S(2)}, u32[]{:S(2)}) collective-permute-start(bf16[1024,128]{1,0:T(8,128)(2,1)S(1)} %add_convert_fusion.refs_8_), channel_id=1, source_target_pairs={{0,2},{1,3},{2,0},{3,1},{4,6},{5,7},{6,4},{7,5},{8,10},{9,11},{10,... | collective-permute-start | bytes 786440 | tf_op jit(solution)/shard_map/ppermute | solution.py:416
  118.3 9.1 %collective-permute-start.29 = (bf16[1024,128]{1,0:T(8,128)(2,1)S(1)}, bf16[1024,128]{1,0:T(8,128)(2,1)S(1)}, u32[]{:S(2)}, u32[]{:S(2)}) collective-permute-start(bf16[1024,128]{1,0:T(8,128)(2,1)S(1)} %add_convert_fusion.refs_8_), channel_id=1, source_target_pairs={{0,4},{4,8},{8,12},{12,16},{16,20},{20,24},{24,28},{28,0},{1,5},{5... | collective-permute-start | bytes 786440 | tf_op jit(solution)/shard_map/ppermute | solution.py:421
  125.7 7.3 %collective-permute-start.33 = (bf16[1024,128]{1,0:T(8,128)(2,1)S(1)}, bf16[1024,128]{1,0:T(8,128)(2,1)S(1)}, u32[]{:S(2)}, u32[]{:S(2)}) collective-permute-start(bf16[1024,128]{1,0:T(8,128)(2,1)S(1)} %collective-permute-done.32.refs_10_), channel_id=1, source_target_pairs={{0,2},{1,3},{2,0},{3,1},{4,6},{5,7},{6,4},{7,5},{8,10},{9,11},{10,... | collective-permute-start | bytes 786440 | tf_op jit(solution)/shard_map/ppermute | solution.py:416
  127.4 8.3 %collective-permute-start.30 = (bf16[1024,128]{1,0:T(8,128)(2,1)S(1)}, bf16[1024,128]{1,0:T(8,128)(2,1)S(1)}, u32[]{:S(2)}, u32[]{:S(2)}) collective-permute-start(bf16[1024,128]{1,0:T(8,128)(2,1)S(1)} %collective-permute-done.29.refs_6_), channel_id=1, source_target_pairs={{0,2},{1,3},{2,0},{3,1},{4,6},{5,7},{6,4},{7,5},{8,10},{9,11},{10,... | collective-permute-start | bytes 786440 | tf_op jit(solution)/shard_map/ppermute | solution.py:416
  137.7 3.1 %copy-start.2 = (bf16[24,256,128]{2,1,0:T(8,128)(2,1)S(1)}, bf16[24,256,128]{2,1,0:T(8,128)(2,1)}, u32[]{:S(2)}) copy-start(bf16[24,256,128]{2,1,0:T(8,128)(2,1)} %basis_ref.1) | copy-start | bytes 4718596
  137.8 3.1 %copy-start.5 = (f32[24,256]{1,0:T(8,128)S(1)}, f32[24,256]{1,0:T(8,128)}, u32[]{:S(2)}) copy-start(f32[24,256]{1,0:T(8,128)} %multiply_select_fusion.scale_ref) | copy-start | bytes 73732
  137.8 3.1 %collective-permute-start.34 = (bf16[24,128,128]{2,1,0:T(8,128)(2,1)S(1)}, bf16[24,128,128]{2,1,0:T(8,128)(2,1)S(1)}, u32[]{:S(2)}, u32[]{:S(2)}) collective-permute-start(bf16[24,128,128]{2,1,0:T(8,128)(2,1)S(1)} %get-tuple-element.82), channel_id=1, source_target_pairs={{0,1},{1,0},{2,3},{3,2},{4,5},{5,4},{6,7},{7,6},{8,9},{9,8},{10,11... | collective-permute-start | bytes 2359304 | tf_op jit(solution)/shard_map/ppermute | solution.py:416
  138.0 2.9 %collective-permute-start.35 = (bf16[1024,256]{1,0:T(8,128)(2,1)S(1)}, bf16[1024,256]{1,0:T(8,128)(2,1)S(1)}, u32[]{:S(2)}, u32[]{:S(2)}) collective-permute-start(bf16[1024,256]{1,0:T(8,128)(2,1)S(1)} %pad_maximum_fusion.half_ref), channel_id=1, source_target_pairs={{0,1},{1,0},{2,3},{3,2},{4,5},{5,4},{6,7},{7,6},{8,9},{9,8},{10,11... | collective-permute-start | bytes 1572872 | tf_op jit(solution)/shard_map/ppermute | solution.py:416
  (1 other events, 1.9 us)

commit v12 on v11

--- a/solution.py
+++ b/solution.py
@@ -55,6 +55,28 @@
             flops=0, bytes_accessed=2 * array.size * array.dtype.itemsize, transcendentals=0
         ),
     )(place_in(array, pltpu.HBM))
+
+
+def load_both_kernel(first_ref, second_ref, first_out, second_out, semaphores):
+    copies = [(first_ref, first_out), (second_ref, second_out)]
+    for copy in fetch(copies, semaphores):
+        copy.wait()
+
+
+def load_both(arrays):
+    return pl.pallas_call(
+        load_both_kernel,
+        out_shape=[pltpu.VMEM(array.shape, array.dtype) for array in arrays],
+        in_specs=[HBM] * 2,
+        out_specs=[VMEM] * 2,
+        scratch_shapes=[pltpu.SemaphoreType.DMA((2,))],
+        compiler_params=params(),
+        cost_estimate=pl.CostEstimate(
+            flops=0,
+            bytes_accessed=2 * sum(array.size * array.dtype.itemsize for array in arrays),
+            transcendentals=0,
+        ),
+    )(place_in(arrays[0], pltpu.HBM), arrays[1])
 
 
 def split_dot(full, other, dims):
@@ -256,8 +278,8 @@
 
 def expand_kernel(fetched, first_ref, part_ref, coming_ref, *refs):
     sources, (out_ref, held, semaphores) = refs[:2], refs[-3:]
-    blocks = semaphores.shape[0] // fetched
-    rows = held.shape[1] // blocks
+    blocks = semaphores.shape[0] // max(fetched, 1)
+    rows = out_ref.shape[0] // blocks
     copies = []
     for i in range(blocks):
         place = pl.ds(i * rows, rows)
@@ -289,14 +311,16 @@
     width = 2 * part.shape[1]
     blocks = 4 if region % 64 == 0 and region > 64 else 1
     near = virtuals[1] if fetched == 2 else place_in(virtuals[1], pltpu.VMEM)
+    own = place_in(virtuals[0], pltpu.HBM if fetched else pltpu.VMEM)
     return pl.pallas_call(
         functools.partial(expand_kernel, fetched),
         out_shape=jax.ShapeDtypeStruct((region, width), kind),
-        in_specs=[SMEM, VMEM, VMEM, HBM, HBM if fetched == 2 else VMEM] + [HBM] * len(ahead),
+        in_specs=[SMEM, VMEM, VMEM, HBM if fetched else VMEM, HBM if fetched == 2 else VMEM]
+        + [HBM] * len(ahead),
         out_specs=VMEM,
         scratch_shapes=[
-            pltpu.VMEM((fetched, region, virt), BF16),
-            pltpu.SemaphoreType.DMA((fetched * blocks,)),
+            pltpu.VMEM((fetched, region, virt) if fetched else (16, 128), BF16),
+            pltpu.SemaphoreType.DMA((max(fetched, 1) * blocks,)),
         ],
         compiler_params=params(6 + 4 * fetched),
         cost_estimate=pl.CostEstimate(
@@ -304,7 +328,7 @@
             bytes_accessed=4 * region * virt if kind == BF16 else 0,
             transcendentals=0,
         ),
-    )(first.reshape(1), part, coming, place_in(virtuals[0], pltpu.HBM), near, *ahead)
+    )(first.reshape(1), part, coming, own, near, *ahead)
 
 
 def overlap_steps(block_ref, occ_ref, resp_ref, out_ref, rows):
@@ -592,7 +616,7 @@
         own.widen(own_rotation)
         far.widen(far_rotation)
         far.part, near = together(far.part, virtuals[1])
-        coef_far = far.result([virt_coef, load(near)], BF16, fetched=1)
+        coef_far = far.result(load_both([virt_coef, near]), BF16, fetched=0)
         coef_own = own.result(virtuals, F32, coef_far)
     else:
         before_far, after_far = flip(occ_before, "tile", 2), flip(occ_after, "tile", 2)

time: 144 us -> 143 us (level)
    pallas_call x0 -> x1, Pallas kernels: none -> 3.33 us  [load_both(): pl.pallas_call(load_both_kernel, out_shape=[pltpu.VMEM(array.shape, array...]
    pallas_call x3 -> x2, Pallas kernels: 6.37 us -> 4.25 us  [load(): pl.pallas_call(load_kernel, out_shape=pltpu.VMEM(array.shape, array.dtype...]
    pallas_call x2, Pallas kernels: 8.62 us -> 6.78 us  [expand(): pl.pallas_call(functools.partial(expand_kernel, fetched), out_shape=jax.S...]
  transfers between devices with their start and end apart: 36 -> 36, of which waited for: 24 -> 22; matrix products, arithmetic and copies ran while one was open for 5% -> 5% of each run, Pallas kernels for 18% -> 17%
where the time goes in v12:
time: 143 us
  waiting for transfers between devices  66.8 us (47%)
  starting transfers between devices  35.1 us (25%)
  Pallas kernels  30 us (21%)
  local copies, waits for them, and re-layouts  3.54 us (2%)
  other arithmetic  3.18 us (2%)
  matrix products  2.97 us (2%)
    ppermute x22, waiting for transfers between devices, flip(): lax.ppermute(array, axis, [(i, i ^ mask) for i in range(lax.axis_size(axi...  30.8 us
    ppermute x8, waiting for transfers between devices, swap(): return lax.ppermute(array, ('grid', 'tile'), pairs)  26.9 us
    ppermute x22, starting transfers between devices, flip(): lax.ppermute(array, axis, [(i, i ^ mask) for i in range(lax.axis_size(axi...  15.7 us
    ppermute x2, starting transfers between devices, neighbours(): lax.ppermute(array, 'grid', [((i + 1) % size, i) for i in range(size)])  9.39 us
    pallas_call x2, Pallas kernels, expand(): pl.pallas_call(functools.partial(expand_kernel, fetched), out_shape=jax.S...  6.78 us
    ppermute x8, starting transfers between devices, swap(): return lax.ppermute(array, ('grid', 'tile'), pairs)  5.33 us
    ppermute x1, starting transfers between devices, per_device(): lax.ppermute(to_before, 'grid', [((i + 1) % size, i) for i in range(size)])  4.71 us
    pallas_call x2, Pallas kernels, integrate(): pl.pallas_call(functools.partial(integrate_kernel, start), out_shape=[plt...  4.37 us
  transfers between devices with their start and end apart: 36, of which 22 were waited for; matrix products, arithmetic and copies ran while one was open for 5% of the time, Pallas kernels for 17%

profile of v12, /device:TPU:0, one launch (start us, length us, event | category | flops | bytes accessed | tf_op | source)
XLA Modules:
  0.0 142.9 jit_solution(18397383056103448244)
XLA Ops:
  1.2 1.1 constant_dynamic-slice_fusion
  2.3 5.7 %collective-permute-start.3 = (bf16[1024,128]{1,0:T(8,128)(2,1)S(1)}, bf16[1024,128]{1,0:T(8,128)(2,1)S(1)}, u32[]{:S(2)}, u32[]{:S(2)}) collective-permute-start(bf16[1024,128]{1,0:T(8,128)(2,1)S(1)} %get-tuple-element.95.refs_13_.refs_2_), channel_id=1, source_target_pairs={{4,0},{8,4},{12,8},{16,12},{20,16},{24,20},{28,24},{0,28},{5,1},{9... | collective-permute-start | bytes 786440 | tf_op jit(solution)/shard_map/ppermute | solution.py:446
  7.9 2.2 %shard_map.104 = (bf16[12,128,128]{2,1,0:T(8,128)(2,1)S(1)}, bf16[800,128]{1,0:T(8,128)(2,1)S(1)}) custom-call(s32[24]{0:T(128)} %counts_hbm.3, bf16[24,256,128]{2,1,0:T(8,128)(2,1)} %basis_ref.1, f32[24,256]{1,0:T(8,128)} %weights_hbm.3), custom_call_target="tpu_custom_call" | custom-call | flops 201326592 | bytes 1376256 | tf_op jit(solution)/shard_map/pallas_call | solution.py:143
  10.1 1.6 %collective-permute-start.1 = (bf16[800,128]{1,0:T(8,128)(2,1)S(1)}, bf16[800,128]{1,0:T(8,128)(2,1)S(1)}, u32[]{:S(2)}, u32[]{:S(2)}) collective-permute-start(bf16[800,128]{1,0:T(8,128)(2,1)S(1)} %get-tuple-element.46), channel_id=1, source_target_pairs={{0,2},{1,3},{2,0},{3,1},{4,6},{5,7},{6,4},{7,5},{8,10},{9,11},{10,... | collective-permute-start | bytes 614408 | tf_op jit(solution)/shard_map/ppermute | solution.py:440
  11.7 2.2 %shard_map.106 = (bf16[12,128,128]{2,1,0:T(8,128)(2,1)S(1)}, bf16[800,128]{1,0:T(8,128)(2,1)S(1)}) custom-call(s32[24]{0:T(128)} %counts_hbm.3, bf16[24,256,128]{2,1,0:T(8,128)(2,1)} %basis_ref.1, f32[24,256]{1,0:T(8,128)} %weights_hbm.3), custom_call_target="tpu_custom_call" | custom-call | flops 201326592 | bytes 1376256 | tf_op jit(solution)/shard_map/pallas_call | solution.py:143
  14.6 3.5 %collective-permute-done.1.packed_ref = bf16[800,128]{1,0:T(8,128)(2,1)S(1)} collective-permute-done((bf16[800,128]{1,0:T(8,128)(2,1)S(1)}, bf16[800,128]{1,0:T(8,128)(2,1)S(1)}, u32[]{:S(2)}, u32[]{:S(2)}) %collective-permute-start.1) | collective-permute-done | bytes 204832 | tf_op jit(solution)/shard_map/ppermute | solution.py:440
  18.1 1.5 %collective-permute-start.4 = (s32[24,2]{1,0:T(8,128)S(1)}, s32[24,2]{1,0:T(8,128)S(1)}, u32[]{:S(2)}, u32[]{:S(2)}) collective-permute-start(s32[24,2]{1,0:T(8,128)S(1)} %copy.16.refs_0_.block_ref), channel_id=1, source_target_pairs={{0,2},{1,3},{2,0},{3,1},{4,6},{5,7},{6,4},{7,5},{8,10},{9,11},{10,... | collective-permute-start | bytes 584 | tf_op jit(solution)/shard_map/ppermute | solution.py:440
  20.1 0.9 shard_map.105.refs_6_
  21.0 1.0 collective-permute-done.4.refs_2_
  22.5 0.9 shard_map.107.refs_10_
  25.8 2.9 %shard_map.108 = (bf16[1024,128]{1,0:T(8,128)(2,1)S(1)}, f32[1024,128]{1,0:T(8,128)S(1)}, bf16[1024,128]{1,0:T(8,128)(2,1)S(1)}) custom-call(s32[24,2]{1,0:T(8,128)S(1)} %copy.16.refs_0_.block_ref, s32[24,2]{1,0:T(8,128)S(1)} %collective-permute-done.refs_1_.block_ref, s32[24,2]{1,0:T(8,128)S(1)} %collective-permute-done.4.refs_2_, ...), custom_call_target="tpu_custom_call" | custom-call | flops 402653184 | bytes 4980736 | tf_op jit(solution)/shard_map/pallas_call | solution.py:253
  28.7 4.7 %collective-permute-start.14 = (bf16[1024,128]{1,0:T(8,128)(2,1)S(1)}, bf16[1024,128]{1,0:T(8,128)(2,1)S(1)}, u32[]{:S(2)}, u32[]{:S(2)}) collective-permute-start(bf16[1024,128]{1,0:T(8,128)(2,1)S(1)} %get-tuple-element.58), channel_id=1, source_target_pairs={{4,0},{8,4},{12,8},{16,12},{20,16},{24,20},{28,24},{0,28},{5,1},{9... | collective-permute-start | bytes 786440 | tf_op jit(solution)/shard_map/ppermute | solution.py:593
  33.5 2.1 %shard_map.109 = bf16[1024,1920]{1,0:T(8,128)(2,1)S(1)} custom-call(bf16[1024,1920]{1,0:T(8,128)(2,1)} %refs_0_.2), custom_call_target="tpu_custom_call" | custom-call | bytes 7864320 | tf_op jit(solution)/shard_map/pallas_call | solution.py:47
  35.7 1.9 %copy-done = bf16[1024,1920]{1,0:T(8,128)(2,1)} copy-done((bf16[1024,1920]{1,0:T(8,128)(2,1)}, bf16[1024,1920]{1,0:T(8,128)(2,1)S(1)}, u32[]{:S(2)}) %copy-start) | copy-done | bytes 3932184
  37.7 2.1 %shard_map.110 = bf16[1024,1920]{1,0:T(8,128)(2,1)S(1)} custom-call(bf16[1024,1920]{1,0:T(8,128)(2,1)} %collective-permute-done.12.source_ref.second_ref.refs_1_), custom_call_target="tpu_custom_call" | custom-call | bytes 7864320 | tf_op jit(solution)/shard_map/pallas_call | solution.py:47
  40.5 2.4 %collective-permute-done.14 = bf16[1024,128]{1,0:T(8,128)(2,1)S(1)} collective-permute-done((bf16[1024,128]{1,0:T(8,128)(2,1)S(1)}, bf16[1024,128]{1,0:T(8,128)(2,1)S(1)}, u32[]{:S(2)}, u32[]{:S(2)}) %collective-permute-start.14) | collective-permute-done | bytes 262176 | tf_op jit(solution)/shard_map/ppermute | solution.py:593
  43.0 1.5 %collective-permute-start.20 = (bf16[1024,128]{1,0:T(8,128)(2,1)S(1)}, bf16[1024,128]{1,0:T(8,128)(2,1)S(1)}, u32[]{:S(2)}, u32[]{:S(2)}) collective-permute-start(bf16[1024,128]{1,0:T(8,128)(2,1)S(1)} %add_convert_fusion.1), channel_id=1, source_target_pairs={{0,2},{1,3},{2,0},{3,1},{4,6},{5,7},{6,4},{7,5},{8,10},{9,11},{10,... | collective-permute-start | bytes 786440 | tf_op jit(solution)/shard_map/ppermute | solution.py:440
  46.3 4.4 %collective-permute-done.20 = bf16[1024,128]{1,0:T(8,128)(2,1)S(1)} collective-permute-done((bf16[1024,128]{1,0:T(8,128)(2,1)S(1)}, bf16[1024,128]{1,0:T(8,128)(2,1)S(1)}, u32[]{:S(2)}, u32[]{:S(2)}) %collective-permute-start.20) | collective-permute-done | bytes 262176 | tf_op jit(solution)/shard_map/ppermute | solution.py:440
  52.6 2.4 %collective-permute-done.15 = bf16[2,64,1920]{2,1,0:T(8,128)(2,1)S(1)} collective-permute-done((bf16[2,64,1920]{2,1,0:T(8,128)(2,1)S(1)}, bf16[2,64,1920]{2,1,0:T(8,128)(2,1)S(1)}, u32[]{:S(2)}, u32[]{:S(2)}) %collective-permute-start.15) | collective-permute-done | bytes 491552 | tf_op jit(solution)/shard_map/ppermute | solution.py:469
  55.3 10.7 %collective-permute-done.21 = bf16[2,64,1920]{2,1,0:T(8,128)(2,1)S(1)} collective-permute-done((bf16[2,64,1920]{2,1,0:T(8,128)(2,1)S(1)}, bf16[2,64,1920]{2,1,0:T(8,128)(2,1)S(1)}, u32[]{:S(2)}, u32[]{:S(2)}) %collective-permute-start.21) | collective-permute-done | bytes 491552 | tf_op jit(solution)/shard_map/ppermute | solution.py:469
  66.2 3.1 %collective-permute-start.17 = (bf16[2,32,1920]{2,1,0:T(8,128)(2,1)S(1)}, bf16[2,32,1920]{2,1,0:T(8,128)(2,1)S(1)}, u32[]{:S(2)}, u32[]{:S(2)}) collective-permute-start(bf16[2,32,1920]{2,1,0:T(8,128)(2,1)S(1)} %get-tuple-element.63), channel_id=1, source_target_pairs={{0,16},{4,20},{8,24},{12,28},{16,0},{20,4},{24,8},{28,12},{1,17},{... | collective-permute-start | bytes 737288 | tf_op jit(solution)/shard_map/ppermute | solution.py:440
  69.3 2.0 %collective-permute-start.19 = (bf16[1024,128]{1,0:T(8,128)(2,1)S(1)}, bf16[1024,128]{1,0:T(8,128)(2,1)S(1)}, u32[]{:S(2)}, u32[]{:S(2)}) collective-permute-start(bf16[1024,128]{1,0:T(8,128)(2,1)S(1)} %collective-permute-done.3.refs_14_.refs_4_), channel_id=1, source_target_pairs={{0,2},{1,3},{2,0},{3,1},{4,6},{5,7},{6,4},{7,5},{8,10},{9,11},{10,... | collective-permute-start | bytes 786440 | tf_op jit(solution)/shard_map/ppermute | solution.py:440
  71.3 3.7 %collective-permute-done.22 = bf16[2,32,1920]{2,1,0:T(8,128)(2,1)S(1)} collective-permute-done((bf16[2,32,1920]{2,1,0:T(8,128)(2,1)S(1)}, bf16[2,32,1920]{2,1,0:T(8,128)(2,1)S(1)}, u32[]{:S(2)}, u32[]{:S(2)}) %collective-permute-start.22) | collective-permute-done | bytes 245792 | tf_op jit(solution)/shard_map/ppermute | solution.py:469
  75.1 0.7 fusion.8
  76.4 7.3 %collective-permute-done.17.refs_1_ = bf16[2,32,1920]{2,1,0:T(8,128)(2,1)S(1)} collective-permute-done((bf16[2,32,1920]{2,1,0:T(8,128)(2,1)S(1)}, bf16[2,32,1920]{2,1,0:T(8,128)(2,1)S(1)}, u32[]{:S(2)}, u32[]{:S(2)}) %collective-permute-start.17) | collective-permute-done | bytes 245792 | tf_op jit(solution)/shard_map/ppermute | solution.py:440
  83.8 2.6 %collective-permute-done.23.refs_4_ = bf16[2,32,1920]{2,1,0:T(8,128)(2,1)S(1)} collective-permute-done((bf16[2,32,1920]{2,1,0:T(8,128)(2,1)}, bf16[2,32,1920]{2,1,0:T(8,128)(2,1)S(1)}, u32[]{:S(2)}, u32[]{:S(2)}) %collective-permute-start.23) | collective-permute-done | bytes 245792 | tf_op jit(solution)/shard_map/ppermute | solution.py:440
  86.4 0.9 shard_map.111
  87.4 2.0 %collective-permute-start.24 = (bf16[2,32,1920]{2,1,0:T(8,128)(2,1)S(1)}, bf16[2,32,1920]{2,1,0:T(8,128)(2,1)S(1)}, u32[]{:S(2)}, u32[]{:S(2)}) collective-permute-start(bf16[2,32,1920]{2,1,0:T(8,128)(2,1)S(1)} %get-tuple-element.74), channel_id=1, source_target_pairs={{0,8},{1,5},{2,10},{3,7},{4,12},{5,1},{6,14},{7,3},{8,0},{9,13},{1... | collective-permute-start | bytes 737288 | tf_op jit(solution)/shard_map/ppermute | solution.py:469
  89.4 4.5 %collective-permute-done.26 = bf16[2,32,1920]{2,1,0:T(8,128)(2,1)S(1)} collective-permute-done((bf16[2,32,1920]{2,1,0:T(8,128)(2,1)}, bf16[2,32,1920]{2,1,0:T(8,128)(2,1)S(1)}, u32[]{:S(2)}, u32[]{:S(2)}) %collective-permute-start.26) | collective-permute-done | bytes 245792 | tf_op jit(solution)/shard_map/ppermute | solution.py:469
  93.9 1.0 broadcast_select_fusion.3
  94.9 1.3 collective-permute-start.27
  96.2 2.9 %collective-permute-done.24 = bf16[2,32,1920]{2,1,0:T(8,128)(2,1)S(1)} collective-permute-done((bf16[2,32,1920]{2,1,0:T(8,128)(2,1)S(1)}, bf16[2,32,1920]{2,1,0:T(8,128)(2,1)S(1)}, u32[]{:S(2)}, u32[]{:S(2)}) %collective-permute-start.24) | collective-permute-done | bytes 245792 | tf_op jit(solution)/shard_map/ppermute | solution.py:469
  99.2 1.3 collective-permute-start.25
  100.5 3.3 %shard_map.112 = (bf16[1024,1920]{1,0:T(8,128)(2,1)S(1)}, bf16[1024,1920]{1,0:T(8,128)(2,1)S(1)}) custom-call(bf16[1024,1920]{1,0:T(8,128)(2,1)} %refs_0_.2, bf16[1024,1920]{1,0:T(8,128)(2,1)} %collective-permute-done.12.source_ref.second_ref.refs_1_), custom_call_target="tpu_custom_call" | custom-call | bytes 15728640 | tf_op jit(solution)/shard_map/pallas_call | solution.py:67
  103.9 2.3 %shard_map.113.refs_2_ = bf16[1024,128]{1,0:T(8,128)(2,1)S(1)} custom-call(s32[1]{0:T(128)} %bitcast.3.first_ref, bf16[2,64,1920]{2,1,0:T(8,128)(2,1)S(1)} %pad_maximum_fusion.2.part_ref, bf16[2,64,1920]{2,1,0:T(8,128)(2,1)S(1)} %collective-permute-done.27.coming_ref, bf16[1024,1920]{1,0:T(8,128)(2,1)S(1)} %get-tuple-element.78.refs_0_, ...), custom_call_target="tpu_custom_call" | custom-call | flops 1006632960 | bytes 7864320 | tf_op jit(solution)/shard_map/pallas_call | solution.py:315
  106.4 2.7 %collective-permute-done.25.coming_ref = bf16[2,64,1920]{2,1,0:T(8,128)(2,1)S(1)} collective-permute-done((bf16[2,64,1920]{2,1,0:T(8,128)(2,1)S(1)}, bf16[2,64,1920]{2,1,0:T(8,128)(2,1)S(1)}, u32[]{:S(2)}, u32[]{:S(2)}) %collective-permute-start.25) | collective-permute-done | bytes 491552 | tf_op jit(solution)/shard_map/ppermute | solution.py:469
  109.1 4.5 %shard_map.114 = f32[1024,128]{1,0:T(8,128)S(1)} custom-call(s32[1]{0:T(128)} %bitcast.3.first_ref, bf16[2,64,1920]{2,1,0:T(8,128)(2,1)S(1)} %pad_maximum_fusion.1.part_ref, bf16[2,64,1920]{2,1,0:T(8,128)(2,1)S(1)} %collective-permute-done.25.coming_ref, bf16[1024,1920]{1,0:T(8,128)(2,1)} %refs_0_.2, ...), custom_call_target="tpu_custom_call" | custom-call | tf_op jit(solution)/shard_map/pallas_call | solution.py:315
  113.7 3.7 %collective-permute-start.32 = (bf16[1024,128]{1,0:T(8,128)(2,1)S(1)}, bf16[1024,128]{1,0:T(8,128)(2,1)S(1)}, u32[]{:S(2)}, u32[]{:S(2)}) collective-permute-start(bf16[1024,128]{1,0:T(8,128)(2,1)S(1)} %add_convert_fusion.refs_8_), channel_id=1, source_target_pairs={{4,0},{8,4},{12,8},{16,12},{20,16},{24,20},{28,24},{0,28},{5,1},{9... | collective-permute-start | bytes 786440 | tf_op jit(solution)/shard_map/ppermute | solution.py:446
  117.4 3.9 %collective-permute-done.32.refs_10_ = bf16[1024,128]{1,0:T(8,128)(2,1)S(1)} collective-permute-done((bf16[1024,128]{1,0:T(8,128)(2,1)S(1)}, bf16[1024,128]{1,0:T(8,128)(2,1)S(1)}, u32[]{:S(2)}, u32[]{:S(2)}) %collective-permute-start.32) | collective-permute-done | bytes 262176 | tf_op jit(solution)/shard_map/ppermute | solution.py:446
  121.3 3.2 %collective-permute-done.31.refs_9_ = bf16[1024,128]{1,0:T(8,128)(2,1)S(1)} collective-permute-done((bf16[1024,128]{1,0:T(8,128)(2,1)S(1)}, bf16[1024,128]{1,0:T(8,128)(2,1)S(1)}, u32[]{:S(2)}, u32[]{:S(2)}) %collective-permute-start.31) | collective-permute-done | bytes 262176 | tf_op jit(solution)/shard_map/ppermute | solution.py:440
  124.5 2.0 %collective-permute-done.29.refs_6_ = bf16[1024,128]{1,0:T(8,128)(2,1)S(1)} collective-permute-done((bf16[1024,128]{1,0:T(8,128)(2,1)S(1)}, bf16[1024,128]{1,0:T(8,128)(2,1)S(1)}, u32[]{:S(2)}, u32[]{:S(2)}) %collective-permute-start.29) | collective-permute-done | bytes 262176 | tf_op jit(solution)/shard_map/ppermute | solution.py:445
  126.5 2.0 %collective-permute-start.30 = (bf16[1024,128]{1,0:T(8,128)(2,1)S(1)}, bf16[1024,128]{1,0:T(8,128)(2,1)S(1)}, u32[]{:S(2)}, u32[]{:S(2)}) collective-permute-start(bf16[1024,128]{1,0:T(8,128)(2,1)S(1)} %collective-permute-done.29.refs_6_), channel_id=1, source_target_pairs={{0,2},{1,3},{2,0},{3,1},{4,6},{5,7},{6,4},{7,5},{8,10},{9,11},{10,... | collective-permute-start | bytes 786440 | tf_op jit(solution)/shard_map/ppermute | solution.py:440
  128.5 3.9 %collective-permute-done.33.refs_11_ = bf16[1024,128]{1,0:T(8,128)(2,1)S(1)} collective-permute-done((bf16[1024,128]{1,0:T(8,128)(2,1)S(1)}, bf16[1024,128]{1,0:T(8,128)(2,1)S(1)}, u32[]{:S(2)}, u32[]{:S(2)}) %collective-permute-start.33) | collective-permute-done | bytes 262176 | tf_op jit(solution)/shard_map/ppermute | solution.py:440
  132.4 2.8 %collective-permute-done.30.refs_7_ = bf16[1024,128]{1,0:T(8,128)(2,1)S(1)} collective-permute-done((bf16[1024,128]{1,0:T(8,128)(2,1)S(1)}, bf16[1024,128]{1,0:T(8,128)(2,1)S(1)}, u32[]{:S(2)}, u32[]{:S(2)}) %collective-permute-start.30) | collective-permute-done | bytes 262176 | tf_op jit(solution)/shard_map/ppermute | solution.py:440
  135.2 2.0 %shard_map.115 = (bf16[24,128,128]{2,1,0:T(8,128)(2,1)S(1)}, bf16[3072,256]{1,0:T(8,128)(2,1)S(1)}, bf16[3072,256]{1,0:T(8,128)(2,1)S(1)}) custom-call(s32[24,2]{1,0:T(8,128)S(1)} %copy-done.7, bf16[1024,128]{1,0:T(8,128)(2,1)S(1)} %collective-permute-done.2.refs_12_.refs_0_, bf16[1024,128]{1,0:T(8,128)(2,1)S(1)} %collective-permute-done.18.refs_1_, ...), custom_call_target="tpu_custom_call" | custom-call | flops 201326592 | bytes 3932160 | tf_op jit(solution)/shard_map/pallas_call | solution.py:362
  138.0 1.3 shard_map.116.first_ref
  139.3 1.0 collective-permute-done.35.near_ref
  140.3 2.4 %shard_map.117 = (f32[24,256]{1,0:T(8,128)}, bf16[1024,512]{1,0:T(8,128)(2,1)}) custom-call(s32[1]{0:T(128)} %bitcast.core_ref, bf16[24,256,128]{2,1,0:T(8,128)(2,1)S(1)} %copy-done.2, f32[24,128,128]{2,1,0:T(8,128)S(1)} %shard_map.116.first_ref, bf16[24,128,128]{2,1,0:T(8,128)(2,1)S(1)} %collective-permute-done.34.second_ref, f32[24,256]{1,0:T(8,128)S(1)} %copy-done.5, ...), custom_call_target="tpu_custom_call" | custom-call | flops 402653184 | bytes 3932160 | tf_op jit(solution)/shard_map/pallas_call | solution.py:421
  (93 shorter events, 11.4 us)
Async XLA Ops:
  0.6 23.4 %copy-start.10 = (s32[24]{0:T(128)S(1)}, s32[24]{0:T(128)}, u32[]{:S(2)}) copy-start(s32[24]{0:T(128)} %counts_hbm.3) | copy-start | bytes 292
  0.6 13.8 %copy-start.11 = (s32[24,2]{0,1:T(2,128)S(1)}, s32[24,2]{0,1:T(2,128)}, u32[]{:S(2)}) copy-start(s32[24,2]{0,1:T(2,128)} %param.10) | copy-start | bytes 580
  0.7 23.3 %copy-start.8 = (f32[24,256]{1,0:T(8,128)S(1)}, f32[24,256]{1,0:T(8,128)}, u32[]{:S(2)}) copy-start(f32[24,256]{1,0:T(8,128)} %param.13) | copy-start | bytes 73732
  0.7 24.0 %copy-start.9 = (f32[1920]{0:T(1024)S(1)}, f32[1920]{0:T(1024)}, u32[]{:S(2)}) copy-start(f32[1920]{0:T(1024)} %param.17) | copy-start | bytes 23044
  0.7 37.0 %collective-permute-start.12 = (bf16[1024,1920]{1,0:T(8,128)(2,1)}, bf16[1024,1920]{1,0:T(8,128)(2,1)}, u32[]{:S(2)}, u32[]{:S(2)}) collective-permute-start(bf16[1024,1920]{1,0:T(8,128)(2,1)} %refs_0_.2), channel_id=1, source_target_pairs={{0,1},{1,0},{2,3},{3,2},{4,5},{5,4},{6,7},{7,6},{8,9},{9,8},{10,11... | collective-permute-start | bytes 11796488 | tf_op jit(solution)/shard_map/ppermute | solution.py:440
  2.3 31.2 %copy-start.12 = (f32[512]{0:T(512)S(1)}, f32[512]{0:T(512)}, u32[]{:S(2)}) copy-start(f32[512]{0:T(512)} %param.16) | copy-start | bytes 6148
  2.3 17.3 %collective-permute-start.3 = (bf16[1024,128]{1,0:T(8,128)(2,1)S(1)}, bf16[1024,128]{1,0:T(8,128)(2,1)S(1)}, u32[]{:S(2)}, u32[]{:S(2)}) collective-permute-start(bf16[1024,128]{1,0:T(8,128)(2,1)S(1)} %get-tuple-element.95.refs_13_.refs_2_), channel_id=1, source_target_pairs={{4,0},{8,4},{12,8},{16,12},{20,16},{24,20},{28,24},{0,28},{5,1},{9... | collective-permute-start | bytes 786440 | tf_op jit(solution)/shard_map/ppermute | solution.py:446
  7.9 11.7 %collective-permute-start.2 = (bf16[1024,128]{1,0:T(8,128)(2,1)S(1)}, bf16[1024,128]{1,0:T(8,128)(2,1)S(1)}, u32[]{:S(2)}, u32[]{:S(2)}) collective-permute-start(bf16[1024,128]{1,0:T(8,128)(2,1)S(1)} %get-tuple-element.95.refs_13_.refs_2_), channel_id=1, source_target_pairs={{0,4},{4,8},{8,12},{12,16},{16,20},{20,24},{24,28},{28,0},{1,5},{5... | collective-permute-start | bytes 786440 | tf_op jit(solution)/shard_map/ppermute | solution.py:445
  10.1 8.0 %collective-permute-start.1 = (bf16[800,128]{1,0:T(8,128)(2,1)S(1)}, bf16[800,128]{1,0:T(8,128)(2,1)S(1)}, u32[]{:S(2)}, u32[]{:S(2)}) collective-permute-start(bf16[800,128]{1,0:T(8,128)(2,1)S(1)} %get-tuple-element.46), channel_id=1, source_target_pairs={{0,2},{1,3},{2,0},{3,1},{4,6},{5,7},{6,4},{7,5},{8,10},{9,11},{10,... | collective-permute-start | bytes 614408 | tf_op jit(solution)/shard_map/ppermute | solution.py:440
  13.9 8.1 %collective-permute-start.9 = (bf16[800,128]{1,0:T(8,128)(2,1)S(1)}, bf16[800,128]{1,0:T(8,128)(2,1)S(1)}, u32[]{:S(2)}, u32[]{:S(2)}) collective-permute-start(bf16[800,128]{1,0:T(8,128)(2,1)S(1)} %get-tuple-element.52), channel_id=1, source_target_pairs={{0,2},{1,3},{2,0},{3,1},{4,6},{5,7},{6,4},{7,5},{8,10},{9,11},{10,... | collective-permute-start | bytes 614408 | tf_op jit(solution)/shard_map/ppermute | solution.py:440
  14.6 21.1 %copy-start.3 = (s32[24,2]{1,0:T(8,128)}, s32[24,2]{1,0:T(8,128)S(1)}, u32[]{:S(2)}) copy-start(s32[24,2]{1,0:T(8,128)S(1)} %copy.16.refs_0_.block_ref) | copy-start | bytes 580
  18.1 3.9 %collective-permute-start.4 = (s32[24,2]{1,0:T(8,128)S(1)}, s32[24,2]{1,0:T(8,128)S(1)}, u32[]{:S(2)}, u32[]{:S(2)}) collective-permute-start(s32[24,2]{1,0:T(8,128)S(1)} %copy.16.refs_0_.block_ref), channel_id=1, source_target_pairs={{0,2},{1,3},{2,0},{3,1},{4,6},{5,7},{6,4},{7,5},{8,10},{9,11},{10,... | collective-permute-start | bytes 584 | tf_op jit(solution)/shard_map/ppermute | solution.py:440
  19.6 3.8 %collective-permute-start = (s32[24,2]{1,0:T(8,128)S(1)}, s32[24,2]{1,0:T(8,128)S(1)}, u32[]{:S(2)}, u32[]{:S(2)}) collective-permute-start(s32[24,2]{1,0:T(8,128)S(1)} %copy.16.refs_0_.block_ref), channel_id=1, source_target_pairs={{0,1},{1,0},{2,3},{3,2},{4,5},{5,4},{6,7},{7,6},{8,9},{9,8},{10,11... | collective-permute-start | bytes 584 | tf_op jit(solution)/shard_map/ppermute | solution.py:440
  19.6 5.0 %collective-permute-start.8 = (bf16[12,128,128]{2,1,0:T(8,128)(2,1)S(1)}, bf16[12,128,128]{2,1,0:T(8,128)(2,1)S(1)}, u32[]{:S(2)}, u32[]{:S(2)}) collective-permute-start(bf16[12,128,128]{2,1,0:T(8,128)(2,1)S(1)} %get-tuple-element.51.refs_8_), channel_id=1, source_target_pairs={{0,1},{1,0},{2,3},{3,2},{4,5},{5,4},{6,7},{7,6},{8,9},{9,8},{10,11... | collective-permute-start | bytes 1179656 | tf_op jit(solution)/shard_map/ppermute | solution.py:440
  22.0 2.9 %collective-permute-start.6 = (bf16[12,128,128]{2,1,0:T(8,128)(2,1)S(1)}, bf16[12,128,128]{2,1,0:T(8,128)(2,1)S(1)}, u32[]{:S(2)}, u32[]{:S(2)}) collective-permute-start(bf16[12,128,128]{2,1,0:T(8,128)(2,1)S(1)} %get-tuple-element.49.refs_4_), channel_id=1, source_target_pairs={{0,1},{1,0},{2,3},{3,2},{4,5},{5,4},{6,7},{7,6},{8,9},{9,8},{10,11... | collective-permute-start | bytes 1179656 | tf_op jit(solution)/shard_map/ppermute | solution.py:440
  22.0 1.7 %collective-permute-start.5 = (s32[24,2]{1,0:T(8,128)S(1)}, s32[24,2]{1,0:T(8,128)S(1)}, u32[]{:S(2)}, u32[]{:S(2)}) collective-permute-start(s32[24,2]{1,0:T(8,128)S(1)} %collective-permute-done.4.refs_2_), channel_id=1, source_target_pairs={{0,1},{1,0},{2,3},{3,2},{4,5},{5,4},{6,7},{7,6},{8,9},{9,8},{10,11... | collective-permute-start | bytes 584 | tf_op jit(solution)/shard_map/ppermute | solution.py:440
  23.4 12.2 %copy-start.6 = (s32[24,2]{1,0:T(8,128)}, s32[24,2]{1,0:T(8,128)S(1)}, u32[]{:S(2)}) copy-start(s32[24,2]{1,0:T(8,128)S(1)} %collective-permute-done.refs_1_.block_ref) | copy-start | bytes 580
  23.4 1.8 %collective-permute-start.10 = (bf16[12,128,128]{2,1,0:T(8,128)(2,1)S(1)}, bf16[12,128,128]{2,1,0:T(8,128)(2,1)S(1)}, u32[]{:S(2)}, u32[]{:S(2)}) collective-permute-start(bf16[12,128,128]{2,1,0:T(8,128)(2,1)S(1)} %shard_map.107.refs_10_), channel_id=1, source_target_pairs={{0,1},{1,0},{2,3},{3,2},{4,5},{5,4},{6,7},{7,6},{8,9},{9,8},{10,11... | collective-permute-start | bytes 1179656 | tf_op jit(solution)/shard_map/ppermute | solution.py:440
  23.8 2.0 %collective-permute-start.7 = (bf16[12,128,128]{2,1,0:T(8,128)(2,1)S(1)}, bf16[12,128,128]{2,1,0:T(8,128)(2,1)S(1)}, u32[]{:S(2)}, u32[]{:S(2)}) collective-permute-start(bf16[12,128,128]{2,1,0:T(8,128)(2,1)S(1)} %shard_map.105.refs_6_), channel_id=1, source_target_pairs={{0,1},{1,0},{2,3},{3,2},{4,5},{5,4},{6,7},{7,6},{8,9},{9,8},{10,11... | collective-permute-start | bytes 1179656 | tf_op jit(solution)/shard_map/ppermute | solution.py:440
  24.7 13.0 %collective-permute-start.11 = (f32[1920]{0:T(1024)S(1)}, f32[1920]{0:T(1024)S(1)}, u32[]{:S(2)}, u32[]{:S(2)}) collective-permute-start(f32[1920]{0:T(1024)S(1)} %copy-done.9), channel_id=1, source_target_pairs={{0,1},{1,0},{2,3},{3,2},{4,5},{5,4},{6,7},{7,6},{8,9},{9,8},{10,11... | collective-permute-start | bytes 23048 | tf_op jit(solution)/shard_map/ppermute | solution.py:440
  28.7 11.8 %collective-permute-start.13 = (bf16[1024,128]{1,0:T(8,128)(2,1)S(1)}, bf16[1024,128]{1,0:T(8,128)(2,1)S(1)}, u32[]{:S(2)}, u32[]{:S(2)}) collective-permute-start(bf16[1024,128]{1,0:T(8,128)(2,1)S(1)} %get-tuple-element.57), channel_id=1, source_target_pairs={{0,4},{4,8},{8,12},{12,16},{16,20},{20,24},{24,28},{28,0},{1,5},{5... | collective-permute-start | bytes 786440 | tf_op jit(solution)/shard_map/ppermute | solution.py:592
  28.7 14.2 %collective-permute-start.14 = (bf16[1024,128]{1,0:T(8,128)(2,1)S(1)}, bf16[1024,128]{1,0:T(8,128)(2,1)S(1)}, u32[]{:S(2)}, u32[]{:S(2)}) collective-permute-start(bf16[1024,128]{1,0:T(8,128)(2,1)S(1)} %get-tuple-element.58), channel_id=1, source_target_pairs={{4,0},{8,4},{12,8},{16,12},{20,16},{24,20},{28,24},{0,28},{5,1},{9... | collective-permute-start | bytes 786440 | tf_op jit(solution)/shard_map/ppermute | solution.py:593
  39.8 5.5 %copy-start.1 = (bf16[1024,1920]{1,0:T(8,128)(2,1)S(1)}, bf16[1024,1920]{1,0:T(8,128)(2,1)}, u32[]{:S(2)}) copy-start(bf16[1024,1920]{1,0:T(8,128)(2,1)} %copy-done) | copy-start | bytes 11796484
  43.0 7.6 %collective-permute-start.20 = (bf16[1024,128]{1,0:T(8,128)(2,1)S(1)}, bf16[1024,128]{1,0:T(8,128)(2,1)S(1)}, u32[]{:S(2)}, u32[]{:S(2)}) collective-permute-start(bf16[1024,128]{1,0:T(8,128)(2,1)S(1)} %add_convert_fusion.1), channel_id=1, source_target_pairs={{0,2},{1,3},{2,0},{3,1},{4,6},{5,7},{6,4},{7,5},{8,10},{9,11},{10,... | collective-permute-start | bytes 786440 | tf_op jit(solution)/shard_map/ppermute | solution.py:440
  46.1 8.9 %collective-permute-start.15 = (bf16[2,64,1920]{2,1,0:T(8,128)(2,1)S(1)}, bf16[2,64,1920]{2,1,0:T(8,128)(2,1)S(1)}, u32[]{:S(2)}, u32[]{:S(2)}) collective-permute-start(bf16[2,64,1920]{2,1,0:T(8,128)(2,1)S(1)} %fusion.5), channel_id=1, source_target_pairs={{0,4},{1,9},{2,6},{3,11},{4,0},{5,13},{6,2},{7,15},{8,12},{9,1},{1... | collective-permute-start | bytes 1474568 | tf_op jit(solution)/shard_map/ppermute | solution.py:469
  52.2 13.8 %collective-permute-start.21 = (bf16[2,64,1920]{2,1,0:T(8,128)(2,1)S(1)}, bf16[2,64,1920]{2,1,0:T(8,128)(2,1)S(1)}, u32[]{:S(2)}, u32[]{:S(2)}) collective-permute-start(bf16[2,64,1920]{2,1,0:T(8,128)(2,1)S(1)} %fusion.1), channel_id=1, source_target_pairs={{0,4},{1,9},{2,6},{3,11},{4,0},{5,13},{6,2},{7,15},{8,12},{9,1},{1... | collective-permute-start | bytes 1474568 | tf_op jit(solution)/shard_map/ppermute | solution.py:469
  55.2 11.0 %collective-permute-start.16 = (bf16[2,32,1920]{2,1,0:T(8,128)(2,1)S(1)}, bf16[2,32,1920]{2,1,0:T(8,128)(2,1)S(1)}, u32[]{:S(2)}, u32[]{:S(2)}) collective-permute-start(bf16[2,32,1920]{2,1,0:T(8,128)(2,1)S(1)} %dynamic-slice_convert_fusion.1), channel_id=1, source_target_pairs={{0,8},{1,5},{2,10},{3,7},{4,12},{5,1},{6,14},{7,3},{8,0},{9,13},{1... | collective-permute-start | bytes 737288 | tf_op jit(solution)/shard_map/ppermute | solution.py:469
  66.1 9.0 %collective-permute-start.22 = (bf16[2,32,1920]{2,1,0:T(8,128)(2,1)S(1)}, bf16[2,32,1920]{2,1,0:T(8,128)(2,1)S(1)}, u32[]{:S(2)}, u32[]{:S(2)}) collective-permute-start(bf16[2,32,1920]{2,1,0:T(8,128)(2,1)S(1)} %dynamic-slice_convert_fusion), channel_id=1, source_target_pairs={{0,8},{1,5},{2,10},{3,7},{4,12},{5,1},{6,14},{7,3},{8,0},{9,13},{1... | collective-permute-start | bytes 737288 | tf_op jit(solution)/shard_map/ppermute | solution.py:469
  66.2 17.5 %collective-permute-start.17 = (bf16[2,32,1920]{2,1,0:T(8,128)(2,1)S(1)}, bf16[2,32,1920]{2,1,0:T(8,128)(2,1)S(1)}, u32[]{:S(2)}, u32[]{:S(2)}) collective-permute-start(bf16[2,32,1920]{2,1,0:T(8,128)(2,1)S(1)} %get-tuple-element.63), channel_id=1, source_target_pairs={{0,16},{4,20},{8,24},{12,28},{16,0},{20,4},{24,8},{28,12},{1,17},{... | collective-permute-start | bytes 737288 | tf_op jit(solution)/shard_map/ppermute | solution.py:440
  69.3 14.5 %collective-permute-start.18 = (bf16[1024,128]{1,0:T(8,128)(2,1)S(1)}, bf16[1024,128]{1,0:T(8,128)(2,1)S(1)}, u32[]{:S(2)}, u32[]{:S(2)}) collective-permute-start(bf16[1024,128]{1,0:T(8,128)(2,1)S(1)} %collective-permute-done.2.refs_12_.refs_0_), channel_id=1, source_target_pairs={{0,2},{1,3},{2,0},{3,1},{4,6},{5,7},{6,4},{7,5},{8,10},{9,11},{10,... | collective-permute-start | bytes 786440 | tf_op jit(solution)/shard_map/ppermute | solution.py:440
  69.3 14.5 %collective-permute-start.19 = (bf16[1024,128]{1,0:T(8,128)(2,1)S(1)}, bf16[1024,128]{1,0:T(8,128)(2,1)S(1)}, u32[]{:S(2)}, u32[]{:S(2)}) collective-permute-start(bf16[1024,128]{1,0:T(8,128)(2,1)S(1)} %collective-permute-done.3.refs_14_.refs_4_), channel_id=1, source_target_pairs={{0,2},{1,3},{2,0},{3,1},{4,6},{5,7},{6,4},{7,5},{8,10},{9,11},{10,... | collective-permute-start | bytes 786440 | tf_op jit(solution)/shard_map/ppermute | solution.py:440
  75.8 10.6 %collective-permute-start.23 = (bf16[2,32,1920]{2,1,0:T(8,128)(2,1)}, bf16[2,32,1920]{2,1,0:T(8,128)(2,1)S(1)}, u32[]{:S(2)}, u32[]{:S(2)}) collective-permute-start(bf16[2,32,1920]{2,1,0:T(8,128)(2,1)} %get-tuple-element.72), channel_id=1, source_target_pairs={{0,16},{4,20},{8,24},{12,28},{16,0},{20,4},{24,8},{28,12},{1,17},{... | collective-permute-start | bytes 737288 | tf_op jit(solution)/shard_map/ppermute | solution.py:440
  87.3 6.5 %collective-permute-start.26 = (bf16[2,32,1920]{2,1,0:T(8,128)(2,1)}, bf16[2,32,1920]{2,1,0:T(8,128)(2,1)S(1)}, u32[]{:S(2)}, u32[]{:S(2)}) collective-permute-start(bf16[2,32,1920]{2,1,0:T(8,128)(2,1)} %get-tuple-element.75), channel_id=1, source_target_pairs={{0,8},{1,5},{2,10},{3,7},{4,12},{5,1},{6,14},{7,3},{8,0},{9,13},{1... | collective-permute-start | bytes 737288 | tf_op jit(solution)/shard_map/ppermute | solution.py:469
  87.4 11.8 %collective-permute-start.24 = (bf16[2,32,1920]{2,1,0:T(8,128)(2,1)S(1)}, bf16[2,32,1920]{2,1,0:T(8,128)(2,1)S(1)}, u32[]{:S(2)}, u32[]{:S(2)}) collective-permute-start(bf16[2,32,1920]{2,1,0:T(8,128)(2,1)S(1)} %get-tuple-element.74), channel_id=1, source_target_pairs={{0,8},{1,5},{2,10},{3,7},{4,12},{5,1},{6,14},{7,3},{8,0},{9,13},{1... | collective-permute-start | bytes 737288 | tf_op jit(solution)/shard_map/ppermute | solution.py:469
  94.9 9.0 %collective-permute-start.27 = (bf16[2,64,1920]{2,1,0:T(8,128)(2,1)S(1)}, bf16[2,64,1920]{2,1,0:T(8,128)(2,1)S(1)}, u32[]{:S(2)}, u32[]{:S(2)}) collective-permute-start(bf16[2,64,1920]{2,1,0:T(8,128)(2,1)S(1)} %pad_maximum_fusion.2.part_ref), channel_id=1, source_target_pairs={{0,4},{1,9},{2,6},{3,11},{4,0},{5,13},{6,2},{7,15},{8,12},{9,1},{1... | collective-permute-start | bytes 1474568 | tf_op jit(solution)/shard_map/ppermute | solution.py:469
  99.2 9.8 %collective-permute-start.25 = (bf16[2,64,1920]{2,1,0:T(8,128)(2,1)S(1)}, bf16[2,64,1920]{2,1,0:T(8,128)(2,1)S(1)}, u32[]{:S(2)}, u32[]{:S(2)}) collective-permute-start(bf16[2,64,1920]{2,1,0:T(8,128)(2,1)S(1)} %pad_maximum_fusion.1.part_ref), channel_id=1, source_target_pairs={{0,4},{1,9},{2,6},{3,11},{4,0},{5,13},{6,2},{7,15},{8,12},{9,1},{1... | collective-permute-start | bytes 1474568 | tf_op jit(solution)/shard_map/ppermute | solution.py:469
  106.2 29.0 %copy-start.7 = (s32[24,2]{1,0:T(8,128)S(1)}, s32[24,2]{1,0:T(8,128)}, u32[]{:S(2)}) copy-start(s32[24,2]{1,0:T(8,128)} %copy-done.6) | copy-start | bytes 580
  106.2 7.4 %collective-permute-start.28 = (bf16[1024,128]{1,0:T(8,128)(2,1)S(1)}, bf16[1024,128]{1,0:T(8,128)(2,1)S(1)}, u32[]{:S(2)}, u32[]{:S(2)}) collective-permute-start(bf16[1024,128]{1,0:T(8,128)(2,1)S(1)} %shard_map.113.refs_2_), channel_id=1, source_target_pairs={{0,2},{1,3},{2,0},{3,1},{4,6},{5,7},{6,4},{7,5},{8,10},{9,11},{10,... | collective-permute-start | bytes 786440 | tf_op jit(solution)/shard_map/ppermute | solution.py:440
  113.6 24.4 %copy-start.4 = (s32[24,2]{1,0:T(8,128)S(1)}, s32[24,2]{1,0:T(8,128)}, u32[]{:S(2)}) copy-start(s32[24,2]{1,0:T(8,128)} %copy-done.3) | copy-start | bytes 580
  113.7 7.6 %collective-permute-start.32 = (bf16[1024,128]{1,0:T(8,128)(2,1)S(1)}, bf16[1024,128]{1,0:T(8,128)(2,1)S(1)}, u32[]{:S(2)}, u32[]{:S(2)}) collective-permute-start(bf16[1024,128]{1,0:T(8,128)(2,1)S(1)} %add_convert_fusion.refs_8_), channel_id=1, source_target_pairs={{4,0},{8,4},{12,8},{16,12},{20,16},{24,20},{28,24},{0,28},{5,1},{9... | collective-permute-start | bytes 786440 | tf_op jit(solution)/shard_map/ppermute | solution.py:446
  117.4 7.1 %collective-permute-start.31 = (bf16[1024,128]{1,0:T(8,128)(2,1)S(1)}, bf16[1024,128]{1,0:T(8,128)(2,1)S(1)}, u32[]{:S(2)}, u32[]{:S(2)}) collective-permute-start(bf16[1024,128]{1,0:T(8,128)(2,1)S(1)} %add_convert_fusion.refs_8_), channel_id=1, source_target_pairs={{0,2},{1,3},{2,0},{3,1},{4,6},{5,7},{6,4},{7,5},{8,10},{9,11},{10,... | collective-permute-start | bytes 786440 | tf_op jit(solution)/shard_map/ppermute | solution.py:440
  117.4 9.1 %collective-permute-start.29 = (bf16[1024,128]{1,0:T(8,128)(2,1)S(1)}, bf16[1024,128]{1,0:T(8,128)(2,1)S(1)}, u32[]{:S(2)}, u32[]{:S(2)}) collective-permute-start(bf16[1024,128]{1,0:T(8,128)(2,1)S(1)} %add_convert_fusion.refs_8_), channel_id=1, source_target_pairs={{0,4},{4,8},{8,12},{12,16},{16,20},{20,24},{24,28},{28,0},{1,5},{5... | collective-permute-start | bytes 786440 | tf_op jit(solution)/shard_map/ppermute | solution.py:445
  124.5 7.9 %collective-permute-start.33 = (bf16[1024,128]{1,0:T(8,128)(2,1)S(1)}, bf16[1024,128]{1,0:T(8,128)(2,1)S(1)}, u32[]{:S(2)}, u32[]{:S(2)}) collective-permute-start(bf16[1024,128]{1,0:T(8,128)(2,1)S(1)} %collective-permute-done.32.refs_10_), channel_id=1, source_target_pairs={{0,2},{1,3},{2,0},{3,1},{4,6},{5,7},{6,4},{7,5},{8,10},{9,11},{10,... | collective-permute-start | bytes 786440 | tf_op jit(solution)/shard_map/ppermute | solution.py:440
  126.5 8.7 %collective-permute-start.30 = (bf16[1024,128]{1,0:T(8,128)(2,1)S(1)}, bf16[1024,128]{1,0:T(8,128)(2,1)S(1)}, u32[]{:S(2)}, u32[]{:S(2)}) collective-permute-start(bf16[1024,128]{1,0:T(8,128)(2,1)S(1)} %collective-permute-done.29.refs_6_), channel_id=1, source_target_pairs={{0,2},{1,3},{2,0},{3,1},{4,6},{5,7},{6,4},{7,5},{8,10},{9,11},{10,... | collective-permute-start | bytes 786440 | tf_op jit(solution)/shard_map/ppermute | solution.py:440
  137.2 3.1 %copy-start.2 = (bf16[24,256,128]{2,1,0:T(8,128)(2,1)S(1)}, bf16[24,256,128]{2,1,0:T(8,128)(2,1)}, u32[]{:S(2)}) copy-start(bf16[24,256,128]{2,1,0:T(8,128)(2,1)} %basis_ref.1) | copy-start | bytes 4718596
  137.2 3.1 %copy-start.5 = (f32[24,256]{1,0:T(8,128)S(1)}, f32[24,256]{1,0:T(8,128)}, u32[]{:S(2)}) copy-start(f32[24,256]{1,0:T(8,128)} %multiply_select_fusion.scale_ref) | copy-start | bytes 73732
  137.2 3.1 %collective-permute-start.34 = (bf16[24,128,128]{2,1,0:T(8,128)(2,1)S(1)}, bf16[24,128,128]{2,1,0:T(8,128)(2,1)S(1)}, u32[]{:S(2)}, u32[]{:S(2)}) collective-permute-start(bf16[24,128,128]{2,1,0:T(8,128)(2,1)S(1)} %get-tuple-element.86), channel_id=1, source_target_pairs={{0,1},{1,0},{2,3},{3,2},{4,5},{5,4},{6,7},{7,6},{8,9},{9,8},{10,11... | collective-permute-start | bytes 2359304 | tf_op jit(solution)/shard_map/ppermute | solution.py:440
  137.4 2.9 %collective-permute-start.35 = (bf16[1024,256]{1,0:T(8,128)(2,1)S(1)}, bf16[1024,256]{1,0:T(8,128)(2,1)S(1)}, u32[]{:S(2)}, u32[]{:S(2)}) collective-permute-start(bf16[1024,256]{1,0:T(8,128)(2,1)S(1)} %pad_maximum_fusion.half_ref), channel_id=1, source_target_pairs={{0,1},{1,0},{2,3},{3,2},{4,5},{5,4},{6,7},{7,6},{8,9},{9,8},{10,11... | collective-permute-start | bytes 1572872 | tf_op jit(solution)/shard_map/ppermute | solution.py:440
  (1 other events, 1.9 us)
